TPU v7x, 32 devices: a whole 2x2x4 slice. The times are simulated.
32 devices in a mesh: parts: 2 (over y), node: 4 (over x, core), local: 4 (over z).
Axes of the slice: x: 2, y: 2, z: 4, core: 2. Of those that a mesh axis runs over, the one named last changes fastest.
Arguments:
- tokens: bfloat16 [2048, 7168], P(('parts', 'node', 'local')), parts along dimension 0, may hold values from -6 to 6
- expert_ids: int32 [2048, 2], P(('parts', 'node', 'local')), parts along dimension 0, may hold values from 0 to 31, all different within a row; in each aligned block of 64 rows (0 to 63, 64 to 127, ...) at most 5 rows name the same one
- gate_weights: float32 [2048, 2], P(('parts', 'node', 'local')), parts along dimension 0, may hold values from 0.1 to 1
- w_gate: bfloat16 [32, 7168, 1024], P('local', None, 'node'), may hold values from -0.0625 to 0.0625
- w_up: bfloat16 [32, 7168, 1024], P('local', None, 'node'), may hold values from -0.0625 to 0.0625
- w_down: bfloat16 [32, 1024, 7168], P('local', 'node'), may hold values from -0.1875 to 0.1875
Outputs:
- mixed: bfloat16 [2048, 7168], P(('parts', 'node', 'local')), parts along dimension 0
There are 2 independent parts, one for each index of `parts`. A program takes and returns all parts, laid end to end along the dimension named above; an argument that names none is the same for every part. Nothing has to cross between parts.
Inputs may be any that keep to these rules, and one draw needn't show every extreme that they name: `expert_ids`: A row names 2 different experts. In each aligned block of 64 rows (the tokens of one device) no expert is named by more than 5 rows, a bound that some block reaches.
All inputs are finite; a program needn't handle non-finite values.
Results may differ from a plain program's by a relative error of at most 0.012.
Values may be sent and summed in bfloat16 or wider, within the bound.
No kernel may reach another device: no remote copies, remote signals or barrier semaphores. Data moves between devices by JAX's collectives and lax.ppermute only.
A program may use at most 256 MiB of HBM per device.

v0:
```python
import jax
import jax.numpy as jnp
from jax import lax
from jax.sharding import PartitionSpec as P

CAP = 5


def pair_slots(id_block, experts):
    pair_ids = id_block.reshape(-1)
    onehot = (pair_ids[:, None] == jnp.arange(experts, dtype=jnp.int32)[None, :]).astype(jnp.int32)
    running = jnp.cumsum(onehot, axis=0)
    return (pair_ids, jnp.sum(running * onehot, axis=1) - 1)


def place_rows(source, target, slots_total, top_count):
    row_count, model_width = source.shape
    senders = jnp.repeat(jnp.arange(row_count, dtype=jnp.int32), top_count)
    owner_row = jnp.full((slots_total,), row_count, jnp.int32).at[target].set(senders)
    padded = jnp.concatenate([source, jnp.zeros((1, model_width), source.dtype)], axis=0)
    return jnp.take(padded, owner_row, axis=0)


def expert_block(slab_rows, w_gate, w_up, w_down):
    gate_part = jnp.einsum("ajsd,jdf->ajsf", slab_rows, w_gate, preferred_element_type=jnp.float32)
    up_part = jnp.einsum("ajsd,jdf->ajsf", slab_rows, w_up, preferred_element_type=jnp.float32)
    hidden = (jax.nn.silu(gate_part) * up_part).astype(jnp.bfloat16)
    return jnp.einsum("ajsf,jfd->ajsd", hidden, w_down, preferred_element_type=jnp.float32).astype(
        jnp.bfloat16
    )


def combine(table, target, gates, top_count):
    model_width = table.shape[-1]
    values = jnp.take(table, target, axis=0).reshape(-1, top_count, model_width)
    return jnp.sum(values * gates[:, :, None], axis=1)


def per_device(tokens, expert_ids, gate_weights, w_gate, w_up, w_down):
    tok_dev, model_width = tokens.shape
    top_count = expert_ids.shape[1]
    exp_dev = w_gate.shape[0]
    local_count = lax.axis_size("local")
    experts = exp_dev * local_count
    node_count = lax.axis_size("node")
    gathered = lax.all_gather(tokens, "node", axis=0, tiled=True)
    routing = jnp.concatenate([gate_weights, expert_ids.astype(jnp.float32)], axis=1)
    routing_all = lax.all_gather(routing, "node", axis=0, tiled=True)
    gates_all = routing_all[:, :top_count]
    ids_all = routing_all[:, top_count:].astype(jnp.int32).reshape(node_count, tok_dev, top_count)
    pair_ids, slot_of = jax.vmap(lambda id_block: pair_slots(id_block, experts))(ids_all)
    anchor = jnp.arange(node_count, dtype=jnp.int32)[:, None]
    target = ((pair_ids * node_count + anchor) * CAP + slot_of).reshape(-1)
    buffer = place_rows(gathered, target, experts * node_count * CAP, top_count)
    buffer = buffer.reshape(local_count, exp_dev, node_count * CAP, model_width)
    outputs = expert_block(
        lax.all_to_all(buffer, "local", split_axis=0, concat_axis=0, tiled=True),
        w_gate,
        w_up,
        w_down,
    )
    returned = lax.all_to_all(outputs, "local", split_axis=0, concat_axis=0, tiled=True)
    partial_value = combine(returned.reshape(-1, model_width), target, gates_all, top_count)
    summed = lax.psum_scatter(
        partial_value.astype(jnp.bfloat16), "node", scatter_dimension=0, tiled=True
    )
    return summed


def solution(mesh):
    return jax.shard_map(
        per_device,
        mesh=mesh,
        in_specs=(
            P(("parts", "node", "local"), None),
            P(("parts", "node", "local"), None),
            P(("parts", "node", "local"), None),
            P("local", None, "node"),
            P("local", None, "node"),
            P("local", "node", None),
        ),
        out_specs=P(("parts", "node", "local"), None),
        check_vma=False,
    )
```

profile of v0, /device:TPU:0, one launch (start us, length us, event | category | flops | bytes accessed | tf_op | source)
XLA Modules:
  0.0 762.6 jit_solution(18026642944660583075)
XLA Ops:
  6.5 0.0 all-gather.3.cloned.1.call-start
  6.5 0.7 all-gather.3.cloned.1.call-update
  7.3 0.7 convert_element_type.24
  7.9 0.7 maximum_bitcast_fusion
  8.6 6.1 all-gather
  14.7 0.1 reshape.121
  14.8 0.1 copy.19
  15.0 0.1 eq.15
  15.1 0.1 copy.22
  15.3 0.2 mul.64
  15.4 0.1 reshape.115
  15.6 0.1 fusion.34
  15.7 0.3 reduce_window_sum.11
  16.0 0.2 select_reduce_fusion
  16.3 2.4 scatter_custom_fusion
  18.7 0.1 broadcast_in_dim.38
  18.9 24.3 %all-gather.3.cloned.1.call-done = bf16[256,7168]{1,0:T(8,128)(2,1)} async-done(((bf16[64,7168]{1,0:T(8,128)(2,1)}), bf16[256,7168]{1,0:T(8,128)(2,1)}) %all-gather.3.cloned.1.call-update) | async-done | bytes 3670032 | tf_op jit(solution)/shard_map/all_gather | solution.py:46
  43.2 4.3 concatenate.7
  47.5 21.7 %gather_fusion = bf16[640,7168]{1,0:T(8,128)(2,1)} fusion(bf16[257,7168]{1,0:T(8,128)(2,1)} %concatenate.7, s32[1024]{0:T(1024)S(1)} %pad_clamp_fusion.1), kind=kCustom, calls=%fused_computation | custom fusion | bytes 18352640 | tf_op jit(solution)/shard_map/jit(_take)/gather | solution.py:21
  69.2 13.3 %gather.13 = bf16[4,8,20,7168]{3,2,1,0:T(8,128)(2,1)} reshape(bf16[640,7168]{1,0:T(8,128)(2,1)} %gather_fusion) | data formatting | bytes 18350080 | tf_op jit(solution)/shard_map/jit(_take)/gather | solution.py:21
  82.5 9.9 %broadcast_select_fusion.1 = bf16[4,8,20,7168]{3,2,1,0:T(8,128)(2,1)} fusion(bf16[4,8,20,7168]{3,2,1,0:T(8,128)(2,1)} %gather.13, pred[4,8,20]{2,1,0:T(8,128)(4,1)S(1)} %broadcast_in_dim.38), kind=kLoop, calls=%fused_computation.12 | loop fusion | flops 4587520 | bytes 18350720 | tf_op jit(solution)/shard_map/jit(_take)/select_n | solution.py:21
  92.3 12.6 %copy.23 = bf16[4,8,20,7168]{3,1,2,0:T(8,128)(2,1)} copy(bf16[4,8,20,7168]{3,2,1,0:T(8,128)(2,1)} %broadcast_select_fusion.1) | data formatting | bytes 18350080 | tf_op jit(solution)/shard_map/jit(_take)/select_n | solution.py:21
  105.0 208.7 %all_to_all.10 = bf16[4,8,20,7168]{3,1,2,0:T(8,128)(2,1)} all-to-all(bf16[4,8,20,7168]{3,1,2,0:T(8,128)(2,1)} %copy.23), channel_id=1, replica_groups=mesh['parts'=2,'node'=4,'local'=4] {'local'}, dimensions={0} | all-to-all | bytes 18350080 | tf_op jit(solution)/shard_map/all_to_all | solution.py:57
  313.7 15.4 %fusion.14 = f32[4,8,20,256]{3,2,0,1:T(8,128)S(1)} fusion(bf16[8,7168,256]{2,1,0:T(8,128)(2,1)} %param.9, bf16[4,8,20,7168]{3,1,2,0:T(8,128)(2,1)} %all_to_all.10), kind=kOutput, calls=%fused_computation.16 | convolution fusion | flops 2348810240 | bytes 39190528 | tf_op jit(solution)/shard_map/ajsd,jdf->ajsf/dot_general | solution.py:25
  329.1 15.6 %fusion.29 = bf16[4,8,20,256]{3,2,0,1:T(8,128)(2,1)S(1)} fusion(bf16[8,7168,256]{2,1,0:T(8,128)(2,1)} %param.10, bf16[4,8,20,7168]{3,1,2,0:T(8,128)(2,1)} %all_to_all.10, f32[4,8,20,256]{3,2,0,1:T(8,128)S(1)} %fusion.14), kind=kOutput, calls=%fused_computation.19 | convolution fusion | flops 2349793280 | bytes 39518208 | tf_op jit(solution)/shard_map/ajsd,jdf->ajsf/dot_general | solution.py:26
  344.8 16.3 %fusion.11 = bf16[4,8,20,7168]{3,2,0,1:T(8,128)(2,1)} fusion(bf16[4,8,20,256]{3,2,0,1:T(8,128)(2,1)S(1)} %fusion.29, bf16[8,256,7168]{2,1,0:T(8,128)(2,1)} %param.11), kind=kOutput, calls=%fused_computation.15 | convolution fusion | flops 2353397760 | bytes 38862848 | tf_op jit(solution)/shard_map/ajsf,jfd->ajsd/dot_general | solution.py:28
  361.1 12.7 %copy.26 = bf16[4,8,20,7168]{3,1,2,0:T(8,128)(2,1)} copy(bf16[4,8,20,7168]{3,2,0,1:T(8,128)(2,1)} %fusion.11) | data formatting | bytes 18350080 | tf_op jit(solution)/shard_map/convert_element_type | solution.py:28
  373.8 5.8 all-to-all-start.1
  379.6 0.0 reduce-scatter.2.cloned.1.call-start
  379.7 0.1 sub.9
  379.8 0.1 copy.20
  379.9 0.2 add.98
  380.0 0.1 copy.18
  380.1 0.2 copy.21
  380.3 0.1 copy.28
  380.5 198.9 %all-to-all-done.1 = bf16[4,8,20,7168]{3,1,2,0:T(8,128)(2,1)} async-done(((bf16[4,8,20,7168]{3,1,2,0:T(8,128)(2,1)}), bf16[4,8,20,7168]{3,1,2,0:T(8,128)(2,1)}, u32[]{:S(2)}, u32[]{:S(2)}) %all-to-all-start.1) | async-done | bytes 9175072 | tf_op jit(solution)/shard_map/all_to_all | solution.py:62
  579.4 12.9 %copy.27 = bf16[4,8,20,7168]{3,2,1,0:T(8,128)(2,1)} copy(bf16[4,8,20,7168]{3,1,2,0:T(8,128)(2,1)} %all-to-all-done.1) | data formatting | bytes 18350080 | tf_op jit(solution)/shard_map/all_to_all | solution.py:62
  592.3 13.5 %reshape.94 = bf16[640,7168]{1,0:T(8,128)(2,1)} reshape(bf16[4,8,20,7168]{3,2,1,0:T(8,128)(2,1)} %copy.27) | data formatting | bytes 18350080 | tf_op jit(solution)/shard_map/reshape | solution.py:63
  605.8 18.6 %gather_fusion.1 = bf16[512,7168]{1,0:T(8,128)(2,1)} fusion(bf16[640,7168]{1,0:T(8,128)(2,1)} %reshape.94, s32[1024]{0:T(1024)S(1)} %pad_clamp_fusion), kind=kCustom, calls=%fused_computation.1 | custom fusion | bytes 14682112 | tf_op jit(solution)/shard_map/jit(_take)/gather | solution.py:35
  624.4 14.9 %gather.15 = bf16[256,2,7168]{2,1,0:T(2,128)(2,1)} reshape(bf16[512,7168]{1,0:T(8,128)(2,1)} %gather_fusion.1) | data formatting | bytes 14680064 | tf_op jit(solution)/shard_map/jit(_take)/gather | solution.py:35
  639.3 76.7 %multiply_reduce_fusion = bf16[256,7168]{1,0:T(8,128)(2,1)} fusion(bf16[256,2,7168]{2,1,0:T(2,128)(2,1)} %gather.15, pred[256,2]{1,0:T(8,128)(4,1)S(1)} %copy.21, f32[256,2]{1,0:T(8,128)S(1)} %copy.28), kind=kLoop, calls=%fused_computation.9 | loop fusion | flops 12845056 | bytes 11012608 | tf_op jit(solution)/shard_map/reduce_sum | solution.py:36
  715.9 0.0 reduce-scatter.2.cloned.1.call-update
  716.0 39.6 %reduce-scatter.2.cloned.1.call-done = bf16[64,7168]{1,0:T(8,128)(2,1)} async-done(((bf16[256,7168]{1,0:T(8,128)(2,1)}), bf16[64,7168]{1,0:T(8,128)(2,1)}) %reduce-scatter.2.cloned.1.call-update) | async-done | bytes 917520 | tf_op jit(solution)/shard_map/reduce_scatter | solution.py:64
  (13 shorter events, 0.1 us)
Async XLA Ops:
  6.5 36.6 %all-gather.3.cloned.1.call-start = ((), (), s32[]{:S(2)}) async-start(), calls=%async_computation.3 | async-start | bytes 4587520 | tf_op jit(solution)/shard_map/all_gather | solution.py:46
  373.8 205.6 %all-to-all-start.1 = ((bf16[4,8,20,7168]{3,1,2,0:T(8,128)(2,1)}), bf16[4,8,20,7168]{3,1,2,0:T(8,128)(2,1)}, u32[]{:S(2)}, u32[]{:S(2)}) async-start(bf16[4,8,20,7168]{3,1,2,0:T(8,128)(2,1)} %copy.26), calls=%async_computation.1 | async-start | bytes 18350080 | tf_op jit(solution)/shard_map/all_to_all | solution.py:62
  379.6 376.0 %reduce-scatter.2.cloned.1.call-start = ((), (), s32[]{:S(2)}) async-start(), calls=%async_computation.4 | async-start | bytes 4587520 | tf_op jit(solution)/shard_map/reduce_scatter | solution.py:64
Sparse Core Ops, SparseCore 0:
  8.9 34.2 all-gather.2
  716.1 39.4 reduce-scatter.1
where the time goes:
time: 767 us; the launch traced here: 763 us
  waiting for transfers between devices  264 us (34%)
  blocking collectives  215 us (28%)
  local copies, waits for them, and re-layouts  129 us (17%)
  other arithmetic  88.6 us (12%)
  matrix products  47.4 us (6%)
  between operations  13.8 us (2%)
    all_to_all x1, blocking collectives, per_device(): lax.all_to_all(buffer, 'local', split_axis=0, concat_axis=0, tiled=True)  209 us
    all_to_all x1, waiting for transfers between devices, per_device(): lax.all_to_all(outputs, 'local', split_axis=0, concat_axis=0, tiled=True)  199 us
    reduce_sum x1, other arithmetic, combine(): return jnp.sum(values * gates[:, :, None], axis=1)  76.7 us
    reduce_scatter x1, waiting for transfers between devices, per_device(): lax.psum_scatter(partial_value.astype(jnp.bfloat16), 'node', scatter_dime...  39.6 us
    gather x2, local copies, waits for them, and re-layouts, place_rows(): return jnp.take(padded, owner_row, axis=0)  35 us
    gather x2, local copies, waits for them, and re-layouts, combine(): values = jnp.take(table, target, axis=0).reshape(-1, top_count, model_width)  33.5 us
    all_gather x1, waiting for transfers between devices, per_device(): gathered = lax.all_gather(tokens, 'node', axis=0, tiled=True)  24.3 us
    dot_general x1, matrix products, expert_block(): jnp.einsum('ajsf,jfd->ajsd', hidden, w_down, preferred_element_type=jnp.f...  16.3 us
  transfers between devices with their start and end apart: 3, of which 3 were waited for; matrix products, arithmetic and copies ran while one was open for 1% of the time, Pallas kernels for 0%

commit v1 on v0

v1 whole, which is shorter than its diff:
```python
import functools

import jax
import jax.numpy as jnp
import numpy as np
from jax import lax
from jax.experimental import pallas as pl
from jax.experimental.pallas import tpu as pltpu
from jax.sharding import PartitionSpec as P

CAP = 5
CHUNKS = 4
VMEM_LIMIT = 56 * 1024 * 1024
F32, BF16 = jnp.float32, jnp.bfloat16


def pad16(n):
    return -(-n // 16) * 16


def params():
    return pltpu.CompilerParams(vmem_limit_bytes=VMEM_LIMIT)


def whole():
    return pl.BlockSpec(memory_space=pltpu.VMEM)


class Sizes:
    def __init__(self, tokens, w_gate, local_count, node_count):
        self.tok, self.width = tokens.shape
        self.exp_dev = w_gate.shape[0]
        self.hidden = w_gate.shape[2]
        self.local = local_count
        self.node = node_count
        self.R = self.exp_dev * CAP
        self.RP = pad16(self.R)
        self.MP = pad16(self.local * CAP)
        self.rows = self.local * self.RP
        self.grouped = self.exp_dev * self.MP
        self.relative = local_count <= 4
        self.groups = [1] * local_count if self.relative else [local_count]
        self.chunks = CHUNKS
        self.dc = self.width // self.chunks

    def columns(self):
        table = np.full((8, self.rows), -1, np.int32)
        for s in range(self.local):
            for q in range(self.R):
                table[:3, s * self.RP + q] = (s, q // CAP, q % CAP)
            table[0, s * self.RP : (s + 1) * self.RP] = s
        return table

    def regroup(self):
        m = np.zeros((self.grouped, self.rows), np.float32)
        for s in range(self.local):
            for j in range(self.exp_dev):
                for c in range(CAP):
                    m[j * self.MP + s * CAP + c, s * self.RP + j * CAP + c] = 1
        return m


def gather_kernel(z, plane_ref, table_ref, ids_ref, gates_ref, tokens_ref, weight_ref, *outs):
    block, expert, slot = (table_ref[i : i + 1, :] for i in range(3))
    plane = block
    if z.relative:
        plane = block + plane_ref[0]
        plane = jnp.where(plane >= z.local, plane - z.local, plane)
    name = jnp.where(slot >= 0, plane * z.exp_dev + expert, -1)
    ids, gates = ids_ref[...], gates_ref[...]
    top = ids.shape[1]
    hits = [ids[:, k : k + 1] == name for k in range(top)]
    named = hits[0].astype(F32)
    for k in range(1, top):
        named = named + hits[k].astype(F32)
    t0 = lax.broadcasted_iota(jnp.int32, (z.tok, z.tok), 0)
    t1 = lax.broadcasted_iota(jnp.int32, (z.tok, z.tok), 1)
    before = jnp.where(t1 < t0, 1.0, 0.0).astype(BF16)
    rank = jnp.dot(before, named.astype(BF16), preferred_element_type=F32)
    here = rank == slot.astype(F32)
    weight = jnp.zeros((z.tok, z.rows), F32)
    for k in range(top):
        weight = weight + jnp.where(hits[k] & here, gates[:, k : k + 1], 0.0)
    weight_ref[...] = weight
    pick = jnp.where(here, named, 0.0).T.astype(BF16)
    at = 0
    for c in range(z.chunks):
        cols = slice(c * z.dc, (c + 1) * z.dc)
        picked = jnp.dot(pick, tokens_ref[:, cols], preferred_element_type=F32).astype(BF16)
        s = 0
        for g in z.groups:
            for i in range(g):
                outs[at][i] = picked[s * z.RP : s * z.RP + z.R]
                s += 1
            at += 1


def gather_rows(z, plane, ids, gates, tokens):
    shapes = [jax.ShapeDtypeStruct((g, z.R, z.dc), BF16) for _ in range(z.chunks) for g in z.groups]
    outs = pl.pallas_call(
        functools.partial(gather_kernel, z),
        out_shape=[jax.ShapeDtypeStruct((z.tok, z.rows), F32)] + shapes,
        in_specs=[pl.BlockSpec(memory_space=pltpu.SMEM)] + [whole()] * 4,
        out_specs=[whole()] * (1 + len(shapes)),
        compiler_params=params(),
        name="gather_rows",
    )(plane, jnp.asarray(z.columns()), ids, gates, tokens)
    n = len(z.groups)
    return outs[0], [outs[1 + c * n : 1 + (c + 1) * n] for c in range(z.chunks)]


def tile_of(width):
    for t in (512, 256, 128):
        if width % t == 0:
            return t
    return width


def up_kernel(z, counts, first, last, *refs):
    pieces = refs[: len(counts)]
    refs = refs[len(counts) :]
    regroup_ref, wg_ref, wu_ref = refs[:3]
    refs = refs[3:]
    if not first:
        gin_ref, uin_ref = refs[:2]
        refs = refs[2:]
    if last:
        hidden_ref, rows_ref, grouped_ref = refs
    else:
        gout_ref, uout_ref, rows_ref, grouped_ref = refs

    @pl.when(pl.program_id(0) == 0)
    def _():
        if z.RP > z.R:
            rows_ref[...] = jnp.zeros_like(rows_ref)
        at = 0
        for ref, count in zip(pieces, counts):
            for i in range(count):
                m, s = divmod(at, z.local)
                rows_ref[m, s * z.RP : s * z.RP + z.R, :] = ref[i]
                at += 1
        tile = tile_of(z.dc)

        def step(i, carry):
            cols = pl.ds(pl.multiple_of(i * tile, tile), tile)
            for m in range(z.node):
                got = jnp.dot(regroup_ref[...], rows_ref[m, :, cols], preferred_element_type=F32).astype(BF16)
                grouped_ref[:, m * z.MP : (m + 1) * z.MP, cols] = got.reshape(z.exp_dev, z.MP, tile)
            return carry

        lax.fori_loop(0, z.dc // tile, step, 0)

    rows = grouped_ref[pl.program_id(0)]
    gate = jnp.dot(rows, wg_ref[0], preferred_element_type=F32)
    up = jnp.dot(rows, wu_ref[0], preferred_element_type=F32)
    if not first:
        gate = gate + gin_ref[0]
        up = up + uin_ref[0]
    if last:
        hidden_ref[0] = (gate / (1.0 + jnp.exp(-gate)) * up).astype(BF16)
    else:
        gout_ref[0] = gate
        uout_ref[0] = up


def up_chunk(z, c, pieces, regroup, w_gate, w_up, sums):
    first, last = sums is None, c == z.chunks - 1
    counts = [p.shape[0] for p in pieces]
    acc = jax.ShapeDtypeStruct((z.exp_dev, z.node * z.MP, z.hidden), F32)
    acc_spec = pl.BlockSpec((1,) + acc.shape[1:], lambda e: (e, 0, 0))
    w_spec = pl.BlockSpec((1, z.dc, z.hidden), lambda e: (e, c, 0))
    out_shape = [jax.ShapeDtypeStruct(acc.shape, BF16)] if last else [acc, acc]
    flops = 4 * z.exp_dev * z.node * z.MP * z.dc * z.hidden
    return pl.pallas_call(
        functools.partial(up_kernel, z, counts, first, last),
        grid=(z.exp_dev,),
        out_shape=out_shape,
        in_specs=[pl.BlockSpec(p.shape, lambda e: (0, 0, 0)) for p in pieces]
        + [pl.BlockSpec(regroup.shape, lambda e: (0, 0)), w_spec, w_spec]
        + ([] if first else [acc_spec, acc_spec]),
        out_specs=[acc_spec] * len(out_shape),
        scratch_shapes=[
            pltpu.VMEM((z.node, z.rows, z.dc), BF16),
            pltpu.VMEM((z.exp_dev, z.node * z.MP, z.dc), BF16),
        ],
        compiler_params=params(),
        cost_estimate=pl.CostEstimate(
            flops=flops, bytes_accessed=4 * z.exp_dev * z.dc * z.hidden, transcendentals=0
        ),
        name="up_chunk",
    )(*pieces, regroup, w_gate, w_up, *(() if first else sums))


def down_kernel(z, order, hidden_ref, ungroup_ref, wd_ref, *refs):
    outs, held_ref = refs[:-1], refs[-1]
    e = pl.program_id(0)
    got = jnp.dot(hidden_ref[0], wd_ref[0], preferred_element_type=F32).astype(BF16)
    for m in range(z.node):
        held_ref[m, pl.ds(pl.multiple_of(e * z.MP, z.MP), z.MP), :] = got[m * z.MP : (m + 1) * z.MP]

    @pl.when(e == z.exp_dev - 1)
    def _():
        tile = tile_of(z.dc)

        def step(i, carry):
            cols = pl.ds(pl.multiple_of(i * tile, tile), tile)
            for out, ms in zip(outs, order):
                for k, m in enumerate(ms):
                    back = jnp.dot(ungroup_ref[...], held_ref[m, :, cols], preferred_element_type=F32).astype(BF16)
                    for s in range(z.local):
                        out[k * z.local + s, :, cols] = back[s * z.RP : s * z.RP + z.R]
            return carry

        lax.fori_loop(0, z.dc // tile, step, 0)


def down_chunk(z, c, hidden, ungroup, w_down, order):
    shapes = [jax.ShapeDtypeStruct((len(ms) * z.local, z.R, z.dc), BF16) for ms in order]
    return pl.pallas_call(
        functools.partial(down_kernel, z, order),
        grid=(z.exp_dev,),
        out_shape=shapes,
        in_specs=[
            pl.BlockSpec((1,) + hidden.shape[1:], lambda e: (e, 0, 0)),
            pl.BlockSpec(ungroup.shape, lambda e: (0, 0)),
            pl.BlockSpec((1, z.hidden, z.dc), lambda e: (e, 0, c)),
        ],
        out_specs=[pl.BlockSpec(s.shape, lambda e: (0, 0, 0)) for s in shapes],
        scratch_shapes=[pltpu.VMEM((z.node, z.grouped, z.dc), BF16)],
        compiler_params=params(),
        cost_estimate=pl.CostEstimate(
            flops=2 * z.exp_dev * z.node * z.MP * z.dc * z.hidden,
            bytes_accessed=2 * z.exp_dev * z.dc * z.hidden,
            transcendentals=0,
        ),
        name="down_chunk",
    )(hidden, ungroup, w_down)


def add_kernel(cuts, a_ref, b_ref, *outs):
    for out, (lo, hi) in zip(outs, cuts):
        out[...] = (a_ref[lo:hi].astype(F32) + b_ref[lo:hi].astype(F32)).astype(BF16)


def add_cut(a, b, cuts):
    return pl.pallas_call(
        functools.partial(add_kernel, cuts),
        out_shape=[jax.ShapeDtypeStruct((hi - lo,) + a.shape[1:], BF16) for lo, hi in cuts],
        in_specs=[whole()] * 2,
        out_specs=[whole()] * len(cuts),
        compiler_params=params(),
        cost_estimate=pl.CostEstimate(flops=a.size, bytes_accessed=6 * a.size, transcendentals=0),
        name="add_cut",
    )(a, b)


def combine_kernel(z, counts, weight_ref, *refs):
    pieces, (out_ref, rows_ref) = refs[: len(counts)], refs[-2:]
    if z.RP > z.R:
        rows_ref[...] = jnp.zeros_like(rows_ref)
    at = 0
    for ref, count in zip(pieces, counts):
        for i in range(count):
            rows_ref[at * z.RP : at * z.RP + z.R, :] = ref[i]
            at += 1
    weight = weight_ref[...]
    high = weight.astype(BF16)
    rest = weight - high.astype(F32)
    middle = rest.astype(BF16)
    low = (rest - middle.astype(F32)).astype(BF16)
    rows = rows_ref[...]
    total = jnp.dot(low, rows, preferred_element_type=F32)
    total = total + jnp.dot(middle, rows, preferred_element_type=F32)
    total = total + jnp.dot(high, rows, preferred_element_type=F32)
    out_ref[...] = total.astype(BF16)


def combine_chunk(z, c, weight, pieces, so_far):
    counts = [p.shape[0] for p in pieces]
    extra = [] if so_far is None else [so_far]
    return pl.pallas_call(
        functools.partial(combine_kernel, z, counts),
        grid=(1,),
        out_shape=jax.ShapeDtypeStruct((z.tok, z.width), BF16),
        in_specs=[pl.BlockSpec(weight.shape, lambda i: (0, 0))]
        + [pl.BlockSpec(p.shape, lambda i: (0, 0, 0)) for p in pieces]
        + [pl.BlockSpec(memory_space=pl.ANY)] * len(extra),
        out_specs=pl.BlockSpec((z.tok, z.dc), lambda i: (0, c)),
        scratch_shapes=[pltpu.VMEM((z.rows, z.dc), BF16)],
        input_output_aliases={1 + len(pieces): 0} if extra else {},
        compiler_params=params(),
        name="combine_chunk",
    )(weight, *pieces, *extra)


def swap(a, mask, count):
    return lax.ppermute(a, "node", [(i, i ^ mask) for i in range(count)])


def shift(a, by, count):
    return lax.ppermute(a, "local", [(i, (i + by) % count) for i in range(count)])


def per_device(tokens, expert_ids, gate_weights, w_gate, w_up, w_down):
    local_count, node_count = lax.axis_size("local"), lax.axis_size("node")
    z = Sizes(tokens, w_gate, local_count, node_count)
    plane = lax.axis_index("local").astype(jnp.int32).reshape(1)
    regroup = z.regroup()
    ungroup = jnp.asarray(regroup.T, BF16)
    regroup = jnp.asarray(regroup, BF16)
    weight, sent = gather_rows(z, plane, expert_ids, gate_weights, tokens)

    masks = []
    while 1 << len(masks) < node_count:
        masks.append(1 << len(masks))

    sums = None
    for c in range(z.chunks):
        if z.relative:
            parts = [sent[c][0]] + [shift(sent[c][s], s, local_count) for s in range(1, local_count)]
            held = {0: [parts[0], jnp.concatenate(parts[1:], axis=0)]}
        else:
            held = {0: [lax.all_to_all(sent[c][0], "local", 0, 0, tiled=True)]}
        for mask in reversed(masks):
            for m in list(held):
                held[m | mask] = [swap(a, mask, node_count) for a in held[m]]
        pieces = [a for m in range(node_count) for a in held[m]]
        sums = up_chunk(z, c, pieces, regroup, w_gate, w_up, sums)
    hidden = sums[0]

    out = None
    for c in range(z.chunks):
        away = [m for m in range(node_count) if m & 1]
        home = [m for m in range(node_count) if not m & 1]
        send, keep = down_chunk(z, c, hidden, ungroup, w_down, [away, home])
        for mask in masks:
            got = swap(send, mask, node_count)
            half = keep.shape[0] // 2
            if mask != masks[-1]:
                nxt = mask << 1
                kept = [m for m in range(node_count) if not m & (nxt - 1)]
                cuts = [(i * local_count, (i + 1) * local_count) for i in range(len(kept))]
                if len(kept) == 2:
                    keep, send = add_cut(keep, got, cuts)
                else:
                    whole_sum = add_cut(keep, got, cuts)
                    keep = jnp.concatenate([a for a, m in zip(whole_sum, kept) if not m & nxt], axis=0)
                    send = jnp.concatenate([a for a, m in zip(whole_sum, kept) if m & nxt], axis=0)
            elif z.relative:
                pieces = add_cut(keep, got, [(s, s + 1) for s in range(local_count)])
            else:
                pieces = add_cut(keep, got, [(0, local_count)])
        if z.relative:
            pieces = [pieces[0]] + [shift(pieces[s], -s, local_count) for s in range(1, local_count)]
        else:
            pieces = [lax.all_to_all(pieces[0], "local", 0, 0, tiled=True)]
        out = combine_chunk(z, c, weight, pieces, out)
    return out


def solution(mesh):
    return jax.shard_map(
        per_device,
        mesh=mesh,
        in_specs=(
            P(("parts", "node", "local"), None),
            P(("parts", "node", "local"), None),
            P(("parts", "node", "local"), None),
            P("local", None, "node"),
            P("local", None, "node"),
            P("local", "node", None),
        ),
        out_specs=P(("parts", "node", "local"), None),
        check_vma=False,
    )
```

time: 767 us -> 313 us (0.41)
  blocking collectives: 215 us -> 0 us
  waiting for transfers between devices: 264 us -> 119 us
  Pallas kernels: 0 us -> 123 us
  local copies, waits for them, and re-layouts: 129 us -> 12.1 us
  other arithmetic: 88.6 us -> 0 us
  starting transfers between devices: 5.86 us -> 57.3 us
  matrix products: 47.4 us -> 0 us
  between operations: 13.8 us -> 0.59 us
    all_to_all x1 -> x0, blocking collectives: 209 us -> none  [per_device(): lax.all_to_all(buffer, 'local', split_axis=0, concat_axis=0, tiled=True)]
    all_to_all x1 -> x0, waiting for transfers between devices: 199 us -> none  [per_device(): lax.all_to_all(outputs, 'local', split_axis=0, concat_axis=0, tiled=True)]
    pallas_call x0 -> x21, Pallas kernels: none -> 123 us  [the longest x4 51.5 us: up_chunk(): pl.pallas_call(functools.partial(up_kernel, z, counts, first, last), grid...]
    ppermute x0 -> x56, waiting for transfers between devices: none -> 119 us  [the longest x24 64.3 us: shift(): lax.ppermute(a, 'local', [(i, (i + by) % count) for i in range(count)])]
    reduce_sum x2 -> x0, other arithmetic: 76.9 us -> none  [the longest x1 76.7 us: combine(): return jnp.sum(values * gates[:, :, None], axis=1)]
    gather x4 -> x0, local copies, waits for them, and re-layouts: 68.4 us -> none  [the longest x2 35 us: place_rows(): return jnp.take(padded, owner_row, axis=0)]
    ppermute x0 -> x56, starting transfers between devices: none -> 57.3 us  [the longest x24 39.5 us: shift(): lax.ppermute(a, 'local', [(i, (i + by) % count) for i in range(count)])]
    dot_general x3 -> x0, matrix products: 47.4 us -> none  [the longest x1 16.3 us: expert_block(): jnp.einsum('ajsf,jfd->ajsd', hidden, w_down, preferred_element_type=jnp.f...]
  transfers between devices with their start and end apart: 3 -> 56, of which waited for: 3 -> 24; matrix products, arithmetic and copies ran while one was open for 1% -> 0% of each run, Pallas kernels for 0% -> 27%
where the time goes in v1:
time: 313 us; the launch traced here: 312 us
  Pallas kernels  123 us (39%)
  waiting for transfers between devices  119 us (38%)
  starting transfers between devices  57.3 us (18%)
  local copies, waits for them, and re-layouts  12.1 us (4%)
    ppermute x24, waiting for transfers between devices, shift(): lax.ppermute(a, 'local', [(i, (i + by) % count) for i in range(count)])  64.3 us
    ppermute x32, waiting for transfers between devices, swap(): return lax.ppermute(a, 'node', [(i, i ^ mask) for i in range(count)])  54.2 us
    pallas_call x4, Pallas kernels, up_chunk(): pl.pallas_call(functools.partial(up_kernel, z, counts, first, last), grid...  51.5 us
    pallas_call x4, Pallas kernels, down_chunk(): pl.pallas_call(functools.partial(down_kernel, z, order), grid=(z.exp_dev,...  39.6 us
    ppermute x24, starting transfers between devices, shift(): lax.ppermute(a, 'local', [(i, (i + by) % count) for i in range(count)])  39.5 us
    pallas_call x8, Pallas kernels, add_cut(): pl.pallas_call(functools.partial(add_kernel, cuts), out_shape=[jax.ShapeD...  19.4 us
    ppermute x32, starting transfers between devices, swap(): return lax.ppermute(a, 'node', [(i, i ^ mask) for i in range(count)])  17.8 us
    unnamed x134, local copies, waits for them, and re-layouts  12 us
  transfers between devices with their start and end apart: 56, of which 24 were waited for; matrix products, arithmetic and copies ran while one was open for 0% of the time, Pallas kernels for 27%

profile of v1, /device:TPU:0, one launch (start us, length us, event | category | flops | bytes accessed | tf_op | source)
XLA Modules:
  0.0 311.5 jit_solution(736290492071417729)
XLA Ops:
  0.0 1.4 copy.13.ids_ref
  1.4 1.4 copy.14.gates_ref
  2.8 3.2 %gather_rows.1 = (f32[64,192]{1,0:T(8,128)}, bf16[1,40,1792]{2,1,0:T(8,128)(2,1)}, bf16[1,40,1792]{2,1,0:T(8,128)(2,1)}, bf16[1,40,1792]{2,1,0:T(8,128)(2,1)}, b...) custom-call(s32[1]{0:T(128)} %bitcast.plane_ref, ...), custom_call_target="tpu_custom_call" | custom-call | tf_op jit(solution)/shard_map/gather_rows/pallas_call | solution.py:100
  6.0 3.1 collective-permute-start.27
  9.1 1.5 collective-permute-start.32
  11.4 3.7 %collective-permute-done.27 = bf16[1,40,1792]{2,1,0:T(8,128)(2,1)S(1)} collective-permute-done((bf16[1,40,1792]{2,1,0:T(8,128)(2,1)}, bf16[1,40,1792]{2,1,0:T(8,128)(2,1)S(1)}, u32[]{:S(2)}, u32[]{:S(2)}) %collective-permute-start.27) | collective-permute-done | bytes 143392 | tf_op jit(solution)/shard_map/ppermute | solution.py:301
  15.1 7.1 %collective-permute-done.18 = bf16[1,40,1792]{2,1,0:T(8,128)(2,1)S(1)} collective-permute-done((bf16[1,40,1792]{2,1,0:T(8,128)(2,1)}, bf16[1,40,1792]{2,1,0:T(8,128)(2,1)S(1)}, u32[]{:S(2)}, u32[]{:S(2)}) %collective-permute-start.18) | collective-permute-done | bytes 143392 | tf_op jit(solution)/shard_map/ppermute | solution.py:301
  22.3 7.1 %collective-permute-done.9 = bf16[1,40,1792]{2,1,0:T(8,128)(2,1)S(1)} collective-permute-done((bf16[1,40,1792]{2,1,0:T(8,128)(2,1)}, bf16[1,40,1792]{2,1,0:T(8,128)(2,1)S(1)}, u32[]{:S(2)}, u32[]{:S(2)}) %collective-permute-start.9) | collective-permute-done | bytes 143392 | tf_op jit(solution)/shard_map/ppermute | solution.py:301
  29.4 7.7 %collective-permute-done = bf16[1,40,1792]{2,1,0:T(8,128)(2,1)S(1)} collective-permute-done((bf16[1,40,1792]{2,1,0:T(8,128)(2,1)}, bf16[1,40,1792]{2,1,0:T(8,128)(2,1)S(1)}, u32[]{:S(2)}, u32[]{:S(2)}) %collective-permute-start) | collective-permute-done | bytes 143392 | tf_op jit(solution)/shard_map/ppermute | solution.py:301
  37.1 6.4 %collective-permute-done.28 = bf16[1,40,1792]{2,1,0:T(8,128)(2,1)S(1)} collective-permute-done((bf16[1,40,1792]{2,1,0:T(8,128)(2,1)}, bf16[1,40,1792]{2,1,0:T(8,128)(2,1)S(1)}, u32[]{:S(2)}, u32[]{:S(2)}) %collective-permute-start.28) | collective-permute-done | bytes 143392 | tf_op jit(solution)/shard_map/ppermute | solution.py:301
  43.5 2.4 collective-permute-start.29
  46.0 3.0 collective-permute-done.29
  48.9 1.3 collective-permute-start.19
  50.3 5.2 %collective-permute-done.19 = bf16[1,40,1792]{2,1,0:T(8,128)(2,1)S(1)} collective-permute-done((bf16[1,40,1792]{2,1,0:T(8,128)(2,1)S(1)}, bf16[1,40,1792]{2,1,0:T(8,128)(2,1)S(1)}, u32[]{:S(2)}, u32[]{:S(2)}) %collective-permute-start.19) | collective-permute-done | bytes 143392 | tf_op jit(solution)/shard_map/ppermute | solution.py:301
  55.5 5.0 %collective-permute-start.20 = (bf16[1,40,1792]{2,1,0:T(8,128)(2,1)S(1)}, bf16[1,40,1792]{2,1,0:T(8,128)(2,1)S(1)}, u32[]{:S(2)}, u32[]{:S(2)}) collective-permute-start(bf16[1,40,1792]{2,1,0:T(8,128)(2,1)S(1)} %copy-done.55), channel_id=1, source_target_pairs={{0,3},{1,0},{2,1},{3,2},{4,7},{5,4},{6,5},{7,6},{8,11},{9,8},{10,9... | collective-permute-start | bytes 430088 | tf_op jit(solution)/shard_map/ppermute | solution.py:301
  60.5 2.6 collective-permute-done.20
  64.1 6.5 %collective-permute-done.10 = bf16[1,40,1792]{2,1,0:T(8,128)(2,1)S(1)} collective-permute-done((bf16[1,40,1792]{2,1,0:T(8,128)(2,1)S(1)}, bf16[1,40,1792]{2,1,0:T(8,128)(2,1)S(1)}, u32[]{:S(2)}, u32[]{:S(2)}) %collective-permute-start.10) | collective-permute-done | bytes 143392 | tf_op jit(solution)/shard_map/ppermute | solution.py:301
  70.7 2.7 collective-permute-start.11
  73.4 1.3 collective-permute-start.14
  74.9 1.7 collective-permute-start.2
  76.6 1.5 collective-permute-start.5
  78.6 1.3 collective-permute-start.33
  79.9 4.0 %collective-permute-done.1 = bf16[1,40,1792]{2,1,0:T(8,128)(2,1)S(1)} collective-permute-done((bf16[1,40,1792]{2,1,0:T(8,128)(2,1)S(1)}, bf16[1,40,1792]{2,1,0:T(8,128)(2,1)S(1)}, u32[]{:S(2)}, u32[]{:S(2)}) %collective-permute-start.1) | collective-permute-done | bytes 143392 | tf_op jit(solution)/shard_map/ppermute | solution.py:301
  86.2 1.3 collective-permute-start.15
  87.5 5.0 %collective-permute-done.33.refs_5_ = bf16[3,40,1792]{2,1,0:T(8,128)(2,1)S(1)} collective-permute-done((bf16[3,40,1792]{2,1,0:T(8,128)(2,1)S(1)}, bf16[3,40,1792]{2,1,0:T(8,128)(2,1)S(1)}, u32[]{:S(2)}, u32[]{:S(2)}) %collective-permute-start.33) | collective-permute-done | bytes 430112 | tf_op jit(solution)/shard_map/ppermute | solution.py:297
  92.4 1.6 collective-permute-start.6
  94.0 7.6 %collective-permute-done.24.refs_5_ = bf16[3,40,1792]{2,1,0:T(8,128)(2,1)S(1)} collective-permute-done((bf16[3,40,1792]{2,1,0:T(8,128)(2,1)S(1)}, bf16[3,40,1792]{2,1,0:T(8,128)(2,1)S(1)}, u32[]{:S(2)}, u32[]{:S(2)}) %collective-permute-start.24) | collective-permute-done | bytes 430112 | tf_op jit(solution)/shard_map/ppermute | solution.py:297
  102.2 8.7 %collective-permute-done.15.refs_5_ = bf16[3,40,1792]{2,1,0:T(8,128)(2,1)S(1)} collective-permute-done((bf16[3,40,1792]{2,1,0:T(8,128)(2,1)S(1)}, bf16[3,40,1792]{2,1,0:T(8,128)(2,1)S(1)}, u32[]{:S(2)}, u32[]{:S(2)}) %collective-permute-start.15) | collective-permute-done | bytes 430112 | tf_op jit(solution)/shard_map/ppermute | solution.py:297
  110.9 8.2 %collective-permute-done.6.refs_5_ = bf16[3,40,1792]{2,1,0:T(8,128)(2,1)S(1)} collective-permute-done((bf16[3,40,1792]{2,1,0:T(8,128)(2,1)S(1)}, bf16[3,40,1792]{2,1,0:T(8,128)(2,1)S(1)}, u32[]{:S(2)}, u32[]{:S(2)}) %collective-permute-start.6) | collective-permute-done | bytes 430112 | tf_op jit(solution)/shard_map/ppermute | solution.py:297
  119.9 12.5 %up_chunk.4 = (f32[8,128,256]{2,1,0:T(8,128)}, f32[8,128,256]{2,1,0:T(8,128)}) custom-call(bf16[1,40,1792]{2,1,0:T(8,128)(2,1)} %get-tuple-element.73.refs_0_, bf16[3,40,1792]{2,1,0:T(8,128)(2,1)} %copy-done.7, bf16[1,40,1792]{2,1,0:T(8,128)(2,1)} %copy-done.29, bf16[3,40,1792]{2,1,0:T(8,128)(2,1)} %copy-done.16, bf16[1,40,1792]{2,1,0:T(8,128)(2,1)} %copy-done.28, ...), custom_call_target="tpu_custom_call" | custom-call | flops 1879048192 | bytes 14680064 | tf_op jit(solution)/shard_map/up_chunk/pallas_call | solution.py:174
  133.3 13.1 %up_chunk.5 = (f32[8,128,256]{2,1,0:T(8,128)}, f32[8,128,256]{2,1,0:T(8,128)}) custom-call(bf16[1,40,1792]{2,1,0:T(8,128)(2,1)} %get-tuple-element.69.refs_0_, bf16[3,40,1792]{2,1,0:T(8,128)(2,1)} %copy-done.6, bf16[1,40,1792]{2,1,0:T(8,128)(2,1)} %copy-done.27, bf16[3,40,1792]{2,1,0:T(8,128)(2,1)} %copy-done.18, bf16[1,40,1792]{2,1,0:T(8,128)(2,1)} %copy-done.26, ...), custom_call_target="tpu_custom_call" | custom-call | flops 1879048192 | bytes 14680064 | tf_op jit(solution)/shard_map/up_chunk/pallas_call | solution.py:174
  147.8 13.1 %up_chunk.6 = (f32[8,128,256]{2,1,0:T(8,128)}, f32[8,128,256]{2,1,0:T(8,128)}) custom-call(bf16[1,40,1792]{2,1,0:T(8,128)(2,1)} %get-tuple-element.65.refs_0_, bf16[3,40,1792]{2,1,0:T(8,128)(2,1)} %copy-done.5, bf16[1,40,1792]{2,1,0:T(8,128)(2,1)} %copy-done.32, bf16[3,40,1792]{2,1,0:T(8,128)(2,1)} %copy-done.20, bf16[1,40,1792]{2,1,0:T(8,128)(2,1)} %copy-done.30, ...), custom_call_target="tpu_custom_call" | custom-call | flops 1879048192 | bytes 14680064 | tf_op jit(solution)/shard_map/up_chunk/pallas_call | solution.py:174
  161.9 12.8 %up_chunk.7.hidden_ref = bf16[8,128,256]{2,1,0:T(8,128)(2,1)} custom-call(bf16[1,40,1792]{2,1,0:T(8,128)(2,1)} %get-tuple-element.61.refs_0_, bf16[3,40,1792]{2,1,0:T(8,128)(2,1)} %copy-done.4, bf16[1,40,1792]{2,1,0:T(8,128)(2,1)} %copy-done.35, bf16[3,40,1792]{2,1,0:T(8,128)(2,1)} %copy-done.17, bf16[1,40,1792]{2,1,0:T(8,128)(2,1)} %copy-done.31, ...), custom_call_target="tpu_custom_call" | custom-call | flops 1879048192 | bytes 14680064 | tf_op jit(solution)/shard_map/up_chunk/pallas_call | solution.py:174
  174.7 9.9 %down_chunk.7 = (bf16[8,40,1792]{2,1,0:T(8,128)(2,1)}, bf16[8,40,1792]{2,1,0:T(8,128)(2,1)}) custom-call(bf16[8,128,256]{2,1,0:T(8,128)(2,1)} %up_chunk.7.hidden_ref, bf16[192,256]{1,0:T(8,128)(2,1)} %constant.10.clone.ungroup_ref, bf16[8,256,7168]{2,1,0:T(8,128)(2,1)} %wd_ref.7), custom_call_target="tpu_custom_call" | custom-call | flops 939524096 | bytes 7340032 | tf_op jit(solution)/shard_map/down_chunk/pallas_call | solution.py:219
  184.7 9.9 %down_chunk.6 = (bf16[8,40,1792]{2,1,0:T(8,128)(2,1)}, bf16[8,40,1792]{2,1,0:T(8,128)(2,1)}) custom-call(bf16[8,128,256]{2,1,0:T(8,128)(2,1)} %up_chunk.7.hidden_ref, bf16[192,256]{1,0:T(8,128)(2,1)} %constant.10.clone.ungroup_ref, bf16[8,256,7168]{2,1,0:T(8,128)(2,1)} %wd_ref.7), custom_call_target="tpu_custom_call" | custom-call | flops 939524096 | bytes 7340032 | tf_op jit(solution)/shard_map/down_chunk/pallas_call | solution.py:219
  195.1 9.8 %down_chunk.5 = (bf16[8,40,1792]{2,1,0:T(8,128)(2,1)}, bf16[8,40,1792]{2,1,0:T(8,128)(2,1)}) custom-call(bf16[8,128,256]{2,1,0:T(8,128)(2,1)} %up_chunk.7.hidden_ref, bf16[192,256]{1,0:T(8,128)(2,1)} %constant.10.clone.ungroup_ref, bf16[8,256,7168]{2,1,0:T(8,128)(2,1)} %wd_ref.7), custom_call_target="tpu_custom_call" | custom-call | flops 939524096 | bytes 7340032 | tf_op jit(solution)/shard_map/down_chunk/pallas_call | solution.py:219
  205.4 9.9 %down_chunk.4 = (bf16[8,40,1792]{2,1,0:T(8,128)(2,1)}, bf16[8,40,1792]{2,1,0:T(8,128)(2,1)}) custom-call(bf16[8,128,256]{2,1,0:T(8,128)(2,1)} %up_chunk.7.hidden_ref, bf16[192,256]{1,0:T(8,128)(2,1)} %constant.10.clone.ungroup_ref, bf16[8,256,7168]{2,1,0:T(8,128)(2,1)} %wd_ref.7), custom_call_target="tpu_custom_call" | custom-call | flops 939524096 | bytes 7340032 | tf_op jit(solution)/shard_map/down_chunk/pallas_call | solution.py:219
  216.3 2.7 add_cut.14
  221.0 2.8 add_cut.12
  223.7 1.3 collective-permute-start.47
  226.0 2.8 add_cut.10
  230.6 2.7 add_cut.8
  233.3 1.3 collective-permute-start.37
  235.9 2.1 add_cut.15
  238.0 2.7 collective-permute-start.53
  240.8 6.6 %collective-permute-done.47.b_ref = bf16[4,40,1792]{2,1,0:T(8,128)(2,1)S(1)} collective-permute-done((bf16[4,40,1792]{2,1,0:T(8,128)(2,1)}, bf16[4,40,1792]{2,1,0:T(8,128)(2,1)S(1)}, u32[]{:S(2)}, u32[]{:S(2)}) %collective-permute-start.47) | collective-permute-done | bytes 573472 | tf_op jit(solution)/shard_map/ppermute | solution.py:297
  248.2 2.1 add_cut.13
  250.3 9.3 %collective-permute-done.42.b_ref = bf16[4,40,1792]{2,1,0:T(8,128)(2,1)S(1)} collective-permute-done((bf16[4,40,1792]{2,1,0:T(8,128)(2,1)}, bf16[4,40,1792]{2,1,0:T(8,128)(2,1)S(1)}, u32[]{:S(2)}, u32[]{:S(2)}) %collective-permute-start.42) | collective-permute-done | bytes 573472 | tf_op jit(solution)/shard_map/ppermute | solution.py:297
  259.6 2.7 collective-permute-start.48
  262.4 2.1 add_cut.11
  264.5 7.0 %collective-permute-done.37.b_ref = bf16[4,40,1792]{2,1,0:T(8,128)(2,1)S(1)} collective-permute-done((bf16[4,40,1792]{2,1,0:T(8,128)(2,1)}, bf16[4,40,1792]{2,1,0:T(8,128)(2,1)S(1)}, u32[]{:S(2)}, u32[]{:S(2)}) %collective-permute-start.37) | collective-permute-done | bytes 573472 | tf_op jit(solution)/shard_map/ppermute | solution.py:297
  271.5 1.6 collective-permute-start.49
  273.1 1.7 collective-permute-start.50
  274.8 2.2 collective-permute-start.43
  277.0 2.1 add_cut.9
  279.9 5.2 %collective-permute-done.49.refs_2_ = bf16[1,40,1792]{2,1,0:T(8,128)(2,1)S(1)} collective-permute-done((bf16[1,40,1792]{2,1,0:T(8,128)(2,1)S(1)}, bf16[1,40,1792]{2,1,0:T(8,128)(2,1)S(1)}, u32[]{:S(2)}, u32[]{:S(2)}) %collective-permute-start.49) | collective-permute-done | bytes 143392 | tf_op jit(solution)/shard_map/ppermute | solution.py:301
  285.1 3.2 %collective-permute-start.38 = (bf16[1,40,1792]{2,1,0:T(8,128)(2,1)}, bf16[1,40,1792]{2,1,0:T(8,128)(2,1)S(1)}, u32[]{:S(2)}, u32[]{:S(2)}) collective-permute-start(bf16[1,40,1792]{2,1,0:T(8,128)(2,1)} %get-tuple-element.88), channel_id=1, source_target_pairs={{0,3},{1,0},{2,1},{3,2},{4,7},{5,4},{6,5},{7,6},{8,11},{9,8},{10,9... | collective-permute-start | bytes 430088 | tf_op jit(solution)/shard_map/ppermute | solution.py:301
  288.3 6.5 %collective-permute-start.39 = (bf16[1,40,1792]{2,1,0:T(8,128)(2,1)}, bf16[1,40,1792]{2,1,0:T(8,128)(2,1)S(1)}, u32[]{:S(2)}, u32[]{:S(2)}) collective-permute-start(bf16[1,40,1792]{2,1,0:T(8,128)(2,1)} %get-tuple-element.89), channel_id=1, source_target_pairs={{0,2},{1,3},{2,0},{3,1},{4,6},{5,7},{6,4},{7,5},{8,10},{9,11},{10,... | collective-permute-start | bytes 430088 | tf_op jit(solution)/shard_map/ppermute | solution.py:301
  294.8 2.4 combine_chunk.4.refs_4_
  297.2 2.3 combine_chunk.5.refs_4_
  299.6 2.9 collective-permute-done.44.refs_2_
  303.2 2.3 combine_chunk.6.refs_4_
  305.6 2.9 collective-permute-done.39.refs_2_
  309.2 2.3 combine_chunk.7
  (207 shorter events, 20.6 us)
Async XLA Ops:
  6.0 57.1 %copy-start.54 = (bf16[1,40,1792]{2,1,0:T(8,128)(2,1)S(1)}, bf16[1,40,1792]{2,1,0:T(8,128)(2,1)}, u32[]{:S(2)}) copy-start(bf16[1,40,1792]{2,1,0:T(8,128)(2,1)} %get-tuple-element.67) | copy-start | bytes 430084
  6.0 9.1 %collective-permute-start.27 = (bf16[1,40,1792]{2,1,0:T(8,128)(2,1)}, bf16[1,40,1792]{2,1,0:T(8,128)(2,1)S(1)}, u32[]{:S(2)}, u32[]{:S(2)}) collective-permute-start(bf16[1,40,1792]{2,1,0:T(8,128)(2,1)} %get-tuple-element.74), channel_id=1, source_target_pairs={{0,1},{1,2},{2,3},{3,0},{4,5},{5,6},{6,7},{7,4},{8,9},{9,10},{10,1... | collective-permute-start | bytes 430088 | tf_op jit(solution)/shard_map/ppermute | solution.py:301
  9.1 64.3 %collective-permute-start.32 = (bf16[1,40,1792]{2,1,0:T(8,128)(2,1)}, bf16[1,40,1792]{2,1,0:T(8,128)(2,1)S(1)}, u32[]{:S(2)}, u32[]{:S(2)}) collective-permute-start(bf16[1,40,1792]{2,1,0:T(8,128)(2,1)} %get-tuple-element.73.refs_0_), channel_id=1, source_target_pairs={{0,8},{4,12},{8,0},{12,4},{1,9},{5,13},{9,1},{13,5},{2,10},{6,14},... | collective-permute-start | bytes 430088 | tf_op jit(solution)/shard_map/ppermute | solution.py:297
  10.6 64.2 %collective-permute-start.30 = (bf16[1,40,1792]{2,1,0:T(8,128)(2,1)}, bf16[1,40,1792]{2,1,0:T(8,128)(2,1)S(1)}, u32[]{:S(2)}, u32[]{:S(2)}) collective-permute-start(bf16[1,40,1792]{2,1,0:T(8,128)(2,1)} %get-tuple-element.73.refs_0_), channel_id=1, source_target_pairs={{0,4},{4,0},{8,12},{12,8},{1,5},{5,1},{9,13},{13,9},{2,6},{6,2},{1... | collective-permute-start | bytes 430088 | tf_op jit(solution)/shard_map/ppermute | solution.py:297
  10.6 64.2 %collective-permute-start.23 = (bf16[1,40,1792]{2,1,0:T(8,128)(2,1)}, bf16[1,40,1792]{2,1,0:T(8,128)(2,1)S(1)}, u32[]{:S(2)}, u32[]{:S(2)}) collective-permute-start(bf16[1,40,1792]{2,1,0:T(8,128)(2,1)} %get-tuple-element.69.refs_0_), channel_id=1, source_target_pairs={{0,8},{4,12},{8,0},{12,4},{1,9},{5,13},{9,1},{13,5},{2,10},{6,14},... | collective-permute-start | bytes 430088 | tf_op jit(solution)/shard_map/ppermute | solution.py:297
  11.1 63.7 %collective-permute-start.21 = (bf16[1,40,1792]{2,1,0:T(8,128)(2,1)}, bf16[1,40,1792]{2,1,0:T(8,128)(2,1)S(1)}, u32[]{:S(2)}, u32[]{:S(2)}) collective-permute-start(bf16[1,40,1792]{2,1,0:T(8,128)(2,1)} %get-tuple-element.69.refs_0_), channel_id=1, source_target_pairs={{0,4},{4,0},{8,12},{12,8},{1,5},{5,1},{9,13},{13,9},{2,6},{6,2},{1... | collective-permute-start | bytes 430088 | tf_op jit(solution)/shard_map/ppermute | solution.py:297
  15.1 55.6 %copy-start.53 = (bf16[1,40,1792]{2,1,0:T(8,128)(2,1)S(1)}, bf16[1,40,1792]{2,1,0:T(8,128)(2,1)}, u32[]{:S(2)}) copy-start(bf16[1,40,1792]{2,1,0:T(8,128)(2,1)} %get-tuple-element.68) | copy-start | bytes 430084
  15.1 7.1 %collective-permute-start.18 = (bf16[1,40,1792]{2,1,0:T(8,128)(2,1)}, bf16[1,40,1792]{2,1,0:T(8,128)(2,1)S(1)}, u32[]{:S(2)}, u32[]{:S(2)}) collective-permute-start(bf16[1,40,1792]{2,1,0:T(8,128)(2,1)} %get-tuple-element.70), channel_id=1, source_target_pairs={{0,1},{1,2},{2,3},{3,0},{4,5},{5,6},{6,7},{7,4},{8,9},{9,10},{10,1... | collective-permute-start | bytes 430088 | tf_op jit(solution)/shard_map/ppermute | solution.py:301
  22.2 54.4 %copy-start.24 = (bf16[1,40,1792]{2,1,0:T(8,128)(2,1)S(1)}, bf16[1,40,1792]{2,1,0:T(8,128)(2,1)}, u32[]{:S(2)}) copy-start(bf16[1,40,1792]{2,1,0:T(8,128)(2,1)} %get-tuple-element.61.refs_0_) | copy-start | bytes 430084
  22.2 7.2 %collective-permute-start.9 = (bf16[1,40,1792]{2,1,0:T(8,128)(2,1)}, bf16[1,40,1792]{2,1,0:T(8,128)(2,1)S(1)}, u32[]{:S(2)}, u32[]{:S(2)}) collective-permute-start(bf16[1,40,1792]{2,1,0:T(8,128)(2,1)} %get-tuple-element.66), channel_id=1, source_target_pairs={{0,1},{1,2},{2,3},{3,0},{4,5},{5,6},{6,7},{7,4},{8,9},{9,10},{10,1... | collective-permute-start | bytes 430088 | tf_op jit(solution)/shard_map/ppermute | solution.py:301
  29.4 7.7 %collective-permute-start = (bf16[1,40,1792]{2,1,0:T(8,128)(2,1)}, bf16[1,40,1792]{2,1,0:T(8,128)(2,1)S(1)}, u32[]{:S(2)}, u32[]{:S(2)}) collective-permute-start(bf16[1,40,1792]{2,1,0:T(8,128)(2,1)} %get-tuple-element.62), channel_id=1, source_target_pairs={{0,1},{1,2},{2,3},{3,0},{4,5},{5,6},{6,7},{7,4},{8,9},{9,10},{10,1... | collective-permute-start | bytes 430088 | tf_op jit(solution)/shard_map/ppermute | solution.py:301
  37.1 6.4 %collective-permute-start.28 = (bf16[1,40,1792]{2,1,0:T(8,128)(2,1)}, bf16[1,40,1792]{2,1,0:T(8,128)(2,1)S(1)}, u32[]{:S(2)}, u32[]{:S(2)}) collective-permute-start(bf16[1,40,1792]{2,1,0:T(8,128)(2,1)} %get-tuple-element.75), channel_id=1, source_target_pairs={{0,2},{1,3},{2,0},{3,1},{4,6},{5,7},{6,4},{7,5},{8,10},{9,11},{10,... | collective-permute-start | bytes 430088 | tf_op jit(solution)/shard_map/ppermute | solution.py:301
  43.5 5.4 %collective-permute-start.29 = (bf16[1,40,1792]{2,1,0:T(8,128)(2,1)S(1)}, bf16[1,40,1792]{2,1,0:T(8,128)(2,1)S(1)}, u32[]{:S(2)}, u32[]{:S(2)}) collective-permute-start(bf16[1,40,1792]{2,1,0:T(8,128)(2,1)S(1)} %copy-done.59), channel_id=1, source_target_pairs={{0,3},{1,0},{2,1},{3,2},{4,7},{5,4},{6,5},{7,6},{8,11},{9,8},{10,9... | collective-permute-start | bytes 430088 | tf_op jit(solution)/shard_map/ppermute | solution.py:301
  48.9 6.6 %collective-permute-start.19 = (bf16[1,40,1792]{2,1,0:T(8,128)(2,1)S(1)}, bf16[1,40,1792]{2,1,0:T(8,128)(2,1)S(1)}, u32[]{:S(2)}, u32[]{:S(2)}) collective-permute-start(bf16[1,40,1792]{2,1,0:T(8,128)(2,1)S(1)} %copy-done.56), channel_id=1, source_target_pairs={{0,2},{1,3},{2,0},{3,1},{4,6},{5,7},{6,4},{7,5},{8,10},{9,11},{10,... | collective-permute-start | bytes 430088 | tf_op jit(solution)/shard_map/ppermute | solution.py:301
  50.3 69.3 %copy-start.7 = (bf16[3,40,1792]{2,1,0:T(8,128)(2,1)}, bf16[3,40,1792]{2,1,0:T(8,128)(2,1)S(1)}, u32[]{:S(2)}) copy-start(bf16[3,40,1792]{2,1,0:T(8,128)(2,1)S(1)} %constant_dynamic-update-slice_fusion.9.refs_1_) | copy-start | bytes 1290244
  55.5 7.6 %collective-permute-start.20 = (bf16[1,40,1792]{2,1,0:T(8,128)(2,1)S(1)}, bf16[1,40,1792]{2,1,0:T(8,128)(2,1)S(1)}, u32[]{:S(2)}, u32[]{:S(2)}) collective-permute-start(bf16[1,40,1792]{2,1,0:T(8,128)(2,1)S(1)} %copy-done.55), channel_id=1, source_target_pairs={{0,3},{1,0},{2,1},{3,2},{4,7},{5,4},{6,5},{7,6},{8,11},{9,8},{10,9... | collective-permute-start | bytes 430088 | tf_op jit(solution)/shard_map/ppermute | solution.py:301
  63.1 7.5 %collective-permute-start.10 = (bf16[1,40,1792]{2,1,0:T(8,128)(2,1)S(1)}, bf16[1,40,1792]{2,1,0:T(8,128)(2,1)S(1)}, u32[]{:S(2)}, u32[]{:S(2)}) collective-permute-start(bf16[1,40,1792]{2,1,0:T(8,128)(2,1)S(1)} %copy-done.54), channel_id=1, source_target_pairs={{0,2},{1,3},{2,0},{3,1},{4,6},{5,7},{6,4},{7,5},{8,10},{9,11},{10,... | collective-permute-start | bytes 430088 | tf_op jit(solution)/shard_map/ppermute | solution.py:301
  64.1 68.2 %copy-start.6 = (bf16[3,40,1792]{2,1,0:T(8,128)(2,1)}, bf16[3,40,1792]{2,1,0:T(8,128)(2,1)S(1)}, u32[]{:S(2)}) copy-start(bf16[3,40,1792]{2,1,0:T(8,128)(2,1)S(1)} %constant_dynamic-update-slice_fusion.6.refs_1_) | copy-start | bytes 1290244
  70.7 5.9 %collective-permute-start.11 = (bf16[1,40,1792]{2,1,0:T(8,128)(2,1)S(1)}, bf16[1,40,1792]{2,1,0:T(8,128)(2,1)S(1)}, u32[]{:S(2)}, u32[]{:S(2)}) collective-permute-start(bf16[1,40,1792]{2,1,0:T(8,128)(2,1)S(1)} %copy-done.53), channel_id=1, source_target_pairs={{0,3},{1,0},{2,1},{3,2},{4,7},{5,4},{6,5},{7,6},{8,11},{9,8},{10,9... | collective-permute-start | bytes 430088 | tf_op jit(solution)/shard_map/ppermute | solution.py:301
  73.4 5.2 %collective-permute-start.14 = (bf16[1,40,1792]{2,1,0:T(8,128)(2,1)S(1)}, bf16[1,40,1792]{2,1,0:T(8,128)(2,1)S(1)}, u32[]{:S(2)}, u32[]{:S(2)}) collective-permute-start(bf16[1,40,1792]{2,1,0:T(8,128)(2,1)S(1)} %copy-done.25), channel_id=1, source_target_pairs={{0,8},{4,12},{8,0},{12,4},{1,9},{5,13},{9,1},{13,5},{2,10},{6,14},... | collective-permute-start | bytes 430088 | tf_op jit(solution)/shard_map/ppermute | solution.py:297
  74.8 5.1 %collective-permute-start.12 = (bf16[1,40,1792]{2,1,0:T(8,128)(2,1)S(1)}, bf16[1,40,1792]{2,1,0:T(8,128)(2,1)S(1)}, u32[]{:S(2)}, u32[]{:S(2)}) collective-permute-start(bf16[1,40,1792]{2,1,0:T(8,128)(2,1)S(1)} %copy-done.25), channel_id=1, source_target_pairs={{0,4},{4,0},{8,12},{12,8},{1,5},{5,1},{9,13},{13,9},{2,6},{6,2},{1... | collective-permute-start | bytes 430088 | tf_op jit(solution)/shard_map/ppermute | solution.py:297
  74.8 57.6 %copy-start.26 = (bf16[1,40,1792]{2,1,0:T(8,128)(2,1)}, bf16[1,40,1792]{2,1,0:T(8,128)(2,1)S(1)}, u32[]{:S(2)}) copy-start(bf16[1,40,1792]{2,1,0:T(8,128)(2,1)S(1)} %collective-permute-done.23.refs_4_) | copy-start | bytes 430084
  74.8 9.0 %collective-permute-start.1 = (bf16[1,40,1792]{2,1,0:T(8,128)(2,1)S(1)}, bf16[1,40,1792]{2,1,0:T(8,128)(2,1)S(1)}, u32[]{:S(2)}, u32[]{:S(2)}) collective-permute-start(bf16[1,40,1792]{2,1,0:T(8,128)(2,1)S(1)} %copy-done.52), channel_id=1, source_target_pairs={{0,2},{1,3},{2,0},{3,1},{4,6},{5,7},{6,4},{7,5},{8,10},{9,11},{10,... | collective-permute-start | bytes 430088 | tf_op jit(solution)/shard_map/ppermute | solution.py:301
  74.9 57.5 %copy-start.27 = (bf16[1,40,1792]{2,1,0:T(8,128)(2,1)}, bf16[1,40,1792]{2,1,0:T(8,128)(2,1)S(1)}, u32[]{:S(2)}) copy-start(bf16[1,40,1792]{2,1,0:T(8,128)(2,1)S(1)} %collective-permute-done.21.refs_2_) | copy-start | bytes 430084
  74.9 9.7 %collective-permute-start.2 = (bf16[1,40,1792]{2,1,0:T(8,128)(2,1)S(1)}, bf16[1,40,1792]{2,1,0:T(8,128)(2,1)S(1)}, u32[]{:S(2)}, u32[]{:S(2)}) collective-permute-start(bf16[1,40,1792]{2,1,0:T(8,128)(2,1)S(1)} %copy-done.51), channel_id=1, source_target_pairs={{0,3},{1,0},{2,1},{3,2},{4,7},{5,4},{6,5},{7,6},{8,11},{9,8},{10,9... | collective-permute-start | bytes 430088 | tf_op jit(solution)/shard_map/ppermute | solution.py:301
  76.6 8.0 %collective-permute-start.5 = (bf16[1,40,1792]{2,1,0:T(8,128)(2,1)S(1)}, bf16[1,40,1792]{2,1,0:T(8,128)(2,1)S(1)}, u32[]{:S(2)}, u32[]{:S(2)}) collective-permute-start(bf16[1,40,1792]{2,1,0:T(8,128)(2,1)S(1)} %copy-done.24), channel_id=1, source_target_pairs={{0,8},{4,12},{8,0},{12,4},{1,9},{5,13},{9,1},{13,5},{2,10},{6,14},... | collective-permute-start | bytes 430088 | tf_op jit(solution)/shard_map/ppermute | solution.py:297
  78.6 13.9 %collective-permute-start.33 = (bf16[3,40,1792]{2,1,0:T(8,128)(2,1)S(1)}, bf16[3,40,1792]{2,1,0:T(8,128)(2,1)S(1)}, u32[]{:S(2)}, u32[]{:S(2)}) collective-permute-start(bf16[3,40,1792]{2,1,0:T(8,128)(2,1)S(1)} %constant_dynamic-update-slice_fusion.9.refs_1_), channel_id=1, source_target_pairs={{0,8},{4,12},{8,0},{12,4},{1,9},{5,13},{9,1},{13,5},{2,10},{6,14},... | collective-permute-start | bytes 1290248 | tf_op jit(solution)/shard_map/ppermute | solution.py:297
  79.9 14.2 %collective-permute-start.31 = (bf16[3,40,1792]{2,1,0:T(8,128)(2,1)S(1)}, bf16[3,40,1792]{2,1,0:T(8,128)(2,1)S(1)}, u32[]{:S(2)}, u32[]{:S(2)}) collective-permute-start(bf16[3,40,1792]{2,1,0:T(8,128)(2,1)S(1)} %constant_dynamic-update-slice_fusion.9.refs_1_), channel_id=1, source_target_pairs={{0,4},{4,0},{8,12},{12,8},{1,5},{5,1},{9,13},{13,9},{2,6},{6,2},{1... | collective-permute-start | bytes 1290248 | tf_op jit(solution)/shard_map/ppermute | solution.py:297
  83.8 17.8 %collective-permute-start.24 = (bf16[3,40,1792]{2,1,0:T(8,128)(2,1)S(1)}, bf16[3,40,1792]{2,1,0:T(8,128)(2,1)S(1)}, u32[]{:S(2)}, u32[]{:S(2)}) collective-permute-start(bf16[3,40,1792]{2,1,0:T(8,128)(2,1)S(1)} %constant_dynamic-update-slice_fusion.6.refs_1_), channel_id=1, source_target_pairs={{0,8},{4,12},{8,0},{12,4},{1,9},{5,13},{9,1},{13,5},{2,10},{6,14},... | collective-permute-start | bytes 1290248 | tf_op jit(solution)/shard_map/ppermute | solution.py:297
  84.6 1.4 collective-permute-start.34
  84.6 62.3 %copy-start.31 = (bf16[1,40,1792]{2,1,0:T(8,128)(2,1)}, bf16[1,40,1792]{2,1,0:T(8,128)(2,1)S(1)}, u32[]{:S(2)}) copy-start(bf16[1,40,1792]{2,1,0:T(8,128)(2,1)S(1)} %collective-permute-done.5.refs_4_) | copy-start | bytes 430084
  84.6 1.6 collective-permute-start.25
  86.0 15.7 %collective-permute-start.22 = (bf16[3,40,1792]{2,1,0:T(8,128)(2,1)S(1)}, bf16[3,40,1792]{2,1,0:T(8,128)(2,1)S(1)}, u32[]{:S(2)}, u32[]{:S(2)}) collective-permute-start(bf16[3,40,1792]{2,1,0:T(8,128)(2,1)S(1)} %constant_dynamic-update-slice_fusion.6.refs_1_), channel_id=1, source_target_pairs={{0,4},{4,0},{8,12},{12,8},{1,5},{5,1},{9,13},{13,9},{2,6},{6,2},{1... | collective-permute-start | bytes 1290248 | tf_op jit(solution)/shard_map/ppermute | solution.py:297
  86.2 24.7 %collective-permute-start.15 = (bf16[3,40,1792]{2,1,0:T(8,128)(2,1)S(1)}, bf16[3,40,1792]{2,1,0:T(8,128)(2,1)S(1)}, u32[]{:S(2)}, u32[]{:S(2)}) collective-permute-start(bf16[3,40,1792]{2,1,0:T(8,128)(2,1)S(1)} %constant_dynamic-update-slice_fusion.3.refs_1_), channel_id=1, source_target_pairs={{0,8},{4,12},{8,0},{12,4},{1,9},{5,13},{9,1},{13,5},{2,10},{6,14},... | collective-permute-start | bytes 1290248 | tf_op jit(solution)/shard_map/ppermute | solution.py:297
  92.4 26.6 %collective-permute-start.6 = (bf16[3,40,1792]{2,1,0:T(8,128)(2,1)S(1)}, bf16[3,40,1792]{2,1,0:T(8,128)(2,1)S(1)}, u32[]{:S(2)}, u32[]{:S(2)}) collective-permute-start(bf16[3,40,1792]{2,1,0:T(8,128)(2,1)S(1)} %constant_dynamic-update-slice_fusion.refs_1_), channel_id=1, source_target_pairs={{0,8},{4,12},{8,0},{12,4},{1,9},{5,13},{9,1},{13,5},{2,10},{6,14},... | collective-permute-start | bytes 1290248 | tf_op jit(solution)/shard_map/ppermute | solution.py:297
  94.0 25.0 %collective-permute-start.35 = (bf16[3,40,1792]{2,1,0:T(8,128)(2,1)S(1)}, bf16[3,40,1792]{2,1,0:T(8,128)(2,1)S(1)}, u32[]{:S(2)}, u32[]{:S(2)}) collective-permute-start(bf16[3,40,1792]{2,1,0:T(8,128)(2,1)S(1)} %collective-permute-done.33.refs_5_), channel_id=1, source_target_pairs={{0,4},{4,0},{8,12},{12,8},{1,5},{5,1},{9,13},{13,9},{2,6},{6,2},{1... | collective-permute-start | bytes 1290248 | tf_op jit(solution)/shard_map/ppermute | solution.py:297
  101.7 30.8 %collective-permute-start.26 = (bf16[3,40,1792]{2,1,0:T(8,128)(2,1)S(1)}, bf16[3,40,1792]{2,1,0:T(8,128)(2,1)S(1)}, u32[]{:S(2)}, u32[]{:S(2)}) collective-permute-start(bf16[3,40,1792]{2,1,0:T(8,128)(2,1)S(1)} %collective-permute-done.24.refs_5_), channel_id=1, source_target_pairs={{0,4},{4,0},{8,12},{12,8},{1,5},{5,1},{9,13},{13,9},{2,6},{6,2},{1... | collective-permute-start | bytes 1290248 | tf_op jit(solution)/shard_map/ppermute | solution.py:297
  101.7 45.2 %collective-permute-start.13 = (bf16[3,40,1792]{2,1,0:T(8,128)(2,1)S(1)}, bf16[3,40,1792]{2,1,0:T(8,128)(2,1)S(1)}, u32[]{:S(2)}, u32[]{:S(2)}) collective-permute-start(bf16[3,40,1792]{2,1,0:T(8,128)(2,1)S(1)} %constant_dynamic-update-slice_fusion.3.refs_1_), channel_id=1, source_target_pairs={{0,4},{4,0},{8,12},{12,8},{1,5},{5,1},{9,13},{13,9},{2,6},{6,2},{1... | collective-permute-start | bytes 1290248 | tf_op jit(solution)/shard_map/ppermute | solution.py:297
  110.9 36.1 %collective-permute-start.17 = (bf16[3,40,1792]{2,1,0:T(8,128)(2,1)S(1)}, bf16[3,40,1792]{2,1,0:T(8,128)(2,1)S(1)}, u32[]{:S(2)}, u32[]{:S(2)}) collective-permute-start(bf16[3,40,1792]{2,1,0:T(8,128)(2,1)S(1)} %collective-permute-done.15.refs_5_), channel_id=1, source_target_pairs={{0,4},{4,0},{8,12},{12,8},{1,5},{5,1},{9,13},{13,9},{2,6},{6,2},{1... | collective-permute-start | bytes 1290248 | tf_op jit(solution)/shard_map/ppermute | solution.py:297
  119.0 41.9 %collective-permute-start.4 = (bf16[3,40,1792]{2,1,0:T(8,128)(2,1)S(1)}, bf16[3,40,1792]{2,1,0:T(8,128)(2,1)S(1)}, u32[]{:S(2)}, u32[]{:S(2)}) collective-permute-start(bf16[3,40,1792]{2,1,0:T(8,128)(2,1)S(1)} %constant_dynamic-update-slice_fusion.refs_1_), channel_id=1, source_target_pairs={{0,4},{4,0},{8,12},{12,8},{1,5},{5,1},{9,13},{13,9},{2,6},{6,2},{1... | collective-permute-start | bytes 1290248 | tf_op jit(solution)/shard_map/ppermute | solution.py:297
  119.1 41.9 %collective-permute-start.8 = (bf16[3,40,1792]{2,1,0:T(8,128)(2,1)S(1)}, bf16[3,40,1792]{2,1,0:T(8,128)(2,1)S(1)}, u32[]{:S(2)}, u32[]{:S(2)}) collective-permute-start(bf16[3,40,1792]{2,1,0:T(8,128)(2,1)S(1)} %collective-permute-done.6.refs_5_), channel_id=1, source_target_pairs={{0,4},{4,0},{8,12},{12,8},{1,5},{5,1},{9,13},{13,9},{2,6},{6,2},{1... | collective-permute-start | bytes 1290248 | tf_op jit(solution)/shard_map/ppermute | solution.py:297
  132.5 13.9 %collective-permute-start.16 = (bf16[1,40,1792]{2,1,0:T(8,128)(2,1)S(1)}, bf16[1,40,1792]{2,1,0:T(8,128)(2,1)S(1)}, u32[]{:S(2)}, u32[]{:S(2)}) collective-permute-start(bf16[1,40,1792]{2,1,0:T(8,128)(2,1)S(1)} %collective-permute-done.14.refs_4_), channel_id=1, source_target_pairs={{0,4},{4,0},{8,12},{12,8},{1,5},{5,1},{9,13},{13,9},{2,6},{6,2},{1... | collective-permute-start | bytes 430088 | tf_op jit(solution)/shard_map/ppermute | solution.py:297
  146.4 14.5 %collective-permute-start.3 = (bf16[1,40,1792]{2,1,0:T(8,128)(2,1)S(1)}, bf16[1,40,1792]{2,1,0:T(8,128)(2,1)S(1)}, u32[]{:S(2)}, u32[]{:S(2)}) collective-permute-start(bf16[1,40,1792]{2,1,0:T(8,128)(2,1)S(1)} %copy-done.24), channel_id=1, source_target_pairs={{0,4},{4,0},{8,12},{12,8},{1,5},{5,1},{9,13},{13,9},{2,6},{6,2},{1... | collective-permute-start | bytes 430088 | tf_op jit(solution)/shard_map/ppermute | solution.py:297
  146.9 14.0 %collective-permute-start.7 = (bf16[1,40,1792]{2,1,0:T(8,128)(2,1)S(1)}, bf16[1,40,1792]{2,1,0:T(8,128)(2,1)S(1)}, u32[]{:S(2)}, u32[]{:S(2)}) collective-permute-start(bf16[1,40,1792]{2,1,0:T(8,128)(2,1)S(1)} %collective-permute-done.5.refs_4_), channel_id=1, source_target_pairs={{0,4},{4,0},{8,12},{12,8},{1,5},{5,1},{9,13},{13,9},{2,6},{6,2},{1... | collective-permute-start | bytes 430088 | tf_op jit(solution)/shard_map/ppermute | solution.py:297
  194.6 20.7 %collective-permute-start.51 = (bf16[8,40,1792]{2,1,0:T(8,128)(2,1)S(1)}, bf16[8,40,1792]{2,1,0:T(8,128)(2,1)S(1)}, u32[]{:S(2)}, u32[]{:S(2)}) collective-permute-start(bf16[8,40,1792]{2,1,0:T(8,128)(2,1)S(1)} %copy-done.50), channel_id=1, source_target_pairs={{0,4},{4,0},{8,12},{12,8},{1,5},{5,1},{9,13},{13,9},{2,6},{6,2},{1... | collective-permute-start | bytes 3440648 | tf_op jit(solution)/shard_map/ppermute | solution.py:297
  195.0 24.8 %collective-permute-start.46 = (bf16[8,40,1792]{2,1,0:T(8,128)(2,1)}, bf16[8,40,1792]{2,1,0:T(8,128)(2,1)S(1)}, u32[]{:S(2)}, u32[]{:S(2)}) collective-permute-start(bf16[8,40,1792]{2,1,0:T(8,128)(2,1)} %get-tuple-element.100), channel_id=1, source_target_pairs={{0,4},{4,0},{8,12},{12,8},{1,5},{5,1},{9,13},{13,9},{2,6},{6,2},{1... | collective-permute-start | bytes 3440648 | tf_op jit(solution)/shard_map/ppermute | solution.py:297
  205.0 20.0 %collective-permute-start.41 = (bf16[8,40,1792]{2,1,0:T(8,128)(2,1)}, bf16[8,40,1792]{2,1,0:T(8,128)(2,1)S(1)}, u32[]{:S(2)}, u32[]{:S(2)}) collective-permute-start(bf16[8,40,1792]{2,1,0:T(8,128)(2,1)} %get-tuple-element.92), channel_id=1, source_target_pairs={{0,4},{4,0},{8,12},{12,8},{1,5},{5,1},{9,13},{13,9},{2,6},{6,2},{1... | collective-permute-start | bytes 3440648 | tf_op jit(solution)/shard_map/ppermute | solution.py:297
  215.3 14.3 %collective-permute-start.36 = (bf16[8,40,1792]{2,1,0:T(8,128)(2,1)}, bf16[8,40,1792]{2,1,0:T(8,128)(2,1)S(1)}, u32[]{:S(2)}, u32[]{:S(2)}) collective-permute-start(bf16[8,40,1792]{2,1,0:T(8,128)(2,1)} %get-tuple-element.84), channel_id=1, source_target_pairs={{0,4},{4,0},{8,12},{12,8},{1,5},{5,1},{9,13},{13,9},{2,6},{6,2},{1... | collective-permute-start | bytes 3440648 | tf_op jit(solution)/shard_map/ppermute | solution.py:297
  219.1 16.0 %collective-permute-start.52 = (bf16[4,40,1792]{2,1,0:T(8,128)(2,1)}, bf16[4,40,1792]{2,1,0:T(8,128)(2,1)S(1)}, u32[]{:S(2)}, u32[]{:S(2)}) collective-permute-start(bf16[4,40,1792]{2,1,0:T(8,128)(2,1)} %get-tuple-element.110), channel_id=1, source_target_pairs={{0,8},{4,12},{8,0},{12,4},{1,9},{5,13},{9,1},{13,5},{2,10},{6,14},... | collective-permute-start | bytes 1720328 | tf_op jit(solution)/shard_map/ppermute | solution.py:297
  223.7 23.6 %collective-permute-start.47 = (bf16[4,40,1792]{2,1,0:T(8,128)(2,1)}, bf16[4,40,1792]{2,1,0:T(8,128)(2,1)S(1)}, u32[]{:S(2)}, u32[]{:S(2)}) collective-permute-start(bf16[4,40,1792]{2,1,0:T(8,128)(2,1)} %get-tuple-element.102), channel_id=1, source_target_pairs={{0,8},{4,12},{8,0},{12,4},{1,9},{5,13},{9,1},{13,5},{2,10},{6,14},... | collective-permute-start | bytes 1720328 | tf_op jit(solution)/shard_map/ppermute | solution.py:297
  228.8 30.8 %collective-permute-start.42 = (bf16[4,40,1792]{2,1,0:T(8,128)(2,1)}, bf16[4,40,1792]{2,1,0:T(8,128)(2,1)S(1)}, u32[]{:S(2)}, u32[]{:S(2)}) collective-permute-start(bf16[4,40,1792]{2,1,0:T(8,128)(2,1)} %get-tuple-element.94), channel_id=1, source_target_pairs={{0,8},{4,12},{8,0},{12,4},{1,9},{5,13},{9,1},{13,5},{2,10},{6,14},... | collective-permute-start | bytes 1720328 | tf_op jit(solution)/shard_map/ppermute | solution.py:297
  233.3 38.2 %collective-permute-start.37 = (bf16[4,40,1792]{2,1,0:T(8,128)(2,1)}, bf16[4,40,1792]{2,1,0:T(8,128)(2,1)S(1)}, u32[]{:S(2)}, u32[]{:S(2)}) collective-permute-start(bf16[4,40,1792]{2,1,0:T(8,128)(2,1)} %get-tuple-element.86), channel_id=1, source_target_pairs={{0,8},{4,12},{8,0},{12,4},{1,9},{5,13},{9,1},{13,5},{2,10},{6,14},... | collective-permute-start | bytes 1720328 | tf_op jit(solution)/shard_map/ppermute | solution.py:297
  238.0 35.1 %collective-permute-start.53 = (bf16[1,40,1792]{2,1,0:T(8,128)(2,1)}, bf16[1,40,1792]{2,1,0:T(8,128)(2,1)S(1)}, u32[]{:S(2)}, u32[]{:S(2)}) collective-permute-start(bf16[1,40,1792]{2,1,0:T(8,128)(2,1)} %get-tuple-element.112), channel_id=1, source_target_pairs={{0,3},{1,0},{2,1},{3,2},{4,7},{5,4},{6,5},{7,6},{8,11},{9,8},{10,9... | collective-permute-start | bytes 430088 | tf_op jit(solution)/shard_map/ppermute | solution.py:301
  240.8 34.1 %collective-permute-start.54 = (bf16[1,40,1792]{2,1,0:T(8,128)(2,1)}, bf16[1,40,1792]{2,1,0:T(8,128)(2,1)S(1)}, u32[]{:S(2)}, u32[]{:S(2)}) collective-permute-start(bf16[1,40,1792]{2,1,0:T(8,128)(2,1)} %get-tuple-element.113), channel_id=1, source_target_pairs={{0,2},{1,3},{2,0},{3,1},{4,6},{5,7},{6,4},{7,5},{8,10},{9,11},{10,... | collective-permute-start | bytes 430088 | tf_op jit(solution)/shard_map/ppermute | solution.py:301
  247.4 31.7 %collective-permute-start.55 = (bf16[1,40,1792]{2,1,0:T(8,128)(2,1)}, bf16[1,40,1792]{2,1,0:T(8,128)(2,1)S(1)}, u32[]{:S(2)}, u32[]{:S(2)}) collective-permute-start(bf16[1,40,1792]{2,1,0:T(8,128)(2,1)} %get-tuple-element.114), channel_id=1, source_target_pairs={{0,1},{1,2},{2,3},{3,0},{4,5},{5,6},{6,7},{7,4},{8,9},{9,10},{10,1... | collective-permute-start | bytes 430088 | tf_op jit(solution)/shard_map/ppermute | solution.py:301
  259.6 19.5 %collective-permute-start.48 = (bf16[1,40,1792]{2,1,0:T(8,128)(2,1)}, bf16[1,40,1792]{2,1,0:T(8,128)(2,1)S(1)}, u32[]{:S(2)}, u32[]{:S(2)}) collective-permute-start(bf16[1,40,1792]{2,1,0:T(8,128)(2,1)} %get-tuple-element.104), channel_id=1, source_target_pairs={{0,3},{1,0},{2,1},{3,2},{4,7},{5,4},{6,5},{7,6},{8,11},{9,8},{10,9... | collective-permute-start | bytes 430088 | tf_op jit(solution)/shard_map/ppermute | solution.py:301
  271.5 13.6 %collective-permute-start.49 = (bf16[1,40,1792]{2,1,0:T(8,128)(2,1)S(1)}, bf16[1,40,1792]{2,1,0:T(8,128)(2,1)S(1)}, u32[]{:S(2)}, u32[]{:S(2)}) collective-permute-start(bf16[1,40,1792]{2,1,0:T(8,128)(2,1)S(1)} %copy-done.61), channel_id=1, source_target_pairs={{0,2},{1,3},{2,0},{3,1},{4,6},{5,7},{6,4},{7,5},{8,10},{9,11},{10,... | collective-permute-start | bytes 430088 | tf_op jit(solution)/shard_map/ppermute | solution.py:301
  273.1 15.1 %collective-permute-start.50 = (bf16[1,40,1792]{2,1,0:T(8,128)(2,1)S(1)}, bf16[1,40,1792]{2,1,0:T(8,128)(2,1)S(1)}, u32[]{:S(2)}, u32[]{:S(2)}) collective-permute-start(bf16[1,40,1792]{2,1,0:T(8,128)(2,1)S(1)} %copy-done.60), channel_id=1, source_target_pairs={{0,1},{1,2},{2,3},{3,0},{4,5},{5,6},{6,7},{7,4},{8,9},{9,10},{10,1... | collective-permute-start | bytes 430088 | tf_op jit(solution)/shard_map/ppermute | solution.py:301
  274.8 20.0 %collective-permute-start.43 = (bf16[1,40,1792]{2,1,0:T(8,128)(2,1)}, bf16[1,40,1792]{2,1,0:T(8,128)(2,1)S(1)}, u32[]{:S(2)}, u32[]{:S(2)}) collective-permute-start(bf16[1,40,1792]{2,1,0:T(8,128)(2,1)} %get-tuple-element.96), channel_id=1, source_target_pairs={{0,3},{1,0},{2,1},{3,2},{4,7},{5,4},{6,5},{7,6},{8,11},{9,8},{10,9... | collective-permute-start | bytes 430088 | tf_op jit(solution)/shard_map/ppermute | solution.py:301
  279.1 23.4 %collective-permute-start.44 = (bf16[1,40,1792]{2,1,0:T(8,128)(2,1)S(1)}, bf16[1,40,1792]{2,1,0:T(8,128)(2,1)S(1)}, u32[]{:S(2)}, u32[]{:S(2)}) collective-permute-start(bf16[1,40,1792]{2,1,0:T(8,128)(2,1)S(1)} %copy-done.58), channel_id=1, source_target_pairs={{0,2},{1,3},{2,0},{3,1},{4,6},{5,7},{6,4},{7,5},{8,10},{9,11},{10,... | collective-permute-start | bytes 430088 | tf_op jit(solution)/shard_map/ppermute | solution.py:301
  279.2 23.3 %collective-permute-start.45 = (bf16[1,40,1792]{2,1,0:T(8,128)(2,1)S(1)}, bf16[1,40,1792]{2,1,0:T(8,128)(2,1)S(1)}, u32[]{:S(2)}, u32[]{:S(2)}) collective-permute-start(bf16[1,40,1792]{2,1,0:T(8,128)(2,1)S(1)} %copy-done.57), channel_id=1, source_target_pairs={{0,1},{1,2},{2,3},{3,0},{4,5},{5,6},{6,7},{7,4},{8,9},{9,10},{10,1... | collective-permute-start | bytes 430088 | tf_op jit(solution)/shard_map/ppermute | solution.py:301
  285.1 20.5 %collective-permute-start.38 = (bf16[1,40,1792]{2,1,0:T(8,128)(2,1)}, bf16[1,40,1792]{2,1,0:T(8,128)(2,1)S(1)}, u32[]{:S(2)}, u32[]{:S(2)}) collective-permute-start(bf16[1,40,1792]{2,1,0:T(8,128)(2,1)} %get-tuple-element.88), channel_id=1, source_target_pairs={{0,3},{1,0},{2,1},{3,2},{4,7},{5,4},{6,5},{7,6},{8,11},{9,8},{10,9... | collective-permute-start | bytes 430088 | tf_op jit(solution)/shard_map/ppermute | solution.py:301
  288.3 20.2 %collective-permute-start.39 = (bf16[1,40,1792]{2,1,0:T(8,128)(2,1)}, bf16[1,40,1792]{2,1,0:T(8,128)(2,1)S(1)}, u32[]{:S(2)}, u32[]{:S(2)}) collective-permute-start(bf16[1,40,1792]{2,1,0:T(8,128)(2,1)} %get-tuple-element.89), channel_id=1, source_target_pairs={{0,2},{1,3},{2,0},{3,1},{4,6},{5,7},{6,4},{7,5},{8,10},{9,11},{10,... | collective-permute-start | bytes 430088 | tf_op jit(solution)/shard_map/ppermute | solution.py:301
  294.8 13.6 %collective-permute-start.40 = (bf16[1,40,1792]{2,1,0:T(8,128)(2,1)}, bf16[1,40,1792]{2,1,0:T(8,128)(2,1)S(1)}, u32[]{:S(2)}, u32[]{:S(2)}) collective-permute-start(bf16[1,40,1792]{2,1,0:T(8,128)(2,1)} %get-tuple-element.90), channel_id=1, source_target_pairs={{0,1},{1,2},{2,3},{3,0},{4,5},{5,6},{6,7},{7,4},{8,9},{9,10},{10,1... | collective-permute-start | bytes 430088 | tf_op jit(solution)/shard_map/ppermute | solution.py:301
  (54 other events, 1023.5 us)

commit v2 on v1

v2 whole, which is shorter than its diff:
```python
import functools

import jax
import jax.numpy as jnp
import numpy as np
from jax import lax
from jax.experimental import pallas as pl
from jax.experimental.pallas import tpu as pltpu
from jax.sharding import PartitionSpec as P

CAP = 5
UP_PARTS = (1, 1, 1, 1)
DOWN_PARTS = (1, 1, 1, 1)
MIB = 1024 * 1024
F32, BF16 = jnp.float32, jnp.bfloat16


def pad16(n):
    return -(-n // 16) * 16


def params(mib):
    return pltpu.CompilerParams(vmem_limit_bytes=mib * MIB)


def in_vmem():
    return pl.BlockSpec(memory_space=pltpu.VMEM)


def in_hbm():
    return pl.BlockSpec(memory_space=pl.ANY)


def tie(a, *after):
    return lax.optimization_barrier((a,) + after)[0]


def cut(width, parts):
    unit = width // sum(parts)
    edges = [sum(parts[:i]) * unit for i in range(len(parts) + 1)]
    return list(zip(edges[:-1], [b - a for a, b in zip(edges[:-1], edges[1:])]))


def tile_of(width):
    for t in (512, 256, 128):
        if width % t == 0:
            return t
    return width


class Sizes:
    def __init__(self, tokens, w_gate, local_count, node_count):
        self.tok, self.width = tokens.shape
        self.exp_dev = w_gate.shape[0]
        self.hidden = w_gate.shape[2]
        self.local = local_count
        self.node = node_count
        self.R = self.exp_dev * CAP
        self.RP = pad16(self.R)
        self.MP = pad16(self.local * CAP)
        self.rows = self.local * self.RP
        self.grouped = self.exp_dev * self.MP
        self.relative = local_count <= 4
        self.up = cut(self.width, UP_PARTS)
        self.down = cut(self.width, DOWN_PARTS)

    def columns(self):
        table = np.full((self.rows, 4), -1, np.int32)
        for s in range(self.local):
            table[s * self.RP : (s + 1) * self.RP, 0] = s
            for q in range(self.R):
                table[s * self.RP + q, 1:3] = (q // CAP, q % CAP)
        return table

    def regroup(self):
        m = np.zeros((self.grouped, self.rows), np.float32)
        for s in range(self.local):
            for j in range(self.exp_dev):
                for c in range(CAP):
                    m[j * self.MP + s * CAP + c, s * self.RP + j * CAP + c] = 1
        return m


def gather_kernel(z, plan, plane_ref, table_ref, ids_ref, gates_ref, tokens_ref, weight_ref, *outs):
    block, expert, slot = (table_ref[:, i : i + 1] for i in range(3))
    plane = block
    if z.relative:
        plane = block + plane_ref[0]
        plane = jnp.where(plane >= z.local, plane - z.local, plane)
    name = jnp.where(slot >= 0, plane * z.exp_dev + expert, -1)
    ids, gates = ids_ref[...], gates_ref[...]
    top = ids.shape[0]
    hits = [ids[k : k + 1, :] == name for k in range(top)]
    named = hits[0].astype(F32)
    for k in range(1, top):
        named = named + hits[k].astype(F32)
    t0 = lax.broadcasted_iota(jnp.int32, (z.tok, z.tok), 0)
    t1 = lax.broadcasted_iota(jnp.int32, (z.tok, z.tok), 1)
    before = jnp.where(t0 < t1, 1.0, 0.0).astype(BF16)
    rank = jnp.dot(named.astype(BF16), before, preferred_element_type=F32)
    here = rank == slot.astype(F32)
    weight = jnp.zeros((z.rows, z.tok), F32)
    for k in range(top):
        weight = weight + jnp.where(hits[k] & here, gates[k : k + 1, :], 0.0)
    weight_ref[...] = weight
    pick = jnp.where(here, named, 0.0).astype(BF16)
    for lo, size, targets in plan:
        picked = jnp.dot(pick, tokens_ref[:, lo : lo + size], preferred_element_type=F32).astype(BF16)
        for s, (out, i, at) in enumerate(targets):
            outs[out][i, :, at : at + size] = picked[s * z.RP : s * z.RP + z.R]


def gather_rows(z, plane, ids, gates, tokens):
    shapes, plan = [], []
    if z.relative:
        shapes.append((1, z.R, z.width))
    for lo, size in z.up:
        if z.relative:
            n = len(shapes)
            shapes += [(1, z.R, size)] * (z.local - 1)
            targets = [(0, 0, lo)] + [(n + s, 0, 0) for s in range(z.local - 1)]
        else:
            targets = [(len(shapes), s, 0) for s in range(z.local)]
            shapes.append((z.local, z.R, size))
        plan.append((lo, size, targets))
    outs = pl.pallas_call(
        functools.partial(gather_kernel, z, plan),
        out_shape=[jax.ShapeDtypeStruct((z.rows, z.tok), F32)] + [jax.ShapeDtypeStruct(s, BF16) for s in shapes],
        in_specs=[pl.BlockSpec(memory_space=pltpu.SMEM)] + [in_vmem()] * 4,
        out_specs=[in_vmem()] * (1 + len(shapes)),
        compiler_params=params(32),
        name="gather_rows",
    )(plane, jnp.asarray(z.columns()), ids.T, gates.T, tokens)
    weight, outs = outs[0], list(outs[1:])
    own = outs.pop(0) if z.relative else None
    each = z.local - 1 if z.relative else 1
    return weight, own, [outs[i * each : (i + 1) * each] for i in range(len(z.up))]


def up_kernel(z, lo, size, counts, first, last, *refs):
    pieces = refs[: len(counts)]
    regroup_ref, wg_ref, wu_ref = refs[len(counts) : len(counts) + 3]
    refs = refs[len(counts) + 3 :]
    if not first:
        gin_ref, uin_ref = refs[:2]
        refs = refs[2:]
    if last:
        hidden_ref = refs[0]
        refs = refs[1:]
    else:
        gout_ref, uout_ref = refs[:2]
        refs = refs[2:]
    piece_ref, gate_ref, up_ref, rows_ref, grouped_ref, psem, gsem, usem = refs

    moves, at = [], 0
    for i, (ref, (count, whole)) in enumerate(zip(pieces, counts)):
        src = ref.at[:, :, pl.ds(lo, size)] if whole else ref
        moves.append(pltpu.make_async_copy(src, piece_ref.at[pl.ds(at, count)], psem.at[i]))
        at += count
    for move in moves:
        move.start()

    def weights(e):
        return (
            pltpu.make_async_copy(wg_ref.at[e, pl.ds(lo, size)], gate_ref.at[e], gsem.at[e]),
            pltpu.make_async_copy(wu_ref.at[e, pl.ds(lo, size)], up_ref.at[e], usem.at[e]),
        )

    for e in range(z.exp_dev):
        for move in weights(e):
            move.start()
    if z.RP > z.R:
        rows_ref[...] = jnp.zeros_like(rows_ref)
    tile = tile_of(size)
    at, moved = 0, 0
    for m in range(z.node):
        while at < (m + 1) * z.local:
            moves[moved].wait()
            count = counts[moved][0]
            for i in range(count):
                s = at - m * z.local
                rows_ref[m, s * z.RP : s * z.RP + z.R, :] = piece_ref[at]
                at += 1
            moved += 1

        def step(i, carry, m=m):
            cols = pl.ds(pl.multiple_of(i * tile, tile), tile)
            got = jnp.dot(regroup_ref[...], rows_ref[m, :, cols], preferred_element_type=F32).astype(BF16)
            grouped_ref[:, m * z.MP : (m + 1) * z.MP, cols] = got.reshape(z.exp_dev, z.MP, tile)
            return carry

        lax.fori_loop(0, size // tile, step, 0)

    def expert(e, carry):
        for move in weights(e):
            move.wait()
        rows = grouped_ref[e]
        gate = jnp.dot(rows, gate_ref[e], preferred_element_type=F32)
        up = jnp.dot(rows, up_ref[e], preferred_element_type=F32)
        if not first:
            gate = gate + gin_ref[e]
            up = up + uin_ref[e]
        if last:
            hidden_ref[e] = (gate / (1.0 + jnp.exp(-gate)) * up).astype(BF16)
        else:
            gout_ref[e] = gate
            uout_ref[e] = up
        return carry

    lax.fori_loop(0, z.exp_dev, expert, 0)


def up_chunk(z, c, pieces, regroup, w_gate, w_up, sums):
    lo, size = z.up[c]
    first, last = sums is None, c == len(z.up) - 1
    counts = [(p.shape[0], p.shape[2] != size) for p in pieces]
    acc = jax.ShapeDtypeStruct((z.exp_dev, z.node * z.MP, z.hidden), F32)
    out_shape = [jax.ShapeDtypeStruct(acc.shape, BF16)] if last else [acc, acc]
    return pl.pallas_call(
        functools.partial(up_kernel, z, lo, size, counts, first, last),
        out_shape=out_shape,
        in_specs=[in_hbm()] * len(pieces) + [in_vmem(), in_hbm(), in_hbm()] + ([] if first else [in_vmem()] * 2),
        out_specs=[in_vmem()] * len(out_shape),
        scratch_shapes=[
            pltpu.VMEM((z.node * z.local, z.R, size), BF16),
            pltpu.VMEM((z.exp_dev, size, z.hidden), BF16),
            pltpu.VMEM((z.exp_dev, size, z.hidden), BF16),
            pltpu.VMEM((z.node, z.rows, size), BF16),
            pltpu.VMEM((z.exp_dev, z.node * z.MP, size), BF16),
            pltpu.SemaphoreType.DMA((len(pieces),)),
            pltpu.SemaphoreType.DMA((z.exp_dev,)),
            pltpu.SemaphoreType.DMA((z.exp_dev,)),
        ],
        compiler_params=params(40),
        cost_estimate=pl.CostEstimate(
            flops=4 * z.exp_dev * z.node * z.MP * size * z.hidden,
            bytes_accessed=4 * z.exp_dev * size * z.hidden,
            transcendentals=0,
        ),
        name="up_chunk",
    )(*pieces, regroup, w_gate, w_up, *(() if first else sums))


def down_kernel(z, lo, size, order, hidden_ref, ungroup_ref, wd_ref, *refs):
    outs, (weight_ref, held_ref, sem) = refs[: len(order)], refs[len(order) :]

    def weights(e):
        return pltpu.make_async_copy(wd_ref.at[e, :, pl.ds(lo, size)], weight_ref.at[e], sem.at[e])

    for e in range(z.exp_dev):
        weights(e).start()

    def expert(e, carry):
        weights(e).wait()
        got = jnp.dot(hidden_ref[e], weight_ref[e], preferred_element_type=F32).astype(BF16)
        for m in range(z.node):
            held_ref[m, pl.ds(pl.multiple_of(e * z.MP, z.MP), z.MP), :] = got[m * z.MP : (m + 1) * z.MP]
        return carry

    lax.fori_loop(0, z.exp_dev, expert, 0)
    tile = tile_of(size)

    def step(i, carry):
        cols = pl.ds(pl.multiple_of(i * tile, tile), tile)
        for out, ms in zip(outs, order):
            for k, m in enumerate(ms):
                back = jnp.dot(ungroup_ref[...], held_ref[m, :, cols], preferred_element_type=F32).astype(BF16)
                for s in range(z.local):
                    out[k * z.local + s, :, cols] = back[s * z.RP : s * z.RP + z.R]
        return carry

    lax.fori_loop(0, size // tile, step, 0)


def down_chunk(z, c, hidden, ungroup, w_down, order):
    lo, size = z.down[c]
    shapes = [jax.ShapeDtypeStruct((len(ms) * z.local, z.R, size), BF16) for ms in order]
    return pl.pallas_call(
        functools.partial(down_kernel, z, lo, size, order),
        out_shape=shapes,
        in_specs=[in_vmem(), in_vmem(), in_hbm()],
        out_specs=[in_vmem()] * len(shapes),
        scratch_shapes=[
            pltpu.VMEM((z.exp_dev, z.hidden, size), BF16),
            pltpu.VMEM((z.node, z.grouped, size), BF16),
            pltpu.SemaphoreType.DMA((z.exp_dev,)),
        ],
        compiler_params=params(32),
        cost_estimate=pl.CostEstimate(
            flops=2 * z.exp_dev * z.node * z.MP * size * z.hidden,
            bytes_accessed=2 * z.exp_dev * size * z.hidden,
            transcendentals=0,
        ),
        name="down_chunk",
    )(hidden, ungroup, w_down)


def add_kernel(cuts, a_ref, b_ref, *outs):
    for out, (lo, hi, start) in zip(outs, cuts):
        out[...] = (a_ref[lo + start : hi + start].astype(F32) + b_ref[lo:hi].astype(F32)).astype(BF16)


def add_cut(a, b, cuts, start=0):
    total = sum(hi - lo for lo, hi in cuts) * a.shape[1] * a.shape[2]
    return pl.pallas_call(
        functools.partial(add_kernel, [(lo, hi, start) for lo, hi in cuts]),
        out_shape=[jax.ShapeDtypeStruct((hi - lo,) + a.shape[1:], BF16) for lo, hi in cuts],
        in_specs=[in_vmem()] * 2,
        out_specs=[in_vmem()] * len(cuts),
        compiler_params=params(32),
        cost_estimate=pl.CostEstimate(flops=total, bytes_accessed=6 * total, transcendentals=0),
        name="add_cut",
    )(a, b)


def combine_kernel(z, lo, size, blocks, weight_ref, *refs):
    pieces, (out_ref, rows_ref) = refs[: len(blocks)], refs[-2:]
    rows_ref[...] = jnp.zeros_like(rows_ref)
    for ref, (at, count) in zip(pieces, blocks):
        for i in range(count):
            rows_ref[at + i * z.RP : at + i * z.RP + z.R, :] = ref[i]
    weight = weight_ref[...].T
    extra = rows_ref.shape[0] - z.rows
    if extra:
        weight = jnp.concatenate([weight, weight[:, :extra]], axis=1)
    high = weight.astype(BF16)
    rest = weight - high.astype(F32)
    middle = rest.astype(BF16)
    low = (rest - middle.astype(F32)).astype(BF16)
    rows = rows_ref[...]
    total = jnp.dot(low, rows, preferred_element_type=F32)
    total = total + jnp.dot(middle, rows, preferred_element_type=F32)
    total = total + jnp.dot(high, rows, preferred_element_type=F32)
    out_ref[...] = total.astype(BF16)


def combine_chunk(z, c, weight, pieces, so_far):
    lo, size = z.down[c]
    blocks = [(at, count) for _, at, count in pieces]
    rows = max(at + count * z.RP for at, count in blocks)
    extra = [] if so_far is None else [so_far]
    return pl.pallas_call(
        functools.partial(combine_kernel, z, lo, size, blocks),
        grid=(1,),
        out_shape=jax.ShapeDtypeStruct((z.tok, z.width), BF16),
        in_specs=[pl.BlockSpec(weight.shape, lambda i: (0, 0))]
        + [pl.BlockSpec((n,) + p.shape[1:], lambda i: (0, 0, 0)) for p, _, n in pieces]
        + [in_hbm()] * len(extra),
        out_specs=pl.BlockSpec((z.tok, size), lambda i: (0, lo // size)),
        scratch_shapes=[pltpu.VMEM((rows, size), BF16)],
        input_output_aliases={1 + len(pieces): 0} if extra else {},
        compiler_params=params(32),
        name="combine_chunk",
    )(weight, *[p for p, _, _ in pieces], *extra)


def swap(a, mask, count):
    return lax.ppermute(a, "node", [(i, i ^ mask) for i in range(count)])


def shift(a, by, count):
    return lax.ppermute(a, "local", [(i, (i + by) % count) for i in range(count)])


def spread(a, masks, count):
    held = {0: a}
    for mask in reversed(masks):
        for m in list(held):
            held[m | mask] = swap(held[m], mask, count)
    return held


def per_device(tokens, expert_ids, gate_weights, w_gate, w_up, w_down):
    local_count, node_count = lax.axis_size("local"), lax.axis_size("node")
    z = Sizes(tokens, w_gate, local_count, node_count)
    plane = lax.axis_index("local").astype(jnp.int32).reshape(1)
    regroup = z.regroup()
    ungroup = jnp.asarray(regroup.T, BF16)
    regroup = jnp.asarray(regroup, BF16)
    weight, own, sent = gather_rows(z, plane, expert_ids, gate_weights, tokens)
    masks = []
    while 1 << len(masks) < node_count:
        masks.append(1 << len(masks))

    if z.relative:
        own_held = spread(own, masks, node_count)
    sums = None
    for c in range(len(z.up)):
        if z.relative:
            came = [shift(sent[c][s - 1], s, local_count) for s in range(1, local_count)]
            held = spread(jnp.concatenate(came, axis=0), masks, node_count)
            pieces = [a for m in range(node_count) for a in (own_held[m], held[m])]
        else:
            held = spread(lax.all_to_all(sent[c][0], "local", 0, 0, tiled=True), masks, node_count)
            pieces = [held[m] for m in range(node_count)]
        sums = up_chunk(z, c, pieces, regroup, w_gate, w_up, sums)
    hidden = sums[0]

    out = None
    count = local_count
    for c in range(len(z.down)):
        away = [m for m in range(node_count) if m & 1]
        kept = [m for m in range(node_count) if not m & 1]
        send, keep = down_chunk(z, c, hidden, ungroup, w_down, [away, kept])
        for mask in masks[:-1]:
            got = swap(send, mask, node_count)
            stay = [m for m in kept if not m & (mask << 1)]
            go = [m for m in kept if m & (mask << 1)]
            place = {m: i * count for i, m in enumerate(kept)}
            if mask << 1 == masks[-1] and z.relative:
                keep, send, send_own = add_cut(keep, got, [(0, count), (count + 1, 2 * count), (count, count + 1)])
            else:
                sums = add_cut(keep, got, [(place[m], place[m] + count) for m in stay + go])
                keep, send = sums if len(sums) == 2 else (
                    jnp.concatenate(sums[: len(stay)], axis=0),
                    jnp.concatenate(sums[len(stay) :], axis=0),
                )
            kept = stay
        got = swap(send, masks[-1], node_count)
        if z.relative:
            got_own = swap(send_own, masks[-1], node_count)
            parts = add_cut(keep, got, [(s, s + 1) for s in range(count - 1)], start=1)
            back = [shift(parts[s - 1], -s, count) for s in range(1, count)]
            pieces = [(keep, 0, 1)] + [(b, (s + 1) * z.RP, 1) for s, b in enumerate(back)] + [(got_own, z.rows, 1)]
        else:
            (summed,) = add_cut(keep, got, [(0, count)])
            pieces = [(lax.all_to_all(summed, "local", 0, 0, tiled=True), 0, count)]
        out = combine_chunk(z, c, weight, pieces, out)
    return out


def solution(mesh):
    return jax.shard_map(
        per_device,
        mesh=mesh,
        in_specs=(
            P(("parts", "node", "local"), None),
            P(("parts", "node", "local"), None),
            P(("parts", "node", "local"), None),
            P("local", None, "node"),
            P("local", None, "node"),
            P("local", "node", None),
        ),
        out_specs=P(("parts", "node", "local"), None),
        check_vma=False,
    )
```

time: 313 us -> 262 us (0.84)
  Pallas kernels: 123 us -> 71.1 us
  waiting for transfers between devices: 119 us -> 130 us
  local copies, waits for them, and re-layouts: 12.1 us -> 3.57 us
    pallas_call x21, Pallas kernels: 123 us -> 71.1 us  [the longest x4 40.7 us: up_chunk(): pl.pallas_call(functools.partial(up_kernel, z, lo, size, counts, first, l...]
    ppermute x32 -> x27, waiting for transfers between devices: 54.2 us -> 67.5 us  [swap(): return lax.ppermute(a, 'node', [(i, i ^ mask) for i in range(count)])]
    unnamed x134 -> x20, local copies, waits for them, and re-layouts: 12 us -> 3.53 us
    ppermute x32 -> x27, starting transfers between devices: 17.8 us -> 17.3 us  [swap(): return lax.ppermute(a, 'node', [(i, i ^ mask) for i in range(count)])]
  transfers between devices with their start and end apart: 56 -> 51, of which waited for: 24 -> 20; matrix products, arithmetic and copies ran while one was open for 0% -> 0% of each run, Pallas kernels for 27% -> 18%
where the time goes in v2:
time: 262 us; the launch traced here: 261 us
  waiting for transfers between devices  130 us (50%)
  Pallas kernels  71.1 us (27%)
  starting transfers between devices  56.1 us (21%)
  local copies, waits for them, and re-layouts  3.57 us (1%)
    ppermute x27, waiting for transfers between devices, swap(): return lax.ppermute(a, 'node', [(i, i ^ mask) for i in range(count)])  67.5 us
    ppermute x24, waiting for transfers between devices, shift(): lax.ppermute(a, 'local', [(i, (i + by) % count) for i in range(count)])  62.7 us
    pallas_call x4, Pallas kernels, up_chunk(): pl.pallas_call(functools.partial(up_kernel, z, lo, size, counts, first, l...  40.7 us
    ppermute x24, starting transfers between devices, shift(): lax.ppermute(a, 'local', [(i, (i + by) % count) for i in range(count)])  38.8 us
    pallas_call x4, Pallas kernels, down_chunk(): pl.pallas_call(functools.partial(down_kernel, z, lo, size, order), out_sh...  22 us
    ppermute x27, starting transfers between devices, swap(): return lax.ppermute(a, 'node', [(i, i ^ mask) for i in range(count)])  17.3 us
    pallas_call x4, Pallas kernels, combine_chunk(): pl.pallas_call(functools.partial(combine_kernel, z, lo, size, blocks), gr...  5.67 us
  transfers between devices with their start and end apart: 51, of which 20 were waited for; matrix products, arithmetic and copies ran while one was open for 0% of the time, Pallas kernels for 18%

profile of v2, /device:TPU:0, one launch (start us, length us, event | category | flops | bytes accessed | tf_op | source)
XLA Modules:
  0.0 261.3 jit_solution(17171878467853783343)
XLA Ops:
  0.0 1.2 copy-done.2
  1.2 0.9 copy-done.3
  2.1 0.7 copy-done.4
  2.8 0.7 copy-done.5
  3.4 1.2 gather_rows.1
  4.6 3.1 %collective-permute-start.21 = (bf16[1,40,1792]{2,1,0:T(8,128)(2,1)S(1)}, bf16[1,40,1792]{2,1,0:T(8,128)(2,1)S(1)}, u32[]{:S(2)}, u32[]{:S(2)}) collective-permute-start(bf16[1,40,1792]{2,1,0:T(8,128)(2,1)S(1)} %get-tuple-element.68), channel_id=1, source_target_pairs={{0,1},{1,2},{2,3},{3,0},{4,5},{5,6},{6,7},{7,4},{8,9},{9,10},{10,1... | collective-permute-start | bytes 430088 | tf_op jit(solution)/shard_map/ppermute | solution.py:362
  7.7 1.5 collective-permute-start.5
  9.2 2.6 collective-permute-start.22
  11.8 1.3 collective-permute-start.23
  13.8 9.7 %collective-permute-done.15 = bf16[1,40,1792]{2,1,0:T(8,128)(2,1)S(1)} collective-permute-done((bf16[1,40,1792]{2,1,0:T(8,128)(2,1)S(1)}, bf16[1,40,1792]{2,1,0:T(8,128)(2,1)S(1)}, u32[]{:S(2)}, u32[]{:S(2)}) %collective-permute-start.15) | collective-permute-done | bytes 143392 | tf_op jit(solution)/shard_map/ppermute | solution.py:362
  23.6 1.4 collective-permute-start.9
  25.0 5.7 %collective-permute-done.9 = bf16[1,40,1792]{2,1,0:T(8,128)(2,1)S(1)} collective-permute-done((bf16[1,40,1792]{2,1,0:T(8,128)(2,1)S(1)}, bf16[1,40,1792]{2,1,0:T(8,128)(2,1)S(1)}, u32[]{:S(2)}, u32[]{:S(2)}) %collective-permute-start.9) | collective-permute-done | bytes 143392 | tf_op jit(solution)/shard_map/ppermute | solution.py:362
  30.7 7.9 %collective-permute-done = bf16[1,40,1792]{2,1,0:T(8,128)(2,1)S(1)} collective-permute-done((bf16[1,40,1792]{2,1,0:T(8,128)(2,1)S(1)}, bf16[1,40,1792]{2,1,0:T(8,128)(2,1)S(1)}, u32[]{:S(2)}, u32[]{:S(2)}) %collective-permute-start) | collective-permute-done | bytes 143392 | tf_op jit(solution)/shard_map/ppermute | solution.py:362
  38.8 3.0 %collective-permute-start.10 = (bf16[1,40,1792]{2,1,0:T(8,128)(2,1)S(1)}, bf16[1,40,1792]{2,1,0:T(8,128)(2,1)S(1)}, u32[]{:S(2)}, u32[]{:S(2)}) collective-permute-start(bf16[1,40,1792]{2,1,0:T(8,128)(2,1)S(1)} %get-tuple-element.63), channel_id=1, source_target_pairs={{0,2},{1,3},{2,0},{3,1},{4,6},{5,7},{6,4},{7,5},{8,10},{9,11},{10,... | collective-permute-start | bytes 430088 | tf_op jit(solution)/shard_map/ppermute | solution.py:362
  41.8 7.2 %collective-permute-done.16 = bf16[1,40,1792]{2,1,0:T(8,128)(2,1)S(1)} collective-permute-done((bf16[1,40,1792]{2,1,0:T(8,128)(2,1)S(1)}, bf16[1,40,1792]{2,1,0:T(8,128)(2,1)S(1)}, u32[]{:S(2)}, u32[]{:S(2)}) %collective-permute-start.16) | collective-permute-done | bytes 143392 | tf_op jit(solution)/shard_map/ppermute | solution.py:362
  49.0 3.3 %collective-permute-start.11 = (bf16[1,40,1792]{2,1,0:T(8,128)(2,1)S(1)}, bf16[1,40,1792]{2,1,0:T(8,128)(2,1)S(1)}, u32[]{:S(2)}, u32[]{:S(2)}) collective-permute-start(bf16[1,40,1792]{2,1,0:T(8,128)(2,1)S(1)} %get-tuple-element.64), channel_id=1, source_target_pairs={{0,3},{1,0},{2,1},{3,2},{4,7},{5,4},{6,5},{7,6},{8,11},{9,8},{10,9... | collective-permute-start | bytes 430088 | tf_op jit(solution)/shard_map/ppermute | solution.py:362
  52.5 4.3 %collective-permute-done.10 = bf16[1,40,1792]{2,1,0:T(8,128)(2,1)S(1)} collective-permute-done((bf16[1,40,1792]{2,1,0:T(8,128)(2,1)S(1)}, bf16[1,40,1792]{2,1,0:T(8,128)(2,1)S(1)}, u32[]{:S(2)}, u32[]{:S(2)}) %collective-permute-start.10) | collective-permute-done | bytes 143392 | tf_op jit(solution)/shard_map/ppermute | solution.py:362
  56.8 5.6 %collective-permute-start.2 = (bf16[1,40,1792]{2,1,0:T(8,128)(2,1)S(1)}, bf16[1,40,1792]{2,1,0:T(8,128)(2,1)S(1)}, u32[]{:S(2)}, u32[]{:S(2)}) collective-permute-start(bf16[1,40,1792]{2,1,0:T(8,128)(2,1)S(1)} %get-tuple-element.61), channel_id=1, source_target_pairs={{0,3},{1,0},{2,1},{3,2},{4,7},{5,4},{6,5},{7,6},{8,11},{9,8},{10,9... | collective-permute-start | bytes 430088 | tf_op jit(solution)/shard_map/ppermute | solution.py:362
  62.5 1.2 collective-permute-start.25
  63.9 1.2 collective-permute-done.2
  65.1 1.1 collective-permute-start.19
  66.2 8.2 %collective-permute-done.25.refs_5_ = bf16[3,40,1792]{2,1,0:T(8,128)(2,1)S(1)} collective-permute-done((bf16[3,40,1792]{2,1,0:T(8,128)(2,1)S(1)}, bf16[3,40,1792]{2,1,0:T(8,128)(2,1)S(1)}, u32[]{:S(2)}, u32[]{:S(2)}) %collective-permute-start.25) | collective-permute-done | bytes 430112 | tf_op jit(solution)/shard_map/ppermute | solution.py:358
  74.4 0.5 collective-permute-start.7
  74.9 1.4 collective-permute-start.13
  76.3 0.7 collective-permute-start.6
  77.0 5.1 %collective-permute-done.19.refs_5_ = bf16[3,40,1792]{2,1,0:T(8,128)(2,1)S(1)} collective-permute-done((bf16[3,40,1792]{2,1,0:T(8,128)(2,1)S(1)}, bf16[3,40,1792]{2,1,0:T(8,128)(2,1)S(1)}, u32[]{:S(2)}, u32[]{:S(2)}) %collective-permute-start.19) | collective-permute-done | bytes 430112 | tf_op jit(solution)/shard_map/ppermute | solution.py:358
  82.1 0.5 collective-permute-start.20
  82.7 8.7 %collective-permute-done.13.refs_5_ = bf16[3,40,1792]{2,1,0:T(8,128)(2,1)S(1)} collective-permute-done((bf16[3,40,1792]{2,1,0:T(8,128)(2,1)S(1)}, bf16[3,40,1792]{2,1,0:T(8,128)(2,1)S(1)}, u32[]{:S(2)}, u32[]{:S(2)}) %collective-permute-start.13) | collective-permute-done | bytes 430112 | tf_op jit(solution)/shard_map/ppermute | solution.py:358
  91.4 7.0 %collective-permute-done.6.refs_5_ = bf16[3,40,1792]{2,1,0:T(8,128)(2,1)S(1)} collective-permute-done((bf16[3,40,1792]{2,1,0:T(8,128)(2,1)S(1)}, bf16[3,40,1792]{2,1,0:T(8,128)(2,1)S(1)}, u32[]{:S(2)}, u32[]{:S(2)}) %collective-permute-start.6) | collective-permute-done | bytes 430112 | tf_op jit(solution)/shard_map/ppermute | solution.py:358
  98.3 0.5 collective-permute-start.4
  98.9 10.1 %up_chunk.4 = (f32[8,128,256]{2,1,0:T(8,128)S(1)}, f32[8,128,256]{2,1,0:T(8,128)S(1)}) custom-call(bf16[1,40,7168]{2,1,0:T(8,128)(2,1)S(1)} %get-tuple-element.58.refs_0_, bf16[3,40,1792]{2,1,0:T(8,128)(2,1)S(1)} %constant_dynamic-update-slice_fusion.9.refs_1_, bf16[1,40,7168]{2,1,0:T(8,128)(2,1)S(1)} %collective-permute-done.3.refs_2_, ...), custom_call_target="tpu_custom_call" | custom-call | flops 1879048192 | bytes 14680064 | tf_op jit(solution)/shard_map/up_chunk/pallas_call | solution.py:219
  109.1 10.1 %up_chunk.5 = (f32[8,128,256]{2,1,0:T(8,128)S(1)}, f32[8,128,256]{2,1,0:T(8,128)S(1)}) custom-call(bf16[1,40,7168]{2,1,0:T(8,128)(2,1)S(1)} %get-tuple-element.58.refs_0_, bf16[3,40,1792]{2,1,0:T(8,128)(2,1)S(1)} %constant_dynamic-update-slice_fusion.6.refs_1_, bf16[1,40,7168]{2,1,0:T(8,128)(2,1)S(1)} %collective-permute-done.3.refs_2_, ...), custom_call_target="tpu_custom_call" | custom-call | flops 1879048192 | bytes 14680064 | tf_op jit(solution)/shard_map/up_chunk/pallas_call | solution.py:219
  119.2 10.1 %up_chunk.6 = (f32[8,128,256]{2,1,0:T(8,128)S(1)}, f32[8,128,256]{2,1,0:T(8,128)S(1)}) custom-call(bf16[1,40,7168]{2,1,0:T(8,128)(2,1)S(1)} %get-tuple-element.58.refs_0_, bf16[3,40,1792]{2,1,0:T(8,128)(2,1)S(1)} %constant_dynamic-update-slice_fusion.3.refs_1_, bf16[1,40,7168]{2,1,0:T(8,128)(2,1)S(1)} %collective-permute-done.3.refs_2_, ...), custom_call_target="tpu_custom_call" | custom-call | flops 1879048192 | bytes 14680064 | tf_op jit(solution)/shard_map/up_chunk/pallas_call | solution.py:219
  129.4 10.3 %up_chunk.7.hidden_ref = bf16[8,128,256]{2,1,0:T(8,128)(2,1)S(1)} custom-call(bf16[1,40,7168]{2,1,0:T(8,128)(2,1)S(1)} %get-tuple-element.58.refs_0_, bf16[3,40,1792]{2,1,0:T(8,128)(2,1)S(1)} %constant_dynamic-update-slice_fusion.refs_1_, bf16[1,40,7168]{2,1,0:T(8,128)(2,1)S(1)} %collective-permute-done.3.refs_2_, ...), custom_call_target="tpu_custom_call" | custom-call | flops 1879048192 | bytes 14680064 | tf_op jit(solution)/shard_map/up_chunk/pallas_call | solution.py:219
  139.8 5.5 %down_chunk.7 = (bf16[8,40,1792]{2,1,0:T(8,128)(2,1)S(1)}, bf16[8,40,1792]{2,1,0:T(8,128)(2,1)S(1)}) custom-call(bf16[8,128,256]{2,1,0:T(8,128)(2,1)S(1)} %up_chunk.7.hidden_ref, bf16[192,256]{1,0:T(8,128)(2,1)S(1)} %copy-done.1, bf16[8,256,7168]{2,1,0:T(8,128)(2,1)} %wd_ref.7), custom_call_target="tpu_custom_call" | custom-call | flops 939524096 | bytes 7340032 | tf_op jit(solution)/shard_map/down_chunk/pallas_call | solution.py:278
  145.3 5.5 %down_chunk.6 = (bf16[8,40,1792]{2,1,0:T(8,128)(2,1)S(1)}, bf16[8,40,1792]{2,1,0:T(8,128)(2,1)S(1)}) custom-call(bf16[8,128,256]{2,1,0:T(8,128)(2,1)S(1)} %up_chunk.7.hidden_ref, bf16[192,256]{1,0:T(8,128)(2,1)S(1)} %copy-done.1, bf16[8,256,7168]{2,1,0:T(8,128)(2,1)} %wd_ref.7), custom_call_target="tpu_custom_call" | custom-call | flops 939524096 | bytes 7340032 | tf_op jit(solution)/shard_map/down_chunk/pallas_call | solution.py:278
  151.4 5.5 %down_chunk.5 = (bf16[8,40,1792]{2,1,0:T(8,128)(2,1)S(1)}, bf16[8,40,1792]{2,1,0:T(8,128)(2,1)S(1)}) custom-call(bf16[8,128,256]{2,1,0:T(8,128)(2,1)S(1)} %up_chunk.7.hidden_ref, bf16[192,256]{1,0:T(8,128)(2,1)S(1)} %copy-done.1, bf16[8,256,7168]{2,1,0:T(8,128)(2,1)} %wd_ref.7), custom_call_target="tpu_custom_call" | custom-call | flops 939524096 | bytes 7340032 | tf_op jit(solution)/shard_map/down_chunk/pallas_call | solution.py:278
  157.4 5.5 %down_chunk.4 = (bf16[8,40,1792]{2,1,0:T(8,128)(2,1)S(1)}, bf16[8,40,1792]{2,1,0:T(8,128)(2,1)S(1)}) custom-call(bf16[8,128,256]{2,1,0:T(8,128)(2,1)S(1)} %up_chunk.7.hidden_ref, bf16[192,256]{1,0:T(8,128)(2,1)S(1)} %copy-done.1, bf16[8,256,7168]{2,1,0:T(8,128)(2,1)} %wd_ref.7), custom_call_target="tpu_custom_call" | custom-call | flops 939524096 | bytes 7340032 | tf_op jit(solution)/shard_map/down_chunk/pallas_call | solution.py:278
  163.3 1.2 collective-permute-start.46
  164.7 1.0 collective-permute-start.40
  166.0 1.2 collective-permute-start.34
  167.2 0.9 collective-permute-start.50
  168.4 1.2 collective-permute-start.28
  169.5 28.1 %collective-permute-done.50.refs_4_ = bf16[1,40,1792]{2,1,0:T(8,128)(2,1)S(1)} collective-permute-done((bf16[1,40,1792]{2,1,0:T(8,128)(2,1)S(1)}, bf16[1,40,1792]{2,1,0:T(8,128)(2,1)S(1)}, u32[]{:S(2)}, u32[]{:S(2)}) %collective-permute-start.50) | collective-permute-done | bytes 143392 | tf_op jit(solution)/shard_map/ppermute | solution.py:358
  197.6 1.1 collective-permute-start.44
  198.7 0.9 collective-permute-start.38
  199.7 10.2 %collective-permute-done.44.refs_4_ = bf16[1,40,1792]{2,1,0:T(8,128)(2,1)S(1)} collective-permute-done((bf16[1,40,1792]{2,1,0:T(8,128)(2,1)S(1)}, bf16[1,40,1792]{2,1,0:T(8,128)(2,1)S(1)}, u32[]{:S(2)}, u32[]{:S(2)}) %collective-permute-start.44) | collective-permute-done | bytes 143392 | tf_op jit(solution)/shard_map/ppermute | solution.py:358
  209.9 0.9 collective-permute-start.48
  210.8 1.2 collective-permute-start.49
  212.5 2.4 collective-permute-start.41
  215.2 1.9 collective-permute-done.47.refs_1_
  217.1 3.8 %collective-permute-start.43 = (bf16[1,40,1792]{2,1,0:T(8,128)(2,1)S(1)}, bf16[1,40,1792]{2,1,0:T(8,128)(2,1)S(1)}, u32[]{:S(2)}, u32[]{:S(2)}) collective-permute-start(bf16[1,40,1792]{2,1,0:T(8,128)(2,1)S(1)} %get-tuple-element.99), channel_id=1, source_target_pairs={{0,1},{1,2},{2,3},{3,0},{4,5},{5,6},{6,7},{7,4},{8,9},{9,10},{10,1... | collective-permute-start | bytes 430088 | tf_op jit(solution)/shard_map/ppermute | solution.py:362
  220.9 8.7 %collective-permute-done.48.refs_2_ = bf16[1,40,1792]{2,1,0:T(8,128)(2,1)S(1)} collective-permute-done((bf16[1,40,1792]{2,1,0:T(8,128)(2,1)S(1)}, bf16[1,40,1792]{2,1,0:T(8,128)(2,1)S(1)}, u32[]{:S(2)}, u32[]{:S(2)}) %collective-permute-start.48) | collective-permute-done | bytes 143392 | tf_op jit(solution)/shard_map/ppermute | solution.py:362
  229.6 3.3 %collective-permute-start.36 = (bf16[1,40,1792]{2,1,0:T(8,128)(2,1)S(1)}, bf16[1,40,1792]{2,1,0:T(8,128)(2,1)S(1)}, u32[]{:S(2)}, u32[]{:S(2)}) collective-permute-start(bf16[1,40,1792]{2,1,0:T(8,128)(2,1)S(1)} %get-tuple-element.90), channel_id=1, source_target_pairs={{0,2},{1,3},{2,0},{3,1},{4,6},{5,7},{6,4},{7,5},{8,10},{9,11},{10,... | collective-permute-start | bytes 430088 | tf_op jit(solution)/shard_map/ppermute | solution.py:362
  233.0 1.2 collective-permute-start.32
  234.2 5.4 %collective-permute-done.42.refs_2_ = bf16[1,40,1792]{2,1,0:T(8,128)(2,1)S(1)} collective-permute-done((bf16[1,40,1792]{2,1,0:T(8,128)(2,1)S(1)}, bf16[1,40,1792]{2,1,0:T(8,128)(2,1)S(1)}, u32[]{:S(2)}, u32[]{:S(2)}) %collective-permute-start.42) | collective-permute-done | bytes 143392 | tf_op jit(solution)/shard_map/ppermute | solution.py:362
  239.6 3.8 %collective-permute-start.29 = (bf16[1,40,1792]{2,1,0:T(8,128)(2,1)S(1)}, bf16[1,40,1792]{2,1,0:T(8,128)(2,1)S(1)}, u32[]{:S(2)}, u32[]{:S(2)}) collective-permute-start(bf16[1,40,1792]{2,1,0:T(8,128)(2,1)S(1)} %get-tuple-element.81), channel_id=1, source_target_pairs={{0,3},{1,0},{2,1},{3,2},{4,7},{5,4},{6,5},{7,6},{8,11},{9,8},{10,9... | collective-permute-start | bytes 430088 | tf_op jit(solution)/shard_map/ppermute | solution.py:362
  243.7 5.3 %collective-permute-done.36.refs_2_ = bf16[1,40,1792]{2,1,0:T(8,128)(2,1)S(1)} collective-permute-done((bf16[1,40,1792]{2,1,0:T(8,128)(2,1)S(1)}, bf16[1,40,1792]{2,1,0:T(8,128)(2,1)S(1)}, u32[]{:S(2)}, u32[]{:S(2)}) %collective-permute-start.36) | collective-permute-done | bytes 143392 | tf_op jit(solution)/shard_map/ppermute | solution.py:362
  249.0 2.0 collective-permute-start.31
  251.0 1.4 combine_chunk.4.refs_5_
  252.4 1.4 combine_chunk.5.refs_5_
  253.9 1.4 combine_chunk.6.refs_5_
  255.3 4.6 %collective-permute-done.30.refs_2_ = bf16[1,40,1792]{2,1,0:T(8,128)(2,1)S(1)} collective-permute-done((bf16[1,40,1792]{2,1,0:T(8,128)(2,1)S(1)}, bf16[1,40,1792]{2,1,0:T(8,128)(2,1)S(1)}, u32[]{:S(2)}, u32[]{:S(2)}) %collective-permute-start.30) | collective-permute-done | bytes 143392 | tf_op jit(solution)/shard_map/ppermute | solution.py:362
  259.9 1.4 combine_chunk.7
  (83 shorter events, 5.0 us)
Async XLA Ops:
  0.0 1.2 copy-start.2
  1.2 0.9 copy-start.3
  2.1 0.7 copy-start.4
  2.8 0.7 copy-start.5
  4.6 8.9 %collective-permute-start.21 = (bf16[1,40,1792]{2,1,0:T(8,128)(2,1)S(1)}, bf16[1,40,1792]{2,1,0:T(8,128)(2,1)S(1)}, u32[]{:S(2)}, u32[]{:S(2)}) collective-permute-start(bf16[1,40,1792]{2,1,0:T(8,128)(2,1)S(1)} %get-tuple-element.68), channel_id=1, source_target_pairs={{0,1},{1,2},{2,3},{3,0},{4,5},{5,6},{6,7},{7,4},{8,9},{9,10},{10,1... | collective-permute-start | bytes 430088 | tf_op jit(solution)/shard_map/ppermute | solution.py:362
  7.7 66.7 %collective-permute-start.5 = (bf16[1,40,7168]{2,1,0:T(8,128)(2,1)S(1)}, bf16[1,40,7168]{2,1,0:T(8,128)(2,1)S(1)}, u32[]{:S(2)}, u32[]{:S(2)}) collective-permute-start(bf16[1,40,7168]{2,1,0:T(8,128)(2,1)S(1)} %get-tuple-element.58.refs_0_), channel_id=1, source_target_pairs={{0,8},{4,12},{8,0},{12,4},{1,9},{5,13},{9,1},{13,5},{2,10},{6,14},... | collective-permute-start | bytes 1720328 | tf_op jit(solution)/shard_map/ppermute | solution.py:358
  9.2 67.1 %collective-permute-start.3 = (bf16[1,40,7168]{2,1,0:T(8,128)(2,1)S(1)}, bf16[1,40,7168]{2,1,0:T(8,128)(2,1)S(1)}, u32[]{:S(2)}, u32[]{:S(2)}) collective-permute-start(bf16[1,40,7168]{2,1,0:T(8,128)(2,1)S(1)} %get-tuple-element.58.refs_0_), channel_id=1, source_target_pairs={{0,4},{4,0},{8,12},{12,8},{1,5},{5,1},{9,13},{13,9},{2,6},{6,2},{1... | collective-permute-start | bytes 1720328 | tf_op jit(solution)/shard_map/ppermute | solution.py:358
  9.2 29.5 %collective-permute-start.22 = (bf16[1,40,1792]{2,1,0:T(8,128)(2,1)S(1)}, bf16[1,40,1792]{2,1,0:T(8,128)(2,1)S(1)}, u32[]{:S(2)}, u32[]{:S(2)}) collective-permute-start(bf16[1,40,1792]{2,1,0:T(8,128)(2,1)S(1)} %get-tuple-element.69), channel_id=1, source_target_pairs={{0,2},{1,3},{2,0},{3,1},{4,6},{5,7},{6,4},{7,5},{8,10},{9,11},{10,... | collective-permute-start | bytes 430088 | tf_op jit(solution)/shard_map/ppermute | solution.py:362
  11.8 27.0 %collective-permute-start.23 = (bf16[1,40,1792]{2,1,0:T(8,128)(2,1)S(1)}, bf16[1,40,1792]{2,1,0:T(8,128)(2,1)S(1)}, u32[]{:S(2)}, u32[]{:S(2)}) collective-permute-start(bf16[1,40,1792]{2,1,0:T(8,128)(2,1)S(1)} %get-tuple-element.70), channel_id=1, source_target_pairs={{0,3},{1,0},{2,1},{3,2},{4,7},{5,4},{6,5},{7,6},{8,11},{9,8},{10,9... | collective-permute-start | bytes 430088 | tf_op jit(solution)/shard_map/ppermute | solution.py:362
  13.5 10.1 %collective-permute-start.15 = (bf16[1,40,1792]{2,1,0:T(8,128)(2,1)S(1)}, bf16[1,40,1792]{2,1,0:T(8,128)(2,1)S(1)}, u32[]{:S(2)}, u32[]{:S(2)}) collective-permute-start(bf16[1,40,1792]{2,1,0:T(8,128)(2,1)S(1)} %get-tuple-element.65), channel_id=1, source_target_pairs={{0,1},{1,2},{2,3},{3,0},{4,5},{5,6},{6,7},{7,4},{8,9},{9,10},{10,1... | collective-permute-start | bytes 430088 | tf_op jit(solution)/shard_map/ppermute | solution.py:362
  23.6 7.1 %collective-permute-start.9 = (bf16[1,40,1792]{2,1,0:T(8,128)(2,1)S(1)}, bf16[1,40,1792]{2,1,0:T(8,128)(2,1)S(1)}, u32[]{:S(2)}, u32[]{:S(2)}) collective-permute-start(bf16[1,40,1792]{2,1,0:T(8,128)(2,1)S(1)} %get-tuple-element.62), channel_id=1, source_target_pairs={{0,1},{1,2},{2,3},{3,0},{4,5},{5,6},{6,7},{7,4},{8,9},{9,10},{10,1... | collective-permute-start | bytes 430088 | tf_op jit(solution)/shard_map/ppermute | solution.py:362
  30.7 7.9 %collective-permute-start = (bf16[1,40,1792]{2,1,0:T(8,128)(2,1)S(1)}, bf16[1,40,1792]{2,1,0:T(8,128)(2,1)S(1)}, u32[]{:S(2)}, u32[]{:S(2)}) collective-permute-start(bf16[1,40,1792]{2,1,0:T(8,128)(2,1)S(1)} %get-tuple-element.59), channel_id=1, source_target_pairs={{0,1},{1,2},{2,3},{3,0},{4,5},{5,6},{6,7},{7,4},{8,9},{9,10},{10,1... | collective-permute-start | bytes 430088 | tf_op jit(solution)/shard_map/ppermute | solution.py:362
  38.6 10.4 %collective-permute-start.16 = (bf16[1,40,1792]{2,1,0:T(8,128)(2,1)S(1)}, bf16[1,40,1792]{2,1,0:T(8,128)(2,1)S(1)}, u32[]{:S(2)}, u32[]{:S(2)}) collective-permute-start(bf16[1,40,1792]{2,1,0:T(8,128)(2,1)S(1)} %get-tuple-element.66), channel_id=1, source_target_pairs={{0,2},{1,3},{2,0},{3,1},{4,6},{5,7},{6,4},{7,5},{8,10},{9,11},{10,... | collective-permute-start | bytes 430088 | tf_op jit(solution)/shard_map/ppermute | solution.py:362
  38.7 60.3 %copy-start = (bf16[256,192]{1,0:T(8,128)(2,1)S(1)}, bf16[256,192]{1,0:T(8,128)(2,1)}, u32[]{:S(2)}) copy-start(bf16[256,192]{1,0:T(8,128)(2,1)} %constant.11.clone.refs_8_) | copy-start | bytes 294916
  38.7 13.7 %collective-permute-start.17 = (bf16[1,40,1792]{2,1,0:T(8,128)(2,1)S(1)}, bf16[1,40,1792]{2,1,0:T(8,128)(2,1)S(1)}, u32[]{:S(2)}, u32[]{:S(2)}) collective-permute-start(bf16[1,40,1792]{2,1,0:T(8,128)(2,1)S(1)} %get-tuple-element.67), channel_id=1, source_target_pairs={{0,3},{1,0},{2,1},{3,2},{4,7},{5,4},{6,5},{7,6},{8,11},{9,8},{10,9... | collective-permute-start | bytes 430088 | tf_op jit(solution)/shard_map/ppermute | solution.py:362
  38.8 18.0 %collective-permute-start.10 = (bf16[1,40,1792]{2,1,0:T(8,128)(2,1)S(1)}, bf16[1,40,1792]{2,1,0:T(8,128)(2,1)S(1)}, u32[]{:S(2)}, u32[]{:S(2)}) collective-permute-start(bf16[1,40,1792]{2,1,0:T(8,128)(2,1)S(1)} %get-tuple-element.63), channel_id=1, source_target_pairs={{0,2},{1,3},{2,0},{3,1},{4,6},{5,7},{6,4},{7,5},{8,10},{9,11},{10,... | collective-permute-start | bytes 430088 | tf_op jit(solution)/shard_map/ppermute | solution.py:362
  49.0 13.4 %collective-permute-start.11 = (bf16[1,40,1792]{2,1,0:T(8,128)(2,1)S(1)}, bf16[1,40,1792]{2,1,0:T(8,128)(2,1)S(1)}, u32[]{:S(2)}, u32[]{:S(2)}) collective-permute-start(bf16[1,40,1792]{2,1,0:T(8,128)(2,1)S(1)} %get-tuple-element.64), channel_id=1, source_target_pairs={{0,3},{1,0},{2,1},{3,2},{4,7},{5,4},{6,5},{7,6},{8,11},{9,8},{10,9... | collective-permute-start | bytes 430088 | tf_op jit(solution)/shard_map/ppermute | solution.py:362
  52.4 11.5 %collective-permute-start.1 = (bf16[1,40,1792]{2,1,0:T(8,128)(2,1)S(1)}, bf16[1,40,1792]{2,1,0:T(8,128)(2,1)S(1)}, u32[]{:S(2)}, u32[]{:S(2)}) collective-permute-start(bf16[1,40,1792]{2,1,0:T(8,128)(2,1)S(1)} %get-tuple-element.60), channel_id=1, source_target_pairs={{0,2},{1,3},{2,0},{3,1},{4,6},{5,7},{6,4},{7,5},{8,10},{9,11},{10,... | collective-permute-start | bytes 430088 | tf_op jit(solution)/shard_map/ppermute | solution.py:362
  56.8 8.3 %collective-permute-start.2 = (bf16[1,40,1792]{2,1,0:T(8,128)(2,1)S(1)}, bf16[1,40,1792]{2,1,0:T(8,128)(2,1)S(1)}, u32[]{:S(2)}, u32[]{:S(2)}) collective-permute-start(bf16[1,40,1792]{2,1,0:T(8,128)(2,1)S(1)} %get-tuple-element.61), channel_id=1, source_target_pairs={{0,3},{1,0},{2,1},{3,2},{4,7},{5,4},{6,5},{7,6},{8,11},{9,8},{10,9... | collective-permute-start | bytes 430088 | tf_op jit(solution)/shard_map/ppermute | solution.py:362
  62.5 12.0 %collective-permute-start.25 = (bf16[3,40,1792]{2,1,0:T(8,128)(2,1)S(1)}, bf16[3,40,1792]{2,1,0:T(8,128)(2,1)S(1)}, u32[]{:S(2)}, u32[]{:S(2)}) collective-permute-start(bf16[3,40,1792]{2,1,0:T(8,128)(2,1)S(1)} %constant_dynamic-update-slice_fusion.9.refs_1_), channel_id=1, source_target_pairs={{0,8},{4,12},{8,0},{12,4},{1,9},{5,13},{9,1},{13,5},{2,10},{6,14},... | collective-permute-start | bytes 1290248 | tf_op jit(solution)/shard_map/ppermute | solution.py:358
  63.9 11.1 %collective-permute-start.24 = (bf16[3,40,1792]{2,1,0:T(8,128)(2,1)S(1)}, bf16[3,40,1792]{2,1,0:T(8,128)(2,1)S(1)}, u32[]{:S(2)}, u32[]{:S(2)}) collective-permute-start(bf16[3,40,1792]{2,1,0:T(8,128)(2,1)S(1)} %constant_dynamic-update-slice_fusion.9.refs_1_), channel_id=1, source_target_pairs={{0,4},{4,0},{8,12},{12,8},{1,5},{5,1},{9,13},{13,9},{2,6},{6,2},{1... | collective-permute-start | bytes 1290248 | tf_op jit(solution)/shard_map/ppermute | solution.py:358
  65.1 17.1 %collective-permute-start.19 = (bf16[3,40,1792]{2,1,0:T(8,128)(2,1)S(1)}, bf16[3,40,1792]{2,1,0:T(8,128)(2,1)S(1)}, u32[]{:S(2)}, u32[]{:S(2)}) collective-permute-start(bf16[3,40,1792]{2,1,0:T(8,128)(2,1)S(1)} %constant_dynamic-update-slice_fusion.6.refs_1_), channel_id=1, source_target_pairs={{0,8},{4,12},{8,0},{12,4},{1,9},{5,13},{9,1},{13,5},{2,10},{6,14},... | collective-permute-start | bytes 1290248 | tf_op jit(solution)/shard_map/ppermute | solution.py:358
  74.4 7.7 %collective-permute-start.18 = (bf16[3,40,1792]{2,1,0:T(8,128)(2,1)S(1)}, bf16[3,40,1792]{2,1,0:T(8,128)(2,1)S(1)}, u32[]{:S(2)}, u32[]{:S(2)}) collective-permute-start(bf16[3,40,1792]{2,1,0:T(8,128)(2,1)S(1)} %constant_dynamic-update-slice_fusion.6.refs_1_), channel_id=1, source_target_pairs={{0,4},{4,0},{8,12},{12,8},{1,5},{5,1},{9,13},{13,9},{2,6},{6,2},{1... | collective-permute-start | bytes 1290248 | tf_op jit(solution)/shard_map/ppermute | solution.py:358
  74.4 24.4 %collective-permute-start.7 = (bf16[1,40,7168]{2,1,0:T(8,128)(2,1)S(1)}, bf16[1,40,7168]{2,1,0:T(8,128)(2,1)S(1)}, u32[]{:S(2)}, u32[]{:S(2)}) collective-permute-start(bf16[1,40,7168]{2,1,0:T(8,128)(2,1)S(1)} %collective-permute-done.5.refs_4_), channel_id=1, source_target_pairs={{0,4},{4,0},{8,12},{12,8},{1,5},{5,1},{9,13},{13,9},{2,6},{6,2},{1... | collective-permute-start | bytes 1720328 | tf_op jit(solution)/shard_map/ppermute | solution.py:358
  74.9 16.4 %collective-permute-start.13 = (bf16[3,40,1792]{2,1,0:T(8,128)(2,1)S(1)}, bf16[3,40,1792]{2,1,0:T(8,128)(2,1)S(1)}, u32[]{:S(2)}, u32[]{:S(2)}) collective-permute-start(bf16[3,40,1792]{2,1,0:T(8,128)(2,1)S(1)} %constant_dynamic-update-slice_fusion.3.refs_1_), channel_id=1, source_target_pairs={{0,8},{4,12},{8,0},{12,4},{1,9},{5,13},{9,1},{13,5},{2,10},{6,14},... | collective-permute-start | bytes 1290248 | tf_op jit(solution)/shard_map/ppermute | solution.py:358
  76.3 22.0 %collective-permute-start.6 = (bf16[3,40,1792]{2,1,0:T(8,128)(2,1)S(1)}, bf16[3,40,1792]{2,1,0:T(8,128)(2,1)S(1)}, u32[]{:S(2)}, u32[]{:S(2)}) collective-permute-start(bf16[3,40,1792]{2,1,0:T(8,128)(2,1)S(1)} %constant_dynamic-update-slice_fusion.refs_1_), channel_id=1, source_target_pairs={{0,8},{4,12},{8,0},{12,4},{1,9},{5,13},{9,1},{13,5},{2,10},{6,14},... | collective-permute-start | bytes 1290248 | tf_op jit(solution)/shard_map/ppermute | solution.py:358
  82.1 16.2 %collective-permute-start.26 = (bf16[3,40,1792]{2,1,0:T(8,128)(2,1)S(1)}, bf16[3,40,1792]{2,1,0:T(8,128)(2,1)S(1)}, u32[]{:S(2)}, u32[]{:S(2)}) collective-permute-start(bf16[3,40,1792]{2,1,0:T(8,128)(2,1)S(1)} %collective-permute-done.25.refs_5_), channel_id=1, source_target_pairs={{0,4},{4,0},{8,12},{12,8},{1,5},{5,1},{9,13},{13,9},{2,6},{6,2},{1... | collective-permute-start | bytes 1290248 | tf_op jit(solution)/shard_map/ppermute | solution.py:358
  82.1 26.9 %collective-permute-start.20 = (bf16[3,40,1792]{2,1,0:T(8,128)(2,1)S(1)}, bf16[3,40,1792]{2,1,0:T(8,128)(2,1)S(1)}, u32[]{:S(2)}, u32[]{:S(2)}) collective-permute-start(bf16[3,40,1792]{2,1,0:T(8,128)(2,1)S(1)} %collective-permute-done.19.refs_5_), channel_id=1, source_target_pairs={{0,4},{4,0},{8,12},{12,8},{1,5},{5,1},{9,13},{13,9},{2,6},{6,2},{1... | collective-permute-start | bytes 1290248 | tf_op jit(solution)/shard_map/ppermute | solution.py:358
  91.4 27.9 %collective-permute-start.12 = (bf16[3,40,1792]{2,1,0:T(8,128)(2,1)S(1)}, bf16[3,40,1792]{2,1,0:T(8,128)(2,1)S(1)}, u32[]{:S(2)}, u32[]{:S(2)}) collective-permute-start(bf16[3,40,1792]{2,1,0:T(8,128)(2,1)S(1)} %constant_dynamic-update-slice_fusion.3.refs_1_), channel_id=1, source_target_pairs={{0,4},{4,0},{8,12},{12,8},{1,5},{5,1},{9,13},{13,9},{2,6},{6,2},{1... | collective-permute-start | bytes 1290248 | tf_op jit(solution)/shard_map/ppermute | solution.py:358
  98.3 20.9 %collective-permute-start.14 = (bf16[3,40,1792]{2,1,0:T(8,128)(2,1)S(1)}, bf16[3,40,1792]{2,1,0:T(8,128)(2,1)S(1)}, u32[]{:S(2)}, u32[]{:S(2)}) collective-permute-start(bf16[3,40,1792]{2,1,0:T(8,128)(2,1)S(1)} %collective-permute-done.13.refs_5_), channel_id=1, source_target_pairs={{0,4},{4,0},{8,12},{12,8},{1,5},{5,1},{9,13},{13,9},{2,6},{6,2},{1... | collective-permute-start | bytes 1290248 | tf_op jit(solution)/shard_map/ppermute | solution.py:358
  98.3 31.0 %collective-permute-start.4 = (bf16[3,40,1792]{2,1,0:T(8,128)(2,1)S(1)}, bf16[3,40,1792]{2,1,0:T(8,128)(2,1)S(1)}, u32[]{:S(2)}, u32[]{:S(2)}) collective-permute-start(bf16[3,40,1792]{2,1,0:T(8,128)(2,1)S(1)} %constant_dynamic-update-slice_fusion.refs_1_), channel_id=1, source_target_pairs={{0,4},{4,0},{8,12},{12,8},{1,5},{5,1},{9,13},{13,9},{2,6},{6,2},{1... | collective-permute-start | bytes 1290248 | tf_op jit(solution)/shard_map/ppermute | solution.py:358
  98.9 30.5 %collective-permute-start.8 = (bf16[3,40,1792]{2,1,0:T(8,128)(2,1)S(1)}, bf16[3,40,1792]{2,1,0:T(8,128)(2,1)S(1)}, u32[]{:S(2)}, u32[]{:S(2)}) collective-permute-start(bf16[3,40,1792]{2,1,0:T(8,128)(2,1)S(1)} %collective-permute-done.6.refs_5_), channel_id=1, source_target_pairs={{0,4},{4,0},{8,12},{12,8},{1,5},{5,1},{9,13},{13,9},{2,6},{6,2},{1... | collective-permute-start | bytes 1290248 | tf_op jit(solution)/shard_map/ppermute | solution.py:358
  129.4 10.4 %copy-start.1 = (bf16[192,256]{1,0:T(8,128)(2,1)S(1)}, bf16[192,256]{1,0:T(8,128)(2,1)}, u32[]{:S(2)}) copy-start(bf16[192,256]{1,0:T(8,128)(2,1)} %constant.10.clone.ungroup_ref) | copy-start | bytes 294916
  150.8 12.2 %collective-permute-start.45 = (bf16[8,40,1792]{2,1,0:T(8,128)(2,1)S(1)}, bf16[8,40,1792]{2,1,0:T(8,128)(2,1)S(1)}, u32[]{:S(2)}, u32[]{:S(2)}) collective-permute-start(bf16[8,40,1792]{2,1,0:T(8,128)(2,1)S(1)} %get-tuple-element.102), channel_id=1, source_target_pairs={{0,4},{4,0},{8,12},{12,8},{1,5},{5,1},{9,13},{13,9},{2,6},{6,2},{1... | collective-permute-start | bytes 3440648 | tf_op jit(solution)/shard_map/ppermute | solution.py:358
  151.3 13.2 %collective-permute-start.39 = (bf16[8,40,1792]{2,1,0:T(8,128)(2,1)S(1)}, bf16[8,40,1792]{2,1,0:T(8,128)(2,1)S(1)}, u32[]{:S(2)}, u32[]{:S(2)}) collective-permute-start(bf16[8,40,1792]{2,1,0:T(8,128)(2,1)S(1)} %get-tuple-element.94), channel_id=1, source_target_pairs={{0,4},{4,0},{8,12},{12,8},{1,5},{5,1},{9,13},{13,9},{2,6},{6,2},{1... | collective-permute-start | bytes 3440648 | tf_op jit(solution)/shard_map/ppermute | solution.py:358
  156.9 8.8 %collective-permute-start.33 = (bf16[8,40,1792]{2,1,0:T(8,128)(2,1)S(1)}, bf16[8,40,1792]{2,1,0:T(8,128)(2,1)S(1)}, u32[]{:S(2)}, u32[]{:S(2)}) collective-permute-start(bf16[8,40,1792]{2,1,0:T(8,128)(2,1)S(1)} %get-tuple-element.86), channel_id=1, source_target_pairs={{0,4},{4,0},{8,12},{12,8},{1,5},{5,1},{9,13},{13,9},{2,6},{6,2},{1... | collective-permute-start | bytes 3440648 | tf_op jit(solution)/shard_map/ppermute | solution.py:358
  162.9 5.2 %collective-permute-start.27 = (bf16[8,40,1792]{2,1,0:T(8,128)(2,1)S(1)}, bf16[8,40,1792]{2,1,0:T(8,128)(2,1)S(1)}, u32[]{:S(2)}, u32[]{:S(2)}) collective-permute-start(bf16[8,40,1792]{2,1,0:T(8,128)(2,1)S(1)} %get-tuple-element.78), channel_id=1, source_target_pairs={{0,4},{4,0},{8,12},{12,8},{1,5},{5,1},{9,13},{13,9},{2,6},{6,2},{1... | collective-permute-start | bytes 3440648 | tf_op jit(solution)/shard_map/ppermute | solution.py:358
  163.3 35.4 %collective-permute-start.46 = (bf16[3,40,1792]{2,1,0:T(8,128)(2,1)S(1)}, bf16[3,40,1792]{2,1,0:T(8,128)(2,1)S(1)}, u32[]{:S(2)}, u32[]{:S(2)}) collective-permute-start(bf16[3,40,1792]{2,1,0:T(8,128)(2,1)S(1)} %get-tuple-element.104), channel_id=1, source_target_pairs={{0,8},{4,12},{8,0},{12,4},{1,9},{5,13},{9,1},{13,5},{2,10},{6,14},... | collective-permute-start | bytes 1290248 | tf_op jit(solution)/shard_map/ppermute | solution.py:358
  164.7 45.1 %collective-permute-start.40 = (bf16[3,40,1792]{2,1,0:T(8,128)(2,1)S(1)}, bf16[3,40,1792]{2,1,0:T(8,128)(2,1)S(1)}, u32[]{:S(2)}, u32[]{:S(2)}) collective-permute-start(bf16[3,40,1792]{2,1,0:T(8,128)(2,1)S(1)} %get-tuple-element.96), channel_id=1, source_target_pairs={{0,8},{4,12},{8,0},{12,4},{1,9},{5,13},{9,1},{13,5},{2,10},{6,14},... | collective-permute-start | bytes 1290248 | tf_op jit(solution)/shard_map/ppermute | solution.py:358
  166.0 44.7 %collective-permute-start.34 = (bf16[3,40,1792]{2,1,0:T(8,128)(2,1)S(1)}, bf16[3,40,1792]{2,1,0:T(8,128)(2,1)S(1)}, u32[]{:S(2)}, u32[]{:S(2)}) collective-permute-start(bf16[3,40,1792]{2,1,0:T(8,128)(2,1)S(1)} %get-tuple-element.88), channel_id=1, source_target_pairs={{0,8},{4,12},{8,0},{12,4},{1,9},{5,13},{9,1},{13,5},{2,10},{6,14},... | collective-permute-start | bytes 1290248 | tf_op jit(solution)/shard_map/ppermute | solution.py:358
  167.2 30.4 %collective-permute-start.50 = (bf16[1,40,1792]{2,1,0:T(8,128)(2,1)S(1)}, bf16[1,40,1792]{2,1,0:T(8,128)(2,1)S(1)}, u32[]{:S(2)}, u32[]{:S(2)}) collective-permute-start(bf16[1,40,1792]{2,1,0:T(8,128)(2,1)S(1)} %get-tuple-element.108), channel_id=1, source_target_pairs={{0,8},{4,12},{8,0},{12,4},{1,9},{5,13},{9,1},{13,5},{2,10},{6,14},... | collective-permute-start | bytes 430088 | tf_op jit(solution)/shard_map/ppermute | solution.py:358
  168.4 46.5 %collective-permute-start.28 = (bf16[3,40,1792]{2,1,0:T(8,128)(2,1)S(1)}, bf16[3,40,1792]{2,1,0:T(8,128)(2,1)S(1)}, u32[]{:S(2)}, u32[]{:S(2)}) collective-permute-start(bf16[3,40,1792]{2,1,0:T(8,128)(2,1)S(1)} %get-tuple-element.80), channel_id=1, source_target_pairs={{0,8},{4,12},{8,0},{12,4},{1,9},{5,13},{9,1},{13,5},{2,10},{6,14},... | collective-permute-start | bytes 1290248 | tf_op jit(solution)/shard_map/ppermute | solution.py:358
  197.6 12.3 %collective-permute-start.44 = (bf16[1,40,1792]{2,1,0:T(8,128)(2,1)S(1)}, bf16[1,40,1792]{2,1,0:T(8,128)(2,1)S(1)}, u32[]{:S(2)}, u32[]{:S(2)}) collective-permute-start(bf16[1,40,1792]{2,1,0:T(8,128)(2,1)S(1)} %get-tuple-element.100), channel_id=1, source_target_pairs={{0,8},{4,12},{8,0},{12,4},{1,9},{5,13},{9,1},{13,5},{2,10},{6,14},... | collective-permute-start | bytes 430088 | tf_op jit(solution)/shard_map/ppermute | solution.py:358
  198.7 13.8 %collective-permute-start.38 = (bf16[1,40,1792]{2,1,0:T(8,128)(2,1)S(1)}, bf16[1,40,1792]{2,1,0:T(8,128)(2,1)S(1)}, u32[]{:S(2)}, u32[]{:S(2)}) collective-permute-start(bf16[1,40,1792]{2,1,0:T(8,128)(2,1)S(1)} %get-tuple-element.92), channel_id=1, source_target_pairs={{0,8},{4,12},{8,0},{12,4},{1,9},{5,13},{9,1},{13,5},{2,10},{6,14},... | collective-permute-start | bytes 430088 | tf_op jit(solution)/shard_map/ppermute | solution.py:358
  209.9 7.2 %collective-permute-start.47 = (bf16[1,40,1792]{2,1,0:T(8,128)(2,1)S(1)}, bf16[1,40,1792]{2,1,0:T(8,128)(2,1)S(1)}, u32[]{:S(2)}, u32[]{:S(2)}) collective-permute-start(bf16[1,40,1792]{2,1,0:T(8,128)(2,1)S(1)} %get-tuple-element.105), channel_id=1, source_target_pairs={{0,3},{1,0},{2,1},{3,2},{4,7},{5,4},{6,5},{7,6},{8,11},{9,8},{10,9... | collective-permute-start | bytes 430088 | tf_op jit(solution)/shard_map/ppermute | solution.py:362
  209.9 19.7 %collective-permute-start.48 = (bf16[1,40,1792]{2,1,0:T(8,128)(2,1)S(1)}, bf16[1,40,1792]{2,1,0:T(8,128)(2,1)S(1)}, u32[]{:S(2)}, u32[]{:S(2)}) collective-permute-start(bf16[1,40,1792]{2,1,0:T(8,128)(2,1)S(1)} %get-tuple-element.106), channel_id=1, source_target_pairs={{0,2},{1,3},{2,0},{3,1},{4,6},{5,7},{6,4},{7,5},{8,10},{9,11},{10,... | collective-permute-start | bytes 430088 | tf_op jit(solution)/shard_map/ppermute | solution.py:362
  210.8 18.8 %collective-permute-start.49 = (bf16[1,40,1792]{2,1,0:T(8,128)(2,1)S(1)}, bf16[1,40,1792]{2,1,0:T(8,128)(2,1)S(1)}, u32[]{:S(2)}, u32[]{:S(2)}) collective-permute-start(bf16[1,40,1792]{2,1,0:T(8,128)(2,1)S(1)} %get-tuple-element.107), channel_id=1, source_target_pairs={{0,1},{1,2},{2,3},{3,0},{4,5},{5,6},{6,7},{7,4},{8,9},{9,10},{10,1... | collective-permute-start | bytes 430088 | tf_op jit(solution)/shard_map/ppermute | solution.py:362
  212.5 20.5 %collective-permute-start.41 = (bf16[1,40,1792]{2,1,0:T(8,128)(2,1)S(1)}, bf16[1,40,1792]{2,1,0:T(8,128)(2,1)S(1)}, u32[]{:S(2)}, u32[]{:S(2)}) collective-permute-start(bf16[1,40,1792]{2,1,0:T(8,128)(2,1)S(1)} %get-tuple-element.97), channel_id=1, source_target_pairs={{0,3},{1,0},{2,1},{3,2},{4,7},{5,4},{6,5},{7,6},{8,11},{9,8},{10,9... | collective-permute-start | bytes 430088 | tf_op jit(solution)/shard_map/ppermute | solution.py:362
  214.9 24.7 %collective-permute-start.42 = (bf16[1,40,1792]{2,1,0:T(8,128)(2,1)S(1)}, bf16[1,40,1792]{2,1,0:T(8,128)(2,1)S(1)}, u32[]{:S(2)}, u32[]{:S(2)}) collective-permute-start(bf16[1,40,1792]{2,1,0:T(8,128)(2,1)S(1)} %get-tuple-element.98), channel_id=1, source_target_pairs={{0,2},{1,3},{2,0},{3,1},{4,6},{5,7},{6,4},{7,5},{8,10},{9,11},{10,... | collective-permute-start | bytes 430088 | tf_op jit(solution)/shard_map/ppermute | solution.py:362
  217.1 22.5 %collective-permute-start.43 = (bf16[1,40,1792]{2,1,0:T(8,128)(2,1)S(1)}, bf16[1,40,1792]{2,1,0:T(8,128)(2,1)S(1)}, u32[]{:S(2)}, u32[]{:S(2)}) collective-permute-start(bf16[1,40,1792]{2,1,0:T(8,128)(2,1)S(1)} %get-tuple-element.99), channel_id=1, source_target_pairs={{0,1},{1,2},{2,3},{3,0},{4,5},{5,6},{6,7},{7,4},{8,9},{9,10},{10,1... | collective-permute-start | bytes 430088 | tf_op jit(solution)/shard_map/ppermute | solution.py:362
  229.6 13.9 %collective-permute-start.35 = (bf16[1,40,1792]{2,1,0:T(8,128)(2,1)S(1)}, bf16[1,40,1792]{2,1,0:T(8,128)(2,1)S(1)}, u32[]{:S(2)}, u32[]{:S(2)}) collective-permute-start(bf16[1,40,1792]{2,1,0:T(8,128)(2,1)S(1)} %get-tuple-element.89), channel_id=1, source_target_pairs={{0,3},{1,0},{2,1},{3,2},{4,7},{5,4},{6,5},{7,6},{8,11},{9,8},{10,9... | collective-permute-start | bytes 430088 | tf_op jit(solution)/shard_map/ppermute | solution.py:362
  229.6 19.4 %collective-permute-start.36 = (bf16[1,40,1792]{2,1,0:T(8,128)(2,1)S(1)}, bf16[1,40,1792]{2,1,0:T(8,128)(2,1)S(1)}, u32[]{:S(2)}, u32[]{:S(2)}) collective-permute-start(bf16[1,40,1792]{2,1,0:T(8,128)(2,1)S(1)} %get-tuple-element.90), channel_id=1, source_target_pairs={{0,2},{1,3},{2,0},{3,1},{4,6},{5,7},{6,4},{7,5},{8,10},{9,11},{10,... | collective-permute-start | bytes 430088 | tf_op jit(solution)/shard_map/ppermute | solution.py:362
  233.0 22.2 %collective-permute-start.32 = (bf16[1,40,1792]{2,1,0:T(8,128)(2,1)S(1)}, bf16[1,40,1792]{2,1,0:T(8,128)(2,1)S(1)}, u32[]{:S(2)}, u32[]{:S(2)}) collective-permute-start(bf16[1,40,1792]{2,1,0:T(8,128)(2,1)S(1)} %get-tuple-element.84), channel_id=1, source_target_pairs={{0,8},{4,12},{8,0},{12,4},{1,9},{5,13},{9,1},{13,5},{2,10},{6,14},... | collective-permute-start | bytes 430088 | tf_op jit(solution)/shard_map/ppermute | solution.py:358
  239.6 14.2 %collective-permute-start.37 = (bf16[1,40,1792]{2,1,0:T(8,128)(2,1)S(1)}, bf16[1,40,1792]{2,1,0:T(8,128)(2,1)S(1)}, u32[]{:S(2)}, u32[]{:S(2)}) collective-permute-start(bf16[1,40,1792]{2,1,0:T(8,128)(2,1)S(1)} %get-tuple-element.91), channel_id=1, source_target_pairs={{0,1},{1,2},{2,3},{3,0},{4,5},{5,6},{6,7},{7,4},{8,9},{9,10},{10,1... | collective-permute-start | bytes 430088 | tf_op jit(solution)/shard_map/ppermute | solution.py:362
  239.6 15.7 %collective-permute-start.29 = (bf16[1,40,1792]{2,1,0:T(8,128)(2,1)S(1)}, bf16[1,40,1792]{2,1,0:T(8,128)(2,1)S(1)}, u32[]{:S(2)}, u32[]{:S(2)}) collective-permute-start(bf16[1,40,1792]{2,1,0:T(8,128)(2,1)S(1)} %get-tuple-element.81), channel_id=1, source_target_pairs={{0,3},{1,0},{2,1},{3,2},{4,7},{5,4},{6,5},{7,6},{8,11},{9,8},{10,9... | collective-permute-start | bytes 430088 | tf_op jit(solution)/shard_map/ppermute | solution.py:362
  243.5 16.4 %collective-permute-start.30 = (bf16[1,40,1792]{2,1,0:T(8,128)(2,1)S(1)}, bf16[1,40,1792]{2,1,0:T(8,128)(2,1)S(1)}, u32[]{:S(2)}, u32[]{:S(2)}) collective-permute-start(bf16[1,40,1792]{2,1,0:T(8,128)(2,1)S(1)} %get-tuple-element.82), channel_id=1, source_target_pairs={{0,2},{1,3},{2,0},{3,1},{4,6},{5,7},{6,4},{7,5},{8,10},{9,11},{10,... | collective-permute-start | bytes 430088 | tf_op jit(solution)/shard_map/ppermute | solution.py:362
  249.0 10.9 %collective-permute-start.31 = (bf16[1,40,1792]{2,1,0:T(8,128)(2,1)S(1)}, bf16[1,40,1792]{2,1,0:T(8,128)(2,1)S(1)}, u32[]{:S(2)}, u32[]{:S(2)}) collective-permute-start(bf16[1,40,1792]{2,1,0:T(8,128)(2,1)S(1)} %get-tuple-element.83), channel_id=1, source_target_pairs={{0,1},{1,2},{2,3},{3,0},{4,5},{5,6},{6,7},{7,4},{8,9},{9,10},{10,1... | collective-permute-start | bytes 430088 | tf_op jit(solution)/shard_map/ppermute | solution.py:362

commit v3 on v2

--- a/solution.py
+++ b/solution.py
@@ -11,6 +11,7 @@
 CAP = 5
 UP_PARTS = (1, 1, 1, 1)
 DOWN_PARTS = (1, 1, 1, 1)
+WINDOW = 3
 MIB = 1024 * 1024
 F32, BF16 = jnp.float32, jnp.bfloat16
 
@@ -60,7 +61,7 @@
         self.MP = pad16(self.local * CAP)
         self.rows = self.local * self.RP
         self.grouped = self.exp_dev * self.MP
-        self.relative = local_count <= 4
+        self.relative = local_count <= 4 and node_count == 4
         self.up = cut(self.width, UP_PARTS)
         self.down = cut(self.width, DOWN_PARTS)
 
@@ -137,10 +138,10 @@
     return weight, own, [outs[i * each : (i + 1) * each] for i in range(len(z.up))]
 
 
-def up_kernel(z, lo, size, counts, first, last, *refs):
-    pieces = refs[: len(counts)]
-    regroup_ref, wg_ref, wu_ref = refs[len(counts) : len(counts) + 3]
-    refs = refs[len(counts) + 3 :]
+def up_kernel(z, lo, size, places, first, last, *refs):
+    pieces = refs[: len(places)]
+    regroup_ref, wg_ref, wu_ref = refs[len(places) : len(places) + 3]
+    refs = refs[len(places) + 3 :]
     if not first:
         gin_ref, uin_ref = refs[:2]
         refs = refs[2:]
@@ -153,12 +154,11 @@
     piece_ref, gate_ref, up_ref, rows_ref, grouped_ref, psem, gsem, usem = refs
 
     moves, at = [], 0
-    for i, (ref, (count, whole)) in enumerate(zip(pieces, counts)):
-        src = ref.at[:, :, pl.ds(lo, size)] if whole else ref
-        moves.append(pltpu.make_async_copy(src, piece_ref.at[pl.ds(at, count)], psem.at[i]))
-        at += count
-    for move in moves:
-        move.start()
+    for i, (ref, where) in enumerate(zip(pieces, places)):
+        src = ref if ref.shape[2] == size else ref.at[:, :, pl.ds(lo, size)]
+        moves.append(pltpu.make_async_copy(src, piece_ref.at[pl.ds(at, len(where))], psem.at[i]))
+        moves[-1].start()
+        at += len(where)
 
     def weights(e):
         return (
@@ -171,25 +171,22 @@
             move.start()
     if z.RP > z.R:
         rows_ref[...] = jnp.zeros_like(rows_ref)
+    at = 0
+    for move, where in zip(moves, places):
+        move.wait()
+        for m, block in where:
+            rows_ref[m, block * z.RP : block * z.RP + z.R, :] = piece_ref[at]
+            at += 1
     tile = tile_of(size)
-    at, moved = 0, 0
-    for m in range(z.node):
-        while at < (m + 1) * z.local:
-            moves[moved].wait()
-            count = counts[moved][0]
-            for i in range(count):
-                s = at - m * z.local
-                rows_ref[m, s * z.RP : s * z.RP + z.R, :] = piece_ref[at]
-                at += 1
-            moved += 1
-
-        def step(i, carry, m=m):
-            cols = pl.ds(pl.multiple_of(i * tile, tile), tile)
+
+    def step(i, carry):
+        cols = pl.ds(pl.multiple_of(i * tile, tile), tile)
+        for m in range(z.node):
             got = jnp.dot(regroup_ref[...], rows_ref[m, :, cols], preferred_element_type=F32).astype(BF16)
             grouped_ref[:, m * z.MP : (m + 1) * z.MP, cols] = got.reshape(z.exp_dev, z.MP, tile)
-            return carry
-
-        lax.fori_loop(0, size // tile, step, 0)
+        return carry
+
+    lax.fori_loop(0, size // tile, step, 0)
 
     def expert(e, carry):
         for move in weights(e):
@@ -213,11 +210,11 @@
 def up_chunk(z, c, pieces, regroup, w_gate, w_up, sums):
     lo, size = z.up[c]
     first, last = sums is None, c == len(z.up) - 1
-    counts = [(p.shape[0], p.shape[2] != size) for p in pieces]
+    pieces, places = zip(*pieces)
     acc = jax.ShapeDtypeStruct((z.exp_dev, z.node * z.MP, z.hidden), F32)
     out_shape = [jax.ShapeDtypeStruct(acc.shape, BF16)] if last else [acc, acc]
     return pl.pallas_call(
-        functools.partial(up_kernel, z, lo, size, counts, first, last),
+        functools.partial(up_kernel, z, lo, size, places, first, last),
         out_shape=out_shape,
         in_specs=[in_hbm()] * len(pieces) + [in_vmem(), in_hbm(), in_hbm()] + ([] if first else [in_vmem()] * 2),
         out_specs=[in_vmem()] * len(out_shape),
@@ -344,7 +341,10 @@
         grid=(1,),
         out_shape=jax.ShapeDtypeStruct((z.tok, z.width), BF16),
         in_specs=[pl.BlockSpec(weight.shape, lambda i: (0, 0))]
-        + [pl.BlockSpec((n,) + p.shape[1:], lambda i: (0, 0, 0)) for p, _, n in pieces]
+        + [
+            pl.BlockSpec((n, z.R, size), lambda i, at=lo // size if p.shape[2] != size else 0: (0, 0, at))
+            for p, _, n in pieces
+        ]
         + [in_hbm()] * len(extra),
         out_specs=pl.BlockSpec((z.tok, size), lambda i: (0, lo // size)),
         scratch_shapes=[pltpu.VMEM((rows, size), BF16)],
@@ -362,12 +362,8 @@
     return lax.ppermute(a, "local", [(i, (i + by) % count) for i in range(count)])
 
 
-def spread(a, masks, count):
-    held = {0: a}
-    for mask in reversed(masks):
-        for m in list(held):
-            held[m | mask] = swap(held[m], mask, count)
-    return held
+def concat(*arrays):
+    return jnp.concatenate(arrays, axis=0)
 
 
 def per_device(tokens, expert_ids, gate_weights, w_gate, w_up, w_down):
@@ -378,54 +374,96 @@
     ungroup = jnp.asarray(regroup.T, BF16)
     regroup = jnp.asarray(regroup, BF16)
     weight, own, sent = gather_rows(z, plane, expert_ids, gate_weights, tokens)
-    masks = []
-    while 1 << len(masks) < node_count:
+    route = by_distance if z.relative else by_plane
+    return route(z, weight, own, sent, w_gate, w_up, w_down, regroup, ungroup)
+
+
+def by_distance(z, weight, own, sent, w_gate, w_up, w_down, regroup, ungroup):
+    count = z.local
+    near, far = swap(own, 1, 4), swap(own, 2, 4)
+    both = swap(far, 1, 4)
+    hold = [near, far, both]
+    order = sorted(range(1, count), key=lambda s: -min(s, count - s))
+    came, done = {}, []
+    for c in range(len(z.up)):
+        for s in order:
+            after = done[-WINDOW:][:1] if len(done) >= WINDOW else []
+            if c > 0 and s == order[0] and hold:
+                after = after + [hold.pop(0)]
+            a = sent[c][s - 1]
+            came[c, s] = shift(tie(a, *after) if after else a, s, count)
+            done.append(came[c, s])
+    sums, history = None, []
+    blocks = range(1, count)
+    for c in range(len(z.up)):
+        stack = concat(*[came[c, s] for s in blocks])
+        pair = concat(stack, swap(stack, 2, 4))
+        if len(history) >= 2:
+            pair = tie(pair, *history[-2])
+        pieces = [
+            (own, [(0, 0)]),
+            (near, [(1, 0)]),
+            (far, [(2, 0)]),
+            (both, [(3, 0)]),
+            (pair, [(m, s) for m in (0, 2) for s in blocks]),
+            (swap(pair, 1, 4), [(m, s) for m in (1, 3) for s in blocks]),
+        ]
+        sums = up_chunk(z, c, pieces, regroup, w_gate, w_up, sums)
+        history.append(sums)
+    hidden = sums[0]
+
+    keep, got, send_own = [], [], []
+    for c in range(len(z.down)):
+        send, kept = down_chunk(z, c, hidden, ungroup, w_down, [[1, 3], [0, 2]])
+        k, away, away_own = add_cut(
+            kept, swap(send, 1, 4), [(0, count), (count + 1, 2 * count), (count, count + 1)]
+        )
+        keep.append(k)
+        got.append(swap(away, 2, 4))
+        send_own.append(away_own)
+        hidden = tie(hidden, away)
+    got_own = swap(tie(jnp.concatenate(send_own, axis=2), got[-1]), 2, 4)
+    done, back = [], {}
+    for c in range(len(z.down)):
+        parts = add_cut(keep[c], got[c], [(s, s + 1) for s in range(count - 1)], start=1)
+        for s in order:
+            a = parts[s - 1]
+            if len(done) >= WINDOW:
+                a = tie(a, done[-WINDOW])
+            back[c, s] = shift(a, -s, count)
+            done.append(back[c, s])
+    out = None
+    for c in range(len(z.down)):
+        pieces = [(keep[c], 0, 1)] + [(back[c, s], s * z.RP, 1) for s in blocks] + [(got_own, z.rows, 1)]
+        out = combine_chunk(z, c, weight, pieces, out)
+    return out
+
+
+def spread(a, masks, count):
+    held = {0: a}
+    for mask in reversed(masks):
+        for m in list(held):
+            held[m | mask] = swap(held[m], mask, count)
+    return held
+
+
+def by_plane(z, weight, own, sent, w_gate, w_up, w_down, regroup, ungroup):
+    count, masks = z.local, []
+    while 1 << len(masks) < z.node:
         masks.append(1 << len(masks))
-
-    if z.relative:
-        own_held = spread(own, masks, node_count)
     sums = None
     for c in range(len(z.up)):
-        if z.relative:
-            came = [shift(sent[c][s - 1], s, local_count) for s in range(1, local_count)]
-            held = spread(jnp.concatenate(came, axis=0), masks, node_count)
-            pieces = [a for m in range(node_count) for a in (own_held[m], held[m])]
-        else:
-            held = spread(lax.all_to_all(sent[c][0], "local", 0, 0, tiled=True), masks, node_count)
-            pieces = [held[m] for m in range(node_count)]
+        held = spread(lax.all_to_all(sent[c][0], "local", 0, 0, tiled=True), masks, z.node)
+        pieces = [(held[m], [(m, s) for s in range(count)]) for m in range(z.node)]
         sums = up_chunk(z, c, pieces, regroup, w_gate, w_up, sums)
-    hidden = sums[0]
-
-    out = None
-    count = local_count
+    hidden, out = sums[0], None
     for c in range(len(z.down)):
-        away = [m for m in range(node_count) if m & 1]
-        kept = [m for m in range(node_count) if not m & 1]
-        send, keep = down_chunk(z, c, hidden, ungroup, w_down, [away, kept])
-        for mask in masks[:-1]:
-            got = swap(send, mask, node_count)
-            stay = [m for m in kept if not m & (mask << 1)]
-            go = [m for m in kept if m & (mask << 1)]
-            place = {m: i * count for i, m in enumerate(kept)}
-            if mask << 1 == masks[-1] and z.relative:
-                keep, send, send_own = add_cut(keep, got, [(0, count), (count + 1, 2 * count), (count, count + 1)])
-            else:
-                sums = add_cut(keep, got, [(place[m], place[m] + count) for m in stay + go])
-                keep, send = sums if len(sums) == 2 else (
-                    jnp.concatenate(sums[: len(stay)], axis=0),
-                    jnp.concatenate(sums[len(stay) :], axis=0),
-                )
-            kept = stay
-        got = swap(send, masks[-1], node_count)
-        if z.relative:
-            got_own = swap(send_own, masks[-1], node_count)
-            parts = add_cut(keep, got, [(s, s + 1) for s in range(count - 1)], start=1)
-            back = [shift(parts[s - 1], -s, count) for s in range(1, count)]
-            pieces = [(keep, 0, 1)] + [(b, (s + 1) * z.RP, 1) for s, b in enumerate(back)] + [(got_own, z.rows, 1)]
-        else:
-            (summed,) = add_cut(keep, got, [(0, count)])
-            pieces = [(lax.all_to_all(summed, "local", 0, 0, tiled=True), 0, count)]
-        out = combine_chunk(z, c, weight, pieces, out)
+        rows = dict(enumerate(down_chunk(z, c, hidden, ungroup, w_down, [[m] for m in range(z.node)])))
+        for mask in masks:
+            for m in [m for m in rows if not m & mask]:
+                (rows[m],) = add_cut(rows[m], swap(rows.pop(m | mask), mask, z.node), [(0, count)])
+        back = lax.all_to_all(rows[0], "local", 0, 0, tiled=True)
+        out = combine_chunk(z, c, weight, [(back, 0, count)], out)
     return out
 
 

time: 262 us -> 206 us (0.79)
  waiting for transfers between devices: 130 us -> 94.6 us
  Pallas kernels: 71.1 us -> 56 us
  starting transfers between devices: 56.1 us -> 50.5 us
    ppermute x27 -> x20, waiting for transfers between devices: 67.5 us -> 37.6 us  [swap(): return lax.ppermute(a, 'node', [(i, i ^ mask) for i in range(count)])]
    pallas_call x4, Pallas kernels: 40.7 us -> 25.6 us  [up_chunk(): pl.pallas_call(functools.partial(up_kernel, z, lo, size, places, first, l...]
    ppermute x24, waiting for transfers between devices: 62.7 us -> 57 us  [shift(): lax.ppermute(a, 'local', [(i, (i + by) % count) for i in range(count)])]
    ppermute x27 -> x20, starting transfers between devices: 17.3 us -> 14.3 us  [swap(): return lax.ppermute(a, 'node', [(i, i ^ mask) for i in range(count)])]
  transfers between devices with their start and end apart: 51 -> 44, of which waited for: 20 -> 21; matrix products, arithmetic and copies ran while one was open for 0% -> 0% of each run, Pallas kernels for 18% -> 12%
where the time goes in v3:
time: 206 us; the launch traced here: 205 us
  waiting for transfers between devices  94.6 us (46%)
  Pallas kernels  56 us (27%)
  starting transfers between devices  50.5 us (25%)
  local copies, waits for them, and re-layouts  3.57 us (2%)
    ppermute x24, waiting for transfers between devices, shift(): lax.ppermute(a, 'local', [(i, (i + by) % count) for i in range(count)])  57 us
    ppermute x20, waiting for transfers between devices, swap(): return lax.ppermute(a, 'node', [(i, i ^ mask) for i in range(count)])  37.6 us
    ppermute x24, starting transfers between devices, shift(): lax.ppermute(a, 'local', [(i, (i + by) % count) for i in range(count)])  36.2 us
    pallas_call x4, Pallas kernels, up_chunk(): pl.pallas_call(functools.partial(up_kernel, z, lo, size, places, first, l...  25.6 us
    pallas_call x4, Pallas kernels, down_chunk(): pl.pallas_call(functools.partial(down_kernel, z, lo, size, order), out_sh...  22 us
    ppermute x20, starting transfers between devices, swap(): return lax.ppermute(a, 'node', [(i, i ^ mask) for i in range(count)])  14.3 us
    pallas_call x4, Pallas kernels, combine_chunk(): pl.pallas_call(functools.partial(combine_kernel, z, lo, size, blocks), gr...  5.67 us
  transfers between devices with their start and end apart: 44, of which 21 were waited for; matrix products, arithmetic and copies ran while one was open for 0% of the time, Pallas kernels for 12%

profile of v3, /device:TPU:0, one launch (start us, length us, event | category | flops | bytes accessed | tf_op | source)
XLA Modules:
  0.0 205.4 jit_solution(14947508122799201598)
XLA Ops:
  0.0 1.2 copy-done.2
  1.2 0.9 copy-done.3
  2.1 0.7 copy-done.4
  2.8 0.7 copy-done.5
  3.4 1.2 gather_rows.1
  4.6 5.1 %collective-permute-start.11 = (bf16[1,40,1792]{2,1,0:T(8,128)(2,1)S(1)}, bf16[1,40,1792]{2,1,0:T(8,128)(2,1)S(1)}, u32[]{:S(2)}, u32[]{:S(2)}) collective-permute-start(bf16[1,40,1792]{2,1,0:T(8,128)(2,1)S(1)} %get-tuple-element.100), channel_id=1, source_target_pairs={{0,3},{1,0},{2,1},{3,2},{4,7},{5,4},{6,5},{7,6},{8,11},{9,8},{10,9... | collective-permute-start | bytes 430088 | tf_op jit(solution)/shard_map/ppermute | solution.py:362
  9.8 1.0 collective-permute-start.7
  10.8 1.5 collective-permute-start.1
  12.3 1.7 collective-permute-done.11
  13.9 4.3 %collective-permute-start.12 = (bf16[1,40,1792]{2,1,0:T(8,128)(2,1)S(1)}, bf16[1,40,1792]{2,1,0:T(8,128)(2,1)S(1)}, u32[]{:S(2)}, u32[]{:S(2)}) collective-permute-start(bf16[1,40,1792]{2,1,0:T(8,128)(2,1)S(1)} %get-tuple-element.101), channel_id=1, source_target_pairs={{0,3},{1,0},{2,1},{3,2},{4,7},{5,4},{6,5},{7,6},{8,11},{9,8},{10,9... | collective-permute-start | bytes 430088 | tf_op jit(solution)/shard_map/ppermute | solution.py:362
  18.3 1.2 collective-permute-start.4
  19.5 6.7 %collective-permute-done.7 = bf16[1,40,1792]{2,1,0:T(8,128)(2,1)S(1)} collective-permute-done((bf16[1,40,1792]{2,1,0:T(8,128)(2,1)S(1)}, bf16[1,40,1792]{2,1,0:T(8,128)(2,1)S(1)}, u32[]{:S(2)}, u32[]{:S(2)}) %collective-permute-start.7) | collective-permute-done | bytes 143392 | tf_op jit(solution)/shard_map/ppermute | solution.py:362
  26.2 1.6 collective-permute-start.18
  27.8 2.6 %collective-permute-start.13 = (bf16[1,40,1792]{2,1,0:T(8,128)(2,1)S(1)}, bf16[1,40,1792]{2,1,0:T(8,128)(2,1)S(1)}, u32[]{:S(2)}, u32[]{:S(2)}) collective-permute-start(bf16[1,40,1792]{2,1,0:T(8,128)(2,1)S(1)} %get-tuple-element.102), channel_id=1, source_target_pairs={{0,3},{1,0},{2,1},{3,2},{4,7},{5,4},{6,5},{7,6},{8,11},{9,8},{10,9... | collective-permute-start | bytes 430088 | tf_op jit(solution)/shard_map/ppermute | solution.py:362
  30.4 5.0 %collective-permute-done.13 = bf16[1,40,1792]{2,1,0:T(8,128)(2,1)S(1)} collective-permute-done((bf16[1,40,1792]{2,1,0:T(8,128)(2,1)S(1)}, bf16[1,40,1792]{2,1,0:T(8,128)(2,1)S(1)}, u32[]{:S(2)}, u32[]{:S(2)}) %collective-permute-start.13) | collective-permute-done | bytes 143392 | tf_op jit(solution)/shard_map/ppermute | solution.py:362
  35.4 2.0 collective-permute-start.14
  37.6 0.7 collective-permute-start.6
  38.4 12.9 %collective-permute-done.8 = bf16[1,40,1792]{2,1,0:T(8,128)(2,1)S(1)} collective-permute-done((bf16[1,40,1792]{2,1,0:T(8,128)(2,1)S(1)}, bf16[1,40,1792]{2,1,0:T(8,128)(2,1)S(1)}, u32[]{:S(2)}, u32[]{:S(2)}) %collective-permute-start.8) | collective-permute-done | bytes 143392 | tf_op jit(solution)/shard_map/ppermute | solution.py:362
  51.4 1.0 collective-permute-start.16
  52.4 5.4 %collective-permute-done.9 = bf16[1,40,1792]{2,1,0:T(8,128)(2,1)S(1)} collective-permute-done((bf16[1,40,1792]{2,1,0:T(8,128)(2,1)S(1)}, bf16[1,40,1792]{2,1,0:T(8,128)(2,1)S(1)}, u32[]{:S(2)}, u32[]{:S(2)}) %collective-permute-start.9) | collective-permute-done | bytes 143392 | tf_op jit(solution)/shard_map/ppermute | solution.py:362
  57.9 0.5 collective-permute-start.21
  58.4 1.6 collective-permute-done.16
  60.0 4.7 %collective-permute-start.10 = (bf16[1,40,1792]{2,1,0:T(8,128)(2,1)S(1)}, bf16[1,40,1792]{2,1,0:T(8,128)(2,1)S(1)}, u32[]{:S(2)}, u32[]{:S(2)}) collective-permute-start(bf16[1,40,1792]{2,1,0:T(8,128)(2,1)S(1)} %get-tuple-element.96), channel_id=1, source_target_pairs={{0,2},{1,3},{2,0},{3,1},{4,6},{5,7},{6,4},{7,5},{8,10},{9,11},{10,... | collective-permute-start | bytes 430088 | tf_op jit(solution)/shard_map/ppermute | solution.py:362
  64.8 2.9 %collective-permute-done.10 = bf16[1,40,1792]{2,1,0:T(8,128)(2,1)S(1)} collective-permute-done((bf16[1,40,1792]{2,1,0:T(8,128)(2,1)S(1)}, bf16[1,40,1792]{2,1,0:T(8,128)(2,1)S(1)}, u32[]{:S(2)}, u32[]{:S(2)}) %collective-permute-start.10) | collective-permute-done | bytes 143392 | tf_op jit(solution)/shard_map/ppermute | solution.py:362
  67.8 2.8 %collective-permute-start.15 = (bf16[3,40,1792]{2,1,0:T(8,128)(2,1)S(1)}, bf16[3,40,1792]{2,1,0:T(8,128)(2,1)S(1)}, u32[]{:S(2)}, u32[]{:S(2)}) collective-permute-start(bf16[3,40,1792]{2,1,0:T(8,128)(2,1)S(1)} %pad_maximum_fusion.3), channel_id=1, source_target_pairs={{0,8},{4,12},{8,0},{12,4},{1,9},{5,13},{9,1},{13,5},{2,10},{6,14},... | collective-permute-start | bytes 1290248 | tf_op jit(solution)/shard_map/ppermute | solution.py:358
  70.7 6.4 %up_chunk.4 = (f32[8,128,256]{2,1,0:T(8,128)S(1)}, f32[8,128,256]{2,1,0:T(8,128)S(1)}) custom-call(bf16[1,40,7168]{2,1,0:T(8,128)(2,1)S(1)} %get-tuple-element.82.refs_0_, bf16[1,40,7168]{2,1,0:T(8,128)(2,1)S(1)} %collective-permute-done.refs_1_, bf16[1,40,7168]{2,1,0:T(8,128)(2,1)S(1)} %collective-permute-done.1.refs_2_, ...), custom_call_target="tpu_custom_call" | custom-call | flops 1879048192 | bytes 14680064 | tf_op jit(solution)/shard_map/up_chunk/pallas_call | solution.py:216
  77.2 2.3 %collective-permute-done.15 = bf16[3,40,1792]{2,1,0:T(8,128)(2,1)S(1)} collective-permute-done((bf16[3,40,1792]{2,1,0:T(8,128)(2,1)S(1)}, bf16[3,40,1792]{2,1,0:T(8,128)(2,1)S(1)}, u32[]{:S(2)}, u32[]{:S(2)}) %collective-permute-start.15) | collective-permute-done | bytes 430112 | tf_op jit(solution)/shard_map/ppermute | solution.py:358
  79.6 6.3 %up_chunk.5 = (f32[8,128,256]{2,1,0:T(8,128)S(1)}, f32[8,128,256]{2,1,0:T(8,128)S(1)}) custom-call(bf16[1,40,7168]{2,1,0:T(8,128)(2,1)S(1)} %get-tuple-element.82.refs_0_, bf16[1,40,7168]{2,1,0:T(8,128)(2,1)S(1)} %collective-permute-done.refs_1_, bf16[1,40,7168]{2,1,0:T(8,128)(2,1)S(1)} %collective-permute-done.1.refs_2_, ...), custom_call_target="tpu_custom_call" | custom-call | flops 1879048192 | bytes 14680064 | tf_op jit(solution)/shard_map/up_chunk/pallas_call | solution.py:216
  86.0 6.3 %up_chunk.6 = (f32[8,128,256]{2,1,0:T(8,128)S(1)}, f32[8,128,256]{2,1,0:T(8,128)S(1)}) custom-call(bf16[1,40,7168]{2,1,0:T(8,128)(2,1)S(1)} %get-tuple-element.82.refs_0_, bf16[1,40,7168]{2,1,0:T(8,128)(2,1)S(1)} %collective-permute-done.refs_1_, bf16[1,40,7168]{2,1,0:T(8,128)(2,1)S(1)} %collective-permute-done.1.refs_2_, ...), custom_call_target="tpu_custom_call" | custom-call | flops 1879048192 | bytes 14680064 | tf_op jit(solution)/shard_map/up_chunk/pallas_call | solution.py:216
  92.4 6.5 %up_chunk.7.hidden_ref = bf16[8,128,256]{2,1,0:T(8,128)(2,1)S(1)} custom-call(bf16[1,40,7168]{2,1,0:T(8,128)(2,1)S(1)} %get-tuple-element.82.refs_0_, bf16[1,40,7168]{2,1,0:T(8,128)(2,1)S(1)} %collective-permute-done.refs_1_, bf16[1,40,7168]{2,1,0:T(8,128)(2,1)S(1)} %collective-permute-done.1.refs_2_, ...), custom_call_target="tpu_custom_call" | custom-call | flops 1879048192 | bytes 14680064 | tf_op jit(solution)/shard_map/up_chunk/pallas_call | solution.py:216
  99.0 5.5 %down_chunk.4 = (bf16[8,40,1792]{2,1,0:T(8,128)(2,1)S(1)}, bf16[8,40,1792]{2,1,0:T(8,128)(2,1)S(1)}) custom-call(bf16[8,128,256]{2,1,0:T(8,128)(2,1)S(1)} %up_chunk.7.hidden_ref, bf16[192,256]{1,0:T(8,128)(2,1)S(1)} %copy-done.1, bf16[8,256,7168]{2,1,0:T(8,128)(2,1)} %wd_ref.7), custom_call_target="tpu_custom_call" | custom-call | flops 939524096 | bytes 7340032 | tf_op jit(solution)/shard_map/down_chunk/pallas_call | solution.py:275
  104.5 0.6 collective-permute-start.23
  105.0 2.4 %collective-permute-done.23.b_ref = bf16[8,40,1792]{2,1,0:T(8,128)(2,1)S(1)} collective-permute-done((bf16[8,40,1792]{2,1,0:T(8,128)(2,1)S(1)}, bf16[8,40,1792]{2,1,0:T(8,128)(2,1)S(1)}, u32[]{:S(2)}, u32[]{:S(2)}) %collective-permute-start.23) | collective-permute-done | bytes 1146912 | tf_op jit(solution)/shard_map/ppermute | solution.py:358
  107.7 5.5 %down_chunk.5 = (bf16[8,40,1792]{2,1,0:T(8,128)(2,1)S(1)}, bf16[8,40,1792]{2,1,0:T(8,128)(2,1)S(1)}) custom-call(bf16[8,128,256]{2,1,0:T(8,128)(2,1)S(1)} %up_chunk.7.hidden_ref, bf16[192,256]{1,0:T(8,128)(2,1)S(1)} %copy-done.1, bf16[8,256,7168]{2,1,0:T(8,128)(2,1)} %wd_ref.7), custom_call_target="tpu_custom_call" | custom-call | flops 939524096 | bytes 7340032 | tf_op jit(solution)/shard_map/down_chunk/pallas_call | solution.py:275
  113.2 0.4 collective-permute-start.24
  113.7 2.4 %collective-permute-done.24.b_ref = bf16[8,40,1792]{2,1,0:T(8,128)(2,1)S(1)} collective-permute-done((bf16[8,40,1792]{2,1,0:T(8,128)(2,1)S(1)}, bf16[8,40,1792]{2,1,0:T(8,128)(2,1)S(1)}, u32[]{:S(2)}, u32[]{:S(2)}) %collective-permute-start.24) | collective-permute-done | bytes 1146912 | tf_op jit(solution)/shard_map/ppermute | solution.py:358
  116.3 5.5 %down_chunk.6 = (bf16[8,40,1792]{2,1,0:T(8,128)(2,1)S(1)}, bf16[8,40,1792]{2,1,0:T(8,128)(2,1)S(1)}) custom-call(bf16[8,128,256]{2,1,0:T(8,128)(2,1)S(1)} %up_chunk.7.hidden_ref, bf16[192,256]{1,0:T(8,128)(2,1)S(1)} %copy-done.1, bf16[8,256,7168]{2,1,0:T(8,128)(2,1)} %wd_ref.7), custom_call_target="tpu_custom_call" | custom-call | flops 939524096 | bytes 7340032 | tf_op jit(solution)/shard_map/down_chunk/pallas_call | solution.py:275
  122.3 2.4 %collective-permute-done.25.b_ref = bf16[8,40,1792]{2,1,0:T(8,128)(2,1)S(1)} collective-permute-done((bf16[8,40,1792]{2,1,0:T(8,128)(2,1)S(1)}, bf16[8,40,1792]{2,1,0:T(8,128)(2,1)S(1)}, u32[]{:S(2)}, u32[]{:S(2)}) %collective-permute-start.25) | collective-permute-done | bytes 1146912 | tf_op jit(solution)/shard_map/ppermute | solution.py:358
  125.0 5.5 %down_chunk.7 = (bf16[8,40,1792]{2,1,0:T(8,128)(2,1)S(1)}, bf16[8,40,1792]{2,1,0:T(8,128)(2,1)S(1)}) custom-call(bf16[8,128,256]{2,1,0:T(8,128)(2,1)S(1)} %up_chunk.7.hidden_ref, bf16[192,256]{1,0:T(8,128)(2,1)S(1)} %copy-done.1, bf16[8,256,7168]{2,1,0:T(8,128)(2,1)} %wd_ref.7), custom_call_target="tpu_custom_call" | custom-call | flops 939524096 | bytes 7340032 | tf_op jit(solution)/shard_map/down_chunk/pallas_call | solution.py:275
  130.9 0.7 collective-permute-start.30
  131.6 1.7 collective-permute-done.26.b_ref
  133.6 0.8 collective-permute-start.27
  134.4 9.3 %collective-permute-done.30.b_ref = bf16[3,40,1792]{2,1,0:T(8,128)(2,1)S(1)} collective-permute-done((bf16[3,40,1792]{2,1,0:T(8,128)(2,1)S(1)}, bf16[3,40,1792]{2,1,0:T(8,128)(2,1)S(1)}, u32[]{:S(2)}, u32[]{:S(2)}) %collective-permute-start.30) | collective-permute-done | bytes 430112 | tf_op jit(solution)/shard_map/ppermute | solution.py:358
  143.8 2.1 %collective-permute-start.31 = (bf16[1,40,1792]{2,1,0:T(8,128)(2,1)S(1)}, bf16[1,40,1792]{2,1,0:T(8,128)(2,1)S(1)}, u32[]{:S(2)}, u32[]{:S(2)}) collective-permute-start(bf16[1,40,1792]{2,1,0:T(8,128)(2,1)S(1)} %get-tuple-element.134), channel_id=1, source_target_pairs={{0,3},{1,0},{2,1},{3,2},{4,7},{5,4},{6,5},{7,6},{8,11},{9,8},{10,9... | collective-permute-start | bytes 430088 | tf_op jit(solution)/shard_map/ppermute | solution.py:362
  145.9 0.5 collective-permute-start.35
  146.3 1.2 collective-permute-start.39
  147.5 2.0 collective-permute-start.29
  149.5 3.4 %collective-permute-done.27.b_ref = bf16[3,40,1792]{2,1,0:T(8,128)(2,1)S(1)} collective-permute-done((bf16[3,40,1792]{2,1,0:T(8,128)(2,1)S(1)}, bf16[3,40,1792]{2,1,0:T(8,128)(2,1)S(1)}, u32[]{:S(2)}, u32[]{:S(2)}) %collective-permute-start.27) | collective-permute-done | bytes 430112 | tf_op jit(solution)/shard_map/ppermute | solution.py:358
  152.9 0.7 collective-permute-start.28
  153.6 8.5 %collective-permute-done.29.b_ref = bf16[3,40,1792]{2,1,0:T(8,128)(2,1)S(1)} collective-permute-done((bf16[3,40,1792]{2,1,0:T(8,128)(2,1)S(1)}, bf16[3,40,1792]{2,1,0:T(8,128)(2,1)S(1)}, u32[]{:S(2)}, u32[]{:S(2)}) %collective-permute-start.29) | collective-permute-done | bytes 430112 | tf_op jit(solution)/shard_map/ppermute | solution.py:358
  162.1 0.7 collective-permute-start.43
  162.9 1.7 collective-permute-start.32
  164.6 1.4 collective-permute-start.36
  166.0 1.9 collective-permute-start.40
  167.9 3.4 %collective-permute-done.28.b_ref = bf16[3,40,1792]{2,1,0:T(8,128)(2,1)S(1)} collective-permute-done((bf16[3,40,1792]{2,1,0:T(8,128)(2,1)S(1)}, bf16[3,40,1792]{2,1,0:T(8,128)(2,1)S(1)}, u32[]{:S(2)}, u32[]{:S(2)}) %collective-permute-start.28) | collective-permute-done | bytes 430112 | tf_op jit(solution)/shard_map/ppermute | solution.py:358
  171.5 2.1 %collective-permute-start.33 = (bf16[1,40,1792]{2,1,0:T(8,128)(2,1)S(1)}, bf16[1,40,1792]{2,1,0:T(8,128)(2,1)S(1)}, u32[]{:S(2)}, u32[]{:S(2)}) collective-permute-start(bf16[1,40,1792]{2,1,0:T(8,128)(2,1)S(1)} %get-tuple-element.136), channel_id=1, source_target_pairs={{0,3},{1,0},{2,1},{3,2},{4,7},{5,4},{6,5},{7,6},{8,11},{9,8},{10,9... | collective-permute-start | bytes 430088 | tf_op jit(solution)/shard_map/ppermute | solution.py:362
  173.5 9.1 %collective-permute-done.36.refs_2_ = bf16[1,40,1792]{2,1,0:T(8,128)(2,1)S(1)} collective-permute-done((bf16[1,40,1792]{2,1,0:T(8,128)(2,1)S(1)}, bf16[1,40,1792]{2,1,0:T(8,128)(2,1)S(1)}, u32[]{:S(2)}, u32[]{:S(2)}) %collective-permute-start.36) | collective-permute-done | bytes 143392 | tf_op jit(solution)/shard_map/ppermute | solution.py:362
  182.7 3.9 %collective-permute-start.34 = (bf16[1,40,1792]{2,1,0:T(8,128)(2,1)S(1)}, bf16[1,40,1792]{2,1,0:T(8,128)(2,1)S(1)}, u32[]{:S(2)}, u32[]{:S(2)}) collective-permute-start(bf16[1,40,1792]{2,1,0:T(8,128)(2,1)S(1)} %get-tuple-element.137), channel_id=1, source_target_pairs={{0,3},{1,0},{2,1},{3,2},{4,7},{5,4},{6,5},{7,6},{8,11},{9,8},{10,9... | collective-permute-start | bytes 430088 | tf_op jit(solution)/shard_map/ppermute | solution.py:362
  186.6 9.8 %collective-permute-done.37.refs_2_ = bf16[1,40,1792]{2,1,0:T(8,128)(2,1)S(1)} collective-permute-done((bf16[1,40,1792]{2,1,0:T(8,128)(2,1)S(1)}, bf16[1,40,1792]{2,1,0:T(8,128)(2,1)S(1)}, u32[]{:S(2)}, u32[]{:S(2)}) %collective-permute-start.37) | collective-permute-done | bytes 143392 | tf_op jit(solution)/shard_map/ppermute | solution.py:362
  196.4 1.4 combine_chunk.4.refs_5_
  197.9 1.4 combine_chunk.5.refs_5_
  199.3 1.4 combine_chunk.6.refs_5_
  200.7 3.3 %collective-permute-done.38.refs_2_ = bf16[1,40,1792]{2,1,0:T(8,128)(2,1)S(1)} collective-permute-done((bf16[1,40,1792]{2,1,0:T(8,128)(2,1)S(1)}, bf16[1,40,1792]{2,1,0:T(8,128)(2,1)S(1)}, u32[]{:S(2)}, u32[]{:S(2)}) %collective-permute-start.38) | collective-permute-done | bytes 143392 | tf_op jit(solution)/shard_map/ppermute | solution.py:362
  204.0 1.4 combine_chunk.7
  (72 shorter events, 3.5 us)
Async XLA Ops:
  0.0 1.2 copy-start.2
  1.2 0.9 copy-start.3
  2.1 0.7 copy-start.4
  2.8 0.7 copy-start.5
  4.6 9.3 %collective-permute-start.11 = (bf16[1,40,1792]{2,1,0:T(8,128)(2,1)S(1)}, bf16[1,40,1792]{2,1,0:T(8,128)(2,1)S(1)}, u32[]{:S(2)}, u32[]{:S(2)}) collective-permute-start(bf16[1,40,1792]{2,1,0:T(8,128)(2,1)S(1)} %get-tuple-element.100), channel_id=1, source_target_pairs={{0,3},{1,0},{2,1},{3,2},{4,7},{5,4},{6,5},{7,6},{8,11},{9,8},{10,9... | collective-permute-start | bytes 430088 | tf_op jit(solution)/shard_map/ppermute | solution.py:362
  9.7 8.5 %collective-permute-start.3 = (bf16[1,40,1792]{2,1,0:T(8,128)(2,1)S(1)}, bf16[1,40,1792]{2,1,0:T(8,128)(2,1)S(1)}, u32[]{:S(2)}, u32[]{:S(2)}) collective-permute-start(bf16[1,40,1792]{2,1,0:T(8,128)(2,1)S(1)} %get-tuple-element.86), channel_id=1, source_target_pairs={{0,1},{1,2},{2,3},{3,0},{4,5},{5,6},{6,7},{7,4},{8,9},{9,10},{10,1... | collective-permute-start | bytes 430088 | tf_op jit(solution)/shard_map/ppermute | solution.py:362
  9.8 16.4 %collective-permute-start.7 = (bf16[1,40,1792]{2,1,0:T(8,128)(2,1)S(1)}, bf16[1,40,1792]{2,1,0:T(8,128)(2,1)S(1)}, u32[]{:S(2)}, u32[]{:S(2)}) collective-permute-start(bf16[1,40,1792]{2,1,0:T(8,128)(2,1)S(1)} %get-tuple-element.93), channel_id=1, source_target_pairs={{0,2},{1,3},{2,0},{3,1},{4,6},{5,7},{6,4},{7,5},{8,10},{9,11},{10,... | collective-permute-start | bytes 430088 | tf_op jit(solution)/shard_map/ppermute | solution.py:362
  10.8 27.5 %collective-permute-start = (bf16[1,40,7168]{2,1,0:T(8,128)(2,1)S(1)}, bf16[1,40,7168]{2,1,0:T(8,128)(2,1)S(1)}, u32[]{:S(2)}, u32[]{:S(2)}) collective-permute-start(bf16[1,40,7168]{2,1,0:T(8,128)(2,1)S(1)} %get-tuple-element.82.refs_0_), channel_id=1, source_target_pairs={{0,4},{4,0},{8,12},{12,8},{1,5},{5,1},{9,13},{13,9},{2,6},{6,2},{1... | collective-permute-start | bytes 1720328 | tf_op jit(solution)/shard_map/ppermute | solution.py:358
  10.8 27.5 %collective-permute-start.1 = (bf16[1,40,7168]{2,1,0:T(8,128)(2,1)S(1)}, bf16[1,40,7168]{2,1,0:T(8,128)(2,1)S(1)}, u32[]{:S(2)}, u32[]{:S(2)}) collective-permute-start(bf16[1,40,7168]{2,1,0:T(8,128)(2,1)S(1)} %get-tuple-element.82.refs_0_), channel_id=1, source_target_pairs={{0,8},{4,12},{8,0},{12,4},{1,9},{5,13},{9,1},{13,5},{2,10},{6,14},... | collective-permute-start | bytes 1720328 | tf_op jit(solution)/shard_map/ppermute | solution.py:358
  13.9 13.9 %collective-permute-start.12 = (bf16[1,40,1792]{2,1,0:T(8,128)(2,1)S(1)}, bf16[1,40,1792]{2,1,0:T(8,128)(2,1)S(1)}, u32[]{:S(2)}, u32[]{:S(2)}) collective-permute-start(bf16[1,40,1792]{2,1,0:T(8,128)(2,1)S(1)} %get-tuple-element.101), channel_id=1, source_target_pairs={{0,3},{1,0},{2,1},{3,2},{4,7},{5,4},{6,5},{7,6},{8,11},{9,8},{10,9... | collective-permute-start | bytes 430088 | tf_op jit(solution)/shard_map/ppermute | solution.py:362
  18.3 12.1 %collective-permute-start.4 = (bf16[1,40,1792]{2,1,0:T(8,128)(2,1)S(1)}, bf16[1,40,1792]{2,1,0:T(8,128)(2,1)S(1)}, u32[]{:S(2)}, u32[]{:S(2)}) collective-permute-start(bf16[1,40,1792]{2,1,0:T(8,128)(2,1)S(1)} %get-tuple-element.87), channel_id=1, source_target_pairs={{0,1},{1,2},{2,3},{3,0},{4,5},{5,6},{6,7},{7,4},{8,9},{9,10},{10,1... | collective-permute-start | bytes 430088 | tf_op jit(solution)/shard_map/ppermute | solution.py:362
  26.2 12.2 %collective-permute-start.18 = (bf16[3,40,1792]{2,1,0:T(8,128)(2,1)S(1)}, bf16[3,40,1792]{2,1,0:T(8,128)(2,1)S(1)}, u32[]{:S(2)}, u32[]{:S(2)}) collective-permute-start(bf16[3,40,1792]{2,1,0:T(8,128)(2,1)S(1)} %pad_maximum_fusion.5), channel_id=1, source_target_pairs={{0,8},{4,12},{8,0},{12,4},{1,9},{5,13},{9,1},{13,5},{2,10},{6,14},... | collective-permute-start | bytes 1290248 | tf_op jit(solution)/shard_map/ppermute | solution.py:358
  27.8 7.6 %collective-permute-start.13 = (bf16[1,40,1792]{2,1,0:T(8,128)(2,1)S(1)}, bf16[1,40,1792]{2,1,0:T(8,128)(2,1)S(1)}, u32[]{:S(2)}, u32[]{:S(2)}) collective-permute-start(bf16[1,40,1792]{2,1,0:T(8,128)(2,1)S(1)} %get-tuple-element.102), channel_id=1, source_target_pairs={{0,3},{1,0},{2,1},{3,2},{4,7},{5,4},{6,5},{7,6},{8,11},{9,8},{10,9... | collective-permute-start | bytes 430088 | tf_op jit(solution)/shard_map/ppermute | solution.py:362
  30.4 7.2 %collective-permute-start.5 = (bf16[1,40,1792]{2,1,0:T(8,128)(2,1)S(1)}, bf16[1,40,1792]{2,1,0:T(8,128)(2,1)S(1)}, u32[]{:S(2)}, u32[]{:S(2)}) collective-permute-start(bf16[1,40,1792]{2,1,0:T(8,128)(2,1)S(1)} %get-tuple-element.88), channel_id=1, source_target_pairs={{0,1},{1,2},{2,3},{3,0},{4,5},{5,6},{6,7},{7,4},{8,9},{9,10},{10,1... | collective-permute-start | bytes 430088 | tf_op jit(solution)/shard_map/ppermute | solution.py:362
  35.4 29.3 %collective-permute-start.14 = (bf16[1,40,1792]{2,1,0:T(8,128)(2,1)S(1)}, bf16[1,40,1792]{2,1,0:T(8,128)(2,1)S(1)}, u32[]{:S(2)}, u32[]{:S(2)}) collective-permute-start(bf16[1,40,1792]{2,1,0:T(8,128)(2,1)S(1)} %get-tuple-element.103), channel_id=1, source_target_pairs={{0,3},{1,0},{2,1},{3,2},{4,7},{5,4},{6,5},{7,6},{8,11},{9,8},{10,9... | collective-permute-start | bytes 430088 | tf_op jit(solution)/shard_map/ppermute | solution.py:362
  37.6 27.2 %collective-permute-start.6 = (bf16[1,40,1792]{2,1,0:T(8,128)(2,1)S(1)}, bf16[1,40,1792]{2,1,0:T(8,128)(2,1)S(1)}, u32[]{:S(2)}, u32[]{:S(2)}) collective-permute-start(bf16[1,40,1792]{2,1,0:T(8,128)(2,1)S(1)} %get-tuple-element.89), channel_id=1, source_target_pairs={{0,1},{1,2},{2,3},{3,0},{4,5},{5,6},{6,7},{7,4},{8,9},{9,10},{10,1... | collective-permute-start | bytes 430088 | tf_op jit(solution)/shard_map/ppermute | solution.py:362
  38.3 13.1 %collective-permute-start.8 = (bf16[1,40,1792]{2,1,0:T(8,128)(2,1)S(1)}, bf16[1,40,1792]{2,1,0:T(8,128)(2,1)S(1)}, u32[]{:S(2)}, u32[]{:S(2)}) collective-permute-start(bf16[1,40,1792]{2,1,0:T(8,128)(2,1)S(1)} %get-tuple-element.94), channel_id=1, source_target_pairs={{0,2},{1,3},{2,0},{3,1},{4,6},{5,7},{6,4},{7,5},{8,10},{9,11},{10,... | collective-permute-start | bytes 430088 | tf_op jit(solution)/shard_map/ppermute | solution.py:362
  38.3 19.5 %collective-permute-start.2 = (bf16[1,40,7168]{2,1,0:T(8,128)(2,1)S(1)}, bf16[1,40,7168]{2,1,0:T(8,128)(2,1)S(1)}, u32[]{:S(2)}, u32[]{:S(2)}) collective-permute-start(bf16[1,40,7168]{2,1,0:T(8,128)(2,1)S(1)} %collective-permute-done.1.refs_2_), channel_id=1, source_target_pairs={{0,4},{4,0},{8,12},{12,8},{1,5},{5,1},{9,13},{13,9},{2,6},{6,2},{1... | collective-permute-start | bytes 1720328 | tf_op jit(solution)/shard_map/ppermute | solution.py:358
  51.4 6.4 %collective-permute-start.9 = (bf16[1,40,1792]{2,1,0:T(8,128)(2,1)S(1)}, bf16[1,40,1792]{2,1,0:T(8,128)(2,1)S(1)}, u32[]{:S(2)}, u32[]{:S(2)}) collective-permute-start(bf16[1,40,1792]{2,1,0:T(8,128)(2,1)S(1)} %get-tuple-element.95), channel_id=1, source_target_pairs={{0,2},{1,3},{2,0},{3,1},{4,6},{5,7},{6,4},{7,5},{8,10},{9,11},{10,... | collective-permute-start | bytes 430088 | tf_op jit(solution)/shard_map/ppermute | solution.py:362
  51.4 8.5 %collective-permute-start.16 = (bf16[3,40,1792]{2,1,0:T(8,128)(2,1)S(1)}, bf16[3,40,1792]{2,1,0:T(8,128)(2,1)S(1)}, u32[]{:S(2)}, u32[]{:S(2)}) collective-permute-start(bf16[3,40,1792]{2,1,0:T(8,128)(2,1)S(1)} %pad_maximum_fusion.4), channel_id=1, source_target_pairs={{0,8},{4,12},{8,0},{12,4},{1,9},{5,13},{9,1},{13,5},{2,10},{6,14},... | collective-permute-start | bytes 1290248 | tf_op jit(solution)/shard_map/ppermute | solution.py:358
  57.8 12.9 %collective-permute-start.19 = (bf16[6,40,1792]{2,1,0:T(8,128)(2,1)S(1)}, bf16[6,40,1792]{2,1,0:T(8,128)(2,1)S(1)}, u32[]{:S(2)}, u32[]{:S(2)}) collective-permute-start(bf16[6,40,1792]{2,1,0:T(8,128)(2,1)S(1)} %constant_dynamic-update-slice_fusion.4.refs_4_), channel_id=1, source_target_pairs={{0,4},{4,0},{8,12},{12,8},{1,5},{5,1},{9,13},{13,9},{2,6},{6,2},{1... | collective-permute-start | bytes 2580488 | tf_op jit(solution)/shard_map/ppermute | solution.py:358
  57.9 12.8 %collective-permute-start.21 = (bf16[3,40,1792]{2,1,0:T(8,128)(2,1)S(1)}, bf16[3,40,1792]{2,1,0:T(8,128)(2,1)S(1)}, u32[]{:S(2)}, u32[]{:S(2)}) collective-permute-start(bf16[3,40,1792]{2,1,0:T(8,128)(2,1)S(1)} %pad_maximum_fusion.6), channel_id=1, source_target_pairs={{0,8},{4,12},{8,0},{12,4},{1,9},{5,13},{9,1},{13,5},{2,10},{6,14},... | collective-permute-start | bytes 1290248 | tf_op jit(solution)/shard_map/ppermute | solution.py:358
  60.0 7.8 %collective-permute-start.10 = (bf16[1,40,1792]{2,1,0:T(8,128)(2,1)S(1)}, bf16[1,40,1792]{2,1,0:T(8,128)(2,1)S(1)}, u32[]{:S(2)}, u32[]{:S(2)}) collective-permute-start(bf16[1,40,1792]{2,1,0:T(8,128)(2,1)S(1)} %get-tuple-element.96), channel_id=1, source_target_pairs={{0,2},{1,3},{2,0},{3,1},{4,6},{5,7},{6,4},{7,5},{8,10},{9,11},{10,... | collective-permute-start | bytes 430088 | tf_op jit(solution)/shard_map/ppermute | solution.py:362
  64.7 6.1 %copy-start = (bf16[256,192]{1,0:T(8,128)(2,1)S(1)}, bf16[256,192]{1,0:T(8,128)(2,1)}, u32[]{:S(2)}) copy-start(bf16[256,192]{1,0:T(8,128)(2,1)} %constant.11.clone.refs_6_) | copy-start | bytes 294916
  64.7 14.9 %collective-permute-start.17 = (bf16[6,40,1792]{2,1,0:T(8,128)(2,1)S(1)}, bf16[6,40,1792]{2,1,0:T(8,128)(2,1)S(1)}, u32[]{:S(2)}, u32[]{:S(2)}) collective-permute-start(bf16[6,40,1792]{2,1,0:T(8,128)(2,1)S(1)} %constant_dynamic-update-slice_fusion.refs_4_), channel_id=1, source_target_pairs={{0,4},{4,0},{8,12},{12,8},{1,5},{5,1},{9,13},{13,9},{2,6},{6,2},{1... | collective-permute-start | bytes 2580488 | tf_op jit(solution)/shard_map/ppermute | solution.py:358
  67.8 11.7 %collective-permute-start.15 = (bf16[3,40,1792]{2,1,0:T(8,128)(2,1)S(1)}, bf16[3,40,1792]{2,1,0:T(8,128)(2,1)S(1)}, u32[]{:S(2)}, u32[]{:S(2)}) collective-permute-start(bf16[3,40,1792]{2,1,0:T(8,128)(2,1)S(1)} %pad_maximum_fusion.3), channel_id=1, source_target_pairs={{0,8},{4,12},{8,0},{12,4},{1,9},{5,13},{9,1},{13,5},{2,10},{6,14},... | collective-permute-start | bytes 1290248 | tf_op jit(solution)/shard_map/ppermute | solution.py:358
  77.1 8.9 %collective-permute-start.22 = (bf16[6,40,1792]{2,1,0:T(8,128)(2,1)S(1)}, bf16[6,40,1792]{2,1,0:T(8,128)(2,1)S(1)}, u32[]{:S(2)}, u32[]{:S(2)}) collective-permute-start(bf16[6,40,1792]{2,1,0:T(8,128)(2,1)S(1)} %pad_maximum_fusion.1.refs_4_), channel_id=1, source_target_pairs={{0,4},{4,0},{8,12},{12,8},{1,5},{5,1},{9,13},{13,9},{2,6},{6,2},{1... | collective-permute-start | bytes 2580488 | tf_op jit(solution)/shard_map/ppermute | solution.py:358
  85.9 6.4 %collective-permute-start.20 = (bf16[6,40,1792]{2,1,0:T(8,128)(2,1)S(1)}, bf16[6,40,1792]{2,1,0:T(8,128)(2,1)S(1)}, u32[]{:S(2)}, u32[]{:S(2)}) collective-permute-start(bf16[6,40,1792]{2,1,0:T(8,128)(2,1)S(1)} %pad_maximum_fusion.refs_4_), channel_id=1, source_target_pairs={{0,4},{4,0},{8,12},{12,8},{1,5},{5,1},{9,13},{13,9},{2,6},{6,2},{1... | collective-permute-start | bytes 2580488 | tf_op jit(solution)/shard_map/ppermute | solution.py:358
  92.4 6.6 %copy-start.1 = (bf16[192,256]{1,0:T(8,128)(2,1)S(1)}, bf16[192,256]{1,0:T(8,128)(2,1)}, u32[]{:S(2)}) copy-start(bf16[192,256]{1,0:T(8,128)(2,1)} %constant.10.clone.ungroup_ref) | copy-start | bytes 294916
  104.5 3.0 %collective-permute-start.23 = (bf16[8,40,1792]{2,1,0:T(8,128)(2,1)S(1)}, bf16[8,40,1792]{2,1,0:T(8,128)(2,1)S(1)}, u32[]{:S(2)}, u32[]{:S(2)}) collective-permute-start(bf16[8,40,1792]{2,1,0:T(8,128)(2,1)S(1)} %get-tuple-element.113), channel_id=1, source_target_pairs={{0,4},{4,0},{8,12},{12,8},{1,5},{5,1},{9,13},{13,9},{2,6},{6,2},{1... | collective-permute-start | bytes 3440648 | tf_op jit(solution)/shard_map/ppermute | solution.py:358
  113.2 2.9 %collective-permute-start.24 = (bf16[8,40,1792]{2,1,0:T(8,128)(2,1)S(1)}, bf16[8,40,1792]{2,1,0:T(8,128)(2,1)S(1)}, u32[]{:S(2)}, u32[]{:S(2)}) collective-permute-start(bf16[8,40,1792]{2,1,0:T(8,128)(2,1)S(1)} %get-tuple-element.117), channel_id=1, source_target_pairs={{0,4},{4,0},{8,12},{12,8},{1,5},{5,1},{9,13},{13,9},{2,6},{6,2},{1... | collective-permute-start | bytes 3440648 | tf_op jit(solution)/shard_map/ppermute | solution.py:358
  121.9 2.9 %collective-permute-start.25 = (bf16[8,40,1792]{2,1,0:T(8,128)(2,1)S(1)}, bf16[8,40,1792]{2,1,0:T(8,128)(2,1)S(1)}, u32[]{:S(2)}, u32[]{:S(2)}) collective-permute-start(bf16[8,40,1792]{2,1,0:T(8,128)(2,1)S(1)} %get-tuple-element.121), channel_id=1, source_target_pairs={{0,4},{4,0},{8,12},{12,8},{1,5},{5,1},{9,13},{13,9},{2,6},{6,2},{1... | collective-permute-start | bytes 3440648 | tf_op jit(solution)/shard_map/ppermute | solution.py:358
  130.5 2.9 %collective-permute-start.26 = (bf16[8,40,1792]{2,1,0:T(8,128)(2,1)S(1)}, bf16[8,40,1792]{2,1,0:T(8,128)(2,1)S(1)}, u32[]{:S(2)}, u32[]{:S(2)}) collective-permute-start(bf16[8,40,1792]{2,1,0:T(8,128)(2,1)S(1)} %get-tuple-element.125), channel_id=1, source_target_pairs={{0,4},{4,0},{8,12},{12,8},{1,5},{5,1},{9,13},{13,9},{2,6},{6,2},{1... | collective-permute-start | bytes 3440648 | tf_op jit(solution)/shard_map/ppermute | solution.py:358
  130.9 12.8 %collective-permute-start.30 = (bf16[3,40,1792]{2,1,0:T(8,128)(2,1)S(1)}, bf16[3,40,1792]{2,1,0:T(8,128)(2,1)S(1)}, u32[]{:S(2)}, u32[]{:S(2)}) collective-permute-start(bf16[3,40,1792]{2,1,0:T(8,128)(2,1)S(1)} %get-tuple-element.114), channel_id=1, source_target_pairs={{0,8},{4,12},{8,0},{12,4},{1,9},{5,13},{9,1},{13,5},{2,10},{6,14},... | collective-permute-start | bytes 1290248 | tf_op jit(solution)/shard_map/ppermute | solution.py:358
  133.6 19.3 %collective-permute-start.27 = (bf16[3,40,1792]{2,1,0:T(8,128)(2,1)S(1)}, bf16[3,40,1792]{2,1,0:T(8,128)(2,1)S(1)}, u32[]{:S(2)}, u32[]{:S(2)}) collective-permute-start(bf16[3,40,1792]{2,1,0:T(8,128)(2,1)S(1)} %get-tuple-element.127), channel_id=1, source_target_pairs={{0,8},{4,12},{8,0},{12,4},{1,9},{5,13},{9,1},{13,5},{2,10},{6,14},... | collective-permute-start | bytes 1290248 | tf_op jit(solution)/shard_map/ppermute | solution.py:358
  143.8 19.1 %collective-permute-start.31 = (bf16[1,40,1792]{2,1,0:T(8,128)(2,1)S(1)}, bf16[1,40,1792]{2,1,0:T(8,128)(2,1)S(1)}, u32[]{:S(2)}, u32[]{:S(2)}) collective-permute-start(bf16[1,40,1792]{2,1,0:T(8,128)(2,1)S(1)} %get-tuple-element.134), channel_id=1, source_target_pairs={{0,3},{1,0},{2,1},{3,2},{4,7},{5,4},{6,5},{7,6},{8,11},{9,8},{10,9... | collective-permute-start | bytes 430088 | tf_op jit(solution)/shard_map/ppermute | solution.py:362
  145.9 18.7 %collective-permute-start.35 = (bf16[1,40,1792]{2,1,0:T(8,128)(2,1)S(1)}, bf16[1,40,1792]{2,1,0:T(8,128)(2,1)S(1)}, u32[]{:S(2)}, u32[]{:S(2)}) collective-permute-start(bf16[1,40,1792]{2,1,0:T(8,128)(2,1)S(1)} %get-tuple-element.141), channel_id=1, source_target_pairs={{0,2},{1,3},{2,0},{3,1},{4,6},{5,7},{6,4},{7,5},{8,10},{9,11},{10,... | collective-permute-start | bytes 430088 | tf_op jit(solution)/shard_map/ppermute | solution.py:362
  146.3 19.6 %collective-permute-start.39 = (bf16[1,40,1792]{2,1,0:T(8,128)(2,1)S(1)}, bf16[1,40,1792]{2,1,0:T(8,128)(2,1)S(1)}, u32[]{:S(2)}, u32[]{:S(2)}) collective-permute-start(bf16[1,40,1792]{2,1,0:T(8,128)(2,1)S(1)} %get-tuple-element.148), channel_id=1, source_target_pairs={{0,1},{1,2},{2,3},{3,0},{4,5},{5,6},{6,7},{7,4},{8,9},{9,10},{10,1... | collective-permute-start | bytes 430088 | tf_op jit(solution)/shard_map/ppermute | solution.py:362
  147.5 14.6 %collective-permute-start.29 = (bf16[3,40,1792]{2,1,0:T(8,128)(2,1)S(1)}, bf16[3,40,1792]{2,1,0:T(8,128)(2,1)S(1)}, u32[]{:S(2)}, u32[]{:S(2)}) collective-permute-start(bf16[3,40,1792]{2,1,0:T(8,128)(2,1)S(1)} %get-tuple-element.118), channel_id=1, source_target_pairs={{0,8},{4,12},{8,0},{12,4},{1,9},{5,13},{9,1},{13,5},{2,10},{6,14},... | collective-permute-start | bytes 1290248 | tf_op jit(solution)/shard_map/ppermute | solution.py:358
  152.9 18.4 %collective-permute-start.28 = (bf16[3,40,1792]{2,1,0:T(8,128)(2,1)S(1)}, bf16[3,40,1792]{2,1,0:T(8,128)(2,1)S(1)}, u32[]{:S(2)}, u32[]{:S(2)}) collective-permute-start(bf16[3,40,1792]{2,1,0:T(8,128)(2,1)S(1)} %get-tuple-element.122), channel_id=1, source_target_pairs={{0,8},{4,12},{8,0},{12,4},{1,9},{5,13},{9,1},{13,5},{2,10},{6,14},... | collective-permute-start | bytes 1290248 | tf_op jit(solution)/shard_map/ppermute | solution.py:358
  162.1 34.3 %collective-permute-start.43 = (bf16[1,40,7168]{2,1,0:T(8,128)(2,1)S(1)}, bf16[1,40,7168]{2,1,0:T(8,128)(2,1)S(1)}, u32[]{:S(2)}, u32[]{:S(2)}) collective-permute-start(bf16[1,40,7168]{2,1,0:T(8,128)(2,1)S(1)} %pad_maximum_fusion.2), channel_id=1, source_target_pairs={{0,8},{4,12},{8,0},{12,4},{1,9},{5,13},{9,1},{13,5},{2,10},{6,14},... | collective-permute-start | bytes 1720328 | tf_op jit(solution)/shard_map/ppermute | solution.py:358
  162.9 8.5 %collective-permute-start.32 = (bf16[1,40,1792]{2,1,0:T(8,128)(2,1)S(1)}, bf16[1,40,1792]{2,1,0:T(8,128)(2,1)S(1)}, u32[]{:S(2)}, u32[]{:S(2)}) collective-permute-start(bf16[1,40,1792]{2,1,0:T(8,128)(2,1)S(1)} %get-tuple-element.135), channel_id=1, source_target_pairs={{0,3},{1,0},{2,1},{3,2},{4,7},{5,4},{6,5},{7,6},{8,11},{9,8},{10,9... | collective-permute-start | bytes 430088 | tf_op jit(solution)/shard_map/ppermute | solution.py:362
  164.6 18.0 %collective-permute-start.36 = (bf16[1,40,1792]{2,1,0:T(8,128)(2,1)S(1)}, bf16[1,40,1792]{2,1,0:T(8,128)(2,1)S(1)}, u32[]{:S(2)}, u32[]{:S(2)}) collective-permute-start(bf16[1,40,1792]{2,1,0:T(8,128)(2,1)S(1)} %get-tuple-element.142), channel_id=1, source_target_pairs={{0,2},{1,3},{2,0},{3,1},{4,6},{5,7},{6,4},{7,5},{8,10},{9,11},{10,... | collective-permute-start | bytes 430088 | tf_op jit(solution)/shard_map/ppermute | solution.py:362
  166.0 16.6 %collective-permute-start.40 = (bf16[1,40,1792]{2,1,0:T(8,128)(2,1)S(1)}, bf16[1,40,1792]{2,1,0:T(8,128)(2,1)S(1)}, u32[]{:S(2)}, u32[]{:S(2)}) collective-permute-start(bf16[1,40,1792]{2,1,0:T(8,128)(2,1)S(1)} %get-tuple-element.149), channel_id=1, source_target_pairs={{0,1},{1,2},{2,3},{3,0},{4,5},{5,6},{6,7},{7,4},{8,9},{9,10},{10,1... | collective-permute-start | bytes 430088 | tf_op jit(solution)/shard_map/ppermute | solution.py:362
  171.5 11.3 %collective-permute-start.33 = (bf16[1,40,1792]{2,1,0:T(8,128)(2,1)S(1)}, bf16[1,40,1792]{2,1,0:T(8,128)(2,1)S(1)}, u32[]{:S(2)}, u32[]{:S(2)}) collective-permute-start(bf16[1,40,1792]{2,1,0:T(8,128)(2,1)S(1)} %get-tuple-element.136), channel_id=1, source_target_pairs={{0,3},{1,0},{2,1},{3,2},{4,7},{5,4},{6,5},{7,6},{8,11},{9,8},{10,9... | collective-permute-start | bytes 430088 | tf_op jit(solution)/shard_map/ppermute | solution.py:362
  182.6 13.8 %collective-permute-start.37 = (bf16[1,40,1792]{2,1,0:T(8,128)(2,1)S(1)}, bf16[1,40,1792]{2,1,0:T(8,128)(2,1)S(1)}, u32[]{:S(2)}, u32[]{:S(2)}) collective-permute-start(bf16[1,40,1792]{2,1,0:T(8,128)(2,1)S(1)} %get-tuple-element.143), channel_id=1, source_target_pairs={{0,2},{1,3},{2,0},{3,1},{4,6},{5,7},{6,4},{7,5},{8,10},{9,11},{10,... | collective-permute-start | bytes 430088 | tf_op jit(solution)/shard_map/ppermute | solution.py:362
  182.6 13.8 %collective-permute-start.41 = (bf16[1,40,1792]{2,1,0:T(8,128)(2,1)S(1)}, bf16[1,40,1792]{2,1,0:T(8,128)(2,1)S(1)}, u32[]{:S(2)}, u32[]{:S(2)}) collective-permute-start(bf16[1,40,1792]{2,1,0:T(8,128)(2,1)S(1)} %get-tuple-element.150), channel_id=1, source_target_pairs={{0,1},{1,2},{2,3},{3,0},{4,5},{5,6},{6,7},{7,4},{8,9},{9,10},{10,1... | collective-permute-start | bytes 430088 | tf_op jit(solution)/shard_map/ppermute | solution.py:362
  182.7 18.0 %collective-permute-start.34 = (bf16[1,40,1792]{2,1,0:T(8,128)(2,1)S(1)}, bf16[1,40,1792]{2,1,0:T(8,128)(2,1)S(1)}, u32[]{:S(2)}, u32[]{:S(2)}) collective-permute-start(bf16[1,40,1792]{2,1,0:T(8,128)(2,1)S(1)} %get-tuple-element.137), channel_id=1, source_target_pairs={{0,3},{1,0},{2,1},{3,2},{4,7},{5,4},{6,5},{7,6},{8,11},{9,8},{10,9... | collective-permute-start | bytes 430088 | tf_op jit(solution)/shard_map/ppermute | solution.py:362
  196.4 7.5 %collective-permute-start.38 = (bf16[1,40,1792]{2,1,0:T(8,128)(2,1)S(1)}, bf16[1,40,1792]{2,1,0:T(8,128)(2,1)S(1)}, u32[]{:S(2)}, u32[]{:S(2)}) collective-permute-start(bf16[1,40,1792]{2,1,0:T(8,128)(2,1)S(1)} %get-tuple-element.144), channel_id=1, source_target_pairs={{0,2},{1,3},{2,0},{3,1},{4,6},{5,7},{6,4},{7,5},{8,10},{9,11},{10,... | collective-permute-start | bytes 430088 | tf_op jit(solution)/shard_map/ppermute | solution.py:362
  196.4 7.5 %collective-permute-start.42 = (bf16[1,40,1792]{2,1,0:T(8,128)(2,1)S(1)}, bf16[1,40,1792]{2,1,0:T(8,128)(2,1)S(1)}, u32[]{:S(2)}, u32[]{:S(2)}) collective-permute-start(bf16[1,40,1792]{2,1,0:T(8,128)(2,1)S(1)} %get-tuple-element.151), channel_id=1, source_target_pairs={{0,1},{1,2},{2,3},{3,0},{4,5},{5,6},{6,7},{7,4},{8,9},{9,10},{10,1... | collective-permute-start | bytes 430088 | tf_op jit(solution)/shard_map/ppermute | solution.py:362

commit v4 on v0

v4 whole, which is shorter than its diff:
```python
import functools
import math

import jax
import jax.numpy as jnp
import numpy as np
from jax import lax
from jax.experimental import pallas as pl
from jax.experimental.pallas import tpu as pltpu
from jax.sharding import PartitionSpec as P

CAP = 5
GROUPS = 4
WINDOW = 3
MIB = 1024 * 1024
F32, BF16 = jnp.float32, jnp.bfloat16


def pad16(n):
    return -(-n // 16) * 16


def params(mib):
    return pltpu.CompilerParams(vmem_limit_bytes=mib * MIB)


def in_vmem():
    return pl.BlockSpec(memory_space=pltpu.VMEM)


def in_hbm():
    return pl.BlockSpec(memory_space=pl.ANY)


def tie(a, *after):
    return lax.optimization_barrier((a,) + after)[0] if after else a


def tile_of(width):
    for t in (512, 256, 128):
        if width % t == 0:
            return t
    return width


class Sizes:
    def __init__(self, tokens, w_gate, local_count, node_count):
        self.tok, self.width = tokens.shape
        self.exp_dev = w_gate.shape[0]
        self.hidden = w_gate.shape[2]
        self.local = local_count
        self.node = node_count
        self.groups = math.gcd(self.exp_dev, GROUPS)
        self.each = self.exp_dev // self.groups
        self.folds = math.gcd(max(1, 8 // self.each), self.width // 128)
        self.dc = self.width // self.folds
        self.V = self.folds * self.each
        self.R = self.V * CAP
        self.RP = pad16(self.R)
        self.MP = pad16(self.local * CAP)
        self.rows = self.local * self.RP
        self.grouped = self.V * self.MP
        self.relative = local_count <= 4 and node_count == 4

    def regroup(self):
        m = np.zeros((self.grouped, self.rows), np.float32)
        for s in range(self.local):
            for j in range(self.V):
                for c in range(CAP):
                    m[j * self.MP + s * CAP + c, s * self.RP + j * CAP + c] = 1
        return m


def steps(a, width, count):
    total = jnp.zeros_like(a)
    for i in range(1, count):
        total = total + (a >= i * width).astype(jnp.int32)
    return total


def slots(z, group, plane_ref, ids):
    row = lax.broadcasted_iota(jnp.int32, (z.rows, 1), 0)
    block = steps(row, z.RP, z.local)
    place = row - block * z.RP
    both = steps(place, CAP, z.V + 1)
    slot = place - both * CAP
    fold = steps(both, z.each, z.folds)
    expert = both - fold * z.each
    plane = block
    if z.relative:
        plane = block + plane_ref[0]
        plane = jnp.where(plane >= z.local, plane - z.local, plane)
    name = jnp.where(place < z.R, plane * z.exp_dev + group * z.each + expert, -1)
    hits = [ids[k : k + 1, :] == name for k in range(ids.shape[0])]
    named = hits[0].astype(F32)
    for hit in hits[1:]:
        named = named + hit.astype(F32)
    t0 = lax.broadcasted_iota(jnp.int32, (z.tok, z.tok), 0)
    t1 = lax.broadcasted_iota(jnp.int32, (z.tok, z.tok), 1)
    before = jnp.where(t0 < t1, 1.0, 0.0).astype(BF16)
    rank = jnp.dot(named.astype(BF16), before, preferred_element_type=F32)
    here = rank == slot.astype(F32)
    return named, here, hits, fold


def gather_kernel(z, plane_ref, ids_ref, tokens_ref, *refs):
    outs, (names_ref, stack_ref, sem) = refs[:-3], refs[-3:]
    moves = [pltpu.make_async_copy(ids_ref, names_ref, sem.at[0])]
    for q in range(z.folds):
        src = tokens_ref.at[:, pl.ds(q * z.dc, z.dc)]
        moves.append(pltpu.make_async_copy(src, stack_ref.at[pl.ds(q * z.tok, z.tok)], sem.at[1 + q]))
    for move in moves:
        move.start()
    moves[0].wait()
    picks = []
    for g in range(z.groups):
        named, here, _, fold = slots(z, g, plane_ref, names_ref[...])
        pick = jnp.where(here, named, 0.0)
        picks.append(jnp.concatenate([jnp.where(fold == q, pick, 0.0) for q in range(z.folds)], axis=1).astype(BF16))
    for move in moves[1:]:
        move.wait()
    tile = tile_of(z.dc)

    def step(i, carry):
        cols = pl.ds(pl.multiple_of(i * tile, tile), tile)
        for g in range(z.groups):
            got = jnp.dot(picks[g], stack_ref[:, cols], preferred_element_type=F32).astype(BF16)
            for s in range(z.local):
                value = got[s * z.RP : s * z.RP + z.R]
                if not z.relative:
                    outs[g][s, :, cols] = value
                elif s == 0:
                    outs[0][g, :, cols] = value
                else:
                    outs[1 + g * (z.local - 1) + s - 1][0, :, cols] = value
        return carry

    lax.fori_loop(0, z.dc // tile, step, 0)


def gather_rows(z, plane, ids, tokens):
    if z.relative:
        shapes = [(z.groups, z.R, z.dc)] + [(1, z.R, z.dc)] * (z.groups * (z.local - 1))
    else:
        shapes = [(z.local, z.R, z.dc)] * z.groups
    outs = pl.pallas_call(
        functools.partial(gather_kernel, z),
        out_shape=[jax.ShapeDtypeStruct(s, BF16) for s in shapes],
        in_specs=[pl.BlockSpec(memory_space=pltpu.SMEM)] + [in_hbm()] * 2,
        out_specs=[in_vmem()] * len(shapes),
        scratch_shapes=[
            pltpu.VMEM((ids.shape[1], z.tok), jnp.int32),
            pltpu.VMEM((z.folds * z.tok, z.dc), BF16),
            pltpu.SemaphoreType.DMA((1 + z.folds,)),
        ],
        compiler_params=params(40),
        name="gather_rows",
    )(plane, ids.T, tokens)
    outs = list(outs)
    own = outs.pop(0) if z.relative else None
    each = z.local - 1 if z.relative else 1
    return own, [outs[i * each : (i + 1) * each] for i in range(z.groups)]


def weight_kernel(z, plane_ref, ids_ref, gates_ref, out_ref):
    gates = gates_ref[...]
    size = z.folds * z.tok
    for g in range(z.groups):
        _, here, hits, fold = slots(z, g, plane_ref, ids_ref[...])
        weight = jnp.zeros((z.rows, z.tok), F32)
        for k, hit in enumerate(hits):
            weight = weight + jnp.where(hit & here, gates[k : k + 1, :], 0.0)
        for q in range(z.folds):
            mine = jnp.where(fold == q, weight, 0.0).T
            high = mine.astype(BF16)
            out_ref[g, q * z.tok : (q + 1) * z.tok, :] = high
            out_ref[g, size + q * z.tok : size + (q + 1) * z.tok, :] = (mine - high.astype(F32)).astype(BF16)


def combine_weights(z, plane, ids, gates):
    return pl.pallas_call(
        functools.partial(weight_kernel, z),
        out_shape=jax.ShapeDtypeStruct((z.groups, 2 * z.folds * z.tok, z.rows), BF16),
        in_specs=[pl.BlockSpec(memory_space=pltpu.SMEM)] + [in_vmem()] * 2,
        out_specs=in_vmem(),
        compiler_params=params(40),
        name="combine_weights",
    )(plane, ids.T, gates.T)


def expert_kernel(z, group, places, order, *refs):
    pieces = refs[: len(places)]
    regroup_ref, ungroup_ref, wg_ref, wu_ref, wd_ref = refs[len(places) : len(places) + 5]
    outs = refs[len(places) + 5 : len(places) + 5 + len(order)]
    piece_ref, gate_ref, up_ref, down_ref, rows_ref, grouped_ref, hidden_ref, psem, wsem = refs[
        len(places) + 5 + len(order) :
    ]
    moves, at = [], 0
    for i, (ref, where) in enumerate(zip(pieces, places)):
        moves.append(pltpu.make_async_copy(ref, piece_ref.at[pl.ds(at, len(where))], psem.at[i]))
        moves[-1].start()
        at += len(where)
    loads = []
    for j in range(z.each):
        e = group * z.each + j
        for i, (src, dst) in enumerate(((wg_ref, gate_ref), (wu_ref, up_ref), (wd_ref, down_ref))):
            loads.append(pltpu.make_async_copy(src.at[e], dst.at[j], wsem.at[3 * j + i]))
    for i in [k for k in range(3 * z.each) if k % 3 < 2] + [k for k in range(3 * z.each) if k % 3 == 2]:
        loads[i].start()

    if z.RP > z.R:
        rows_ref[...] = jnp.zeros_like(rows_ref)
    at = 0
    for move, where in zip(moves, places):
        move.wait()
        for m, block in where:
            rows_ref[m, block * z.RP : block * z.RP + z.R, :] = piece_ref[at]
            at += 1
    tile = tile_of(z.dc)

    def step(i, carry):
        cols = pl.ds(pl.multiple_of(i * tile, tile), tile)
        for m in range(z.node):
            got = jnp.dot(regroup_ref[...], rows_ref[m, :, cols], preferred_element_type=F32).astype(BF16)
            got = got.reshape(z.V, z.MP, tile)
            for q in range(z.folds):
                there = pl.ds(pl.multiple_of(q * z.dc + i * tile, tile), tile)
                grouped_ref[:, m * z.MP : (m + 1) * z.MP, there] = got[q * z.each : (q + 1) * z.each]
        return carry

    lax.fori_loop(0, z.dc // tile, step, 0)

    for j in range(z.each):
        loads[3 * j].wait()
        gate = jnp.dot(grouped_ref[j], gate_ref[j], preferred_element_type=F32)
        loads[3 * j + 1].wait()
        up = jnp.dot(grouped_ref[j], up_ref[j], preferred_element_type=F32)
        hidden_ref[j] = (gate / (1.0 + jnp.exp(-gate)) * up).astype(BF16)

    for j in range(z.each):
        loads[3 * j + 2].wait()
        for q in range(z.folds):
            there = slice(q * z.dc, (q + 1) * z.dc)
            got = jnp.dot(hidden_ref[j], down_ref[j, :, there], preferred_element_type=F32)
            grouped_ref[j, :, there] = got.astype(BF16)

    def back(i, carry):
        cols = pl.ds(pl.multiple_of(i * tile, tile), tile)
        for out, ms in zip(outs, order):
            for k, m in enumerate(ms):
                held = []
                for q in range(z.folds):
                    there = pl.ds(pl.multiple_of(q * z.dc + i * tile, tile), tile)
                    held.append(grouped_ref[:, m * z.MP : (m + 1) * z.MP, there].reshape(z.each * z.MP, tile))
                got = jnp.dot(ungroup_ref[...], concat(*held), preferred_element_type=F32).astype(BF16)
                for s in range(z.local):
                    out[k * z.local + s, :, cols] = got[s * z.RP : s * z.RP + z.R]
        return carry

    lax.fori_loop(0, z.dc // tile, back, 0)


def expert_group(z, group, pieces, regroup, ungroup, w_gate, w_up, w_down, order):
    pieces, places = zip(*pieces)
    shapes = [jax.ShapeDtypeStruct((len(ms) * z.local, z.R, z.dc), BF16) for ms in order]
    scratch = [
        ((z.node * z.local, z.R, z.dc), BF16),
        ((z.each, z.width, z.hidden), BF16),
        ((z.each, z.width, z.hidden), BF16),
        ((z.each, z.hidden, z.width), BF16),
        ((z.node, z.rows, z.dc), BF16),
        ((z.each, z.node * z.MP, z.width), BF16),
        ((z.each, z.node * z.MP, z.hidden), BF16),
    ]
    return pl.pallas_call(
        functools.partial(expert_kernel, z, group, places, order),
        out_shape=shapes,
        in_specs=[in_hbm()] * len(pieces) + [in_vmem()] * 2 + [in_hbm()] * 3,
        out_specs=[in_vmem()] * len(shapes),
        scratch_shapes=[pltpu.VMEM(s, t) for s, t in scratch]
        + [pltpu.SemaphoreType.DMA((len(pieces),)), pltpu.SemaphoreType.DMA((3 * z.each,))],
        compiler_params=params(48 if z.relative else 60),
        cost_estimate=pl.CostEstimate(
            flops=6 * z.each * z.node * z.MP * z.width * z.hidden,
            bytes_accessed=6 * z.each * z.width * z.hidden,
            transcendentals=0,
        ),
        name="expert_group",
    )(*pieces, regroup, ungroup, w_gate, w_up, w_down)


def add_kernel(cuts, a_ref, b_ref, *outs):
    for out, (lo, hi) in zip(outs, cuts):
        out[...] = (a_ref[lo:hi].astype(F32) + b_ref[lo:hi].astype(F32)).astype(BF16)


def add_cut(a, b, cuts):
    return pl.pallas_call(
        functools.partial(add_kernel, cuts),
        out_shape=[jax.ShapeDtypeStruct((hi - lo,) + a.shape[1:], BF16) for lo, hi in cuts],
        in_specs=[in_vmem()] * 2,
        out_specs=[in_vmem()] * len(cuts),
        compiler_params=params(32),
        cost_estimate=pl.CostEstimate(flops=a.size, bytes_accessed=6 * a.size, transcendentals=0),
        name="add_cut",
    )(a, b)


def combine_kernel(z, group, counts, last, weight_ref, *refs):
    pieces = refs[: len(counts)]
    refs = refs[len(counts) :]
    if group > 0:
        before_ref = refs[0]
        refs = refs[1:]
    out_ref, rows_ref = refs
    if z.RP > z.R:
        rows_ref[...] = jnp.zeros_like(rows_ref)
    at = 0
    for ref, count in zip(pieces, counts):
        for i in range(count):
            rows_ref[at * z.RP : at * z.RP + z.R, :] = ref[i]
            at += 1
    size = z.folds * z.tok
    tile = tile_of(z.dc)
    for i in range(z.dc // tile):
        cols = slice(i * tile, (i + 1) * tile)
        terms = jnp.dot(weight_ref[group], rows_ref[:, cols], preferred_element_type=F32)
        total = terms[:size] + terms[size:]
        if group > 0:
            total = total + before_ref[:, cols]
        if last:
            for q in range(z.folds):
                there = slice(q * z.dc + i * tile, q * z.dc + (i + 1) * tile)
                out_ref[:, there] = total[q * z.tok : (q + 1) * z.tok].astype(BF16)
        else:
            out_ref[:, cols] = total


def combine_group(z, group, weight, pieces, before):
    last = group == z.groups - 1
    shape = jax.ShapeDtypeStruct((z.tok, z.width), BF16) if last else jax.ShapeDtypeStruct((z.folds * z.tok, z.dc), F32)
    extra = [] if group == 0 else [before]
    return pl.pallas_call(
        functools.partial(combine_kernel, z, group, [p.shape[0] for p in pieces], last),
        out_shape=shape,
        in_specs=[in_vmem()] * (1 + len(pieces) + len(extra)),
        out_specs=in_vmem(),
        scratch_shapes=[pltpu.VMEM((z.rows, z.dc), BF16)],
        compiler_params=params(32),
        name="combine_group",
    )(weight, *pieces, *extra)


def swap(a, mask, count):
    return lax.ppermute(a, "node", [(i, i ^ mask) for i in range(count)])


def shift(a, by, count):
    return lax.ppermute(a, "local", [(i, (i + by) % count) for i in range(count)])


def concat(*arrays):
    return jnp.concatenate(arrays, axis=0)


def per_device(tokens, expert_ids, gate_weights, w_gate, w_up, w_down):
    local_count, node_count = lax.axis_size("local"), lax.axis_size("node")
    z = Sizes(tokens, w_gate, local_count, node_count)
    plane = lax.axis_index("local").astype(jnp.int32).reshape(1)
    regroup = z.regroup()
    matrices = jnp.asarray(regroup, BF16), jnp.asarray(regroup.T, BF16)
    own, sent = gather_rows(z, plane, expert_ids, tokens)
    weight = combine_weights(z, plane, expert_ids, gate_weights)
    route = by_distance if z.relative else by_plane
    return route(z, weight, own, sent, matrices, (w_gate, w_up, w_down))


def by_distance(z, weight, own, sent, matrices, weights):
    count, blocks = z.local, range(1, z.local)
    order = sorted(blocks, key=lambda s: -min(s, count - s))
    done, result = [], None

    def recent():
        return done[-WINDOW - 2 : len(done) - WINDOW + 1] if len(done) >= WINDOW else []

    far = swap(own, 2, 4)
    came = {}
    for g in range(z.groups):
        for s in order:
            came[g, s] = shift(tie(sent[g][s - 1], *recent()), s, count)
            done.append(came[g, s])
    stacks = [concat(*[came[g, s] for s in blocks]) for g in range(z.groups)]
    across = [swap(stack, 2, 4) for stack in stacks]
    pairs, beside = [], []

    def pair_up(*after):
        g = len(pairs)
        if g < z.groups:
            next_ones = [came[g + 1, s] for s in blocks] if g + 1 < z.groups else []
            a = tie(across[g], *next_ones, *after)
            pairs.append(concat(own[g : g + 1], stacks[g], far[g : g + 1], a))
            beside.append(swap(pairs[g], 1, 4))

    pair_up()
    pair_up()
    returned, away, summed, parts, back = [], [], [], [], []
    for g in range(z.groups):
        before = stacks[g + 2 : g + 3] + across[g + 1 : g + 2]
        before += away[g - 2 : g - 1] if g >= 2 else []
        before += parts[g - 3] if g >= 3 else []
        pieces = [(tie(pairs[g], *before), [(m, s) for m in (0, 2) for s in range(count)])]
        pieces.append((beside[g], [(m, s) for m in (1, 3) for s in range(count)]))
        send, kept = expert_group(z, g, pieces, *matrices, *weights, [[1, 3], [0, 2]])
        pair_up(send)
        beside_it = [came[g + 3, s] for s in blocks] if g + 3 < z.groups else []
        beside_it += across[g + 2 : g + 3] + beside[g + 1 : g + 2]
        beside_it += returned[g - 1 : g] if g >= 1 else []
        beside_it += summed[g - 2 : g - 1] if g >= 2 else []
        beside_it += list(back[g - 3].values()) if g >= 3 else []
        returned.append(swap(tie(send, *beside_it), 1, 4))
        keep, a = add_cut(kept, returned[g], [(0, count), (count, 2 * count)])
        away.append(a)
        summed.append(swap(a, 2, 4))
        parts.append(add_cut(keep, summed[g], [(s, s + 1) for s in range(count)]))
        back.append({})
        for s in order:
            back[g][s] = shift(tie(parts[g][s], *recent()), -s, count)
            done.append(back[g][s])
    for g in range(z.groups):
        result = combine_group(z, g, weight, [parts[g][0]] + [back[g][s] for s in blocks], result)
    return result


def spread(a, masks, count):
    held = {0: a}
    for mask in reversed(masks):
        for m in list(held):
            held[m | mask] = swap(held[m], mask, count)
    return held


def by_plane(z, weight, own, sent, matrices, weights):
    count, masks, result = z.local, [], None
    while 1 << len(masks) < z.node:
        masks.append(1 << len(masks))
    for g in range(z.groups):
        held = spread(lax.all_to_all(sent[g][0], "local", 0, 0, tiled=True), masks, z.node)
        pieces = [(held[m], [(m, s) for s in range(count)]) for m in range(z.node)]
        rows = expert_group(z, g, pieces, *matrices, *weights, [[m] for m in range(z.node)])
        rows = dict(enumerate(rows))
        for mask in masks:
            for m in [m for m in rows if not m & mask]:
                (rows[m],) = add_cut(rows[m], swap(rows.pop(m | mask), mask, z.node), [(0, count)])
        back = lax.all_to_all(rows[0], "local", 0, 0, tiled=True)
        result = combine_group(z, g, weight, [back], result)
    return result


def solution(mesh):
    return jax.shard_map(
        per_device,
        mesh=mesh,
        in_specs=(
            P(("parts", "node", "local"), None),
            P(("parts", "node", "local"), None),
            P(("parts", "node", "local"), None),
            P("local", None, "node"),
            P("local", None, "node"),
            P("local", "node", None),
        ),
        out_specs=P(("parts", "node", "local"), None),
        check_vma=False,
    )
```

time: 767 us -> 167 us (0.22)
  blocking collectives: 215 us -> 0 us
  waiting for transfers between devices: 264 us -> 52.8 us
  local copies, waits for them, and re-layouts: 129 us -> 2.27 us
  other arithmetic: 88.6 us -> 0.1 us
  starting transfers between devices: 5.86 us -> 60.7 us
  Pallas kernels: 0 us -> 50.7 us
  matrix products: 47.4 us -> 0 us
  between operations: 13.8 us -> 0.42 us
    all_to_all x1 -> x0, blocking collectives: 209 us -> none  [per_device(): lax.all_to_all(buffer, 'local', split_axis=0, concat_axis=0, tiled=True)]
    all_to_all x1 -> x0, waiting for transfers between devices: 199 us -> none  [per_device(): lax.all_to_all(outputs, 'local', split_axis=0, concat_axis=0, tiled=True)]
    reduce_sum x2 -> x0, other arithmetic: 76.9 us -> none  [the longest x1 76.7 us: combine(): return jnp.sum(values * gates[:, :, None], axis=1)]
    gather x4 -> x0, local copies, waits for them, and re-layouts: 68.4 us -> none  [the longest x2 35 us: place_rows(): return jnp.take(padded, owner_row, axis=0)]
    ppermute x0 -> x41, starting transfers between devices: none -> 60.7 us  [the longest x24 47.1 us: shift(): lax.ppermute(a, 'local', [(i, (i + by) % count) for i in range(count)])]
    ppermute x0 -> x41, waiting for transfers between devices: none -> 52.8 us  [the longest x24 36.3 us: shift(): lax.ppermute(a, 'local', [(i, (i + by) % count) for i in range(count)])]
    pallas_call x0 -> x18, Pallas kernels: none -> 50.7 us  [the longest x4 42.5 us: expert_group(): pl.pallas_call(functools.partial(expert_kernel, z, group, places, order),...]
    dot_general x3 -> x0, matrix products: 47.4 us -> none  [the longest x1 16.3 us: expert_block(): jnp.einsum('ajsf,jfd->ajsd', hidden, w_down, preferred_element_type=jnp.f...]
  transfers between devices with their start and end apart: 3 -> 41, of which waited for: 3 -> 14; matrix products, arithmetic and copies ran while one was open for 1% -> 0% of each run, Pallas kernels for 0% -> 28%
where the time goes in v4:
time: 167 us
  starting transfers between devices  60.7 us (36%)
  waiting for transfers between devices  52.8 us (32%)
  Pallas kernels  50.7 us (30%)
  local copies, waits for them, and re-layouts  2.27 us (1%)
    ppermute x24, starting transfers between devices, shift(): lax.ppermute(a, 'local', [(i, (i + by) % count) for i in range(count)])  47.1 us
    pallas_call x4, Pallas kernels, expert_group(): pl.pallas_call(functools.partial(expert_kernel, z, group, places, order),...  42.5 us
    ppermute x24, waiting for transfers between devices, shift(): lax.ppermute(a, 'local', [(i, (i + by) % count) for i in range(count)])  36.3 us
    ppermute x17, waiting for transfers between devices, swap(): return lax.ppermute(a, 'node', [(i, i ^ mask) for i in range(count)])  16.5 us
    ppermute x17, starting transfers between devices, swap(): return lax.ppermute(a, 'node', [(i, i ^ mask) for i in range(count)])  13.7 us
    pallas_call x4, Pallas kernels, combine_group(): pl.pallas_call(functools.partial(combine_kernel, z, group, [p.shape[0] fo...  3.48 us
  transfers between devices with their start and end apart: 41, of which 14 were waited for; matrix products, arithmetic and copies ran while one was open for 0% of the time, Pallas kernels for 28%

profile of v4, /device:TPU:0, one launch (start us, length us, event | category | flops | bytes accessed | tf_op | source)
XLA Modules:
  0.0 167.0 jit_solution(16176847032053629304)
XLA Ops:
  0.0 1.2 copy-done.2
  1.2 0.7 copy-done.3
  1.9 2.5 %gather_rows.1 = (bf16[4,40,1792]{2,1,0:T(8,128)(2,1)S(1)}, bf16[1,40,1792]{2,1,0:T(8,128)(2,1)S(1)}, bf16[1,40,1792]{2,1,0:T(8,128)(2,1)S(1)}, bf16[1,40,1792]{...) custom-call(s32[1]{0:T(128)} %bitcast.plane_ref, ...), custom_call_target="tpu_custom_call" | custom-call | tf_op jit(solution)/shard_map/gather_rows/pallas_call | solution.py:146
  4.3 3.1 %collective-permute-start.1 = (bf16[1,40,1792]{2,1,0:T(8,128)(2,1)S(1)}, bf16[1,40,1792]{2,1,0:T(8,128)(2,1)S(1)}, u32[]{:S(2)}, u32[]{:S(2)}) collective-permute-start(bf16[1,40,1792]{2,1,0:T(8,128)(2,1)S(1)} %get-tuple-element.87), channel_id=1, source_target_pairs={{0,1},{1,2},{2,3},{3,0},{4,5},{5,6},{6,7},{7,4},{8,9},{9,10},{10,1... | collective-permute-start | bytes 430088 | tf_op jit(solution)/shard_map/ppermute | solution.py:359
  7.4 2.6 %collective-permute-start = (bf16[1,40,1792]{2,1,0:T(8,128)(2,1)S(1)}, bf16[1,40,1792]{2,1,0:T(8,128)(2,1)S(1)}, u32[]{:S(2)}, u32[]{:S(2)}) collective-permute-start(bf16[1,40,1792]{2,1,0:T(8,128)(2,1)S(1)} %get-tuple-element.86), channel_id=1, source_target_pairs={{0,2},{1,3},{2,0},{3,1},{4,6},{5,7},{6,4},{7,5},{8,10},{9,11},{10,... | collective-permute-start | bytes 430088 | tf_op jit(solution)/shard_map/ppermute | solution.py:359
  10.0 1.3 collective-permute-start.2
  11.4 1.5 collective-permute-start.12
  12.9 6.6 %collective-permute-done = bf16[1,40,1792]{2,1,0:T(8,128)(2,1)S(1)} collective-permute-done((bf16[1,40,1792]{2,1,0:T(8,128)(2,1)S(1)}, bf16[1,40,1792]{2,1,0:T(8,128)(2,1)S(1)}, u32[]{:S(2)}, u32[]{:S(2)}) %collective-permute-start) | collective-permute-done | bytes 143392 | tf_op jit(solution)/shard_map/ppermute | solution.py:359
  19.4 5.2 %collective-permute-start.6 = (bf16[1,40,1792]{2,1,0:T(8,128)(2,1)S(1)}, bf16[1,40,1792]{2,1,0:T(8,128)(2,1)S(1)}, u32[]{:S(2)}, u32[]{:S(2)}) collective-permute-start(bf16[1,40,1792]{2,1,0:T(8,128)(2,1)S(1)} %get-tuple-element.96), channel_id=1, source_target_pairs={{0,1},{1,2},{2,3},{3,0},{4,5},{5,6},{6,7},{7,4},{8,9},{9,10},{10,1... | collective-permute-start | bytes 430088 | tf_op jit(solution)/shard_map/ppermute | solution.py:359
  24.7 1.5 collective-permute-start.17
  26.3 6.8 %collective-permute-done.4 = bf16[1,40,1792]{2,1,0:T(8,128)(2,1)S(1)} collective-permute-done((bf16[1,40,1792]{2,1,0:T(8,128)(2,1)S(1)}, bf16[1,40,1792]{2,1,0:T(8,128)(2,1)S(1)}, u32[]{:S(2)}, u32[]{:S(2)}) %collective-permute-start.4) | collective-permute-done | bytes 143392 | tf_op jit(solution)/shard_map/ppermute | solution.py:359
  33.1 0.4 collective-permute-start.7
  33.5 1.9 %collective-permute-start.5 = (bf16[1,40,1792]{2,1,0:T(8,128)(2,1)S(1)}, bf16[1,40,1792]{2,1,0:T(8,128)(2,1)S(1)}, u32[]{:S(2)}, u32[]{:S(2)}) collective-permute-start(bf16[1,40,1792]{2,1,0:T(8,128)(2,1)S(1)} %get-tuple-element.93), channel_id=1, source_target_pairs={{0,2},{1,3},{2,0},{3,1},{4,6},{5,7},{6,4},{7,5},{8,10},{9,11},{10,... | collective-permute-start | bytes 430088 | tf_op jit(solution)/shard_map/ppermute | solution.py:359
  35.4 2.9 %collective-permute-start.10 = (bf16[1,40,1792]{2,1,0:T(8,128)(2,1)S(1)}, bf16[1,40,1792]{2,1,0:T(8,128)(2,1)S(1)}, u32[]{:S(2)}, u32[]{:S(2)}) collective-permute-start(bf16[1,40,1792]{2,1,0:T(8,128)(2,1)S(1)} %get-tuple-element.103), channel_id=1, source_target_pairs={{0,3},{1,0},{2,1},{3,2},{4,7},{5,4},{6,5},{7,6},{8,11},{9,8},{10,9... | collective-permute-start | bytes 430088 | tf_op jit(solution)/shard_map/ppermute | solution.py:359
  38.5 3.1 %collective-permute-done.7 = bf16[1,40,1792]{2,1,0:T(8,128)(2,1)S(1)} collective-permute-done((bf16[1,40,1792]{2,1,0:T(8,128)(2,1)S(1)}, bf16[1,40,1792]{2,1,0:T(8,128)(2,1)S(1)}, u32[]{:S(2)}, u32[]{:S(2)}) %collective-permute-start.7) | collective-permute-done | bytes 143392 | tf_op jit(solution)/shard_map/ppermute | solution.py:359
  41.6 1.5 collective-permute-start.14
  43.1 2.1 %collective-permute-done.5 = bf16[1,40,1792]{2,1,0:T(8,128)(2,1)S(1)} collective-permute-done((bf16[1,40,1792]{2,1,0:T(8,128)(2,1)S(1)}, bf16[1,40,1792]{2,1,0:T(8,128)(2,1)S(1)}, u32[]{:S(2)}, u32[]{:S(2)}) %collective-permute-start.5) | collective-permute-done | bytes 143392 | tf_op jit(solution)/shard_map/ppermute | solution.py:359
  45.2 2.8 %collective-permute-start.8 = (bf16[1,40,1792]{2,1,0:T(8,128)(2,1)S(1)}, bf16[1,40,1792]{2,1,0:T(8,128)(2,1)S(1)}, u32[]{:S(2)}, u32[]{:S(2)}) collective-permute-start(bf16[1,40,1792]{2,1,0:T(8,128)(2,1)S(1)} %get-tuple-element.98), channel_id=1, source_target_pairs={{0,1},{1,2},{2,3},{3,0},{4,5},{5,6},{6,7},{7,4},{8,9},{9,10},{10,1... | collective-permute-start | bytes 430088 | tf_op jit(solution)/shard_map/ppermute | solution.py:359
  48.0 3.4 %collective-permute-start.9 = (bf16[1,40,1792]{2,1,0:T(8,128)(2,1)S(1)}, bf16[1,40,1792]{2,1,0:T(8,128)(2,1)S(1)}, u32[]{:S(2)}, u32[]{:S(2)}) collective-permute-start(bf16[1,40,1792]{2,1,0:T(8,128)(2,1)S(1)} %get-tuple-element.100), channel_id=1, source_target_pairs={{0,2},{1,3},{2,0},{3,1},{4,6},{5,7},{6,4},{7,5},{8,10},{9,11},{10,... | collective-permute-start | bytes 430088 | tf_op jit(solution)/shard_map/ppermute | solution.py:359
  51.5 2.6 %collective-permute-done.8 = bf16[1,40,1792]{2,1,0:T(8,128)(2,1)S(1)} collective-permute-done((bf16[1,40,1792]{2,1,0:T(8,128)(2,1)S(1)}, bf16[1,40,1792]{2,1,0:T(8,128)(2,1)S(1)}, u32[]{:S(2)}, u32[]{:S(2)}) %collective-permute-start.8) | collective-permute-done | bytes 143392 | tf_op jit(solution)/shard_map/ppermute | solution.py:359
  54.1 1.9 %collective-permute-start.11 = (bf16[1,40,1792]{2,1,0:T(8,128)(2,1)S(1)}, bf16[1,40,1792]{2,1,0:T(8,128)(2,1)S(1)}, u32[]{:S(2)}, u32[]{:S(2)}) collective-permute-start(bf16[1,40,1792]{2,1,0:T(8,128)(2,1)S(1)} %get-tuple-element.104), channel_id=1, source_target_pairs={{0,3},{1,0},{2,1},{3,2},{4,7},{5,4},{6,5},{7,6},{8,11},{9,8},{10,9... | collective-permute-start | bytes 430088 | tf_op jit(solution)/shard_map/ppermute | solution.py:359
  56.0 2.6 %collective-permute-done.9 = bf16[1,40,1792]{2,1,0:T(8,128)(2,1)S(1)} collective-permute-done((bf16[1,40,1792]{2,1,0:T(8,128)(2,1)S(1)}, bf16[1,40,1792]{2,1,0:T(8,128)(2,1)S(1)}, u32[]{:S(2)}, u32[]{:S(2)}) %collective-permute-start.9) | collective-permute-done | bytes 143392 | tf_op jit(solution)/shard_map/ppermute | solution.py:359
  58.6 1.4 collective-permute-done.11
  60.3 0.5 collective-permute-start.16
  60.9 1.5 collective-permute-start.15
  62.4 0.7 collective-permute-done.18.refs_1_
  63.1 10.5 %expert_group.5 = (bf16[8,40,1792]{2,1,0:T(8,128)(2,1)S(1)}, bf16[8,40,1792]{2,1,0:T(8,128)(2,1)S(1)}) custom-call(bf16[8,40,1792]{2,1,0:T(8,128)(2,1)S(1)} %constant_dynamic-update-slice_fusion.14.refs_0_, bf16[8,40,1792]{2,1,0:T(8,128)(2,1)S(1)} %collective-permute-done.18.refs_1_, bf16[256,192]{1,0:T(8,128)(2,1)S(1)} %copy-done, ...), custom_call_target="tpu_custom_call" | custom-call | flops 2818572288 | bytes 22020096 | tf_op jit(solution)/shard_map/expert_group/pallas_call | solution.py:275
  73.7 0.2 collective-permute-start.19
  73.9 0.4 collective-permute-start.20
  74.2 1.5 collective-permute-start.13
  75.7 10.5 %expert_group.4 = (bf16[8,40,1792]{2,1,0:T(8,128)(2,1)S(1)}, bf16[8,40,1792]{2,1,0:T(8,128)(2,1)S(1)}) custom-call(bf16[8,40,1792]{2,1,0:T(8,128)(2,1)S(1)} %constant_dynamic-update-slice_fusion.3.refs_0_, bf16[8,40,1792]{2,1,0:T(8,128)(2,1)S(1)} %collective-permute-done.16.refs_1_, bf16[256,192]{1,0:T(8,128)(2,1)S(1)} %copy-done, ...), custom_call_target="tpu_custom_call" | custom-call | flops 2818572288 | bytes 22020096 | tf_op jit(solution)/shard_map/expert_group/pallas_call | solution.py:275
  86.4 0.5 collective-permute-start.21
  86.9 0.3 add_cut.9
  87.2 1.5 collective-permute-start.22
  88.6 10.7 %expert_group.7 = (bf16[8,40,1792]{2,1,0:T(8,128)(2,1)S(1)}, bf16[8,40,1792]{2,1,0:T(8,128)(2,1)S(1)}) custom-call(bf16[8,40,1792]{2,1,0:T(8,128)(2,1)S(1)} %constant_dynamic-update-slice_fusion.18.refs_0_, bf16[8,40,1792]{2,1,0:T(8,128)(2,1)S(1)} %collective-permute-done.19.refs_1_, bf16[256,192]{1,0:T(8,128)(2,1)S(1)} %copy-done, ...), custom_call_target="tpu_custom_call" | custom-call | flops 2818572288 | bytes 22020096 | tf_op jit(solution)/shard_map/expert_group/pallas_call | solution.py:275
  99.4 2.8 %collective-permute-done.22.b_ref = bf16[4,40,1792]{2,1,0:T(8,128)(2,1)S(1)} collective-permute-done((bf16[4,40,1792]{2,1,0:T(8,128)(2,1)S(1)}, bf16[4,40,1792]{2,1,0:T(8,128)(2,1)S(1)}, u32[]{:S(2)}, u32[]{:S(2)}) %collective-permute-start.22) | collective-permute-done | bytes 573472 | tf_op jit(solution)/shard_map/ppermute | solution.py:355
  102.2 0.3 add_cut.8
  102.5 1.5 collective-permute-start.25
  103.9 0.1 add_cut.10
  104.1 1.1 collective-permute-start.26
  105.2 3.4 %collective-permute-start.27 = (bf16[1,40,1792]{2,1,0:T(8,128)(2,1)S(1)}, bf16[1,40,1792]{2,1,0:T(8,128)(2,1)S(1)}, u32[]{:S(2)}, u32[]{:S(2)}) collective-permute-start(bf16[1,40,1792]{2,1,0:T(8,128)(2,1)S(1)} %get-tuple-element.131), channel_id=1, source_target_pairs={{0,3},{1,0},{2,1},{3,2},{4,7},{5,4},{6,5},{7,6},{8,11},{9,8},{10,9... | collective-permute-start | bytes 430088 | tf_op jit(solution)/shard_map/ppermute | solution.py:359
  108.6 10.7 %expert_group.6 = (bf16[8,40,1792]{2,1,0:T(8,128)(2,1)S(1)}, bf16[8,40,1792]{2,1,0:T(8,128)(2,1)S(1)}) custom-call(bf16[8,40,1792]{2,1,0:T(8,128)(2,1)S(1)} %constant_dynamic-update-slice_fusion.10.refs_0_, bf16[8,40,1792]{2,1,0:T(8,128)(2,1)S(1)} %collective-permute-done.23.refs_1_, bf16[256,192]{1,0:T(8,128)(2,1)S(1)} %copy-done, ...), custom_call_target="tpu_custom_call" | custom-call | flops 2818572288 | bytes 22020096 | tf_op jit(solution)/shard_map/expert_group/pallas_call | solution.py:275
  119.4 0.3 add_cut.14
  119.7 0.7 collective-permute-start.32
  120.4 1.8 %collective-permute-done.29.b_ref = bf16[8,40,1792]{2,1,0:T(8,128)(2,1)S(1)} collective-permute-done((bf16[8,40,1792]{2,1,0:T(8,128)(2,1)S(1)}, bf16[8,40,1792]{2,1,0:T(8,128)(2,1)S(1)}, u32[]{:S(2)}, u32[]{:S(2)}) %collective-permute-start.29) | collective-permute-done | bytes 1146912 | tf_op jit(solution)/shard_map/ppermute | solution.py:355
  122.2 0.3 add_cut.11
  122.5 0.7 collective-permute-start.30
  123.3 1.9 %collective-permute-start.33 = (bf16[1,40,1792]{2,1,0:T(8,128)(2,1)S(1)}, bf16[1,40,1792]{2,1,0:T(8,128)(2,1)S(1)}, u32[]{:S(2)}, u32[]{:S(2)}) collective-permute-start(bf16[1,40,1792]{2,1,0:T(8,128)(2,1)S(1)} %get-tuple-element.146), channel_id=1, source_target_pairs={{0,2},{1,3},{2,0},{3,1},{4,6},{5,7},{6,4},{7,5},{8,10},{9,11},{10,... | collective-permute-start | bytes 430088 | tf_op jit(solution)/shard_map/ppermute | solution.py:359
  125.3 2.0 %collective-permute-start.35 = (bf16[1,40,1792]{2,1,0:T(8,128)(2,1)S(1)}, bf16[1,40,1792]{2,1,0:T(8,128)(2,1)S(1)}, u32[]{:S(2)}, u32[]{:S(2)}) collective-permute-start(bf16[1,40,1792]{2,1,0:T(8,128)(2,1)S(1)} %get-tuple-element.150), channel_id=1, source_target_pairs={{0,3},{1,0},{2,1},{3,2},{4,7},{5,4},{6,5},{7,6},{8,11},{9,8},{10,9... | collective-permute-start | bytes 430088 | tf_op jit(solution)/shard_map/ppermute | solution.py:359
  127.3 0.5 collective-permute-start.31
  127.8 7.8 %collective-permute-done.32.b_ref = bf16[4,40,1792]{2,1,0:T(8,128)(2,1)S(1)} collective-permute-done((bf16[4,40,1792]{2,1,0:T(8,128)(2,1)S(1)}, bf16[4,40,1792]{2,1,0:T(8,128)(2,1)S(1)}, u32[]{:S(2)}, u32[]{:S(2)}) %collective-permute-start.32) | collective-permute-done | bytes 573472 | tf_op jit(solution)/shard_map/ppermute | solution.py:355
  135.7 1.9 %collective-permute-start.34 = (bf16[1,40,1792]{2,1,0:T(8,128)(2,1)S(1)}, bf16[1,40,1792]{2,1,0:T(8,128)(2,1)S(1)}, u32[]{:S(2)}, u32[]{:S(2)}) collective-permute-start(bf16[1,40,1792]{2,1,0:T(8,128)(2,1)S(1)} %get-tuple-element.147), channel_id=1, source_target_pairs={{0,2},{1,3},{2,0},{3,1},{4,6},{5,7},{6,4},{7,5},{8,10},{9,11},{10,... | collective-permute-start | bytes 430088 | tf_op jit(solution)/shard_map/ppermute | solution.py:359
  137.7 2.0 %collective-permute-start.36 = (bf16[1,40,1792]{2,1,0:T(8,128)(2,1)S(1)}, bf16[1,40,1792]{2,1,0:T(8,128)(2,1)S(1)}, u32[]{:S(2)}, u32[]{:S(2)}) collective-permute-start(bf16[1,40,1792]{2,1,0:T(8,128)(2,1)S(1)} %get-tuple-element.151), channel_id=1, source_target_pairs={{0,3},{1,0},{2,1},{3,2},{4,7},{5,4},{6,5},{7,6},{8,11},{9,8},{10,9... | collective-permute-start | bytes 430088 | tf_op jit(solution)/shard_map/ppermute | solution.py:359
  139.7 4.4 %collective-permute-start.39 = (bf16[1,40,1792]{2,1,0:T(8,128)(2,1)S(1)}, bf16[1,40,1792]{2,1,0:T(8,128)(2,1)S(1)}, u32[]{:S(2)}, u32[]{:S(2)}) collective-permute-start(bf16[1,40,1792]{2,1,0:T(8,128)(2,1)S(1)} %get-tuple-element.157), channel_id=1, source_target_pairs={{0,1},{1,2},{2,3},{3,0},{4,5},{5,6},{6,7},{7,4},{8,9},{9,10},{10,1... | collective-permute-start | bytes 430088 | tf_op jit(solution)/shard_map/ppermute | solution.py:359
  144.0 3.4 %collective-permute-done.30.b_ref = bf16[4,40,1792]{2,1,0:T(8,128)(2,1)S(1)} collective-permute-done((bf16[4,40,1792]{2,1,0:T(8,128)(2,1)S(1)}, bf16[4,40,1792]{2,1,0:T(8,128)(2,1)S(1)}, u32[]{:S(2)}, u32[]{:S(2)}) %collective-permute-start.30) | collective-permute-done | bytes 573472 | tf_op jit(solution)/shard_map/ppermute | solution.py:355
  147.6 1.6 collective-permute-done.34.refs_2_
  149.1 2.3 %collective-permute-start.37 = (bf16[1,40,1792]{2,1,0:T(8,128)(2,1)S(1)}, bf16[1,40,1792]{2,1,0:T(8,128)(2,1)S(1)}, u32[]{:S(2)}, u32[]{:S(2)}) collective-permute-start(bf16[1,40,1792]{2,1,0:T(8,128)(2,1)S(1)} %get-tuple-element.152), channel_id=1, source_target_pairs={{0,3},{1,0},{2,1},{3,2},{4,7},{5,4},{6,5},{7,6},{8,11},{9,8},{10,9... | collective-permute-start | bytes 430088 | tf_op jit(solution)/shard_map/ppermute | solution.py:359
  151.5 1.9 %collective-permute-start.38 = (bf16[1,40,1792]{2,1,0:T(8,128)(2,1)S(1)}, bf16[1,40,1792]{2,1,0:T(8,128)(2,1)S(1)}, u32[]{:S(2)}, u32[]{:S(2)}) collective-permute-start(bf16[1,40,1792]{2,1,0:T(8,128)(2,1)S(1)} %get-tuple-element.154), channel_id=1, source_target_pairs={{0,2},{1,3},{2,0},{3,1},{4,6},{5,7},{6,4},{7,5},{8,10},{9,11},{10,... | collective-permute-start | bytes 430088 | tf_op jit(solution)/shard_map/ppermute | solution.py:359
  153.4 0.7 combine_weights.1.weight_ref
  154.1 0.6 combine_group.4.refs_4_
  154.7 0.6 combine_group.5.refs_4_
  155.3 0.6 combine_group.6.refs_4_
  156.0 9.4 %collective-permute-done.38.refs_2_ = bf16[1,40,1792]{2,1,0:T(8,128)(2,1)S(1)} collective-permute-done((bf16[1,40,1792]{2,1,0:T(8,128)(2,1)S(1)}, bf16[1,40,1792]{2,1,0:T(8,128)(2,1)S(1)}, u32[]{:S(2)}, u32[]{:S(2)}) %collective-permute-start.38) | collective-permute-done | bytes 143392 | tf_op jit(solution)/shard_map/ppermute | solution.py:359
  165.4 1.6 combine_group.7
  (68 shorter events, 1.2 us)
Async XLA Ops:
  0.0 1.2 copy-start.2
  1.2 0.7 copy-start.3
  4.3 15.1 %collective-permute-start.1 = (bf16[1,40,1792]{2,1,0:T(8,128)(2,1)S(1)}, bf16[1,40,1792]{2,1,0:T(8,128)(2,1)S(1)}, u32[]{:S(2)}, u32[]{:S(2)}) collective-permute-start(bf16[1,40,1792]{2,1,0:T(8,128)(2,1)S(1)} %get-tuple-element.87), channel_id=1, source_target_pairs={{0,1},{1,2},{2,3},{3,0},{4,5},{5,6},{6,7},{7,4},{8,9},{9,10},{10,1... | collective-permute-start | bytes 430088 | tf_op jit(solution)/shard_map/ppermute | solution.py:359
  7.4 12.0 %collective-permute-start = (bf16[1,40,1792]{2,1,0:T(8,128)(2,1)S(1)}, bf16[1,40,1792]{2,1,0:T(8,128)(2,1)S(1)}, u32[]{:S(2)}, u32[]{:S(2)}) collective-permute-start(bf16[1,40,1792]{2,1,0:T(8,128)(2,1)S(1)} %get-tuple-element.86), channel_id=1, source_target_pairs={{0,2},{1,3},{2,0},{3,1},{4,6},{5,7},{6,4},{7,5},{8,10},{9,11},{10,... | collective-permute-start | bytes 430088 | tf_op jit(solution)/shard_map/ppermute | solution.py:359
  10.0 14.6 %collective-permute-start.2 = (bf16[1,40,1792]{2,1,0:T(8,128)(2,1)S(1)}, bf16[1,40,1792]{2,1,0:T(8,128)(2,1)S(1)}, u32[]{:S(2)}, u32[]{:S(2)}) collective-permute-start(bf16[1,40,1792]{2,1,0:T(8,128)(2,1)S(1)} %get-tuple-element.88), channel_id=1, source_target_pairs={{0,3},{1,0},{2,1},{3,2},{4,7},{5,4},{6,5},{7,6},{8,11},{9,8},{10,9... | collective-permute-start | bytes 430088 | tf_op jit(solution)/shard_map/ppermute | solution.py:359
  11.4 48.7 %collective-permute-start.12 = (bf16[4,40,1792]{2,1,0:T(8,128)(2,1)S(1)}, bf16[4,40,1792]{2,1,0:T(8,128)(2,1)S(1)}, u32[]{:S(2)}, u32[]{:S(2)}) collective-permute-start(bf16[4,40,1792]{2,1,0:T(8,128)(2,1)S(1)} %get-tuple-element.83), channel_id=1, source_target_pairs={{0,8},{4,12},{8,0},{12,4},{1,9},{5,13},{9,1},{13,5},{2,10},{6,14},... | collective-permute-start | bytes 1720328 | tf_op jit(solution)/shard_map/ppermute | solution.py:355
  19.4 13.7 %collective-permute-start.4 = (bf16[1,40,1792]{2,1,0:T(8,128)(2,1)S(1)}, bf16[1,40,1792]{2,1,0:T(8,128)(2,1)S(1)}, u32[]{:S(2)}, u32[]{:S(2)}) collective-permute-start(bf16[1,40,1792]{2,1,0:T(8,128)(2,1)S(1)} %get-tuple-element.92), channel_id=1, source_target_pairs={{0,2},{1,3},{2,0},{3,1},{4,6},{5,7},{6,4},{7,5},{8,10},{9,11},{10,... | collective-permute-start | bytes 430088 | tf_op jit(solution)/shard_map/ppermute | solution.py:359
  19.4 13.7 %collective-permute-start.6 = (bf16[1,40,1792]{2,1,0:T(8,128)(2,1)S(1)}, bf16[1,40,1792]{2,1,0:T(8,128)(2,1)S(1)}, u32[]{:S(2)}, u32[]{:S(2)}) collective-permute-start(bf16[1,40,1792]{2,1,0:T(8,128)(2,1)S(1)} %get-tuple-element.96), channel_id=1, source_target_pairs={{0,1},{1,2},{2,3},{3,0},{4,5},{5,6},{6,7},{7,4},{8,9},{9,10},{10,1... | collective-permute-start | bytes 430088 | tf_op jit(solution)/shard_map/ppermute | solution.py:359
  24.6 10.8 %collective-permute-start.3 = (bf16[1,40,1792]{2,1,0:T(8,128)(2,1)S(1)}, bf16[1,40,1792]{2,1,0:T(8,128)(2,1)S(1)}, u32[]{:S(2)}, u32[]{:S(2)}) collective-permute-start(bf16[1,40,1792]{2,1,0:T(8,128)(2,1)S(1)} %get-tuple-element.89), channel_id=1, source_target_pairs={{0,3},{1,0},{2,1},{3,2},{4,7},{5,4},{6,5},{7,6},{8,11},{9,8},{10,9... | collective-permute-start | bytes 430088 | tf_op jit(solution)/shard_map/ppermute | solution.py:359
  24.7 31.3 %collective-permute-start.17 = (bf16[3,40,1792]{2,1,0:T(8,128)(2,1)S(1)}, bf16[3,40,1792]{2,1,0:T(8,128)(2,1)S(1)}, u32[]{:S(2)}, u32[]{:S(2)}) collective-permute-start(bf16[3,40,1792]{2,1,0:T(8,128)(2,1)S(1)} %pad_maximum_fusion.1), channel_id=1, source_target_pairs={{0,8},{4,12},{8,0},{12,4},{1,9},{5,13},{9,1},{13,5},{2,10},{6,14},... | collective-permute-start | bytes 1290248 | tf_op jit(solution)/shard_map/ppermute | solution.py:355
  33.1 8.5 %collective-permute-start.7 = (bf16[1,40,1792]{2,1,0:T(8,128)(2,1)S(1)}, bf16[1,40,1792]{2,1,0:T(8,128)(2,1)S(1)}, u32[]{:S(2)}, u32[]{:S(2)}) collective-permute-start(bf16[1,40,1792]{2,1,0:T(8,128)(2,1)S(1)} %get-tuple-element.97), channel_id=1, source_target_pairs={{0,1},{1,2},{2,3},{3,0},{4,5},{5,6},{6,7},{7,4},{8,9},{9,10},{10,1... | collective-permute-start | bytes 430088 | tf_op jit(solution)/shard_map/ppermute | solution.py:359
  33.5 11.7 %collective-permute-start.5 = (bf16[1,40,1792]{2,1,0:T(8,128)(2,1)S(1)}, bf16[1,40,1792]{2,1,0:T(8,128)(2,1)S(1)}, u32[]{:S(2)}, u32[]{:S(2)}) collective-permute-start(bf16[1,40,1792]{2,1,0:T(8,128)(2,1)S(1)} %get-tuple-element.93), channel_id=1, source_target_pairs={{0,2},{1,3},{2,0},{3,1},{4,6},{5,7},{6,4},{7,5},{8,10},{9,11},{10,... | collective-permute-start | bytes 430088 | tf_op jit(solution)/shard_map/ppermute | solution.py:359
  35.4 12.5 %collective-permute-start.10 = (bf16[1,40,1792]{2,1,0:T(8,128)(2,1)S(1)}, bf16[1,40,1792]{2,1,0:T(8,128)(2,1)S(1)}, u32[]{:S(2)}, u32[]{:S(2)}) collective-permute-start(bf16[1,40,1792]{2,1,0:T(8,128)(2,1)S(1)} %get-tuple-element.103), channel_id=1, source_target_pairs={{0,3},{1,0},{2,1},{3,2},{4,7},{5,4},{6,5},{7,6},{8,11},{9,8},{10,9... | collective-permute-start | bytes 430088 | tf_op jit(solution)/shard_map/ppermute | solution.py:359
  41.6 18.7 %collective-permute-start.14 = (bf16[3,40,1792]{2,1,0:T(8,128)(2,1)S(1)}, bf16[3,40,1792]{2,1,0:T(8,128)(2,1)S(1)}, u32[]{:S(2)}, u32[]{:S(2)}) collective-permute-start(bf16[3,40,1792]{2,1,0:T(8,128)(2,1)S(1)} %pad_maximum_fusion), channel_id=1, source_target_pairs={{0,8},{4,12},{8,0},{12,4},{1,9},{5,13},{9,1},{13,5},{2,10},{6,14},... | collective-permute-start | bytes 1290248 | tf_op jit(solution)/shard_map/ppermute | solution.py:355
  45.2 8.9 %collective-permute-start.8 = (bf16[1,40,1792]{2,1,0:T(8,128)(2,1)S(1)}, bf16[1,40,1792]{2,1,0:T(8,128)(2,1)S(1)}, u32[]{:S(2)}, u32[]{:S(2)}) collective-permute-start(bf16[1,40,1792]{2,1,0:T(8,128)(2,1)S(1)} %get-tuple-element.98), channel_id=1, source_target_pairs={{0,1},{1,2},{2,3},{3,0},{4,5},{5,6},{6,7},{7,4},{8,9},{9,10},{10,1... | collective-permute-start | bytes 430088 | tf_op jit(solution)/shard_map/ppermute | solution.py:359
  48.0 10.6 %collective-permute-start.9 = (bf16[1,40,1792]{2,1,0:T(8,128)(2,1)S(1)}, bf16[1,40,1792]{2,1,0:T(8,128)(2,1)S(1)}, u32[]{:S(2)}, u32[]{:S(2)}) collective-permute-start(bf16[1,40,1792]{2,1,0:T(8,128)(2,1)S(1)} %get-tuple-element.100), channel_id=1, source_target_pairs={{0,2},{1,3},{2,0},{3,1},{4,6},{5,7},{6,4},{7,5},{8,10},{9,11},{10,... | collective-permute-start | bytes 430088 | tf_op jit(solution)/shard_map/ppermute | solution.py:359
  54.1 6.0 %collective-permute-start.11 = (bf16[1,40,1792]{2,1,0:T(8,128)(2,1)S(1)}, bf16[1,40,1792]{2,1,0:T(8,128)(2,1)S(1)}, u32[]{:S(2)}, u32[]{:S(2)}) collective-permute-start(bf16[1,40,1792]{2,1,0:T(8,128)(2,1)S(1)} %get-tuple-element.104), channel_id=1, source_target_pairs={{0,3},{1,0},{2,1},{3,2},{4,7},{5,4},{6,5},{7,6},{8,11},{9,8},{10,9... | collective-permute-start | bytes 430088 | tf_op jit(solution)/shard_map/ppermute | solution.py:359
  60.1 2.9 %copy-start = (bf16[256,192]{1,0:T(8,128)(2,1)S(1)}, bf16[256,192]{1,0:T(8,128)(2,1)}, u32[]{:S(2)}) copy-start(bf16[256,192]{1,0:T(8,128)(2,1)} %constant.8.clone.refs_2_) | copy-start | bytes 294916
  60.2 2.9 %copy-start.1 = (bf16[192,256]{1,0:T(8,128)(2,1)S(1)}, bf16[192,256]{1,0:T(8,128)(2,1)}, u32[]{:S(2)}) copy-start(bf16[192,256]{1,0:T(8,128)(2,1)} %constant.9.clone.refs_3_) | copy-start | bytes 294916
  60.2 2.9 %collective-permute-start.18 = (bf16[8,40,1792]{2,1,0:T(8,128)(2,1)S(1)}, bf16[8,40,1792]{2,1,0:T(8,128)(2,1)S(1)}, u32[]{:S(2)}, u32[]{:S(2)}) collective-permute-start(bf16[8,40,1792]{2,1,0:T(8,128)(2,1)S(1)} %constant_dynamic-update-slice_fusion.14.refs_0_), channel_id=1, source_target_pairs={{0,4},{4,0},{8,12},{12,8},{1,5},{5,1},{9,13},{13,9},{2,6},{6,2},{1... | collective-permute-start | bytes 3440648 | tf_op jit(solution)/shard_map/ppermute | solution.py:355
  60.3 13.5 %collective-permute-start.16 = (bf16[8,40,1792]{2,1,0:T(8,128)(2,1)S(1)}, bf16[8,40,1792]{2,1,0:T(8,128)(2,1)S(1)}, u32[]{:S(2)}, u32[]{:S(2)}) collective-permute-start(bf16[8,40,1792]{2,1,0:T(8,128)(2,1)S(1)} %constant_dynamic-update-slice_fusion.3.refs_0_), channel_id=1, source_target_pairs={{0,4},{4,0},{8,12},{12,8},{1,5},{5,1},{9,13},{13,9},{2,6},{6,2},{1... | collective-permute-start | bytes 3440648 | tf_op jit(solution)/shard_map/ppermute | solution.py:355
  60.9 12.7 %collective-permute-start.15 = (bf16[3,40,1792]{2,1,0:T(8,128)(2,1)S(1)}, bf16[3,40,1792]{2,1,0:T(8,128)(2,1)S(1)}, u32[]{:S(2)}, u32[]{:S(2)}) collective-permute-start(bf16[3,40,1792]{2,1,0:T(8,128)(2,1)S(1)} %get-tuple-element.170), channel_id=1, source_target_pairs={{0,8},{4,12},{8,0},{12,4},{1,9},{5,13},{9,1},{13,5},{2,10},{6,14},... | collective-permute-start | bytes 1290248 | tf_op jit(solution)/shard_map/ppermute | solution.py:355
  73.7 12.7 %collective-permute-start.19 = (bf16[8,40,1792]{2,1,0:T(8,128)(2,1)S(1)}, bf16[8,40,1792]{2,1,0:T(8,128)(2,1)S(1)}, u32[]{:S(2)}, u32[]{:S(2)}) collective-permute-start(bf16[8,40,1792]{2,1,0:T(8,128)(2,1)S(1)} %constant_dynamic-update-slice_fusion.18.refs_0_), channel_id=1, source_target_pairs={{0,4},{4,0},{8,12},{12,8},{1,5},{5,1},{9,13},{13,9},{2,6},{6,2},{1... | collective-permute-start | bytes 3440648 | tf_op jit(solution)/shard_map/ppermute | solution.py:355
  73.9 12.5 %collective-permute-start.20 = (bf16[8,40,1792]{2,1,0:T(8,128)(2,1)S(1)}, bf16[8,40,1792]{2,1,0:T(8,128)(2,1)S(1)}, u32[]{:S(2)}, u32[]{:S(2)}) collective-permute-start(bf16[8,40,1792]{2,1,0:T(8,128)(2,1)S(1)} %get-tuple-element.114), channel_id=1, source_target_pairs={{0,4},{4,0},{8,12},{12,8},{1,5},{5,1},{9,13},{13,9},{2,6},{6,2},{1... | collective-permute-start | bytes 3440648 | tf_op jit(solution)/shard_map/ppermute | solution.py:355
  74.2 12.0 %collective-permute-start.13 = (bf16[3,40,1792]{2,1,0:T(8,128)(2,1)S(1)}, bf16[3,40,1792]{2,1,0:T(8,128)(2,1)S(1)}, u32[]{:S(2)}, u32[]{:S(2)}) collective-permute-start(bf16[3,40,1792]{2,1,0:T(8,128)(2,1)S(1)} %get-tuple-element.175), channel_id=1, source_target_pairs={{0,8},{4,12},{8,0},{12,4},{1,9},{5,13},{9,1},{13,5},{2,10},{6,14},... | collective-permute-start | bytes 1290248 | tf_op jit(solution)/shard_map/ppermute | solution.py:355
  86.3 13.1 %collective-permute-start.23 = (bf16[8,40,1792]{2,1,0:T(8,128)(2,1)S(1)}, bf16[8,40,1792]{2,1,0:T(8,128)(2,1)S(1)}, u32[]{:S(2)}, u32[]{:S(2)}) collective-permute-start(bf16[8,40,1792]{2,1,0:T(8,128)(2,1)S(1)} %constant_dynamic-update-slice_fusion.10.refs_0_), channel_id=1, source_target_pairs={{0,4},{4,0},{8,12},{12,8},{1,5},{5,1},{9,13},{13,9},{2,6},{6,2},{1... | collective-permute-start | bytes 3440648 | tf_op jit(solution)/shard_map/ppermute | solution.py:355
  86.4 15.8 %collective-permute-start.21 = (bf16[8,40,1792]{2,1,0:T(8,128)(2,1)S(1)}, bf16[8,40,1792]{2,1,0:T(8,128)(2,1)S(1)}, u32[]{:S(2)}, u32[]{:S(2)}) collective-permute-start(bf16[8,40,1792]{2,1,0:T(8,128)(2,1)S(1)} %get-tuple-element.115), channel_id=1, source_target_pairs={{0,4},{4,0},{8,12},{12,8},{1,5},{5,1},{9,13},{13,9},{2,6},{6,2},{1... | collective-permute-start | bytes 3440648 | tf_op jit(solution)/shard_map/ppermute | solution.py:355
  87.2 15.0 %collective-permute-start.22 = (bf16[4,40,1792]{2,1,0:T(8,128)(2,1)S(1)}, bf16[4,40,1792]{2,1,0:T(8,128)(2,1)S(1)}, u32[]{:S(2)}, u32[]{:S(2)}) collective-permute-start(bf16[4,40,1792]{2,1,0:T(8,128)(2,1)S(1)} %get-tuple-element.119), channel_id=1, source_target_pairs={{0,8},{4,12},{8,0},{12,4},{1,9},{5,13},{9,1},{13,5},{2,10},{6,14},... | collective-permute-start | bytes 1720328 | tf_op jit(solution)/shard_map/ppermute | solution.py:355
  102.2 17.1 %collective-permute-start.24 = (bf16[8,40,1792]{2,1,0:T(8,128)(2,1)S(1)}, bf16[8,40,1792]{2,1,0:T(8,128)(2,1)S(1)}, u32[]{:S(2)}, u32[]{:S(2)}) collective-permute-start(bf16[8,40,1792]{2,1,0:T(8,128)(2,1)S(1)} %get-tuple-element.129), channel_id=1, source_target_pairs={{0,4},{4,0},{8,12},{12,8},{1,5},{5,1},{9,13},{13,9},{2,6},{6,2},{1... | collective-permute-start | bytes 3440648 | tf_op jit(solution)/shard_map/ppermute | solution.py:355
  102.5 16.9 %collective-permute-start.25 = (bf16[4,40,1792]{2,1,0:T(8,128)(2,1)S(1)}, bf16[4,40,1792]{2,1,0:T(8,128)(2,1)S(1)}, u32[]{:S(2)}, u32[]{:S(2)}) collective-permute-start(bf16[4,40,1792]{2,1,0:T(8,128)(2,1)S(1)} %get-tuple-element.116), channel_id=1, source_target_pairs={{0,8},{4,12},{8,0},{12,4},{1,9},{5,13},{9,1},{13,5},{2,10},{6,14},... | collective-permute-start | bytes 1720328 | tf_op jit(solution)/shard_map/ppermute | solution.py:355
  104.1 15.2 %collective-permute-start.26 = (bf16[1,40,1792]{2,1,0:T(8,128)(2,1)S(1)}, bf16[1,40,1792]{2,1,0:T(8,128)(2,1)S(1)}, u32[]{:S(2)}, u32[]{:S(2)}) collective-permute-start(bf16[1,40,1792]{2,1,0:T(8,128)(2,1)S(1)} %get-tuple-element.130), channel_id=1, source_target_pairs={{0,2},{1,3},{2,0},{3,1},{4,6},{5,7},{6,4},{7,5},{8,10},{9,11},{10,... | collective-permute-start | bytes 430088 | tf_op jit(solution)/shard_map/ppermute | solution.py:359
  105.2 14.1 %collective-permute-start.27 = (bf16[1,40,1792]{2,1,0:T(8,128)(2,1)S(1)}, bf16[1,40,1792]{2,1,0:T(8,128)(2,1)S(1)}, u32[]{:S(2)}, u32[]{:S(2)}) collective-permute-start(bf16[1,40,1792]{2,1,0:T(8,128)(2,1)S(1)} %get-tuple-element.131), channel_id=1, source_target_pairs={{0,3},{1,0},{2,1},{3,2},{4,7},{5,4},{6,5},{7,6},{8,11},{9,8},{10,9... | collective-permute-start | bytes 430088 | tf_op jit(solution)/shard_map/ppermute | solution.py:359
  108.6 10.7 %collective-permute-start.28 = (bf16[1,40,1792]{2,1,0:T(8,128)(2,1)S(1)}, bf16[1,40,1792]{2,1,0:T(8,128)(2,1)S(1)}, u32[]{:S(2)}, u32[]{:S(2)}) collective-permute-start(bf16[1,40,1792]{2,1,0:T(8,128)(2,1)S(1)} %get-tuple-element.132), channel_id=1, source_target_pairs={{0,1},{1,2},{2,3},{3,0},{4,5},{5,6},{6,7},{7,4},{8,9},{9,10},{10,1... | collective-permute-start | bytes 430088 | tf_op jit(solution)/shard_map/ppermute | solution.py:359
  119.4 2.9 %collective-permute-start.29 = (bf16[8,40,1792]{2,1,0:T(8,128)(2,1)S(1)}, bf16[8,40,1792]{2,1,0:T(8,128)(2,1)S(1)}, u32[]{:S(2)}, u32[]{:S(2)}) collective-permute-start(bf16[8,40,1792]{2,1,0:T(8,128)(2,1)S(1)} %get-tuple-element.133), channel_id=1, source_target_pairs={{0,4},{4,0},{8,12},{12,8},{1,5},{5,1},{9,13},{13,9},{2,6},{6,2},{1... | collective-permute-start | bytes 3440648 | tf_op jit(solution)/shard_map/ppermute | solution.py:355
  119.7 15.8 %collective-permute-start.32 = (bf16[4,40,1792]{2,1,0:T(8,128)(2,1)S(1)}, bf16[4,40,1792]{2,1,0:T(8,128)(2,1)S(1)}, u32[]{:S(2)}, u32[]{:S(2)}) collective-permute-start(bf16[4,40,1792]{2,1,0:T(8,128)(2,1)S(1)} %get-tuple-element.143), channel_id=1, source_target_pairs={{0,8},{4,12},{8,0},{12,4},{1,9},{5,13},{9,1},{13,5},{2,10},{6,14},... | collective-permute-start | bytes 1720328 | tf_op jit(solution)/shard_map/ppermute | solution.py:355
  122.5 24.9 %collective-permute-start.30 = (bf16[4,40,1792]{2,1,0:T(8,128)(2,1)S(1)}, bf16[4,40,1792]{2,1,0:T(8,128)(2,1)S(1)}, u32[]{:S(2)}, u32[]{:S(2)}) collective-permute-start(bf16[4,40,1792]{2,1,0:T(8,128)(2,1)S(1)} %get-tuple-element.135), channel_id=1, source_target_pairs={{0,8},{4,12},{8,0},{12,4},{1,9},{5,13},{9,1},{13,5},{2,10},{6,14},... | collective-permute-start | bytes 1720328 | tf_op jit(solution)/shard_map/ppermute | solution.py:355
  123.3 12.4 %collective-permute-start.33 = (bf16[1,40,1792]{2,1,0:T(8,128)(2,1)S(1)}, bf16[1,40,1792]{2,1,0:T(8,128)(2,1)S(1)}, u32[]{:S(2)}, u32[]{:S(2)}) collective-permute-start(bf16[1,40,1792]{2,1,0:T(8,128)(2,1)S(1)} %get-tuple-element.146), channel_id=1, source_target_pairs={{0,2},{1,3},{2,0},{3,1},{4,6},{5,7},{6,4},{7,5},{8,10},{9,11},{10,... | collective-permute-start | bytes 430088 | tf_op jit(solution)/shard_map/ppermute | solution.py:359
  125.3 12.4 %collective-permute-start.35 = (bf16[1,40,1792]{2,1,0:T(8,128)(2,1)S(1)}, bf16[1,40,1792]{2,1,0:T(8,128)(2,1)S(1)}, u32[]{:S(2)}, u32[]{:S(2)}) collective-permute-start(bf16[1,40,1792]{2,1,0:T(8,128)(2,1)S(1)} %get-tuple-element.150), channel_id=1, source_target_pairs={{0,3},{1,0},{2,1},{3,2},{4,7},{5,4},{6,5},{7,6},{8,11},{9,8},{10,9... | collective-permute-start | bytes 430088 | tf_op jit(solution)/shard_map/ppermute | solution.py:359
  127.3 12.4 %collective-permute-start.31 = (bf16[1,40,1792]{2,1,0:T(8,128)(2,1)S(1)}, bf16[1,40,1792]{2,1,0:T(8,128)(2,1)S(1)}, u32[]{:S(2)}, u32[]{:S(2)}) collective-permute-start(bf16[1,40,1792]{2,1,0:T(8,128)(2,1)S(1)} %get-tuple-element.140), channel_id=1, source_target_pairs={{0,1},{1,2},{2,3},{3,0},{4,5},{5,6},{6,7},{7,4},{8,9},{9,10},{10,1... | collective-permute-start | bytes 430088 | tf_op jit(solution)/shard_map/ppermute | solution.py:359
  135.5 17.8 %copy-start.4 = (s32[64,2]{0,1:T(2,128)S(1)}, s32[64,2]{0,1:T(2,128)}, u32[]{:S(2)}) copy-start(s32[64,2]{0,1:T(2,128)} %param.9) | copy-start | bytes 1540
  135.6 17.8 %copy-start.5 = (f32[64,2]{0,1:T(2,128)S(1)}, f32[64,2]{0,1:T(2,128)}, u32[]{:S(2)}) copy-start(f32[64,2]{0,1:T(2,128)} %param.10) | copy-start | bytes 1540
  135.7 13.4 %collective-permute-start.34 = (bf16[1,40,1792]{2,1,0:T(8,128)(2,1)S(1)}, bf16[1,40,1792]{2,1,0:T(8,128)(2,1)S(1)}, u32[]{:S(2)}, u32[]{:S(2)}) collective-permute-start(bf16[1,40,1792]{2,1,0:T(8,128)(2,1)S(1)} %get-tuple-element.147), channel_id=1, source_target_pairs={{0,2},{1,3},{2,0},{3,1},{4,6},{5,7},{6,4},{7,5},{8,10},{9,11},{10,... | collective-permute-start | bytes 430088 | tf_op jit(solution)/shard_map/ppermute | solution.py:359
  137.7 11.5 %collective-permute-start.36 = (bf16[1,40,1792]{2,1,0:T(8,128)(2,1)S(1)}, bf16[1,40,1792]{2,1,0:T(8,128)(2,1)S(1)}, u32[]{:S(2)}, u32[]{:S(2)}) collective-permute-start(bf16[1,40,1792]{2,1,0:T(8,128)(2,1)S(1)} %get-tuple-element.151), channel_id=1, source_target_pairs={{0,3},{1,0},{2,1},{3,2},{4,7},{5,4},{6,5},{7,6},{8,11},{9,8},{10,9... | collective-permute-start | bytes 430088 | tf_op jit(solution)/shard_map/ppermute | solution.py:359
  139.7 13.7 %collective-permute-start.39 = (bf16[1,40,1792]{2,1,0:T(8,128)(2,1)S(1)}, bf16[1,40,1792]{2,1,0:T(8,128)(2,1)S(1)}, u32[]{:S(2)}, u32[]{:S(2)}) collective-permute-start(bf16[1,40,1792]{2,1,0:T(8,128)(2,1)S(1)} %get-tuple-element.157), channel_id=1, source_target_pairs={{0,1},{1,2},{2,3},{3,0},{4,5},{5,6},{6,7},{7,4},{8,9},{9,10},{10,1... | collective-permute-start | bytes 430088 | tf_op jit(solution)/shard_map/ppermute | solution.py:359
  149.1 6.9 %collective-permute-start.37 = (bf16[1,40,1792]{2,1,0:T(8,128)(2,1)S(1)}, bf16[1,40,1792]{2,1,0:T(8,128)(2,1)S(1)}, u32[]{:S(2)}, u32[]{:S(2)}) collective-permute-start(bf16[1,40,1792]{2,1,0:T(8,128)(2,1)S(1)} %get-tuple-element.152), channel_id=1, source_target_pairs={{0,3},{1,0},{2,1},{3,2},{4,7},{5,4},{6,5},{7,6},{8,11},{9,8},{10,9... | collective-permute-start | bytes 430088 | tf_op jit(solution)/shard_map/ppermute | solution.py:359
  151.5 14.0 %collective-permute-start.38 = (bf16[1,40,1792]{2,1,0:T(8,128)(2,1)S(1)}, bf16[1,40,1792]{2,1,0:T(8,128)(2,1)S(1)}, u32[]{:S(2)}, u32[]{:S(2)}) collective-permute-start(bf16[1,40,1792]{2,1,0:T(8,128)(2,1)S(1)} %get-tuple-element.154), channel_id=1, source_target_pairs={{0,2},{1,3},{2,0},{3,1},{4,6},{5,7},{6,4},{7,5},{8,10},{9,11},{10,... | collective-permute-start | bytes 430088 | tf_op jit(solution)/shard_map/ppermute | solution.py:359
  153.4 12.1 %collective-permute-start.40 = (bf16[1,40,1792]{2,1,0:T(8,128)(2,1)S(1)}, bf16[1,40,1792]{2,1,0:T(8,128)(2,1)S(1)}, u32[]{:S(2)}, u32[]{:S(2)}) collective-permute-start(bf16[1,40,1792]{2,1,0:T(8,128)(2,1)S(1)} %get-tuple-element.158), channel_id=1, source_target_pairs={{0,1},{1,2},{2,3},{3,0},{4,5},{5,6},{6,7},{7,4},{8,9},{9,10},{10,1... | collective-permute-start | bytes 430088 | tf_op jit(solution)/shard_map/ppermute | solution.py:359

commit v5 on v4

--- a/solution.py
+++ b/solution.py
@@ -12,6 +12,8 @@
 CAP = 5
 GROUPS = 4
 WINDOW = 3
+AHEAD = 3
+LAG = 2
 MIB = 1024 * 1024
 F32, BF16 = jnp.float32, jnp.bfloat16
 
@@ -384,48 +386,58 @@
         return done[-WINDOW - 2 : len(done) - WINDOW + 1] if len(done) >= WINDOW else []
 
     far = swap(own, 2, 4)
-    came = {}
+    came, stacks, across = {}, [], []
+
+    def bring(*after):
+        g = len(stacks)
+        for s in order:
+            came[g, s] = shift(tie(sent[g][s - 1], *recent(), *after), s, count)
+            done.append(came[g, s])
+        stacks.append(concat(*[came[g, s] for s in blocks]))
+        across.append(swap(stacks[g], 2, 4))
+
+    def pair_up(g, *after):
+        a = tie(across[g], *after)
+        pair = concat(own[g : g + 1], stacks[g], far[g : g + 1], a)
+        return pair, swap(pair, 1, 4)
+
+    def arrived(g, some):
+        return [came[g, s] for s in some if (g, s) in came]
+
+    for _ in range(min(AHEAD, z.groups)):
+        bring()
+    pair, beside = pair_up(0, *arrived(1, blocks))
+    while len(stacks) < z.groups:
+        bring(beside)
+    keep, away, summed, parts, back = [], [], [], [], []
+
+    def bring_back():
+        k = len(parts)
+        parts.append(add_cut(keep[k], summed[k], [(s, s + 1) for s in range(count)]))
+        back.append({})
+        for s in order:
+            back[k][s] = shift(tie(parts[k][s], *recent()), -s, count)
+            done.append(back[k][s])
+
     for g in range(z.groups):
-        for s in order:
-            came[g, s] = shift(tie(sent[g][s - 1], *recent()), s, count)
-            done.append(came[g, s])
-    stacks = [concat(*[came[g, s] for s in blocks]) for g in range(z.groups)]
-    across = [swap(stack, 2, 4) for stack in stacks]
-    pairs, beside = [], []
-
-    def pair_up(*after):
-        g = len(pairs)
-        if g < z.groups:
-            next_ones = [came[g + 1, s] for s in blocks] if g + 1 < z.groups else []
-            a = tie(across[g], *next_ones, *after)
-            pairs.append(concat(own[g : g + 1], stacks[g], far[g : g + 1], a))
-            beside.append(swap(pairs[g], 1, 4))
-
-    pair_up()
-    pair_up()
-    returned, away, summed, parts, back = [], [], [], [], []
-    for g in range(z.groups):
-        before = stacks[g + 2 : g + 3] + across[g + 1 : g + 2]
-        before += away[g - 2 : g - 1] if g >= 2 else []
-        before += parts[g - 3] if g >= 3 else []
-        pieces = [(tie(pairs[g], *before), [(m, s) for m in (0, 2) for s in range(count)])]
-        pieces.append((beside[g], [(m, s) for m in (1, 3) for s in range(count)]))
+        before = stacks[g + 2 : g + 3] + away[-1:] + list(parts[-1] if parts else ())
+        pieces = [(tie(pair, *before), [(m, s) for m in (0, 2) for s in range(count)])]
+        pieces.append((beside, [(m, s) for m in (1, 3) for s in range(count)]))
         send, kept = expert_group(z, g, pieces, *matrices, *weights, [[1, 3], [0, 2]])
-        pair_up(send)
-        beside_it = [came[g + 3, s] for s in blocks] if g + 3 < z.groups else []
-        beside_it += across[g + 2 : g + 3] + beside[g + 1 : g + 2]
-        beside_it += returned[g - 1 : g] if g >= 1 else []
-        beside_it += summed[g - 2 : g - 1] if g >= 2 else []
-        beside_it += list(back[g - 3].values()) if g >= 3 else []
-        returned.append(swap(tie(send, *beside_it), 1, 4))
-        keep, a = add_cut(kept, returned[g], [(0, count), (count, 2 * count)])
+        if g + 1 < z.groups:
+            pair, beside = pair_up(g + 1, send)
+        beside_it = across[g + 1 : g + 3] if g == 0 else across[g + 2 : g + 3]
+        beside_it += [back[-1][s] for s in order] if back else []
+        if g >= LAG:
+            beside_it.append(summed[g - LAG])
+            bring_back()
+        got = swap(tie(send, *beside_it), 1, 4)
+        k, a = add_cut(kept, got, [(0, count), (count, 2 * count)])
+        keep.append(k)
         away.append(a)
         summed.append(swap(a, 2, 4))
-        parts.append(add_cut(keep, summed[g], [(s, s + 1) for s in range(count)]))
-        back.append({})
-        for s in order:
-            back[g][s] = shift(tie(parts[g][s], *recent()), -s, count)
-            done.append(back[g][s])
+    while len(parts) < z.groups:
+        bring_back()
     for g in range(z.groups):
         result = combine_group(z, g, weight, [parts[g][0]] + [back[g][s] for s in blocks], result)
     return result

time: 167 us -> 162 us (0.970)
  waiting for transfers between devices: 52.8 us -> 42.4 us
  starting transfers between devices: 60.7 us -> 65.6 us
    ppermute x24, waiting for transfers between devices: 36.3 us -> 25.5 us  [shift(): lax.ppermute(a, 'local', [(i, (i + by) % count) for i in range(count)])]
    ppermute x24, starting transfers between devices: 47.1 us -> 54 us  [shift(): lax.ppermute(a, 'local', [(i, (i + by) % count) for i in range(count)])]
    ppermute x17, starting transfers between devices: 13.7 us -> 11.6 us  [swap(): return lax.ppermute(a, 'node', [(i, i ^ mask) for i in range(count)])]
  transfers between devices with their start and end apart: 41 -> 41, of which waited for: 14 -> 15; matrix products, arithmetic and copies ran while one was open for 0% -> 0% of each run, Pallas kernels for 28% -> 29%
where the time goes in v5:
time: 162 us; the launch traced here: 161 us
  starting transfers between devices  65.6 us (40%)
  Pallas kernels  50.7 us (31%)
  waiting for transfers between devices  42.4 us (26%)
  local copies, waits for them, and re-layouts  2.27 us (1%)
    ppermute x24, starting transfers between devices, shift(): lax.ppermute(a, 'local', [(i, (i + by) % count) for i in range(count)])  54 us
    pallas_call x4, Pallas kernels, expert_group(): pl.pallas_call(functools.partial(expert_kernel, z, group, places, order),...  42.5 us
    ppermute x24, waiting for transfers between devices, shift(): lax.ppermute(a, 'local', [(i, (i + by) % count) for i in range(count)])  25.5 us
    ppermute x17, waiting for transfers between devices, swap(): return lax.ppermute(a, 'node', [(i, i ^ mask) for i in range(count)])  16.9 us
    ppermute x17, starting transfers between devices, swap(): return lax.ppermute(a, 'node', [(i, i ^ mask) for i in range(count)])  11.6 us
    pallas_call x4, Pallas kernels, combine_group(): pl.pallas_call(functools.partial(combine_kernel, z, group, [p.shape[0] fo...  3.47 us
  transfers between devices with their start and end apart: 41, of which 15 were waited for; matrix products, arithmetic and copies ran while one was open for 0% of the time, Pallas kernels for 29%

profile of v5, /device:TPU:0, one launch (start us, length us, event | category | flops | bytes accessed | tf_op | source)
XLA Modules:
  0.0 161.5 jit_solution(14901029842985581537)
XLA Ops:
  0.0 1.2 copy-done.2
  1.2 0.7 copy-done.3
  1.9 2.5 %gather_rows.1 = (bf16[4,40,1792]{2,1,0:T(8,128)(2,1)S(1)}, bf16[1,40,1792]{2,1,0:T(8,128)(2,1)S(1)}, bf16[1,40,1792]{2,1,0:T(8,128)(2,1)S(1)}, bf16[1,40,1792]{...) custom-call(s32[1]{0:T(128)} %bitcast.plane_ref, ...), custom_call_target="tpu_custom_call" | custom-call | tf_op jit(solution)/shard_map/gather_rows/pallas_call | solution.py:148
  4.3 4.1 %collective-permute-start = (bf16[1,40,1792]{2,1,0:T(8,128)(2,1)S(1)}, bf16[1,40,1792]{2,1,0:T(8,128)(2,1)S(1)}, u32[]{:S(2)}, u32[]{:S(2)}) collective-permute-start(bf16[1,40,1792]{2,1,0:T(8,128)(2,1)S(1)} %get-tuple-element.86), channel_id=1, source_target_pairs={{0,2},{1,3},{2,0},{3,1},{4,6},{5,7},{6,4},{7,5},{8,10},{9,11},{10,... | collective-permute-start | bytes 430088 | tf_op jit(solution)/shard_map/ppermute | solution.py:361
  8.4 1.6 collective-permute-start.1
  10.0 2.2 %collective-permute-start.2 = (bf16[1,40,1792]{2,1,0:T(8,128)(2,1)S(1)}, bf16[1,40,1792]{2,1,0:T(8,128)(2,1)S(1)}, u32[]{:S(2)}, u32[]{:S(2)}) collective-permute-start(bf16[1,40,1792]{2,1,0:T(8,128)(2,1)S(1)} %get-tuple-element.88), channel_id=1, source_target_pairs={{0,3},{1,0},{2,1},{3,2},{4,7},{5,4},{6,5},{7,6},{8,11},{9,8},{10,9... | collective-permute-start | bytes 430088 | tf_op jit(solution)/shard_map/ppermute | solution.py:361
  12.3 1.5 collective-permute-start.8
  13.8 5.4 %collective-permute-done = bf16[1,40,1792]{2,1,0:T(8,128)(2,1)S(1)} collective-permute-done((bf16[1,40,1792]{2,1,0:T(8,128)(2,1)S(1)}, bf16[1,40,1792]{2,1,0:T(8,128)(2,1)S(1)}, u32[]{:S(2)}, u32[]{:S(2)}) %collective-permute-start) | collective-permute-done | bytes 143392 | tf_op jit(solution)/shard_map/ppermute | solution.py:361
  19.2 2.9 %collective-permute-start.6 = (bf16[1,40,1792]{2,1,0:T(8,128)(2,1)S(1)}, bf16[1,40,1792]{2,1,0:T(8,128)(2,1)S(1)}, u32[]{:S(2)}, u32[]{:S(2)}) collective-permute-start(bf16[1,40,1792]{2,1,0:T(8,128)(2,1)S(1)} %get-tuple-element.96), channel_id=1, source_target_pairs={{0,1},{1,2},{2,3},{3,0},{4,5},{5,6},{6,7},{7,4},{8,9},{9,10},{10,1... | collective-permute-start | bytes 430088 | tf_op jit(solution)/shard_map/ppermute | solution.py:361
  22.1 1.9 %collective-permute-start.4 = (bf16[1,40,1792]{2,1,0:T(8,128)(2,1)S(1)}, bf16[1,40,1792]{2,1,0:T(8,128)(2,1)S(1)}, u32[]{:S(2)}, u32[]{:S(2)}) collective-permute-start(bf16[1,40,1792]{2,1,0:T(8,128)(2,1)S(1)} %get-tuple-element.92), channel_id=1, source_target_pairs={{0,2},{1,3},{2,0},{3,1},{4,6},{5,7},{6,4},{7,5},{8,10},{9,11},{10,... | collective-permute-start | bytes 430088 | tf_op jit(solution)/shard_map/ppermute | solution.py:361
  24.1 2.9 %collective-permute-start.3 = (bf16[1,40,1792]{2,1,0:T(8,128)(2,1)S(1)}, bf16[1,40,1792]{2,1,0:T(8,128)(2,1)S(1)}, u32[]{:S(2)}, u32[]{:S(2)}) collective-permute-start(bf16[1,40,1792]{2,1,0:T(8,128)(2,1)S(1)} %get-tuple-element.89), channel_id=1, source_target_pairs={{0,3},{1,0},{2,1},{3,2},{4,7},{5,4},{6,5},{7,6},{8,11},{9,8},{10,9... | collective-permute-start | bytes 430088 | tf_op jit(solution)/shard_map/ppermute | solution.py:361
  27.0 1.6 collective-permute-start.9
  28.7 4.1 %collective-permute-done.4 = bf16[1,40,1792]{2,1,0:T(8,128)(2,1)S(1)} collective-permute-done((bf16[1,40,1792]{2,1,0:T(8,128)(2,1)S(1)}, bf16[1,40,1792]{2,1,0:T(8,128)(2,1)S(1)}, u32[]{:S(2)}, u32[]{:S(2)}) %collective-permute-start.4) | collective-permute-done | bytes 143392 | tf_op jit(solution)/shard_map/ppermute | solution.py:361
  32.8 4.6 %collective-permute-start.7 = (bf16[1,40,1792]{2,1,0:T(8,128)(2,1)S(1)}, bf16[1,40,1792]{2,1,0:T(8,128)(2,1)S(1)}, u32[]{:S(2)}, u32[]{:S(2)}) collective-permute-start(bf16[1,40,1792]{2,1,0:T(8,128)(2,1)S(1)} %get-tuple-element.97), channel_id=1, source_target_pairs={{0,1},{1,2},{2,3},{3,0},{4,5},{5,6},{6,7},{7,4},{8,9},{9,10},{10,1... | collective-permute-start | bytes 430088 | tf_op jit(solution)/shard_map/ppermute | solution.py:361
  37.4 3.4 %collective-permute-start.5 = (bf16[1,40,1792]{2,1,0:T(8,128)(2,1)S(1)}, bf16[1,40,1792]{2,1,0:T(8,128)(2,1)S(1)}, u32[]{:S(2)}, u32[]{:S(2)}) collective-permute-start(bf16[1,40,1792]{2,1,0:T(8,128)(2,1)S(1)} %get-tuple-element.93), channel_id=1, source_target_pairs={{0,2},{1,3},{2,0},{3,1},{4,6},{5,7},{6,4},{7,5},{8,10},{9,11},{10,... | collective-permute-start | bytes 430088 | tf_op jit(solution)/shard_map/ppermute | solution.py:361
  40.9 1.6 collective-permute-start.17
  42.6 2.4 %collective-permute-done.7 = bf16[1,40,1792]{2,1,0:T(8,128)(2,1)S(1)} collective-permute-done((bf16[1,40,1792]{2,1,0:T(8,128)(2,1)S(1)}, bf16[1,40,1792]{2,1,0:T(8,128)(2,1)S(1)}, u32[]{:S(2)}, u32[]{:S(2)}) %collective-permute-start.7) | collective-permute-done | bytes 143392 | tf_op jit(solution)/shard_map/ppermute | solution.py:361
  45.1 4.1 %collective-permute-done.5 = bf16[1,40,1792]{2,1,0:T(8,128)(2,1)S(1)} collective-permute-done((bf16[1,40,1792]{2,1,0:T(8,128)(2,1)S(1)}, bf16[1,40,1792]{2,1,0:T(8,128)(2,1)S(1)}, u32[]{:S(2)}, u32[]{:S(2)}) %collective-permute-start.5) | collective-permute-done | bytes 143392 | tf_op jit(solution)/shard_map/ppermute | solution.py:361
  49.3 1.6 collective-permute-start.16
  50.8 3.6 %collective-permute-start.11 = (bf16[1,40,1792]{2,1,0:T(8,128)(2,1)S(1)}, bf16[1,40,1792]{2,1,0:T(8,128)(2,1)S(1)}, u32[]{:S(2)}, u32[]{:S(2)}) collective-permute-start(bf16[1,40,1792]{2,1,0:T(8,128)(2,1)S(1)} %get-tuple-element.99), channel_id=1, source_target_pairs={{0,1},{1,2},{2,3},{3,0},{4,5},{5,6},{6,7},{7,4},{8,9},{9,10},{10,1... | collective-permute-start | bytes 430088 | tf_op jit(solution)/shard_map/ppermute | solution.py:361
  54.4 2.4 %collective-permute-start.14 = (bf16[1,40,1792]{2,1,0:T(8,128)(2,1)S(1)}, bf16[1,40,1792]{2,1,0:T(8,128)(2,1)S(1)}, u32[]{:S(2)}, u32[]{:S(2)}) collective-permute-start(bf16[1,40,1792]{2,1,0:T(8,128)(2,1)S(1)} %get-tuple-element.105), channel_id=1, source_target_pairs={{0,3},{1,0},{2,1},{3,2},{4,7},{5,4},{6,5},{7,6},{8,11},{9,8},{10,9... | collective-permute-start | bytes 430088 | tf_op jit(solution)/shard_map/ppermute | solution.py:361
  56.8 10.5 %expert_group.4 = (bf16[8,40,1792]{2,1,0:T(8,128)(2,1)S(1)}, bf16[8,40,1792]{2,1,0:T(8,128)(2,1)S(1)}) custom-call(bf16[8,40,1792]{2,1,0:T(8,128)(2,1)S(1)} %constant_dynamic-update-slice_fusion.refs_0_, bf16[8,40,1792]{2,1,0:T(8,128)(2,1)S(1)} %collective-permute-done.10.refs_1_, bf16[256,192]{1,0:T(8,128)(2,1)S(1)} %copy-done, ...), custom_call_target="tpu_custom_call" | custom-call | flops 2818572288 | bytes 22020096 | tf_op jit(solution)/shard_map/expert_group/pallas_call | solution.py:277
  67.7 0.5 collective-permute-start.19
  68.2 0.5 collective-permute-start.15
  68.8 1.5 collective-permute-done.18.b_ref
  70.3 0.3 add_cut.8
  70.5 1.4 collective-permute-done.19.refs_1_
  71.9 10.5 %expert_group.5 = (bf16[8,40,1792]{2,1,0:T(8,128)(2,1)S(1)}, bf16[8,40,1792]{2,1,0:T(8,128)(2,1)S(1)}) custom-call(bf16[8,40,1792]{2,1,0:T(8,128)(2,1)S(1)} %constant_dynamic-update-slice_fusion.10.refs_0_, bf16[8,40,1792]{2,1,0:T(8,128)(2,1)S(1)} %collective-permute-done.19.refs_1_, bf16[256,192]{1,0:T(8,128)(2,1)S(1)} %copy-done, ...), custom_call_target="tpu_custom_call" | custom-call | flops 2818572288 | bytes 22020096 | tf_op jit(solution)/shard_map/expert_group/pallas_call | solution.py:277
  82.5 0.2 collective-permute-start.20
  82.7 0.4 collective-permute-start.21
  83.1 0.5 collective-permute-start.22
  83.7 1.7 %collective-permute-done.20.b_ref = bf16[8,40,1792]{2,1,0:T(8,128)(2,1)S(1)} collective-permute-done((bf16[8,40,1792]{2,1,0:T(8,128)(2,1)S(1)}, bf16[8,40,1792]{2,1,0:T(8,128)(2,1)S(1)}, u32[]{:S(2)}, u32[]{:S(2)}) %collective-permute-start.20) | collective-permute-done | bytes 1146912 | tf_op jit(solution)/shard_map/ppermute | solution.py:357
  85.3 0.3 add_cut.9
  85.6 1.4 collective-permute-done.21.refs_1_
  87.0 10.7 %expert_group.6 = (bf16[8,40,1792]{2,1,0:T(8,128)(2,1)S(1)}, bf16[8,40,1792]{2,1,0:T(8,128)(2,1)S(1)}) custom-call(bf16[8,40,1792]{2,1,0:T(8,128)(2,1)S(1)} %constant_dynamic-update-slice_fusion.14.refs_0_, bf16[8,40,1792]{2,1,0:T(8,128)(2,1)S(1)} %collective-permute-done.21.refs_1_, bf16[256,192]{1,0:T(8,128)(2,1)S(1)} %copy-done, ...), custom_call_target="tpu_custom_call" | custom-call | flops 2818572288 | bytes 22020096 | tf_op jit(solution)/shard_map/expert_group/pallas_call | solution.py:277
  97.7 0.4 collective-permute-done.22.b_ref
  98.2 0.6 collective-permute-start.24
  98.8 0.5 collective-permute-start.28
  99.4 0.6 collective-permute-start.25
  100.0 1.5 collective-permute-start.26
  101.5 0.5 collective-permute-start.27
  102.0 0.3 add_cut.10
  102.3 0.3 collective-permute-done.24.refs_1_
  102.6 10.7 %expert_group.7 = (bf16[8,40,1792]{2,1,0:T(8,128)(2,1)S(1)}, bf16[8,40,1792]{2,1,0:T(8,128)(2,1)S(1)}) custom-call(bf16[8,40,1792]{2,1,0:T(8,128)(2,1)S(1)} %constant_dynamic-update-slice_fusion.18.refs_0_, bf16[8,40,1792]{2,1,0:T(8,128)(2,1)S(1)} %collective-permute-done.24.refs_1_, bf16[256,192]{1,0:T(8,128)(2,1)S(1)} %copy-done, ...), custom_call_target="tpu_custom_call" | custom-call | flops 2818572288 | bytes 22020096 | tf_op jit(solution)/shard_map/expert_group/pallas_call | solution.py:277
  113.3 0.4 collective-permute-done.28.b_ref
  113.7 1.0 collective-permute-start.32
  114.7 1.8 %collective-permute-done.29.b_ref = bf16[8,40,1792]{2,1,0:T(8,128)(2,1)S(1)} collective-permute-done((bf16[8,40,1792]{2,1,0:T(8,128)(2,1)S(1)}, bf16[8,40,1792]{2,1,0:T(8,128)(2,1)S(1)}, u32[]{:S(2)}, u32[]{:S(2)}) %collective-permute-start.29) | collective-permute-done | bytes 1146912 | tf_op jit(solution)/shard_map/ppermute | solution.py:357
  116.5 0.3 add_cut.12
  116.8 1.0 collective-permute-start.30
  117.9 2.6 %collective-permute-start.33 = (bf16[1,40,1792]{2,1,0:T(8,128)(2,1)S(1)}, bf16[1,40,1792]{2,1,0:T(8,128)(2,1)S(1)}, u32[]{:S(2)}, u32[]{:S(2)}) collective-permute-start(bf16[1,40,1792]{2,1,0:T(8,128)(2,1)S(1)} %get-tuple-element.146), channel_id=1, source_target_pairs={{0,2},{1,3},{2,0},{3,1},{4,6},{5,7},{6,4},{7,5},{8,10},{9,11},{10,... | collective-permute-start | bytes 430088 | tf_op jit(solution)/shard_map/ppermute | solution.py:361
  120.4 1.9 %collective-permute-start.35 = (bf16[1,40,1792]{2,1,0:T(8,128)(2,1)S(1)}, bf16[1,40,1792]{2,1,0:T(8,128)(2,1)S(1)}, u32[]{:S(2)}, u32[]{:S(2)}) collective-permute-start(bf16[1,40,1792]{2,1,0:T(8,128)(2,1)S(1)} %get-tuple-element.150), channel_id=1, source_target_pairs={{0,3},{1,0},{2,1},{3,2},{4,7},{5,4},{6,5},{7,6},{8,11},{9,8},{10,9... | collective-permute-start | bytes 430088 | tf_op jit(solution)/shard_map/ppermute | solution.py:361
  122.5 7.0 %collective-permute-done.32.b_ref = bf16[4,40,1792]{2,1,0:T(8,128)(2,1)S(1)} collective-permute-done((bf16[4,40,1792]{2,1,0:T(8,128)(2,1)S(1)}, bf16[4,40,1792]{2,1,0:T(8,128)(2,1)S(1)}, u32[]{:S(2)}, u32[]{:S(2)}) %collective-permute-start.32) | collective-permute-done | bytes 573472 | tf_op jit(solution)/shard_map/ppermute | solution.py:357
  129.6 2.0 %collective-permute-start.34 = (bf16[1,40,1792]{2,1,0:T(8,128)(2,1)S(1)}, bf16[1,40,1792]{2,1,0:T(8,128)(2,1)S(1)}, u32[]{:S(2)}, u32[]{:S(2)}) collective-permute-start(bf16[1,40,1792]{2,1,0:T(8,128)(2,1)S(1)} %get-tuple-element.147), channel_id=1, source_target_pairs={{0,2},{1,3},{2,0},{3,1},{4,6},{5,7},{6,4},{7,5},{8,10},{9,11},{10,... | collective-permute-start | bytes 430088 | tf_op jit(solution)/shard_map/ppermute | solution.py:361
  131.7 2.4 %collective-permute-start.36 = (bf16[1,40,1792]{2,1,0:T(8,128)(2,1)S(1)}, bf16[1,40,1792]{2,1,0:T(8,128)(2,1)S(1)}, u32[]{:S(2)}, u32[]{:S(2)}) collective-permute-start(bf16[1,40,1792]{2,1,0:T(8,128)(2,1)S(1)} %get-tuple-element.151), channel_id=1, source_target_pairs={{0,3},{1,0},{2,1},{3,2},{4,7},{5,4},{6,5},{7,6},{8,11},{9,8},{10,9... | collective-permute-start | bytes 430088 | tf_op jit(solution)/shard_map/ppermute | solution.py:361
  134.0 6.4 %collective-permute-start.39 = (bf16[1,40,1792]{2,1,0:T(8,128)(2,1)S(1)}, bf16[1,40,1792]{2,1,0:T(8,128)(2,1)S(1)}, u32[]{:S(2)}, u32[]{:S(2)}) collective-permute-start(bf16[1,40,1792]{2,1,0:T(8,128)(2,1)S(1)} %get-tuple-element.157), channel_id=1, source_target_pairs={{0,1},{1,2},{2,3},{3,0},{4,5},{5,6},{6,7},{7,4},{8,9},{9,10},{10,1... | collective-permute-start | bytes 430088 | tf_op jit(solution)/shard_map/ppermute | solution.py:361
  140.4 1.0 collective-permute-done.30.b_ref
  141.6 4.8 %collective-permute-start.37 = (bf16[1,40,1792]{2,1,0:T(8,128)(2,1)S(1)}, bf16[1,40,1792]{2,1,0:T(8,128)(2,1)S(1)}, u32[]{:S(2)}, u32[]{:S(2)}) collective-permute-start(bf16[1,40,1792]{2,1,0:T(8,128)(2,1)S(1)} %get-tuple-element.152), channel_id=1, source_target_pairs={{0,3},{1,0},{2,1},{3,2},{4,7},{5,4},{6,5},{7,6},{8,11},{9,8},{10,9... | collective-permute-start | bytes 430088 | tf_op jit(solution)/shard_map/ppermute | solution.py:361
  146.3 1.6 collective-permute-start.38
  147.9 0.7 combine_weights.1.weight_ref
  148.6 0.6 combine_group.4.refs_4_
  149.2 0.6 combine_group.5.refs_4_
  149.9 0.6 combine_group.6.refs_4_
  150.5 9.4 %collective-permute-done.38.refs_2_ = bf16[1,40,1792]{2,1,0:T(8,128)(2,1)S(1)} collective-permute-done((bf16[1,40,1792]{2,1,0:T(8,128)(2,1)S(1)}, bf16[1,40,1792]{2,1,0:T(8,128)(2,1)S(1)}, u32[]{:S(2)}, u32[]{:S(2)}) %collective-permute-start.38) | collective-permute-done | bytes 143392 | tf_op jit(solution)/shard_map/ppermute | solution.py:361
  159.9 1.6 combine_group.7
  (69 shorter events, 1.4 us)
Async XLA Ops:
  0.0 1.2 copy-start.2
  1.2 0.7 copy-start.3
  4.3 14.9 %collective-permute-start = (bf16[1,40,1792]{2,1,0:T(8,128)(2,1)S(1)}, bf16[1,40,1792]{2,1,0:T(8,128)(2,1)S(1)}, u32[]{:S(2)}, u32[]{:S(2)}) collective-permute-start(bf16[1,40,1792]{2,1,0:T(8,128)(2,1)S(1)} %get-tuple-element.86), channel_id=1, source_target_pairs={{0,2},{1,3},{2,0},{3,1},{4,6},{5,7},{6,4},{7,5},{8,10},{9,11},{10,... | collective-permute-start | bytes 430088 | tf_op jit(solution)/shard_map/ppermute | solution.py:361
  8.4 10.8 %collective-permute-start.1 = (bf16[1,40,1792]{2,1,0:T(8,128)(2,1)S(1)}, bf16[1,40,1792]{2,1,0:T(8,128)(2,1)S(1)}, u32[]{:S(2)}, u32[]{:S(2)}) collective-permute-start(bf16[1,40,1792]{2,1,0:T(8,128)(2,1)S(1)} %get-tuple-element.87), channel_id=1, source_target_pairs={{0,1},{1,2},{2,3},{3,0},{4,5},{5,6},{6,7},{7,4},{8,9},{9,10},{10,1... | collective-permute-start | bytes 430088 | tf_op jit(solution)/shard_map/ppermute | solution.py:361
  10.0 14.0 %collective-permute-start.2 = (bf16[1,40,1792]{2,1,0:T(8,128)(2,1)S(1)}, bf16[1,40,1792]{2,1,0:T(8,128)(2,1)S(1)}, u32[]{:S(2)}, u32[]{:S(2)}) collective-permute-start(bf16[1,40,1792]{2,1,0:T(8,128)(2,1)S(1)} %get-tuple-element.88), channel_id=1, source_target_pairs={{0,3},{1,0},{2,1},{3,2},{4,7},{5,4},{6,5},{7,6},{8,11},{9,8},{10,9... | collective-permute-start | bytes 430088 | tf_op jit(solution)/shard_map/ppermute | solution.py:361
  12.3 30.2 %collective-permute-start.8 = (bf16[4,40,1792]{2,1,0:T(8,128)(2,1)S(1)}, bf16[4,40,1792]{2,1,0:T(8,128)(2,1)S(1)}, u32[]{:S(2)}, u32[]{:S(2)}) collective-permute-start(bf16[4,40,1792]{2,1,0:T(8,128)(2,1)S(1)} %get-tuple-element.83), channel_id=1, source_target_pairs={{0,8},{4,12},{8,0},{12,4},{1,9},{5,13},{9,1},{13,5},{2,10},{6,14},... | collective-permute-start | bytes 1720328 | tf_op jit(solution)/shard_map/ppermute | solution.py:357
  19.2 9.4 %collective-permute-start.6 = (bf16[1,40,1792]{2,1,0:T(8,128)(2,1)S(1)}, bf16[1,40,1792]{2,1,0:T(8,128)(2,1)S(1)}, u32[]{:S(2)}, u32[]{:S(2)}) collective-permute-start(bf16[1,40,1792]{2,1,0:T(8,128)(2,1)S(1)} %get-tuple-element.96), channel_id=1, source_target_pairs={{0,1},{1,2},{2,3},{3,0},{4,5},{5,6},{6,7},{7,4},{8,9},{9,10},{10,1... | collective-permute-start | bytes 430088 | tf_op jit(solution)/shard_map/ppermute | solution.py:361
  22.1 10.6 %collective-permute-start.4 = (bf16[1,40,1792]{2,1,0:T(8,128)(2,1)S(1)}, bf16[1,40,1792]{2,1,0:T(8,128)(2,1)S(1)}, u32[]{:S(2)}, u32[]{:S(2)}) collective-permute-start(bf16[1,40,1792]{2,1,0:T(8,128)(2,1)S(1)} %get-tuple-element.92), channel_id=1, source_target_pairs={{0,2},{1,3},{2,0},{3,1},{4,6},{5,7},{6,4},{7,5},{8,10},{9,11},{10,... | collective-permute-start | bytes 430088 | tf_op jit(solution)/shard_map/ppermute | solution.py:361
  24.1 16.7 %collective-permute-start.3 = (bf16[1,40,1792]{2,1,0:T(8,128)(2,1)S(1)}, bf16[1,40,1792]{2,1,0:T(8,128)(2,1)S(1)}, u32[]{:S(2)}, u32[]{:S(2)}) collective-permute-start(bf16[1,40,1792]{2,1,0:T(8,128)(2,1)S(1)} %get-tuple-element.89), channel_id=1, source_target_pairs={{0,3},{1,0},{2,1},{3,2},{4,7},{5,4},{6,5},{7,6},{8,11},{9,8},{10,9... | collective-permute-start | bytes 430088 | tf_op jit(solution)/shard_map/ppermute | solution.py:361
  27.0 13.8 %collective-permute-start.9 = (bf16[3,40,1792]{2,1,0:T(8,128)(2,1)S(1)}, bf16[3,40,1792]{2,1,0:T(8,128)(2,1)S(1)}, u32[]{:S(2)}, u32[]{:S(2)}) collective-permute-start(bf16[3,40,1792]{2,1,0:T(8,128)(2,1)S(1)} %pad_maximum_fusion), channel_id=1, source_target_pairs={{0,8},{4,12},{8,0},{12,4},{1,9},{5,13},{9,1},{13,5},{2,10},{6,14},... | collective-permute-start | bytes 1290248 | tf_op jit(solution)/shard_map/ppermute | solution.py:357
  32.8 12.2 %collective-permute-start.7 = (bf16[1,40,1792]{2,1,0:T(8,128)(2,1)S(1)}, bf16[1,40,1792]{2,1,0:T(8,128)(2,1)S(1)}, u32[]{:S(2)}, u32[]{:S(2)}) collective-permute-start(bf16[1,40,1792]{2,1,0:T(8,128)(2,1)S(1)} %get-tuple-element.97), channel_id=1, source_target_pairs={{0,1},{1,2},{2,3},{3,0},{4,5},{5,6},{6,7},{7,4},{8,9},{9,10},{10,1... | collective-permute-start | bytes 430088 | tf_op jit(solution)/shard_map/ppermute | solution.py:361
  37.4 11.8 %collective-permute-start.5 = (bf16[1,40,1792]{2,1,0:T(8,128)(2,1)S(1)}, bf16[1,40,1792]{2,1,0:T(8,128)(2,1)S(1)}, u32[]{:S(2)}, u32[]{:S(2)}) collective-permute-start(bf16[1,40,1792]{2,1,0:T(8,128)(2,1)S(1)} %get-tuple-element.93), channel_id=1, source_target_pairs={{0,2},{1,3},{2,0},{3,1},{4,6},{5,7},{6,4},{7,5},{8,10},{9,11},{10,... | collective-permute-start | bytes 430088 | tf_op jit(solution)/shard_map/ppermute | solution.py:361
  40.8 8.4 %collective-permute-start.13 = (bf16[1,40,1792]{2,1,0:T(8,128)(2,1)S(1)}, bf16[1,40,1792]{2,1,0:T(8,128)(2,1)S(1)}, u32[]{:S(2)}, u32[]{:S(2)}) collective-permute-start(bf16[1,40,1792]{2,1,0:T(8,128)(2,1)S(1)} %get-tuple-element.104), channel_id=1, source_target_pairs={{0,3},{1,0},{2,1},{3,2},{4,7},{5,4},{6,5},{7,6},{8,11},{9,8},{10,9... | collective-permute-start | bytes 430088 | tf_op jit(solution)/shard_map/ppermute | solution.py:361
  40.9 26.5 %collective-permute-start.17 = (bf16[3,40,1792]{2,1,0:T(8,128)(2,1)S(1)}, bf16[3,40,1792]{2,1,0:T(8,128)(2,1)S(1)}, u32[]{:S(2)}, u32[]{:S(2)}) collective-permute-start(bf16[3,40,1792]{2,1,0:T(8,128)(2,1)S(1)} %pad_maximum_fusion.1), channel_id=1, source_target_pairs={{0,8},{4,12},{8,0},{12,4},{1,9},{5,13},{9,1},{13,5},{2,10},{6,14},... | collective-permute-start | bytes 1290248 | tf_op jit(solution)/shard_map/ppermute | solution.py:357
  42.5 14.3 %copy-start = (bf16[256,192]{1,0:T(8,128)(2,1)S(1)}, bf16[256,192]{1,0:T(8,128)(2,1)}, u32[]{:S(2)}) copy-start(bf16[256,192]{1,0:T(8,128)(2,1)} %constant.8.clone.refs_2_) | copy-start | bytes 294916
  42.5 14.3 %copy-start.1 = (bf16[192,256]{1,0:T(8,128)(2,1)S(1)}, bf16[192,256]{1,0:T(8,128)(2,1)}, u32[]{:S(2)}) copy-start(bf16[192,256]{1,0:T(8,128)(2,1)} %constant.9.clone.refs_3_) | copy-start | bytes 294916
  42.5 8.3 %collective-permute-start.10 = (bf16[8,40,1792]{2,1,0:T(8,128)(2,1)S(1)}, bf16[8,40,1792]{2,1,0:T(8,128)(2,1)S(1)}, u32[]{:S(2)}, u32[]{:S(2)}) collective-permute-start(bf16[8,40,1792]{2,1,0:T(8,128)(2,1)S(1)} %constant_dynamic-update-slice_fusion.refs_0_), channel_id=1, source_target_pairs={{0,4},{4,0},{8,12},{12,8},{1,5},{5,1},{9,13},{13,9},{2,6},{6,2},{1... | collective-permute-start | bytes 3440648 | tf_op jit(solution)/shard_map/ppermute | solution.py:357
  49.3 18.1 %collective-permute-start.16 = (bf16[3,40,1792]{2,1,0:T(8,128)(2,1)S(1)}, bf16[3,40,1792]{2,1,0:T(8,128)(2,1)S(1)}, u32[]{:S(2)}, u32[]{:S(2)}) collective-permute-start(bf16[3,40,1792]{2,1,0:T(8,128)(2,1)S(1)} %get-tuple-element.168), channel_id=1, source_target_pairs={{0,8},{4,12},{8,0},{12,4},{1,9},{5,13},{9,1},{13,5},{2,10},{6,14},... | collective-permute-start | bytes 1290248 | tf_op jit(solution)/shard_map/ppermute | solution.py:357
  50.8 16.6 %collective-permute-start.11 = (bf16[1,40,1792]{2,1,0:T(8,128)(2,1)S(1)}, bf16[1,40,1792]{2,1,0:T(8,128)(2,1)S(1)}, u32[]{:S(2)}, u32[]{:S(2)}) collective-permute-start(bf16[1,40,1792]{2,1,0:T(8,128)(2,1)S(1)} %get-tuple-element.99), channel_id=1, source_target_pairs={{0,1},{1,2},{2,3},{3,0},{4,5},{5,6},{6,7},{7,4},{8,9},{9,10},{10,1... | collective-permute-start | bytes 430088 | tf_op jit(solution)/shard_map/ppermute | solution.py:361
  54.4 13.1 %collective-permute-start.12 = (bf16[1,40,1792]{2,1,0:T(8,128)(2,1)S(1)}, bf16[1,40,1792]{2,1,0:T(8,128)(2,1)S(1)}, u32[]{:S(2)}, u32[]{:S(2)}) collective-permute-start(bf16[1,40,1792]{2,1,0:T(8,128)(2,1)S(1)} %get-tuple-element.101), channel_id=1, source_target_pairs={{0,2},{1,3},{2,0},{3,1},{4,6},{5,7},{6,4},{7,5},{8,10},{9,11},{10,... | collective-permute-start | bytes 430088 | tf_op jit(solution)/shard_map/ppermute | solution.py:361
  54.4 13.2 %collective-permute-start.14 = (bf16[1,40,1792]{2,1,0:T(8,128)(2,1)S(1)}, bf16[1,40,1792]{2,1,0:T(8,128)(2,1)S(1)}, u32[]{:S(2)}, u32[]{:S(2)}) collective-permute-start(bf16[1,40,1792]{2,1,0:T(8,128)(2,1)S(1)} %get-tuple-element.105), channel_id=1, source_target_pairs={{0,3},{1,0},{2,1},{3,2},{4,7},{5,4},{6,5},{7,6},{8,11},{9,8},{10,9... | collective-permute-start | bytes 430088 | tf_op jit(solution)/shard_map/ppermute | solution.py:361
  67.4 2.9 %collective-permute-start.18 = (bf16[8,40,1792]{2,1,0:T(8,128)(2,1)S(1)}, bf16[8,40,1792]{2,1,0:T(8,128)(2,1)S(1)}, u32[]{:S(2)}, u32[]{:S(2)}) collective-permute-start(bf16[8,40,1792]{2,1,0:T(8,128)(2,1)S(1)} %get-tuple-element.110), channel_id=1, source_target_pairs={{0,4},{4,0},{8,12},{12,8},{1,5},{5,1},{9,13},{13,9},{2,6},{6,2},{1... | collective-permute-start | bytes 3440648 | tf_op jit(solution)/shard_map/ppermute | solution.py:357
  67.7 4.2 %collective-permute-start.19 = (bf16[8,40,1792]{2,1,0:T(8,128)(2,1)S(1)}, bf16[8,40,1792]{2,1,0:T(8,128)(2,1)S(1)}, u32[]{:S(2)}, u32[]{:S(2)}) collective-permute-start(bf16[8,40,1792]{2,1,0:T(8,128)(2,1)S(1)} %constant_dynamic-update-slice_fusion.10.refs_0_), channel_id=1, source_target_pairs={{0,4},{4,0},{8,12},{12,8},{1,5},{5,1},{9,13},{13,9},{2,6},{6,2},{1... | collective-permute-start | bytes 3440648 | tf_op jit(solution)/shard_map/ppermute | solution.py:357
  68.2 14.2 %collective-permute-start.15 = (bf16[3,40,1792]{2,1,0:T(8,128)(2,1)S(1)}, bf16[3,40,1792]{2,1,0:T(8,128)(2,1)S(1)}, u32[]{:S(2)}, u32[]{:S(2)}) collective-permute-start(bf16[3,40,1792]{2,1,0:T(8,128)(2,1)S(1)} %get-tuple-element.174), channel_id=1, source_target_pairs={{0,8},{4,12},{8,0},{12,4},{1,9},{5,13},{9,1},{13,5},{2,10},{6,14},... | collective-permute-start | bytes 1290248 | tf_op jit(solution)/shard_map/ppermute | solution.py:357
  82.5 2.9 %collective-permute-start.20 = (bf16[8,40,1792]{2,1,0:T(8,128)(2,1)S(1)}, bf16[8,40,1792]{2,1,0:T(8,128)(2,1)S(1)}, u32[]{:S(2)}, u32[]{:S(2)}) collective-permute-start(bf16[8,40,1792]{2,1,0:T(8,128)(2,1)S(1)} %get-tuple-element.116), channel_id=1, source_target_pairs={{0,4},{4,0},{8,12},{12,8},{1,5},{5,1},{9,13},{13,9},{2,6},{6,2},{1... | collective-permute-start | bytes 3440648 | tf_op jit(solution)/shard_map/ppermute | solution.py:357
  82.7 4.3 %collective-permute-start.21 = (bf16[8,40,1792]{2,1,0:T(8,128)(2,1)S(1)}, bf16[8,40,1792]{2,1,0:T(8,128)(2,1)S(1)}, u32[]{:S(2)}, u32[]{:S(2)}) collective-permute-start(bf16[8,40,1792]{2,1,0:T(8,128)(2,1)S(1)} %constant_dynamic-update-slice_fusion.14.refs_0_), channel_id=1, source_target_pairs={{0,4},{4,0},{8,12},{12,8},{1,5},{5,1},{9,13},{13,9},{2,6},{6,2},{1... | collective-permute-start | bytes 3440648 | tf_op jit(solution)/shard_map/ppermute | solution.py:357
  83.1 15.0 %collective-permute-start.22 = (bf16[4,40,1792]{2,1,0:T(8,128)(2,1)S(1)}, bf16[4,40,1792]{2,1,0:T(8,128)(2,1)S(1)}, u32[]{:S(2)}, u32[]{:S(2)}) collective-permute-start(bf16[4,40,1792]{2,1,0:T(8,128)(2,1)S(1)} %get-tuple-element.111), channel_id=1, source_target_pairs={{0,8},{4,12},{8,0},{12,4},{1,9},{5,13},{9,1},{13,5},{2,10},{6,14},... | collective-permute-start | bytes 1720328 | tf_op jit(solution)/shard_map/ppermute | solution.py:357
  98.1 3.4 %collective-permute-start.23 = (bf16[8,40,1792]{2,1,0:T(8,128)(2,1)S(1)}, bf16[8,40,1792]{2,1,0:T(8,128)(2,1)S(1)}, u32[]{:S(2)}, u32[]{:S(2)}) collective-permute-start(bf16[8,40,1792]{2,1,0:T(8,128)(2,1)S(1)} %get-tuple-element.122), channel_id=1, source_target_pairs={{0,4},{4,0},{8,12},{12,8},{1,5},{5,1},{9,13},{13,9},{2,6},{6,2},{1... | collective-permute-start | bytes 3440648 | tf_op jit(solution)/shard_map/ppermute | solution.py:357
  98.2 4.4 %collective-permute-start.24 = (bf16[8,40,1792]{2,1,0:T(8,128)(2,1)S(1)}, bf16[8,40,1792]{2,1,0:T(8,128)(2,1)S(1)}, u32[]{:S(2)}, u32[]{:S(2)}) collective-permute-start(bf16[8,40,1792]{2,1,0:T(8,128)(2,1)S(1)} %constant_dynamic-update-slice_fusion.18.refs_0_), channel_id=1, source_target_pairs={{0,4},{4,0},{8,12},{12,8},{1,5},{5,1},{9,13},{13,9},{2,6},{6,2},{1... | collective-permute-start | bytes 3440648 | tf_op jit(solution)/shard_map/ppermute | solution.py:357
  98.8 15.0 %collective-permute-start.28 = (bf16[4,40,1792]{2,1,0:T(8,128)(2,1)S(1)}, bf16[4,40,1792]{2,1,0:T(8,128)(2,1)S(1)}, u32[]{:S(2)}, u32[]{:S(2)}) collective-permute-start(bf16[4,40,1792]{2,1,0:T(8,128)(2,1)S(1)} %get-tuple-element.117), channel_id=1, source_target_pairs={{0,8},{4,12},{8,0},{12,4},{1,9},{5,13},{9,1},{13,5},{2,10},{6,14},... | collective-permute-start | bytes 1720328 | tf_op jit(solution)/shard_map/ppermute | solution.py:357
  99.4 13.9 %collective-permute-start.25 = (bf16[1,40,1792]{2,1,0:T(8,128)(2,1)S(1)}, bf16[1,40,1792]{2,1,0:T(8,128)(2,1)S(1)}, u32[]{:S(2)}, u32[]{:S(2)}) collective-permute-start(bf16[1,40,1792]{2,1,0:T(8,128)(2,1)S(1)} %get-tuple-element.132), channel_id=1, source_target_pairs={{0,2},{1,3},{2,0},{3,1},{4,6},{5,7},{6,4},{7,5},{8,10},{9,11},{10,... | collective-permute-start | bytes 430088 | tf_op jit(solution)/shard_map/ppermute | solution.py:361
  100.0 13.3 %collective-permute-start.26 = (bf16[1,40,1792]{2,1,0:T(8,128)(2,1)S(1)}, bf16[1,40,1792]{2,1,0:T(8,128)(2,1)S(1)}, u32[]{:S(2)}, u32[]{:S(2)}) collective-permute-start(bf16[1,40,1792]{2,1,0:T(8,128)(2,1)S(1)} %get-tuple-element.133), channel_id=1, source_target_pairs={{0,3},{1,0},{2,1},{3,2},{4,7},{5,4},{6,5},{7,6},{8,11},{9,8},{10,9... | collective-permute-start | bytes 430088 | tf_op jit(solution)/shard_map/ppermute | solution.py:361
  101.5 11.8 %collective-permute-start.27 = (bf16[1,40,1792]{2,1,0:T(8,128)(2,1)S(1)}, bf16[1,40,1792]{2,1,0:T(8,128)(2,1)S(1)}, u32[]{:S(2)}, u32[]{:S(2)}) collective-permute-start(bf16[1,40,1792]{2,1,0:T(8,128)(2,1)S(1)} %get-tuple-element.134), channel_id=1, source_target_pairs={{0,1},{1,2},{2,3},{3,0},{4,5},{5,6},{6,7},{7,4},{8,9},{9,10},{10,1... | collective-permute-start | bytes 430088 | tf_op jit(solution)/shard_map/ppermute | solution.py:361
  113.7 2.8 %collective-permute-start.29 = (bf16[8,40,1792]{2,1,0:T(8,128)(2,1)S(1)}, bf16[8,40,1792]{2,1,0:T(8,128)(2,1)S(1)}, u32[]{:S(2)}, u32[]{:S(2)}) collective-permute-start(bf16[8,40,1792]{2,1,0:T(8,128)(2,1)S(1)} %get-tuple-element.135), channel_id=1, source_target_pairs={{0,4},{4,0},{8,12},{12,8},{1,5},{5,1},{9,13},{13,9},{2,6},{6,2},{1... | collective-permute-start | bytes 3440648 | tf_op jit(solution)/shard_map/ppermute | solution.py:357
  113.7 15.8 %collective-permute-start.32 = (bf16[4,40,1792]{2,1,0:T(8,128)(2,1)S(1)}, bf16[4,40,1792]{2,1,0:T(8,128)(2,1)S(1)}, u32[]{:S(2)}, u32[]{:S(2)}) collective-permute-start(bf16[4,40,1792]{2,1,0:T(8,128)(2,1)S(1)} %get-tuple-element.123), channel_id=1, source_target_pairs={{0,8},{4,12},{8,0},{12,4},{1,9},{5,13},{9,1},{13,5},{2,10},{6,14},... | collective-permute-start | bytes 1720328 | tf_op jit(solution)/shard_map/ppermute | solution.py:357
  116.8 24.6 %collective-permute-start.30 = (bf16[4,40,1792]{2,1,0:T(8,128)(2,1)S(1)}, bf16[4,40,1792]{2,1,0:T(8,128)(2,1)S(1)}, u32[]{:S(2)}, u32[]{:S(2)}) collective-permute-start(bf16[4,40,1792]{2,1,0:T(8,128)(2,1)S(1)} %get-tuple-element.137), channel_id=1, source_target_pairs={{0,8},{4,12},{8,0},{12,4},{1,9},{5,13},{9,1},{13,5},{2,10},{6,14},... | collective-permute-start | bytes 1720328 | tf_op jit(solution)/shard_map/ppermute | solution.py:357
  117.9 11.8 %collective-permute-start.33 = (bf16[1,40,1792]{2,1,0:T(8,128)(2,1)S(1)}, bf16[1,40,1792]{2,1,0:T(8,128)(2,1)S(1)}, u32[]{:S(2)}, u32[]{:S(2)}) collective-permute-start(bf16[1,40,1792]{2,1,0:T(8,128)(2,1)S(1)} %get-tuple-element.146), channel_id=1, source_target_pairs={{0,2},{1,3},{2,0},{3,1},{4,6},{5,7},{6,4},{7,5},{8,10},{9,11},{10,... | collective-permute-start | bytes 430088 | tf_op jit(solution)/shard_map/ppermute | solution.py:361
  120.4 11.2 %collective-permute-start.35 = (bf16[1,40,1792]{2,1,0:T(8,128)(2,1)S(1)}, bf16[1,40,1792]{2,1,0:T(8,128)(2,1)S(1)}, u32[]{:S(2)}, u32[]{:S(2)}) collective-permute-start(bf16[1,40,1792]{2,1,0:T(8,128)(2,1)S(1)} %get-tuple-element.150), channel_id=1, source_target_pairs={{0,3},{1,0},{2,1},{3,2},{4,7},{5,4},{6,5},{7,6},{8,11},{9,8},{10,9... | collective-permute-start | bytes 430088 | tf_op jit(solution)/shard_map/ppermute | solution.py:361
  122.3 11.7 %collective-permute-start.31 = (bf16[1,40,1792]{2,1,0:T(8,128)(2,1)S(1)}, bf16[1,40,1792]{2,1,0:T(8,128)(2,1)S(1)}, u32[]{:S(2)}, u32[]{:S(2)}) collective-permute-start(bf16[1,40,1792]{2,1,0:T(8,128)(2,1)S(1)} %get-tuple-element.142), channel_id=1, source_target_pairs={{0,1},{1,2},{2,3},{3,0},{4,5},{5,6},{6,7},{7,4},{8,9},{9,10},{10,1... | collective-permute-start | bytes 430088 | tf_op jit(solution)/shard_map/ppermute | solution.py:361
  129.5 18.4 %copy-start.4 = (s32[64,2]{0,1:T(2,128)S(1)}, s32[64,2]{0,1:T(2,128)}, u32[]{:S(2)}) copy-start(s32[64,2]{0,1:T(2,128)} %param.9) | copy-start | bytes 1540
  129.5 18.4 %copy-start.5 = (f32[64,2]{0,1:T(2,128)S(1)}, f32[64,2]{0,1:T(2,128)}, u32[]{:S(2)}) copy-start(f32[64,2]{0,1:T(2,128)} %param.10) | copy-start | bytes 1540
  129.6 11.9 %collective-permute-start.34 = (bf16[1,40,1792]{2,1,0:T(8,128)(2,1)S(1)}, bf16[1,40,1792]{2,1,0:T(8,128)(2,1)S(1)}, u32[]{:S(2)}, u32[]{:S(2)}) collective-permute-start(bf16[1,40,1792]{2,1,0:T(8,128)(2,1)S(1)} %get-tuple-element.147), channel_id=1, source_target_pairs={{0,2},{1,3},{2,0},{3,1},{4,6},{5,7},{6,4},{7,5},{8,10},{9,11},{10,... | collective-permute-start | bytes 430088 | tf_op jit(solution)/shard_map/ppermute | solution.py:361
  131.7 9.9 %collective-permute-start.36 = (bf16[1,40,1792]{2,1,0:T(8,128)(2,1)S(1)}, bf16[1,40,1792]{2,1,0:T(8,128)(2,1)S(1)}, u32[]{:S(2)}, u32[]{:S(2)}) collective-permute-start(bf16[1,40,1792]{2,1,0:T(8,128)(2,1)S(1)} %get-tuple-element.151), channel_id=1, source_target_pairs={{0,3},{1,0},{2,1},{3,2},{4,7},{5,4},{6,5},{7,6},{8,11},{9,8},{10,9... | collective-permute-start | bytes 430088 | tf_op jit(solution)/shard_map/ppermute | solution.py:361
  134.0 13.8 %collective-permute-start.39 = (bf16[1,40,1792]{2,1,0:T(8,128)(2,1)S(1)}, bf16[1,40,1792]{2,1,0:T(8,128)(2,1)S(1)}, u32[]{:S(2)}, u32[]{:S(2)}) collective-permute-start(bf16[1,40,1792]{2,1,0:T(8,128)(2,1)S(1)} %get-tuple-element.157), channel_id=1, source_target_pairs={{0,1},{1,2},{2,3},{3,0},{4,5},{5,6},{6,7},{7,4},{8,9},{9,10},{10,1... | collective-permute-start | bytes 430088 | tf_op jit(solution)/shard_map/ppermute | solution.py:361
  141.6 9.0 %collective-permute-start.37 = (bf16[1,40,1792]{2,1,0:T(8,128)(2,1)S(1)}, bf16[1,40,1792]{2,1,0:T(8,128)(2,1)S(1)}, u32[]{:S(2)}, u32[]{:S(2)}) collective-permute-start(bf16[1,40,1792]{2,1,0:T(8,128)(2,1)S(1)} %get-tuple-element.152), channel_id=1, source_target_pairs={{0,3},{1,0},{2,1},{3,2},{4,7},{5,4},{6,5},{7,6},{8,11},{9,8},{10,9... | collective-permute-start | bytes 430088 | tf_op jit(solution)/shard_map/ppermute | solution.py:361
  146.3 13.6 %collective-permute-start.38 = (bf16[1,40,1792]{2,1,0:T(8,128)(2,1)S(1)}, bf16[1,40,1792]{2,1,0:T(8,128)(2,1)S(1)}, u32[]{:S(2)}, u32[]{:S(2)}) collective-permute-start(bf16[1,40,1792]{2,1,0:T(8,128)(2,1)S(1)} %get-tuple-element.154), channel_id=1, source_target_pairs={{0,2},{1,3},{2,0},{3,1},{4,6},{5,7},{6,4},{7,5},{8,10},{9,11},{10,... | collective-permute-start | bytes 430088 | tf_op jit(solution)/shard_map/ppermute | solution.py:361
  147.9 12.0 %collective-permute-start.40 = (bf16[1,40,1792]{2,1,0:T(8,128)(2,1)S(1)}, bf16[1,40,1792]{2,1,0:T(8,128)(2,1)S(1)}, u32[]{:S(2)}, u32[]{:S(2)}) collective-permute-start(bf16[1,40,1792]{2,1,0:T(8,128)(2,1)S(1)} %get-tuple-element.158), channel_id=1, source_target_pairs={{0,1},{1,2},{2,3},{3,0},{4,5},{5,6},{6,7},{7,4},{8,9},{9,10},{10,1... | collective-permute-start | bytes 430088 | tf_op jit(solution)/shard_map/ppermute | solution.py:361

commit v6 on v5

--- a/solution.py
+++ b/solution.py
@@ -230,7 +230,7 @@
                 grouped_ref[:, m * z.MP : (m + 1) * z.MP, there] = got[q * z.each : (q + 1) * z.each]
         return carry
 
-    lax.fori_loop(0, z.dc // tile, step, 0)
+    lax.fori_loop(0, z.dc // tile, step, 0, unroll=z.relative)
 
     for j in range(z.each):
         loads[3 * j].wait()
@@ -259,7 +259,7 @@
                     out[k * z.local + s, :, cols] = got[s * z.RP : s * z.RP + z.R]
         return carry
 
-    lax.fori_loop(0, z.dc // tile, back, 0)
+    lax.fori_loop(0, z.dc // tile, back, 0, unroll=z.relative)
 
 
 def expert_group(z, group, pieces, regroup, ungroup, w_gate, w_up, w_down, order):

time: 162 us -> 159 us (0.981)
  waiting for transfers between devices: 42.4 us -> 47.5 us
  Pallas kernels: 50.7 us -> 45.8 us
  starting transfers between devices: 65.6 us -> 62.9 us
    pallas_call x4, Pallas kernels: 42.5 us -> 37.6 us  [expert_group(): pl.pallas_call(functools.partial(expert_kernel, z, group, places, order),...]
    ppermute x17, waiting for transfers between devices: 16.9 us -> 19.4 us  [swap(): return lax.ppermute(a, 'node', [(i, i ^ mask) for i in range(count)])]
    ppermute x24, waiting for transfers between devices: 25.5 us -> 28 us  [shift(): lax.ppermute(a, 'local', [(i, (i + by) % count) for i in range(count)])]
    ppermute x24, starting transfers between devices: 54 us -> 52 us  [shift(): lax.ppermute(a, 'local', [(i, (i + by) % count) for i in range(count)])]
  transfers between devices with their start and end apart: 41 -> 41, of which waited for: 15 -> 18; matrix products, arithmetic and copies ran while one was open for 0% -> 0% of each run, Pallas kernels for 29% -> 26%
where the time goes in v6:
time: 159 us
  starting transfers between devices  62.9 us (40%)
  waiting for transfers between devices  47.5 us (30%)
  Pallas kernels  45.8 us (29%)
  local copies, waits for them, and re-layouts  2.27 us (1%)
    ppermute x24, starting transfers between devices, shift(): lax.ppermute(a, 'local', [(i, (i + by) % count) for i in range(count)])  52 us
    pallas_call x4, Pallas kernels, expert_group(): pl.pallas_call(functools.partial(expert_kernel, z, group, places, order),...  37.6 us
    ppermute x24, waiting for transfers between devices, shift(): lax.ppermute(a, 'local', [(i, (i + by) % count) for i in range(count)])  28 us
    ppermute x17, waiting for transfers between devices, swap(): return lax.ppermute(a, 'node', [(i, i ^ mask) for i in range(count)])  19.4 us
    ppermute x17, starting transfers between devices, swap(): return lax.ppermute(a, 'node', [(i, i ^ mask) for i in range(count)])  10.8 us
    pallas_call x4, Pallas kernels, combine_group(): pl.pallas_call(functools.partial(combine_kernel, z, group, [p.shape[0] fo...  3.47 us
  transfers between devices with their start and end apart: 41, of which 18 were waited for; matrix products, arithmetic and copies ran while one was open for 0% of the time, Pallas kernels for 26%

profile of v6, /device:TPU:0, one launch (start us, length us, event | category | flops | bytes accessed | tf_op | source)
XLA Modules:
  0.0 158.9 jit_solution(17994537688067574630)
XLA Ops:
  0.0 1.2 copy-done.2
  1.2 0.7 copy-done.3
  1.9 2.5 %gather_rows.1 = (bf16[4,40,1792]{2,1,0:T(8,128)(2,1)S(1)}, bf16[1,40,1792]{2,1,0:T(8,128)(2,1)S(1)}, bf16[1,40,1792]{2,1,0:T(8,128)(2,1)S(1)}, bf16[1,40,1792]{...) custom-call(s32[1]{0:T(128)} %bitcast.plane_ref, ...), custom_call_target="tpu_custom_call" | custom-call | tf_op jit(solution)/shard_map/gather_rows/pallas_call | solution.py:148
  4.3 4.1 %collective-permute-start = (bf16[1,40,1792]{2,1,0:T(8,128)(2,1)S(1)}, bf16[1,40,1792]{2,1,0:T(8,128)(2,1)S(1)}, u32[]{:S(2)}, u32[]{:S(2)}) collective-permute-start(bf16[1,40,1792]{2,1,0:T(8,128)(2,1)S(1)} %get-tuple-element.86), channel_id=1, source_target_pairs={{0,2},{1,3},{2,0},{3,1},{4,6},{5,7},{6,4},{7,5},{8,10},{9,11},{10,... | collective-permute-start | bytes 430088 | tf_op jit(solution)/shard_map/ppermute | solution.py:361
  8.4 1.6 collective-permute-start.1
  10.0 2.2 %collective-permute-start.2 = (bf16[1,40,1792]{2,1,0:T(8,128)(2,1)S(1)}, bf16[1,40,1792]{2,1,0:T(8,128)(2,1)S(1)}, u32[]{:S(2)}, u32[]{:S(2)}) collective-permute-start(bf16[1,40,1792]{2,1,0:T(8,128)(2,1)S(1)} %get-tuple-element.88), channel_id=1, source_target_pairs={{0,3},{1,0},{2,1},{3,2},{4,7},{5,4},{6,5},{7,6},{8,11},{9,8},{10,9... | collective-permute-start | bytes 430088 | tf_op jit(solution)/shard_map/ppermute | solution.py:361
  12.3 1.5 collective-permute-start.8
  13.8 5.4 %collective-permute-done = bf16[1,40,1792]{2,1,0:T(8,128)(2,1)S(1)} collective-permute-done((bf16[1,40,1792]{2,1,0:T(8,128)(2,1)S(1)}, bf16[1,40,1792]{2,1,0:T(8,128)(2,1)S(1)}, u32[]{:S(2)}, u32[]{:S(2)}) %collective-permute-start) | collective-permute-done | bytes 143392 | tf_op jit(solution)/shard_map/ppermute | solution.py:361
  19.2 2.9 %collective-permute-start.6 = (bf16[1,40,1792]{2,1,0:T(8,128)(2,1)S(1)}, bf16[1,40,1792]{2,1,0:T(8,128)(2,1)S(1)}, u32[]{:S(2)}, u32[]{:S(2)}) collective-permute-start(bf16[1,40,1792]{2,1,0:T(8,128)(2,1)S(1)} %get-tuple-element.96), channel_id=1, source_target_pairs={{0,1},{1,2},{2,3},{3,0},{4,5},{5,6},{6,7},{7,4},{8,9},{9,10},{10,1... | collective-permute-start | bytes 430088 | tf_op jit(solution)/shard_map/ppermute | solution.py:361
  22.1 1.9 %collective-permute-start.4 = (bf16[1,40,1792]{2,1,0:T(8,128)(2,1)S(1)}, bf16[1,40,1792]{2,1,0:T(8,128)(2,1)S(1)}, u32[]{:S(2)}, u32[]{:S(2)}) collective-permute-start(bf16[1,40,1792]{2,1,0:T(8,128)(2,1)S(1)} %get-tuple-element.92), channel_id=1, source_target_pairs={{0,2},{1,3},{2,0},{3,1},{4,6},{5,7},{6,4},{7,5},{8,10},{9,11},{10,... | collective-permute-start | bytes 430088 | tf_op jit(solution)/shard_map/ppermute | solution.py:361
  24.1 2.9 %collective-permute-start.3 = (bf16[1,40,1792]{2,1,0:T(8,128)(2,1)S(1)}, bf16[1,40,1792]{2,1,0:T(8,128)(2,1)S(1)}, u32[]{:S(2)}, u32[]{:S(2)}) collective-permute-start(bf16[1,40,1792]{2,1,0:T(8,128)(2,1)S(1)} %get-tuple-element.89), channel_id=1, source_target_pairs={{0,3},{1,0},{2,1},{3,2},{4,7},{5,4},{6,5},{7,6},{8,11},{9,8},{10,9... | collective-permute-start | bytes 430088 | tf_op jit(solution)/shard_map/ppermute | solution.py:361
  27.0 1.6 collective-permute-start.9
  28.7 4.1 %collective-permute-done.4 = bf16[1,40,1792]{2,1,0:T(8,128)(2,1)S(1)} collective-permute-done((bf16[1,40,1792]{2,1,0:T(8,128)(2,1)S(1)}, bf16[1,40,1792]{2,1,0:T(8,128)(2,1)S(1)}, u32[]{:S(2)}, u32[]{:S(2)}) %collective-permute-start.4) | collective-permute-done | bytes 143392 | tf_op jit(solution)/shard_map/ppermute | solution.py:361
  32.8 4.6 %collective-permute-start.7 = (bf16[1,40,1792]{2,1,0:T(8,128)(2,1)S(1)}, bf16[1,40,1792]{2,1,0:T(8,128)(2,1)S(1)}, u32[]{:S(2)}, u32[]{:S(2)}) collective-permute-start(bf16[1,40,1792]{2,1,0:T(8,128)(2,1)S(1)} %get-tuple-element.97), channel_id=1, source_target_pairs={{0,1},{1,2},{2,3},{3,0},{4,5},{5,6},{6,7},{7,4},{8,9},{9,10},{10,1... | collective-permute-start | bytes 430088 | tf_op jit(solution)/shard_map/ppermute | solution.py:361
  37.4 3.4 %collective-permute-start.5 = (bf16[1,40,1792]{2,1,0:T(8,128)(2,1)S(1)}, bf16[1,40,1792]{2,1,0:T(8,128)(2,1)S(1)}, u32[]{:S(2)}, u32[]{:S(2)}) collective-permute-start(bf16[1,40,1792]{2,1,0:T(8,128)(2,1)S(1)} %get-tuple-element.93), channel_id=1, source_target_pairs={{0,2},{1,3},{2,0},{3,1},{4,6},{5,7},{6,4},{7,5},{8,10},{9,11},{10,... | collective-permute-start | bytes 430088 | tf_op jit(solution)/shard_map/ppermute | solution.py:361
  40.9 1.6 collective-permute-start.17
  42.6 2.4 %collective-permute-done.7 = bf16[1,40,1792]{2,1,0:T(8,128)(2,1)S(1)} collective-permute-done((bf16[1,40,1792]{2,1,0:T(8,128)(2,1)S(1)}, bf16[1,40,1792]{2,1,0:T(8,128)(2,1)S(1)}, u32[]{:S(2)}, u32[]{:S(2)}) %collective-permute-start.7) | collective-permute-done | bytes 143392 | tf_op jit(solution)/shard_map/ppermute | solution.py:361
  45.1 4.1 %collective-permute-done.5 = bf16[1,40,1792]{2,1,0:T(8,128)(2,1)S(1)} collective-permute-done((bf16[1,40,1792]{2,1,0:T(8,128)(2,1)S(1)}, bf16[1,40,1792]{2,1,0:T(8,128)(2,1)S(1)}, u32[]{:S(2)}, u32[]{:S(2)}) %collective-permute-start.5) | collective-permute-done | bytes 143392 | tf_op jit(solution)/shard_map/ppermute | solution.py:361
  49.3 1.6 collective-permute-start.16
  50.8 3.6 %collective-permute-start.11 = (bf16[1,40,1792]{2,1,0:T(8,128)(2,1)S(1)}, bf16[1,40,1792]{2,1,0:T(8,128)(2,1)S(1)}, u32[]{:S(2)}, u32[]{:S(2)}) collective-permute-start(bf16[1,40,1792]{2,1,0:T(8,128)(2,1)S(1)} %get-tuple-element.99), channel_id=1, source_target_pairs={{0,1},{1,2},{2,3},{3,0},{4,5},{5,6},{6,7},{7,4},{8,9},{9,10},{10,1... | collective-permute-start | bytes 430088 | tf_op jit(solution)/shard_map/ppermute | solution.py:361
  54.4 2.4 %collective-permute-start.14 = (bf16[1,40,1792]{2,1,0:T(8,128)(2,1)S(1)}, bf16[1,40,1792]{2,1,0:T(8,128)(2,1)S(1)}, u32[]{:S(2)}, u32[]{:S(2)}) collective-permute-start(bf16[1,40,1792]{2,1,0:T(8,128)(2,1)S(1)} %get-tuple-element.105), channel_id=1, source_target_pairs={{0,3},{1,0},{2,1},{3,2},{4,7},{5,4},{6,5},{7,6},{8,11},{9,8},{10,9... | collective-permute-start | bytes 430088 | tf_op jit(solution)/shard_map/ppermute | solution.py:361
  56.8 9.2 %expert_group.4 = (bf16[8,40,1792]{2,1,0:T(8,128)(2,1)S(1)}, bf16[8,40,1792]{2,1,0:T(8,128)(2,1)S(1)}) custom-call(bf16[8,40,1792]{2,1,0:T(8,128)(2,1)S(1)} %constant_dynamic-update-slice_fusion.refs_0_, bf16[8,40,1792]{2,1,0:T(8,128)(2,1)S(1)} %collective-permute-done.10.refs_1_, bf16[256,192]{1,0:T(8,128)(2,1)S(1)} %copy-done, ...), custom_call_target="tpu_custom_call" | custom-call | flops 2818572288 | bytes 22020096 | tf_op jit(solution)/shard_map/expert_group/pallas_call | solution.py:277
  66.3 0.5 collective-permute-start.19
  66.9 0.5 collective-permute-start.15
  67.4 1.5 collective-permute-done.18.b_ref
  68.9 0.3 add_cut.8
  69.2 1.4 collective-permute-done.19.refs_1_
  70.5 9.4 %expert_group.5 = (bf16[8,40,1792]{2,1,0:T(8,128)(2,1)S(1)}, bf16[8,40,1792]{2,1,0:T(8,128)(2,1)S(1)}) custom-call(bf16[8,40,1792]{2,1,0:T(8,128)(2,1)S(1)} %constant_dynamic-update-slice_fusion.10.refs_0_, bf16[8,40,1792]{2,1,0:T(8,128)(2,1)S(1)} %collective-permute-done.19.refs_1_, bf16[256,192]{1,0:T(8,128)(2,1)S(1)} %copy-done, ...), custom_call_target="tpu_custom_call" | custom-call | flops 2818572288 | bytes 22020096 | tf_op jit(solution)/shard_map/expert_group/pallas_call | solution.py:277
  79.9 0.2 collective-permute-start.20
  80.2 0.4 collective-permute-start.21
  80.6 0.5 collective-permute-start.22
  81.1 1.6 %collective-permute-done.20.b_ref = bf16[8,40,1792]{2,1,0:T(8,128)(2,1)S(1)} collective-permute-done((bf16[8,40,1792]{2,1,0:T(8,128)(2,1)S(1)}, bf16[8,40,1792]{2,1,0:T(8,128)(2,1)S(1)}, u32[]{:S(2)}, u32[]{:S(2)}) %collective-permute-start.20) | collective-permute-done | bytes 1146912 | tf_op jit(solution)/shard_map/ppermute | solution.py:357
  82.8 0.3 add_cut.9
  83.0 1.4 collective-permute-done.21.refs_1_
  84.4 9.4 %expert_group.6 = (bf16[8,40,1792]{2,1,0:T(8,128)(2,1)S(1)}, bf16[8,40,1792]{2,1,0:T(8,128)(2,1)S(1)}) custom-call(bf16[8,40,1792]{2,1,0:T(8,128)(2,1)S(1)} %constant_dynamic-update-slice_fusion.14.refs_0_, bf16[8,40,1792]{2,1,0:T(8,128)(2,1)S(1)} %collective-permute-done.21.refs_1_, bf16[256,192]{1,0:T(8,128)(2,1)S(1)} %copy-done, ...), custom_call_target="tpu_custom_call" | custom-call | flops 2818572288 | bytes 22020096 | tf_op jit(solution)/shard_map/expert_group/pallas_call | solution.py:277
  93.8 1.8 %collective-permute-done.22.b_ref = bf16[4,40,1792]{2,1,0:T(8,128)(2,1)S(1)} collective-permute-done((bf16[4,40,1792]{2,1,0:T(8,128)(2,1)S(1)}, bf16[4,40,1792]{2,1,0:T(8,128)(2,1)S(1)}, u32[]{:S(2)}, u32[]{:S(2)}) %collective-permute-start.22) | collective-permute-done | bytes 573472 | tf_op jit(solution)/shard_map/ppermute | solution.py:357
  95.6 0.6 collective-permute-start.24
  96.2 0.5 collective-permute-start.28
  96.9 0.6 collective-permute-start.25
  97.5 2.1 %collective-permute-start.26 = (bf16[1,40,1792]{2,1,0:T(8,128)(2,1)S(1)}, bf16[1,40,1792]{2,1,0:T(8,128)(2,1)S(1)}, u32[]{:S(2)}, u32[]{:S(2)}) collective-permute-start(bf16[1,40,1792]{2,1,0:T(8,128)(2,1)S(1)} %get-tuple-element.133), channel_id=1, source_target_pairs={{0,3},{1,0},{2,1},{3,2},{4,7},{5,4},{6,5},{7,6},{8,11},{9,8},{10,9... | collective-permute-start | bytes 430088 | tf_op jit(solution)/shard_map/ppermute | solution.py:361
  99.7 0.3 add_cut.10
  100.1 9.6 %expert_group.7 = (bf16[8,40,1792]{2,1,0:T(8,128)(2,1)S(1)}, bf16[8,40,1792]{2,1,0:T(8,128)(2,1)S(1)}) custom-call(bf16[8,40,1792]{2,1,0:T(8,128)(2,1)S(1)} %constant_dynamic-update-slice_fusion.18.refs_0_, bf16[8,40,1792]{2,1,0:T(8,128)(2,1)S(1)} %collective-permute-done.24.refs_1_, bf16[256,192]{1,0:T(8,128)(2,1)S(1)} %copy-done, ...), custom_call_target="tpu_custom_call" | custom-call | flops 2818572288 | bytes 22020096 | tf_op jit(solution)/shard_map/expert_group/pallas_call | solution.py:277
  109.7 1.4 collective-permute-done.28.b_ref
  111.2 0.5 collective-permute-start.32
  111.7 2.2 %collective-permute-done.29.b_ref = bf16[8,40,1792]{2,1,0:T(8,128)(2,1)S(1)} collective-permute-done((bf16[8,40,1792]{2,1,0:T(8,128)(2,1)S(1)}, bf16[8,40,1792]{2,1,0:T(8,128)(2,1)S(1)}, u32[]{:S(2)}, u32[]{:S(2)}) %collective-permute-start.29) | collective-permute-done | bytes 1146912 | tf_op jit(solution)/shard_map/ppermute | solution.py:357
  114.0 0.3 add_cut.12
  114.2 0.6 collective-permute-start.30
  115.0 2.9 %collective-permute-start.33 = (bf16[1,40,1792]{2,1,0:T(8,128)(2,1)S(1)}, bf16[1,40,1792]{2,1,0:T(8,128)(2,1)S(1)}, u32[]{:S(2)}, u32[]{:S(2)}) collective-permute-start(bf16[1,40,1792]{2,1,0:T(8,128)(2,1)S(1)} %get-tuple-element.146), channel_id=1, source_target_pairs={{0,2},{1,3},{2,0},{3,1},{4,6},{5,7},{6,4},{7,5},{8,10},{9,11},{10,... | collective-permute-start | bytes 430088 | tf_op jit(solution)/shard_map/ppermute | solution.py:361
  117.9 2.1 %collective-permute-start.35 = (bf16[1,40,1792]{2,1,0:T(8,128)(2,1)S(1)}, bf16[1,40,1792]{2,1,0:T(8,128)(2,1)S(1)}, u32[]{:S(2)}, u32[]{:S(2)}) collective-permute-start(bf16[1,40,1792]{2,1,0:T(8,128)(2,1)S(1)} %get-tuple-element.150), channel_id=1, source_target_pairs={{0,3},{1,0},{2,1},{3,2},{4,7},{5,4},{6,5},{7,6},{8,11},{9,8},{10,9... | collective-permute-start | bytes 430088 | tf_op jit(solution)/shard_map/ppermute | solution.py:361
  120.0 6.9 %collective-permute-done.32.b_ref = bf16[4,40,1792]{2,1,0:T(8,128)(2,1)S(1)} collective-permute-done((bf16[4,40,1792]{2,1,0:T(8,128)(2,1)S(1)}, bf16[4,40,1792]{2,1,0:T(8,128)(2,1)S(1)}, u32[]{:S(2)}, u32[]{:S(2)}) %collective-permute-start.32) | collective-permute-done | bytes 573472 | tf_op jit(solution)/shard_map/ppermute | solution.py:357
  127.1 2.0 %collective-permute-start.34 = (bf16[1,40,1792]{2,1,0:T(8,128)(2,1)S(1)}, bf16[1,40,1792]{2,1,0:T(8,128)(2,1)S(1)}, u32[]{:S(2)}, u32[]{:S(2)}) collective-permute-start(bf16[1,40,1792]{2,1,0:T(8,128)(2,1)S(1)} %get-tuple-element.147), channel_id=1, source_target_pairs={{0,2},{1,3},{2,0},{3,1},{4,6},{5,7},{6,4},{7,5},{8,10},{9,11},{10,... | collective-permute-start | bytes 430088 | tf_op jit(solution)/shard_map/ppermute | solution.py:361
  129.1 2.4 %collective-permute-start.36 = (bf16[1,40,1792]{2,1,0:T(8,128)(2,1)S(1)}, bf16[1,40,1792]{2,1,0:T(8,128)(2,1)S(1)}, u32[]{:S(2)}, u32[]{:S(2)}) collective-permute-start(bf16[1,40,1792]{2,1,0:T(8,128)(2,1)S(1)} %get-tuple-element.151), channel_id=1, source_target_pairs={{0,3},{1,0},{2,1},{3,2},{4,7},{5,4},{6,5},{7,6},{8,11},{9,8},{10,9... | collective-permute-start | bytes 430088 | tf_op jit(solution)/shard_map/ppermute | solution.py:361
  131.5 6.4 %collective-permute-start.39 = (bf16[1,40,1792]{2,1,0:T(8,128)(2,1)S(1)}, bf16[1,40,1792]{2,1,0:T(8,128)(2,1)S(1)}, u32[]{:S(2)}, u32[]{:S(2)}) collective-permute-start(bf16[1,40,1792]{2,1,0:T(8,128)(2,1)S(1)} %get-tuple-element.157), channel_id=1, source_target_pairs={{0,1},{1,2},{2,3},{3,0},{4,5},{5,6},{6,7},{7,4},{8,9},{9,10},{10,1... | collective-permute-start | bytes 430088 | tf_op jit(solution)/shard_map/ppermute | solution.py:361
  137.9 1.0 collective-permute-done.30.b_ref
  139.0 2.0 %collective-permute-done.34.refs_2_ = bf16[1,40,1792]{2,1,0:T(8,128)(2,1)S(1)} collective-permute-done((bf16[1,40,1792]{2,1,0:T(8,128)(2,1)S(1)}, bf16[1,40,1792]{2,1,0:T(8,128)(2,1)S(1)}, u32[]{:S(2)}, u32[]{:S(2)}) %collective-permute-start.34) | collective-permute-done | bytes 143392 | tf_op jit(solution)/shard_map/ppermute | solution.py:361
  141.0 0.4 collective-permute-done.36.refs_1_
  141.4 2.4 %collective-permute-start.37 = (bf16[1,40,1792]{2,1,0:T(8,128)(2,1)S(1)}, bf16[1,40,1792]{2,1,0:T(8,128)(2,1)S(1)}, u32[]{:S(2)}, u32[]{:S(2)}) collective-permute-start(bf16[1,40,1792]{2,1,0:T(8,128)(2,1)S(1)} %get-tuple-element.152), channel_id=1, source_target_pairs={{0,3},{1,0},{2,1},{3,2},{4,7},{5,4},{6,5},{7,6},{8,11},{9,8},{10,9... | collective-permute-start | bytes 430088 | tf_op jit(solution)/shard_map/ppermute | solution.py:361
  143.8 1.4 collective-permute-start.38
  145.2 0.7 combine_weights.1.weight_ref
  145.9 0.6 combine_group.4.refs_4_
  146.6 0.6 combine_group.5.refs_4_
  147.2 0.6 combine_group.6.refs_4_
  148.0 9.3 %collective-permute-done.38.refs_2_ = bf16[1,40,1792]{2,1,0:T(8,128)(2,1)S(1)} collective-permute-done((bf16[1,40,1792]{2,1,0:T(8,128)(2,1)S(1)}, bf16[1,40,1792]{2,1,0:T(8,128)(2,1)S(1)}, u32[]{:S(2)}, u32[]{:S(2)}) %collective-permute-start.38) | collective-permute-done | bytes 143392 | tf_op jit(solution)/shard_map/ppermute | solution.py:361
  157.3 1.6 combine_group.7
  (69 shorter events, 1.6 us)
Async XLA Ops:
  0.0 1.2 copy-start.2
  1.2 0.7 copy-start.3
  4.3 14.9 %collective-permute-start = (bf16[1,40,1792]{2,1,0:T(8,128)(2,1)S(1)}, bf16[1,40,1792]{2,1,0:T(8,128)(2,1)S(1)}, u32[]{:S(2)}, u32[]{:S(2)}) collective-permute-start(bf16[1,40,1792]{2,1,0:T(8,128)(2,1)S(1)} %get-tuple-element.86), channel_id=1, source_target_pairs={{0,2},{1,3},{2,0},{3,1},{4,6},{5,7},{6,4},{7,5},{8,10},{9,11},{10,... | collective-permute-start | bytes 430088 | tf_op jit(solution)/shard_map/ppermute | solution.py:361
  8.4 10.8 %collective-permute-start.1 = (bf16[1,40,1792]{2,1,0:T(8,128)(2,1)S(1)}, bf16[1,40,1792]{2,1,0:T(8,128)(2,1)S(1)}, u32[]{:S(2)}, u32[]{:S(2)}) collective-permute-start(bf16[1,40,1792]{2,1,0:T(8,128)(2,1)S(1)} %get-tuple-element.87), channel_id=1, source_target_pairs={{0,1},{1,2},{2,3},{3,0},{4,5},{5,6},{6,7},{7,4},{8,9},{9,10},{10,1... | collective-permute-start | bytes 430088 | tf_op jit(solution)/shard_map/ppermute | solution.py:361
  10.0 14.0 %collective-permute-start.2 = (bf16[1,40,1792]{2,1,0:T(8,128)(2,1)S(1)}, bf16[1,40,1792]{2,1,0:T(8,128)(2,1)S(1)}, u32[]{:S(2)}, u32[]{:S(2)}) collective-permute-start(bf16[1,40,1792]{2,1,0:T(8,128)(2,1)S(1)} %get-tuple-element.88), channel_id=1, source_target_pairs={{0,3},{1,0},{2,1},{3,2},{4,7},{5,4},{6,5},{7,6},{8,11},{9,8},{10,9... | collective-permute-start | bytes 430088 | tf_op jit(solution)/shard_map/ppermute | solution.py:361
  12.3 30.2 %collective-permute-start.8 = (bf16[4,40,1792]{2,1,0:T(8,128)(2,1)S(1)}, bf16[4,40,1792]{2,1,0:T(8,128)(2,1)S(1)}, u32[]{:S(2)}, u32[]{:S(2)}) collective-permute-start(bf16[4,40,1792]{2,1,0:T(8,128)(2,1)S(1)} %get-tuple-element.83), channel_id=1, source_target_pairs={{0,8},{4,12},{8,0},{12,4},{1,9},{5,13},{9,1},{13,5},{2,10},{6,14},... | collective-permute-start | bytes 1720328 | tf_op jit(solution)/shard_map/ppermute | solution.py:357
  19.2 9.4 %collective-permute-start.6 = (bf16[1,40,1792]{2,1,0:T(8,128)(2,1)S(1)}, bf16[1,40,1792]{2,1,0:T(8,128)(2,1)S(1)}, u32[]{:S(2)}, u32[]{:S(2)}) collective-permute-start(bf16[1,40,1792]{2,1,0:T(8,128)(2,1)S(1)} %get-tuple-element.96), channel_id=1, source_target_pairs={{0,1},{1,2},{2,3},{3,0},{4,5},{5,6},{6,7},{7,4},{8,9},{9,10},{10,1... | collective-permute-start | bytes 430088 | tf_op jit(solution)/shard_map/ppermute | solution.py:361
  22.1 10.6 %collective-permute-start.4 = (bf16[1,40,1792]{2,1,0:T(8,128)(2,1)S(1)}, bf16[1,40,1792]{2,1,0:T(8,128)(2,1)S(1)}, u32[]{:S(2)}, u32[]{:S(2)}) collective-permute-start(bf16[1,40,1792]{2,1,0:T(8,128)(2,1)S(1)} %get-tuple-element.92), channel_id=1, source_target_pairs={{0,2},{1,3},{2,0},{3,1},{4,6},{5,7},{6,4},{7,5},{8,10},{9,11},{10,... | collective-permute-start | bytes 430088 | tf_op jit(solution)/shard_map/ppermute | solution.py:361
  24.1 16.7 %collective-permute-start.3 = (bf16[1,40,1792]{2,1,0:T(8,128)(2,1)S(1)}, bf16[1,40,1792]{2,1,0:T(8,128)(2,1)S(1)}, u32[]{:S(2)}, u32[]{:S(2)}) collective-permute-start(bf16[1,40,1792]{2,1,0:T(8,128)(2,1)S(1)} %get-tuple-element.89), channel_id=1, source_target_pairs={{0,3},{1,0},{2,1},{3,2},{4,7},{5,4},{6,5},{7,6},{8,11},{9,8},{10,9... | collective-permute-start | bytes 430088 | tf_op jit(solution)/shard_map/ppermute | solution.py:361
  27.0 13.8 %collective-permute-start.9 = (bf16[3,40,1792]{2,1,0:T(8,128)(2,1)S(1)}, bf16[3,40,1792]{2,1,0:T(8,128)(2,1)S(1)}, u32[]{:S(2)}, u32[]{:S(2)}) collective-permute-start(bf16[3,40,1792]{2,1,0:T(8,128)(2,1)S(1)} %pad_maximum_fusion), channel_id=1, source_target_pairs={{0,8},{4,12},{8,0},{12,4},{1,9},{5,13},{9,1},{13,5},{2,10},{6,14},... | collective-permute-start | bytes 1290248 | tf_op jit(solution)/shard_map/ppermute | solution.py:357
  32.8 12.2 %collective-permute-start.7 = (bf16[1,40,1792]{2,1,0:T(8,128)(2,1)S(1)}, bf16[1,40,1792]{2,1,0:T(8,128)(2,1)S(1)}, u32[]{:S(2)}, u32[]{:S(2)}) collective-permute-start(bf16[1,40,1792]{2,1,0:T(8,128)(2,1)S(1)} %get-tuple-element.97), channel_id=1, source_target_pairs={{0,1},{1,2},{2,3},{3,0},{4,5},{5,6},{6,7},{7,4},{8,9},{9,10},{10,1... | collective-permute-start | bytes 430088 | tf_op jit(solution)/shard_map/ppermute | solution.py:361
  37.4 11.8 %collective-permute-start.5 = (bf16[1,40,1792]{2,1,0:T(8,128)(2,1)S(1)}, bf16[1,40,1792]{2,1,0:T(8,128)(2,1)S(1)}, u32[]{:S(2)}, u32[]{:S(2)}) collective-permute-start(bf16[1,40,1792]{2,1,0:T(8,128)(2,1)S(1)} %get-tuple-element.93), channel_id=1, source_target_pairs={{0,2},{1,3},{2,0},{3,1},{4,6},{5,7},{6,4},{7,5},{8,10},{9,11},{10,... | collective-permute-start | bytes 430088 | tf_op jit(solution)/shard_map/ppermute | solution.py:361
  40.8 8.4 %collective-permute-start.13 = (bf16[1,40,1792]{2,1,0:T(8,128)(2,1)S(1)}, bf16[1,40,1792]{2,1,0:T(8,128)(2,1)S(1)}, u32[]{:S(2)}, u32[]{:S(2)}) collective-permute-start(bf16[1,40,1792]{2,1,0:T(8,128)(2,1)S(1)} %get-tuple-element.104), channel_id=1, source_target_pairs={{0,3},{1,0},{2,1},{3,2},{4,7},{5,4},{6,5},{7,6},{8,11},{9,8},{10,9... | collective-permute-start | bytes 430088 | tf_op jit(solution)/shard_map/ppermute | solution.py:361
  40.9 25.1 %collective-permute-start.17 = (bf16[3,40,1792]{2,1,0:T(8,128)(2,1)S(1)}, bf16[3,40,1792]{2,1,0:T(8,128)(2,1)S(1)}, u32[]{:S(2)}, u32[]{:S(2)}) collective-permute-start(bf16[3,40,1792]{2,1,0:T(8,128)(2,1)S(1)} %pad_maximum_fusion.1), channel_id=1, source_target_pairs={{0,8},{4,12},{8,0},{12,4},{1,9},{5,13},{9,1},{13,5},{2,10},{6,14},... | collective-permute-start | bytes 1290248 | tf_op jit(solution)/shard_map/ppermute | solution.py:357
  42.5 14.3 %copy-start = (bf16[256,192]{1,0:T(8,128)(2,1)S(1)}, bf16[256,192]{1,0:T(8,128)(2,1)}, u32[]{:S(2)}) copy-start(bf16[256,192]{1,0:T(8,128)(2,1)} %constant.8.clone.refs_2_) | copy-start | bytes 294916
  42.5 14.3 %copy-start.1 = (bf16[192,256]{1,0:T(8,128)(2,1)S(1)}, bf16[192,256]{1,0:T(8,128)(2,1)}, u32[]{:S(2)}) copy-start(bf16[192,256]{1,0:T(8,128)(2,1)} %constant.9.clone.refs_3_) | copy-start | bytes 294916
  42.5 8.3 %collective-permute-start.10 = (bf16[8,40,1792]{2,1,0:T(8,128)(2,1)S(1)}, bf16[8,40,1792]{2,1,0:T(8,128)(2,1)S(1)}, u32[]{:S(2)}, u32[]{:S(2)}) collective-permute-start(bf16[8,40,1792]{2,1,0:T(8,128)(2,1)S(1)} %constant_dynamic-update-slice_fusion.refs_0_), channel_id=1, source_target_pairs={{0,4},{4,0},{8,12},{12,8},{1,5},{5,1},{9,13},{13,9},{2,6},{6,2},{1... | collective-permute-start | bytes 3440648 | tf_op jit(solution)/shard_map/ppermute | solution.py:357
  49.3 16.8 %collective-permute-start.16 = (bf16[3,40,1792]{2,1,0:T(8,128)(2,1)S(1)}, bf16[3,40,1792]{2,1,0:T(8,128)(2,1)S(1)}, u32[]{:S(2)}, u32[]{:S(2)}) collective-permute-start(bf16[3,40,1792]{2,1,0:T(8,128)(2,1)S(1)} %get-tuple-element.168), channel_id=1, source_target_pairs={{0,8},{4,12},{8,0},{12,4},{1,9},{5,13},{9,1},{13,5},{2,10},{6,14},... | collective-permute-start | bytes 1290248 | tf_op jit(solution)/shard_map/ppermute | solution.py:357
  50.8 15.3 %collective-permute-start.11 = (bf16[1,40,1792]{2,1,0:T(8,128)(2,1)S(1)}, bf16[1,40,1792]{2,1,0:T(8,128)(2,1)S(1)}, u32[]{:S(2)}, u32[]{:S(2)}) collective-permute-start(bf16[1,40,1792]{2,1,0:T(8,128)(2,1)S(1)} %get-tuple-element.99), channel_id=1, source_target_pairs={{0,1},{1,2},{2,3},{3,0},{4,5},{5,6},{6,7},{7,4},{8,9},{9,10},{10,1... | collective-permute-start | bytes 430088 | tf_op jit(solution)/shard_map/ppermute | solution.py:361
  54.4 11.8 %collective-permute-start.12 = (bf16[1,40,1792]{2,1,0:T(8,128)(2,1)S(1)}, bf16[1,40,1792]{2,1,0:T(8,128)(2,1)S(1)}, u32[]{:S(2)}, u32[]{:S(2)}) collective-permute-start(bf16[1,40,1792]{2,1,0:T(8,128)(2,1)S(1)} %get-tuple-element.101), channel_id=1, source_target_pairs={{0,2},{1,3},{2,0},{3,1},{4,6},{5,7},{6,4},{7,5},{8,10},{9,11},{10,... | collective-permute-start | bytes 430088 | tf_op jit(solution)/shard_map/ppermute | solution.py:361
  54.4 11.8 %collective-permute-start.14 = (bf16[1,40,1792]{2,1,0:T(8,128)(2,1)S(1)}, bf16[1,40,1792]{2,1,0:T(8,128)(2,1)S(1)}, u32[]{:S(2)}, u32[]{:S(2)}) collective-permute-start(bf16[1,40,1792]{2,1,0:T(8,128)(2,1)S(1)} %get-tuple-element.105), channel_id=1, source_target_pairs={{0,3},{1,0},{2,1},{3,2},{4,7},{5,4},{6,5},{7,6},{8,11},{9,8},{10,9... | collective-permute-start | bytes 430088 | tf_op jit(solution)/shard_map/ppermute | solution.py:361
  66.0 2.9 %collective-permute-start.18 = (bf16[8,40,1792]{2,1,0:T(8,128)(2,1)S(1)}, bf16[8,40,1792]{2,1,0:T(8,128)(2,1)S(1)}, u32[]{:S(2)}, u32[]{:S(2)}) collective-permute-start(bf16[8,40,1792]{2,1,0:T(8,128)(2,1)S(1)} %get-tuple-element.110), channel_id=1, source_target_pairs={{0,4},{4,0},{8,12},{12,8},{1,5},{5,1},{9,13},{13,9},{2,6},{6,2},{1... | collective-permute-start | bytes 3440648 | tf_op jit(solution)/shard_map/ppermute | solution.py:357
  66.3 4.2 %collective-permute-start.19 = (bf16[8,40,1792]{2,1,0:T(8,128)(2,1)S(1)}, bf16[8,40,1792]{2,1,0:T(8,128)(2,1)S(1)}, u32[]{:S(2)}, u32[]{:S(2)}) collective-permute-start(bf16[8,40,1792]{2,1,0:T(8,128)(2,1)S(1)} %constant_dynamic-update-slice_fusion.10.refs_0_), channel_id=1, source_target_pairs={{0,4},{4,0},{8,12},{12,8},{1,5},{5,1},{9,13},{13,9},{2,6},{6,2},{1... | collective-permute-start | bytes 3440648 | tf_op jit(solution)/shard_map/ppermute | solution.py:357
  66.9 13.0 %collective-permute-start.15 = (bf16[3,40,1792]{2,1,0:T(8,128)(2,1)S(1)}, bf16[3,40,1792]{2,1,0:T(8,128)(2,1)S(1)}, u32[]{:S(2)}, u32[]{:S(2)}) collective-permute-start(bf16[3,40,1792]{2,1,0:T(8,128)(2,1)S(1)} %get-tuple-element.174), channel_id=1, source_target_pairs={{0,8},{4,12},{8,0},{12,4},{1,9},{5,13},{9,1},{13,5},{2,10},{6,14},... | collective-permute-start | bytes 1290248 | tf_op jit(solution)/shard_map/ppermute | solution.py:357
  79.9 2.9 %collective-permute-start.20 = (bf16[8,40,1792]{2,1,0:T(8,128)(2,1)S(1)}, bf16[8,40,1792]{2,1,0:T(8,128)(2,1)S(1)}, u32[]{:S(2)}, u32[]{:S(2)}) collective-permute-start(bf16[8,40,1792]{2,1,0:T(8,128)(2,1)S(1)} %get-tuple-element.116), channel_id=1, source_target_pairs={{0,4},{4,0},{8,12},{12,8},{1,5},{5,1},{9,13},{13,9},{2,6},{6,2},{1... | collective-permute-start | bytes 3440648 | tf_op jit(solution)/shard_map/ppermute | solution.py:357
  80.2 4.3 %collective-permute-start.21 = (bf16[8,40,1792]{2,1,0:T(8,128)(2,1)S(1)}, bf16[8,40,1792]{2,1,0:T(8,128)(2,1)S(1)}, u32[]{:S(2)}, u32[]{:S(2)}) collective-permute-start(bf16[8,40,1792]{2,1,0:T(8,128)(2,1)S(1)} %constant_dynamic-update-slice_fusion.14.refs_0_), channel_id=1, source_target_pairs={{0,4},{4,0},{8,12},{12,8},{1,5},{5,1},{9,13},{13,9},{2,6},{6,2},{1... | collective-permute-start | bytes 3440648 | tf_op jit(solution)/shard_map/ppermute | solution.py:357
  80.6 15.0 %collective-permute-start.22 = (bf16[4,40,1792]{2,1,0:T(8,128)(2,1)S(1)}, bf16[4,40,1792]{2,1,0:T(8,128)(2,1)S(1)}, u32[]{:S(2)}, u32[]{:S(2)}) collective-permute-start(bf16[4,40,1792]{2,1,0:T(8,128)(2,1)S(1)} %get-tuple-element.111), channel_id=1, source_target_pairs={{0,8},{4,12},{8,0},{12,4},{1,9},{5,13},{9,1},{13,5},{2,10},{6,14},... | collective-permute-start | bytes 1720328 | tf_op jit(solution)/shard_map/ppermute | solution.py:357
  95.6 3.9 %collective-permute-start.23 = (bf16[8,40,1792]{2,1,0:T(8,128)(2,1)S(1)}, bf16[8,40,1792]{2,1,0:T(8,128)(2,1)S(1)}, u32[]{:S(2)}, u32[]{:S(2)}) collective-permute-start(bf16[8,40,1792]{2,1,0:T(8,128)(2,1)S(1)} %get-tuple-element.122), channel_id=1, source_target_pairs={{0,4},{4,0},{8,12},{12,8},{1,5},{5,1},{9,13},{13,9},{2,6},{6,2},{1... | collective-permute-start | bytes 3440648 | tf_op jit(solution)/shard_map/ppermute | solution.py:357
  95.6 4.4 %collective-permute-start.24 = (bf16[8,40,1792]{2,1,0:T(8,128)(2,1)S(1)}, bf16[8,40,1792]{2,1,0:T(8,128)(2,1)S(1)}, u32[]{:S(2)}, u32[]{:S(2)}) collective-permute-start(bf16[8,40,1792]{2,1,0:T(8,128)(2,1)S(1)} %constant_dynamic-update-slice_fusion.18.refs_0_), channel_id=1, source_target_pairs={{0,4},{4,0},{8,12},{12,8},{1,5},{5,1},{9,13},{13,9},{2,6},{6,2},{1... | collective-permute-start | bytes 3440648 | tf_op jit(solution)/shard_map/ppermute | solution.py:357
  96.2 15.0 %collective-permute-start.28 = (bf16[4,40,1792]{2,1,0:T(8,128)(2,1)S(1)}, bf16[4,40,1792]{2,1,0:T(8,128)(2,1)S(1)}, u32[]{:S(2)}, u32[]{:S(2)}) collective-permute-start(bf16[4,40,1792]{2,1,0:T(8,128)(2,1)S(1)} %get-tuple-element.117), channel_id=1, source_target_pairs={{0,8},{4,12},{8,0},{12,4},{1,9},{5,13},{9,1},{13,5},{2,10},{6,14},... | collective-permute-start | bytes 1720328 | tf_op jit(solution)/shard_map/ppermute | solution.py:357
  96.9 12.8 %collective-permute-start.25 = (bf16[1,40,1792]{2,1,0:T(8,128)(2,1)S(1)}, bf16[1,40,1792]{2,1,0:T(8,128)(2,1)S(1)}, u32[]{:S(2)}, u32[]{:S(2)}) collective-permute-start(bf16[1,40,1792]{2,1,0:T(8,128)(2,1)S(1)} %get-tuple-element.132), channel_id=1, source_target_pairs={{0,2},{1,3},{2,0},{3,1},{4,6},{5,7},{6,4},{7,5},{8,10},{9,11},{10,... | collective-permute-start | bytes 430088 | tf_op jit(solution)/shard_map/ppermute | solution.py:361
  97.5 12.3 %collective-permute-start.26 = (bf16[1,40,1792]{2,1,0:T(8,128)(2,1)S(1)}, bf16[1,40,1792]{2,1,0:T(8,128)(2,1)S(1)}, u32[]{:S(2)}, u32[]{:S(2)}) collective-permute-start(bf16[1,40,1792]{2,1,0:T(8,128)(2,1)S(1)} %get-tuple-element.133), channel_id=1, source_target_pairs={{0,3},{1,0},{2,1},{3,2},{4,7},{5,4},{6,5},{7,6},{8,11},{9,8},{10,9... | collective-permute-start | bytes 430088 | tf_op jit(solution)/shard_map/ppermute | solution.py:361
  99.6 10.2 %collective-permute-start.27 = (bf16[1,40,1792]{2,1,0:T(8,128)(2,1)S(1)}, bf16[1,40,1792]{2,1,0:T(8,128)(2,1)S(1)}, u32[]{:S(2)}, u32[]{:S(2)}) collective-permute-start(bf16[1,40,1792]{2,1,0:T(8,128)(2,1)S(1)} %get-tuple-element.134), channel_id=1, source_target_pairs={{0,1},{1,2},{2,3},{3,0},{4,5},{5,6},{6,7},{7,4},{8,9},{9,10},{10,1... | collective-permute-start | bytes 430088 | tf_op jit(solution)/shard_map/ppermute | solution.py:361
  111.2 2.8 %collective-permute-start.29 = (bf16[8,40,1792]{2,1,0:T(8,128)(2,1)S(1)}, bf16[8,40,1792]{2,1,0:T(8,128)(2,1)S(1)}, u32[]{:S(2)}, u32[]{:S(2)}) collective-permute-start(bf16[8,40,1792]{2,1,0:T(8,128)(2,1)S(1)} %get-tuple-element.135), channel_id=1, source_target_pairs={{0,4},{4,0},{8,12},{12,8},{1,5},{5,1},{9,13},{13,9},{2,6},{6,2},{1... | collective-permute-start | bytes 3440648 | tf_op jit(solution)/shard_map/ppermute | solution.py:357
  111.2 15.8 %collective-permute-start.32 = (bf16[4,40,1792]{2,1,0:T(8,128)(2,1)S(1)}, bf16[4,40,1792]{2,1,0:T(8,128)(2,1)S(1)}, u32[]{:S(2)}, u32[]{:S(2)}) collective-permute-start(bf16[4,40,1792]{2,1,0:T(8,128)(2,1)S(1)} %get-tuple-element.123), channel_id=1, source_target_pairs={{0,8},{4,12},{8,0},{12,4},{1,9},{5,13},{9,1},{13,5},{2,10},{6,14},... | collective-permute-start | bytes 1720328 | tf_op jit(solution)/shard_map/ppermute | solution.py:357
  114.2 24.6 %collective-permute-start.30 = (bf16[4,40,1792]{2,1,0:T(8,128)(2,1)S(1)}, bf16[4,40,1792]{2,1,0:T(8,128)(2,1)S(1)}, u32[]{:S(2)}, u32[]{:S(2)}) collective-permute-start(bf16[4,40,1792]{2,1,0:T(8,128)(2,1)S(1)} %get-tuple-element.137), channel_id=1, source_target_pairs={{0,8},{4,12},{8,0},{12,4},{1,9},{5,13},{9,1},{13,5},{2,10},{6,14},... | collective-permute-start | bytes 1720328 | tf_op jit(solution)/shard_map/ppermute | solution.py:357
  115.0 12.1 %collective-permute-start.33 = (bf16[1,40,1792]{2,1,0:T(8,128)(2,1)S(1)}, bf16[1,40,1792]{2,1,0:T(8,128)(2,1)S(1)}, u32[]{:S(2)}, u32[]{:S(2)}) collective-permute-start(bf16[1,40,1792]{2,1,0:T(8,128)(2,1)S(1)} %get-tuple-element.146), channel_id=1, source_target_pairs={{0,2},{1,3},{2,0},{3,1},{4,6},{5,7},{6,4},{7,5},{8,10},{9,11},{10,... | collective-permute-start | bytes 430088 | tf_op jit(solution)/shard_map/ppermute | solution.py:361
  117.9 11.2 %collective-permute-start.35 = (bf16[1,40,1792]{2,1,0:T(8,128)(2,1)S(1)}, bf16[1,40,1792]{2,1,0:T(8,128)(2,1)S(1)}, u32[]{:S(2)}, u32[]{:S(2)}) collective-permute-start(bf16[1,40,1792]{2,1,0:T(8,128)(2,1)S(1)} %get-tuple-element.150), channel_id=1, source_target_pairs={{0,3},{1,0},{2,1},{3,2},{4,7},{5,4},{6,5},{7,6},{8,11},{9,8},{10,9... | collective-permute-start | bytes 430088 | tf_op jit(solution)/shard_map/ppermute | solution.py:361
  120.0 11.5 %collective-permute-start.31 = (bf16[1,40,1792]{2,1,0:T(8,128)(2,1)S(1)}, bf16[1,40,1792]{2,1,0:T(8,128)(2,1)S(1)}, u32[]{:S(2)}, u32[]{:S(2)}) collective-permute-start(bf16[1,40,1792]{2,1,0:T(8,128)(2,1)S(1)} %get-tuple-element.142), channel_id=1, source_target_pairs={{0,1},{1,2},{2,3},{3,0},{4,5},{5,6},{6,7},{7,4},{8,9},{9,10},{10,1... | collective-permute-start | bytes 430088 | tf_op jit(solution)/shard_map/ppermute | solution.py:361
  127.0 18.3 %copy-start.4 = (s32[64,2]{0,1:T(2,128)S(1)}, s32[64,2]{0,1:T(2,128)}, u32[]{:S(2)}) copy-start(s32[64,2]{0,1:T(2,128)} %param.9) | copy-start | bytes 1540
  127.0 18.3 %copy-start.5 = (f32[64,2]{0,1:T(2,128)S(1)}, f32[64,2]{0,1:T(2,128)}, u32[]{:S(2)}) copy-start(f32[64,2]{0,1:T(2,128)} %param.10) | copy-start | bytes 1540
  127.1 13.9 %collective-permute-start.34 = (bf16[1,40,1792]{2,1,0:T(8,128)(2,1)S(1)}, bf16[1,40,1792]{2,1,0:T(8,128)(2,1)S(1)}, u32[]{:S(2)}, u32[]{:S(2)}) collective-permute-start(bf16[1,40,1792]{2,1,0:T(8,128)(2,1)S(1)} %get-tuple-element.147), channel_id=1, source_target_pairs={{0,2},{1,3},{2,0},{3,1},{4,6},{5,7},{6,4},{7,5},{8,10},{9,11},{10,... | collective-permute-start | bytes 430088 | tf_op jit(solution)/shard_map/ppermute | solution.py:361
  129.1 12.3 %collective-permute-start.36 = (bf16[1,40,1792]{2,1,0:T(8,128)(2,1)S(1)}, bf16[1,40,1792]{2,1,0:T(8,128)(2,1)S(1)}, u32[]{:S(2)}, u32[]{:S(2)}) collective-permute-start(bf16[1,40,1792]{2,1,0:T(8,128)(2,1)S(1)} %get-tuple-element.151), channel_id=1, source_target_pairs={{0,3},{1,0},{2,1},{3,2},{4,7},{5,4},{6,5},{7,6},{8,11},{9,8},{10,9... | collective-permute-start | bytes 430088 | tf_op jit(solution)/shard_map/ppermute | solution.py:361
  131.5 13.7 %collective-permute-start.39 = (bf16[1,40,1792]{2,1,0:T(8,128)(2,1)S(1)}, bf16[1,40,1792]{2,1,0:T(8,128)(2,1)S(1)}, u32[]{:S(2)}, u32[]{:S(2)}) collective-permute-start(bf16[1,40,1792]{2,1,0:T(8,128)(2,1)S(1)} %get-tuple-element.157), channel_id=1, source_target_pairs={{0,1},{1,2},{2,3},{3,0},{4,5},{5,6},{6,7},{7,4},{8,9},{9,10},{10,1... | collective-permute-start | bytes 430088 | tf_op jit(solution)/shard_map/ppermute | solution.py:361
  141.4 6.6 %collective-permute-start.37 = (bf16[1,40,1792]{2,1,0:T(8,128)(2,1)S(1)}, bf16[1,40,1792]{2,1,0:T(8,128)(2,1)S(1)}, u32[]{:S(2)}, u32[]{:S(2)}) collective-permute-start(bf16[1,40,1792]{2,1,0:T(8,128)(2,1)S(1)} %get-tuple-element.152), channel_id=1, source_target_pairs={{0,3},{1,0},{2,1},{3,2},{4,7},{5,4},{6,5},{7,6},{8,11},{9,8},{10,9... | collective-permute-start | bytes 430088 | tf_op jit(solution)/shard_map/ppermute | solution.py:361
  143.8 13.5 %collective-permute-start.38 = (bf16[1,40,1792]{2,1,0:T(8,128)(2,1)S(1)}, bf16[1,40,1792]{2,1,0:T(8,128)(2,1)S(1)}, u32[]{:S(2)}, u32[]{:S(2)}) collective-permute-start(bf16[1,40,1792]{2,1,0:T(8,128)(2,1)S(1)} %get-tuple-element.154), channel_id=1, source_target_pairs={{0,2},{1,3},{2,0},{3,1},{4,6},{5,7},{6,4},{7,5},{8,10},{9,11},{10,... | collective-permute-start | bytes 430088 | tf_op jit(solution)/shard_map/ppermute | solution.py:361
  145.2 12.1 %collective-permute-start.40 = (bf16[1,40,1792]{2,1,0:T(8,128)(2,1)S(1)}, bf16[1,40,1792]{2,1,0:T(8,128)(2,1)S(1)}, u32[]{:S(2)}, u32[]{:S(2)}) collective-permute-start(bf16[1,40,1792]{2,1,0:T(8,128)(2,1)S(1)} %get-tuple-element.158), channel_id=1, source_target_pairs={{0,1},{1,2},{2,3},{3,0},{4,5},{5,6},{6,7},{7,4},{8,9},{9,10},{10,1... | collective-permute-start | bytes 430088 | tf_op jit(solution)/shard_map/ppermute | solution.py:361
